TPU v7x, 32 devices: a whole 2x2x4 slice. The times are simulated.
32 devices in a mesh: dp: 4 (over x, core), blk: 8 (over z, y).
Axes of the slice: x: 2, y: 2, z: 4, core: 2. Of those that a mesh axis runs over, the one named last changes fastest.
Arguments:
- x_a: bfloat16 [8, 4096, 512], P('dp', 'blk'), may hold values from -6 to 6
- x_b: bfloat16 [16, 2048, 512], P('dp', 'blk'), may hold values from -6 to 6
- sel_a: int32 [8, 64], P('dp', 'blk'), may hold values from 0 to 63, as said below
- sel_b: int32 [16, 64], P('dp', 'blk'), may hold values from 0 to 63, as said below
- gain_one: bfloat16 [512], replicated, may hold values from 0.099609375 to 1.8984375
- w_qkv: bfloat16 [512, 1536], replicated, may hold values from -0.25 to 0.25
- w_out: bfloat16 [512, 512], replicated, may hold values from -2 to 2
- w_sort: bfloat16 [512, 64], replicated, may hold values from -0.125 to 0.125
- gain_two: bfloat16 [512], replicated, may hold values from 0.099609375 to 1.8984375
- w_up: bfloat16 [512, 2048], replicated, may hold values from -0.25 to 0.25
- w_down: bfloat16 [2048, 512], replicated, may hold values from -0.125 to 0.125
- cot_a: bfloat16 [8, 4096, 512], P('dp', 'blk'), may hold values from -6 to 6
- cot_b: bfloat16 [16, 2048, 512], P('dp', 'blk'), may hold values from -6 to 6
Outputs:
- out_a: bfloat16 [8, 4096, 512], P('dp', 'blk')
- out_b: bfloat16 [16, 2048, 512], P('dp', 'blk')
- grad_x_a: bfloat16 [8, 4096, 512], P('dp', 'blk')
- grad_x_b: bfloat16 [16, 2048, 512], P('dp', 'blk')
- grad_gain_one: float32 [512], replicated
- grad_qkv: float32 [512, 1536], replicated
- grad_w_out: float32 [512, 512], replicated
- grad_sort: float32 [512, 64], replicated
- grad_gain_two: float32 [512], replicated
- grad_up: float32 [512, 2048], replicated
- grad_down: float32 [2048, 512], replicated
Inputs may be any that keep to these rules, and one draw needn't show every extreme that they name: `sel_a`: each entry is the block of the same sequence chosen as keys for that query block. Counting a chosen block of x_a as two units and one of x_b as one, the query blocks held by one device of blk choose at most 14 units among the blocks held by any one device of blk (block k is held by device k // 8), and in every draw exactly 14 from some device. `sel_b`: as for sel_a, the two counted together.
All inputs are finite; a program needn't handle non-finite values.
Results may differ from a plain program's by a relative error of at most 0.014.
Values may be sent and summed in bfloat16 or wider, within the bound.
No kernel may reach another device: no remote copies, remote signals or barrier semaphores. Data moves between devices by JAX's collectives and lax.ppermute only.
A program may use at most 320 MiB of HBM per device.

v0:
```python
import jax
import jax.numpy as jnp
from jax import lax
from jax.sharding import PartitionSpec as P

HEADS = 8
SINK_ITERS = 8


EPSILON = 1e-05
SOFTMAX_HEAT = 0.75
PRECISE = lax.Precision.HIGHEST


def normalize(values, gain_row):
    inverse = lax.rsqrt(jnp.mean(values * values, axis=-1, keepdims=True) + EPSILON)
    return (values * inverse * gain_row, inverse)


def normalize_back(values, inverse, gain_row, upstream):
    scaled = upstream * gain_row
    gain_grad = jnp.sum(upstream * values * inverse, axis=0)
    inner = jnp.mean(scaled * values, axis=-1, keepdims=True)
    return (inverse * (scaled - values * inverse * inverse * inner), gain_grad)


def doubly_stochastic_normalizer(unscaled_ranking_affinity):
    for repeat in range(SINK_ITERS):
        unscaled_ranking_affinity = unscaled_ranking_affinity - jax.nn.logsumexp(
            unscaled_ranking_affinity, axis=-1, keepdims=True
        )
        unscaled_ranking_affinity = unscaled_ranking_affinity - jax.nn.logsumexp(
            unscaled_ranking_affinity, axis=-2, keepdims=True
        )
    return jnp.exp(unscaled_ranking_affinity)


def contract_rows(left_side, right_side):
    return lax.dot_general(
        left_side, right_side, (((0,), (0,)), ((), ())), preferred_element_type=jnp.float32
    )


def times_transpose(left_side, right_side):
    return lax.dot_general(
        left_side, right_side, (((1,), (1,)), ((), ())), preferred_element_type=jnp.float32
    )


def split_heads(matrix, block_size):
    return matrix.reshape(-1, block_size, HEADS, matrix.shape[-1] // HEADS)


def attend_scores(queries, keys_near, keys_far, head_scale):
    near_scores = (
        jnp.einsum("nqhd,nkhd->nhqk", queries, keys_near, preferred_element_type=jnp.float32)
        * head_scale
    )
    far_scores = (
        jnp.einsum("nqhd,nkhd->nhqk", queries, keys_far, preferred_element_type=jnp.float32)
        * head_scale
    )
    return jnp.concatenate([near_scores, far_scores], axis=-1)


def attend(queries, keys_near, values_near, keys_far, values_far, weights, head_scale):
    scores = attend_scores(queries, keys_near, keys_far, head_scale)
    highest = jnp.max(scores, axis=-1, keepdims=True)
    log_total = highest + jnp.log(jnp.sum(jnp.exp(scores - highest), axis=-1, keepdims=True))
    probabilities = jnp.exp(scores - log_total).astype(jnp.bfloat16)
    block_size = queries.shape[1]
    near_out = jnp.einsum(
        "nhqk,nkhd->nqhd",
        probabilities[..., :block_size],
        values_near,
        preferred_element_type=jnp.float32,
    )
    far_out = jnp.einsum(
        "nhqk,nkhd->nqhd",
        probabilities[..., block_size:],
        values_far,
        preferred_element_type=jnp.float32,
    )
    mixture = near_out + weights[:, None, None, None] * far_out
    return (mixture, log_total, far_out)


def attend_back(
    queries,
    keys_near,
    values_near,
    keys_far,
    values_far,
    weights,
    head_scale,
    log_total,
    far_out,
    upstream,
):
    block_size = queries.shape[1]
    scores = attend_scores(queries, keys_near, keys_far, head_scale)
    probabilities = jnp.exp(scores - log_total)
    rounded = probabilities.astype(jnp.bfloat16)
    near_dp = jnp.einsum(
        "nqhd,nkhd->nhqk", upstream, values_near, preferred_element_type=jnp.float32
    )
    far_dp = (
        jnp.einsum("nqhd,nkhd->nhqk", upstream, values_far, preferred_element_type=jnp.float32)
        * weights[:, None, None, None]
    )
    prob_grad = jnp.concatenate([near_dp, far_dp], axis=-1)
    dscore = (
        probabilities * (prob_grad - jnp.sum(probabilities * prob_grad, axis=-1, keepdims=True))
    ).astype(jnp.bfloat16)
    near_ds = dscore[..., :block_size]
    far_ds = dscore[..., block_size:]
    query_grad = (
        jnp.einsum("nhqk,nkhd->nqhd", near_ds, keys_near, preferred_element_type=jnp.float32)
        + jnp.einsum("nhqk,nkhd->nqhd", far_ds, keys_far, preferred_element_type=jnp.float32)
    ) * head_scale
    key_near_grad = (
        jnp.einsum("nhqk,nqhd->nkhd", near_ds, queries, preferred_element_type=jnp.float32)
        * head_scale
    )
    key_far_grad = (
        jnp.einsum("nhqk,nqhd->nkhd", far_ds, queries, preferred_element_type=jnp.float32)
        * head_scale
    )
    value_near_grad = jnp.einsum(
        "nhqk,nqhd->nkhd", rounded[..., :block_size], upstream, preferred_element_type=jnp.float32
    )
    value_far_grad = (
        jnp.einsum(
            "nhqk,nqhd->nkhd",
            rounded[..., block_size:],
            upstream,
            preferred_element_type=jnp.float32,
        )
        * weights[:, None, None, None]
    )
    weight_grad = jnp.sum(upstream.astype(jnp.float32) * far_out, axis=(1, 2, 3))
    return (query_grad, key_near_grad, key_far_grad, value_near_grad, value_far_grad, weight_grad)


def per_device(
    x_a, x_b, sel_a, sel_b, gain_one, w_qkv, w_out, w_sort, gain_two, w_up, w_down, cot_a, cot_b
):
    devices = lax.axis_size("blk")
    self_position = lax.axis_index("blk")
    seqs_a, rows_a, features = x_a.shape
    seqs_b, rows_b = (x_b.shape[0], x_b.shape[1])
    per_shard_rows = sel_a.shape[1]
    block_count = per_shard_rows * devices
    length_left = rows_a // per_shard_rows
    length_right = rows_b // per_shard_rows
    units_a = seqs_a * per_shard_rows * 2
    units_b = seqs_b * per_shard_rows
    unit_count = units_a + units_b
    capacity = 2 * max(1, (4 * unit_count + 5 * devices - 1) // (5 * devices))
    head_scale = (features // HEADS) ** (-0.5)
    total_a = seqs_a * rows_a
    pair_width = 2 * features
    inputs = jnp.concatenate([x_a.reshape(-1, features), x_b.reshape(-1, features)], axis=0).astype(
        jnp.float32
    )
    gain_first = gain_one.astype(jnp.float32)
    gain_second = gain_two.astype(jnp.float32)
    normed, inverse_one = normalize(inputs, gain_first)
    normed_low = normed.astype(jnp.bfloat16)
    projected = jnp.dot(normed_low, w_qkv, preferred_element_type=jnp.float32).astype(jnp.bfloat16)

    def sort_logits(summary):
        inverse = lax.rsqrt(jnp.mean(summary * summary, axis=-1, keepdims=True) + EPSILON)
        unit_vec = (summary * inverse).astype(jnp.bfloat16)
        unscaled_ranking_affinity = (
            jnp.einsum("spd,dk->spk", unit_vec, w_sort, preferred_element_type=jnp.float32)
            / SOFTMAX_HEAT
        )
        return (unscaled_ranking_affinity, unit_vec, inverse)

    pooled_digest_left = jnp.mean(
        normed[:total_a].reshape(seqs_a, per_shard_rows, length_left, features), axis=2
    )
    pooled_digest_right = jnp.mean(
        normed[total_a:].reshape(seqs_b, per_shard_rows, length_right, features), axis=2
    )
    logits_a, member_left, undo_order_left = sort_logits(pooled_digest_left)
    logits_b, member_right, undo_order_right = sort_logits(pooled_digest_right)
    finished_left_plan, finished_right_plan = (
        lax.all_gather(logits_a, "blk", axis=1, tiled=True),
        lax.all_gather(logits_b, "blk", axis=1, tiled=True),
    )
    chosen_a, chosen_b = (
        lax.all_gather(sel_a, "blk", axis=1, tiled=True),
        lax.all_gather(sel_b, "blk", axis=1, tiled=True),
    )
    group_transport_left, normalizer_backprop_left = jax.vjp(
        doubly_stochastic_normalizer, finished_left_plan
    )
    group_transport_right, normalizer_backprop_right = jax.vjp(
        doubly_stochastic_normalizer, finished_right_plan
    )
    columns = jnp.arange(block_count, dtype=jnp.int32)
    indicator_left = (chosen_a[..., None] == columns).astype(jnp.float32)
    indicator_right = (chosen_b[..., None] == columns).astype(jnp.float32)
    own_a = lax.dynamic_slice_in_dim(
        group_transport_left * indicator_left, self_position * per_shard_rows, per_shard_rows, 1
    )
    own_b = lax.dynamic_slice_in_dim(
        group_transport_right * indicator_right, self_position * per_shard_rows, per_shard_rows, 1
    )
    weights_a = block_count * jnp.sum(own_a, axis=-1).reshape(-1)
    weights_b = block_count * jnp.sum(own_b, axis=-1).reshape(-1)
    grouped_a = chosen_a.reshape(seqs_a, devices, per_shard_rows).transpose(1, 0, 2)
    grouped_b = chosen_b.reshape(seqs_b, devices, per_shard_rows).transpose(1, 0, 2)
    halves = jnp.arange(2, dtype=jnp.int32)
    source_a = jnp.broadcast_to(
        (grouped_a // per_shard_rows)[..., None], grouped_a.shape + (2,)
    ).reshape(devices, units_a)
    base_a = (
        jnp.arange(seqs_a, dtype=jnp.int32)[None, :, None] * per_shard_rows
        + grouped_a % per_shard_rows
    ) * 2
    local_a = (base_a[..., None] + halves).reshape(devices, units_a)
    source_b = (grouped_b // per_shard_rows).reshape(devices, units_b)
    local_b = (
        units_a
        + jnp.arange(seqs_b, dtype=jnp.int32)[None, :, None] * per_shard_rows
        + grouped_b % per_shard_rows
    ).reshape(devices, units_b)
    sources = jnp.concatenate([source_a, source_b], axis=1)
    local_index = jnp.concatenate([local_a, local_b], axis=1)
    same_source = sources[:, :, None] == sources[:, None, :]
    earlier = jnp.arange(unit_count)[None, :] < jnp.arange(unit_count)[:, None]
    slot_rank = jnp.sum(same_source & earlier[None], axis=2)
    slot_ids = jnp.arange(capacity, dtype=jnp.int32)
    matches = (sources == self_position)[:, None, :] & (
        slot_rank[:, None, :] == slot_ids[None, :, None]
    )
    send_index = (
        jnp.sum(jnp.where(matches, local_index[:, None, :], 0), axis=2)
        + jnp.where(jnp.any(matches, axis=2), 0, unit_count)
    ).reshape(-1)
    my_sources = lax.dynamic_index_in_dim(sources, self_position, 0, keepdims=False)
    my_ranks = lax.dynamic_index_in_dim(slot_rank, self_position, 0, keepdims=False)
    receive_index = my_sources * capacity + my_ranks
    keys_values = projected[:, features:]

    def outgoing_blocks():
        pieces = jnp.concatenate(
            [
                keys_values[:total_a].reshape(units_a, length_right, pair_width),
                keys_values[total_a:].reshape(units_b, length_right, pair_width),
                jnp.zeros((1, length_right, pair_width), jnp.bfloat16),
            ],
            axis=0,
        )
        return jnp.take(pieces, send_index, axis=0).reshape(
            devices, capacity, length_right, pair_width
        )

    def arrange(arrived):
        remote = jnp.take(
            arrived.reshape(devices * capacity, length_right, pair_width), receive_index, axis=0
        )
        far_a = remote[:units_a].reshape(seqs_a * per_shard_rows, length_left, pair_width)
        far_b = remote[units_a:]
        return (
            split_heads(far_a[..., :features], length_left),
            split_heads(far_a[..., features:], length_left),
            split_heads(far_b[..., :features], length_right),
            split_heads(far_b[..., features:], length_right),
        )

    far_keys_a, far_values_a, far_keys_b, far_values_b = arrange(
        lax.all_to_all(outgoing_blocks(), "blk", split_axis=0, concat_axis=0, tiled=True)
    )
    queries_a = split_heads(projected[:total_a, :features], length_left)
    keys_a = split_heads(projected[:total_a, features:pair_width], length_left)
    values_a = split_heads(projected[:total_a, pair_width:], length_left)
    queries_b = split_heads(projected[total_a:, :features], length_right)
    keys_b = split_heads(projected[total_a:, features:pair_width], length_right)
    values_b = split_heads(projected[total_a:, pair_width:], length_right)
    mixture_a, log_total_a, far_out_a = attend(
        queries_a, keys_a, values_a, far_keys_a, far_values_a, weights_a, head_scale
    )
    mixture_b, log_total_b, far_out_b = attend(
        queries_b, keys_b, values_b, far_keys_b, far_values_b, weights_b, head_scale
    )
    attended = jnp.concatenate(
        [mixture_a.reshape(-1, features), mixture_b.reshape(-1, features)], axis=0
    ).astype(jnp.bfloat16)
    middle = inputs + jnp.dot(attended, w_out, preferred_element_type=jnp.float32)
    normed_two, inverse_two = normalize(middle, gain_second)
    second_low = normed_two.astype(jnp.bfloat16)
    hidden = jnp.dot(second_low, w_up, preferred_element_type=jnp.float32)
    active, gelu_back = jax.vjp(jax.nn.gelu, hidden)
    active_low = active.astype(jnp.bfloat16)
    result = middle + jnp.dot(active_low, w_down, preferred_element_type=jnp.float32)
    out_a = result[:total_a].reshape(x_a.shape).astype(jnp.bfloat16)
    out_b = result[total_a:].reshape(x_b.shape).astype(jnp.bfloat16)
    upstream = jnp.concatenate([cot_a.reshape(-1, features), cot_b.reshape(-1, features)], axis=0)
    grad_down = contract_rows(active_low, upstream)
    grad_active = times_transpose(upstream, w_down)
    grad_hidden = gelu_back(grad_active)[0].astype(jnp.bfloat16)
    grad_up = contract_rows(second_low, grad_hidden)
    grad_second = times_transpose(grad_hidden, w_up)
    middle_part, grad_gain_two = normalize_back(middle, inverse_two, gain_second, grad_second)
    grad_middle = upstream.astype(jnp.float32) + middle_part
    grad_branch = grad_middle.astype(jnp.bfloat16)
    grad_w_out = contract_rows(attended, grad_branch)
    grad_attended = times_transpose(grad_branch, w_out).astype(jnp.bfloat16)
    far_keys_a, far_values_a, far_keys_b, far_values_b = arrange(
        lax.all_to_all(outgoing_blocks(), "blk", split_axis=0, concat_axis=0, tiled=True)
    )
    back_a = attend_back(
        queries_a,
        keys_a,
        values_a,
        far_keys_a,
        far_values_a,
        weights_a,
        head_scale,
        log_total_a,
        far_out_a,
        split_heads(grad_attended[:total_a], length_left),
    )
    back_b = attend_back(
        queries_b,
        keys_b,
        values_b,
        far_keys_b,
        far_values_b,
        weights_b,
        head_scale,
        log_total_b,
        far_out_b,
        split_heads(grad_attended[total_a:], length_right),
    )
    far_grad_a = jnp.concatenate(
        [
            back_a[2].reshape(-1, length_left, features),
            back_a[4].reshape(-1, length_left, features),
        ],
        axis=-1,
    )
    far_grad_b = jnp.concatenate(
        [
            back_b[2].reshape(-1, length_right, features),
            back_b[4].reshape(-1, length_right, features),
        ],
        axis=-1,
    )
    unit_grads = jnp.concatenate(
        [far_grad_a.reshape(units_a, length_right, pair_width), far_grad_b], axis=0
    )
    placed = (
        jnp.zeros((devices * capacity, length_right, pair_width), jnp.float32)
        .at[receive_index]
        .set(unit_grads)
    )
    returned = lax.all_to_all(
        placed.reshape(devices, capacity, length_right, pair_width).astype(jnp.bfloat16),
        "blk",
        split_axis=0,
        concat_axis=0,
        tiled=True,
    ).astype(jnp.float32)
    summed = jax.ops.segment_sum(
        returned.reshape(-1, length_right, pair_width), send_index, num_segments=unit_count + 1
    )[:unit_count]
    remote_grad = summed.reshape(-1, pair_width)
    near_grad = jnp.concatenate(
        [
            jnp.concatenate(
                [back_a[1].reshape(-1, features), back_a[3].reshape(-1, features)], axis=-1
            ),
            jnp.concatenate(
                [back_b[1].reshape(-1, features), back_b[3].reshape(-1, features)], axis=-1
            ),
        ],
        axis=0,
    )
    query_grad = jnp.concatenate(
        [back_a[0].reshape(-1, features), back_b[0].reshape(-1, features)], axis=0
    )
    grad_projected = jnp.concatenate([query_grad, near_grad + remote_grad], axis=-1).astype(
        jnp.bfloat16
    )
    entire_coupling_left, entire_coupling_right = (
        lax.all_gather(back_a[5].reshape(seqs_a, per_shard_rows), "blk", axis=1, tiled=True),
        lax.all_gather(back_b[5].reshape(seqs_b, per_shard_rows), "blk", axis=1, tiled=True),
    )

    def sort_back(sink_back, onehot, all_weight, unit_vec, summary, inverse, block_size):
        logit_gradient = sink_back(block_count * onehot * all_weight[..., None])[0]
        own_rows = (
            lax.dynamic_slice_in_dim(
                logit_gradient, self_position * per_shard_rows, per_shard_rows, 1
            )
            / SOFTMAX_HEAT
        )
        sort_grad = jnp.einsum(
            "spd,spk->dk", unit_vec.astype(jnp.float32), own_rows, precision=PRECISE
        )
        unit_grad = jnp.einsum(
            "spk,dk->spd", own_rows, w_sort.astype(jnp.float32), precision=PRECISE
        )
        summary_grad = inverse * (
            unit_grad
            - summary * inverse * inverse * jnp.mean(unit_grad * summary, axis=-1, keepdims=True)
        )
        spread = jnp.broadcast_to(
            summary_grad[:, :, None, :] / block_size,
            summary.shape[:2] + (block_size, summary.shape[2]),
        )
        return (sort_grad, spread.reshape(-1, summary.shape[2]))

    sort_grad_a, row_grad_a = sort_back(
        normalizer_backprop_left,
        indicator_left,
        entire_coupling_left,
        member_left,
        pooled_digest_left,
        undo_order_left,
        length_left,
    )
    sort_grad_b, row_grad_b = sort_back(
        normalizer_backprop_right,
        indicator_right,
        entire_coupling_right,
        member_right,
        pooled_digest_right,
        undo_order_right,
        length_right,
    )
    grad_sort = sort_grad_a + sort_grad_b
    grad_normed = times_transpose(grad_projected, w_qkv) + jnp.concatenate(
        [row_grad_a, row_grad_b], axis=0
    )
    grad_qkv = contract_rows(normed_low, grad_projected)
    input_part, grad_gain_one = normalize_back(inputs, inverse_one, gain_first, grad_normed)
    grad_inputs = grad_middle + input_part
    grad_x_a = grad_inputs[:total_a].reshape(x_a.shape).astype(jnp.bfloat16)
    grad_x_b = grad_inputs[total_a:].reshape(x_b.shape).astype(jnp.bfloat16)
    sum_gain_one, sum_qkv, sum_out, sum_sort, sum_gain_two, sum_up, sum_down = lax.psum(
        (grad_gain_one, grad_qkv, grad_w_out, grad_sort, grad_gain_two, grad_up, grad_down),
        ("dp", "blk"),
    )
    return (
        out_a,
        out_b,
        grad_x_a,
        grad_x_b,
        sum_gain_one,
        sum_qkv,
        sum_out,
        sum_sort,
        sum_gain_two,
        sum_up,
        sum_down,
    )


def solution(mesh):
    in_specs = (
        P("dp", "blk", None),
        P("dp", "blk", None),
        P("dp", "blk"),
        P("dp", "blk"),
        P(),
        P(),
        P(),
        P(),
        P(),
        P(),
        P(),
        P("dp", "blk", None),
        P("dp", "blk", None),
    )
    out_specs = (
        P("dp", "blk", None),
        P("dp", "blk", None),
        P("dp", "blk", None),
        P("dp", "blk", None),
        P(),
        P(),
        P(),
        P(),
        P(),
        P(),
        P(),
    )
    return jax.shard_map(
        per_device, mesh=mesh, in_specs=in_specs, out_specs=out_specs, check_vma=False
    )
```

profile of v0, /device:TPU:0, one launch (start us, length us, event | category | flops | bytes accessed | tf_op | source)
XLA Modules:
  0.0 1277.9 jit_solution(14307199071752608029)
XLA Ops:
  7.2 28.1 %all-gather.1 = s32[8,8,4]{1,2,0:T(4,128)S(1)} all-gather(s32[1,8,4]{1,2,0:T(4,128)} %bitcast.280), channel_id=1, replica_groups=mesh['dp'=4,'blk'=8] {'blk'}, dimensions={0}, use_global_device_ids=true | all-gather | bytes 1152 | tf_op jit(solution)/shard_map/all_gather | solution.py:195
  35.6 19.1 %all-gather = s32[8,8,2]{1,2,0:T(2,128)S(1)} all-gather(s32[1,8,2]{1,2,0:T(2,128)} %bitcast.281), channel_id=1, replica_groups=mesh['dp'=4,'blk'=8] {'blk'}, dimensions={0}, use_global_device_ids=true | all-gather | bytes 576 | tf_op jit(solution)/shard_map/all_gather | solution.py:194
  61.4 5.5 convolution_convert_fusion
  72.0 8.4 gather_fusion
  80.5 6.7 broadcast_select_fusion
  87.2 5.0 all-to-all-start
  94.7 5.6 fusion.214
  101.9 163.8 %all_gather.21 = f32[4,64,64]{2,1,0:T(8,128)S(1)} all-gather(f32[4,8,64]{2,1,0:T(8,128)S(1)} %convolution_multiply_fusion.6), channel_id=1, replica_groups=mesh['dp'=4,'blk'=8] {'blk'}, dimensions={1}, use_global_device_ids=true | all-gather | bytes 73728 | tf_op jit(solution)/shard_map/all_gather | solution.py:191
  282.8 30.9 %all_gather.20 = f32[2,64,64]{2,1,0:T(8,128)S(1)} all-gather(f32[2,8,64]{2,1,0:T(8,128)S(1)} %convolution_multiply_fusion.7), channel_id=1, replica_groups=mesh['dp'=4,'blk'=8] {'blk'}, dimensions={1}, use_global_device_ids=true | all-gather | bytes 36864 | tf_op jit(solution)/shard_map/all_gather | solution.py:190
  360.3 5.6 fusion.223
  368.9 5.9 gather_fusion.1
  449.3 8.6 fusion.198
  457.9 17.5 %fusion.8 = bf16[2048,2048]{1,0:T(8,128)(2,1)S(1)} fusion(f32[2048,2048]{1,0:T(8,128)} %fusion.198, bf16[2048,512]{1,0:T(8,128)(2,1)S(1)} %copy-done.248, bf16[1024,512]{1,0:T(8,128)(2,1)S(1)} %bitcast.250, bf16[1024,512]{1,0:T(8,128)(2,1)S(1)} %bitcast.253), kind=kOutput, calls=%fused_computation.14 | convolution fusion | flops 4383047680 | bytes 29360128 | tf_op jit(solution)/shard_map/dot_general | solution.py:45
  475.4 6.2 multiply_reduce_fusion
  523.8 48.9 %multiply_convert_fusion.4 = bf16[16,8,64,128]{3,2,1,0:T(8,128)(2,1)S(1)} fusion(f32[16,8,64,128]{3,2,1,0:T(8,128)S(1)} %copy-done.26, f32[16,8,64]{2,1,0:T(8,128)S(1)} %log_add_fusion.1, f32[16,8,64,64]{3,2,1,0:T(8,128)S(1)} %copy-done.28, f32[16,8,64,64]{3,2,1,0:T(8,128)} %fusion.59), kind=kOutput, calls=%fused_computation.67 | output fusion | flops 8396927 | bytes 10518528 | tf_op jit(solution)/shard_map/sub | solution.py:113
  572.7 5.6 fusion.46
  581.4 53.1 %multiply_convert_fusion.2 = bf16[32,8,32,64]{3,2,1,0:T(8,128)(2,1)S(1)} fusion(f32[32,8,32,64]{3,2,1,0:T(8,128)S(1)} %copy-done.24, f32[32,8,32]{2,1,0:T(8,128)S(1)} %log_add_fusion, f32[32,8,32,32]{3,2,1,0:T(8,128)} %convolution_multiply_fusion, f32[32,8,32,32]{3,2,1,0:T(8,128)} %fusion.63), kind=kOutput, calls=%fused_computation.63 | output fusion | flops 4202559 | bytes 5275648 | tf_op jit(solution)/shard_map/sub | solution.py:113
  653.2 18.6 %all-gather.2 = f32[8,8,2]{1,2,0:T(2,128)S(1)} all-gather(f32[1,8,2]{1,2,0:T(2,128)S(1)} %bitcast.282), channel_id=1, replica_groups=mesh['dp'=4,'blk'=8] {'blk'}, dimensions={0}, use_global_device_ids=true | all-gather | bytes 576 | tf_op jit(solution)/shard_map/all_gather | solution.py:391
  680.8 26.0 %all-gather.3 = f32[8,8,4]{1,2,0:T(4,128)S(1)} all-gather(f32[1,8,4]{1,2,0:T(4,128)S(1)} %bitcast.279), channel_id=1, replica_groups=mesh['dp'=4,'blk'=8] {'blk'}, dimensions={0}, use_global_device_ids=true | all-gather | bytes 1152 | tf_op jit(solution)/shard_map/all_gather | solution.py:392
  706.9 5.4 fusion.70
  727.0 5.3 copy.287
  735.8 8.0 copy.293
  748.6 5.4 copy.285
  754.0 5.0 concatenate.92
  759.0 8.0 copy.290
  771.7 5.7 maximum_maximum_fusion
  777.4 7.0 broadcast_in_dim.118
  784.4 16.3 %scatter_fusion = f32[112,32,1024]{2,1,0:T(8,128)} fusion(f32[112,32,1024]{2,1,0:T(8,128)} %broadcast_in_dim.118, s32[64]{0:T(128)S(1)} %copy-done.245, f32[64,32,1024]{2,1,0:T(8,128)} %maximum_maximum_fusion), kind=kCustom, calls=%fused_computation.2 | custom fusion | bytes 25166080 | tf_op jit(solution)/shard_map/scatter | solution.py:360
  800.7 9.4 convert_element_type.113
  810.0 4.9 all-to-all-start.1
  815.0 5.8 copy.275
  820.8 4.8 reshape.1277
  825.6 5.3 copy.277
  835.7 8.1 copy.280
  843.7 4.8 reshape.1279
  848.6 7.9 copy.283
  856.8 5.0 reshape.1280
  890.0 10.1 fusion.197
  900.1 9.7 fusion.92
  909.8 44.1 %all-to-all-done.1 = bf16[8,14,32,1024]{3,2,1,0:T(8,128)(2,1)} async-done(((bf16[8,14,32,1024]{3,2,1,0:T(8,128)(2,1)}), bf16[8,14,32,1024]{3,2,1,0:T(8,128)(2,1)}, u32[]{:S(2)}, u32[]{:S(2)}) %all-to-all-start.1) | async-done | bytes 7340064 | tf_op jit(solution)/shard_map/all_to_all | solution.py:362
  953.9 10.2 bitcast_convert_fusion
  968.6 32.6 %scatter_fusion.1 = f32[65,32,1024]{2,1,0:T(8,128)} fusion(f32[65,32,1024]{2,1,0:T(8,128)} %broadcast_in_dim.117, s32[112]{0:T(128)S(1)} %copy-done.244, f32[112,32,1024]{2,1,0:T(8,128)} %bitcast_convert_fusion), kind=kCustom, calls=%fused_computation.3 | custom fusion | flops 3670016 | bytes 44040640 | tf_op jit(solution)/shard_map/scatter-add | solution.py:369
  1005.6 8.3 fusion.9
  1013.8 7.7 fusion.35
  1022.3 11.3 add_convert_fusion
  1037.5 14.2 %fusion.20 = (f32[512]{0:T(512)S(1)}, f32[2048]{0:T(1024)S(1)}, f32[2048,512]{1,0:T(8,128)}) fusion(f32[2048]{0:T(1024)S(1)} %copy-done.132, bf16[1024,512]{1,0:T(8,128)(2,1)S(1)} %bitcast.236, bf16[1024,512]{1,0:T(8,128)(2,1)S(1)} %bitcast.243, f32[512]{0:T(512)S(1)} %copy-done.196, f32[1024,512]{1,0:T(8,128)S(1)} %bitcast.249, ...), kind=kOutput, calls=%fused_computation.39 | convolution fusion | flops 3252680192 | bytes 18370560 | tf_op jit(solution)/shard_map/dot_general | solution.py:45
  1051.6 39.2 %all-reduce = (f32[512]{0:T(512)}, f32[512]{0:T(512)}) all-reduce(f32[512]{0:T(512)S(1)} %get-tuple-element.15, f32[512]{0:T(512)S(1)} %copy-done.246), channel_id=1, replica_groups=mesh['dp'=4,'blk'=8] {'dp','blk'}, use_global_device_ids=true, to_apply=%region_124.127 | all-reduce | flops 1024 | bytes 8192 | tf_op jit(solution)/shard_map/psum | solution.py:446
  1097.0 162.3 %all-reduce.4.cloned.1.call-done = (f32[512,1536]{1,0:T(8,128)}, f32[512,512]{1,0:T(8,128)}, f32[512,64]{0,1:T(8,128)}, f32[512,2048]{1,0:T(8,128)}, f32[2048,512]{1,0:T(8,128)}) async-done(((f32[512,1536]{1,0:T(8,128)}, f32[512,512]{1,0:T(8,128)}, f32[512,64]{0,1:T(8,128)}, f32[512,2048]{1,0:T(8,128)}, f32[2048,512]{1,0:T(8,128)}), (f32[512,1536]{1,0:T(8,128)}, f32[512,512]{1,0:T(8,128)}, ...) | async-done | bytes 12714000 | tf_op jit(solution)/shard_map/psum | solution.py:446
  (864 shorter events, 318.8 us)
Async XLA Ops:
  7.2 442.0 %copy-start = (bf16[512,2048]{1,0:T(8,128)(2,1)S(1)}, bf16[512,2048]{1,0:T(8,128)(2,1)}, u32[]{:S(2)}) copy-start(bf16[512,2048]{1,0:T(8,128)(2,1)} %param.26) | copy-start | bytes 6291460
  35.4 58.6 %copy-start.112 = (s32[64,4]{0,1:T(4,128)}, s32[64,4]{0,1:T(4,128)S(1)}, u32[]{:S(2)}) copy-start(s32[64,4]{0,1:T(4,128)S(1)} %reshape.1330) | copy-start | bytes 3076
  60.7 31.6 %copy-start.131 = (f32[2048]{0:T(1024)}, f32[2048]{0:T(1024)S(1)}, u32[]{:S(2)}) copy-start(f32[2048]{0:T(1024)S(1)} %add_rsqrt_fusion.1) | copy-start | bytes 24580
  61.4 30.9 %copy-start.195 = (f32[512]{0:T(512)}, f32[512]{0:T(512)S(1)}, u32[]{:S(2)}) copy-start(f32[512]{0:T(512)S(1)} %convert_element_type.94) | copy-start | bytes 6148
  87.2 281.6 %all-to-all-start = ((bf16[8,14,32,1024]{3,2,1,0:T(8,128)(2,1)}), bf16[8,14,32,1024]{3,2,1,0:T(8,128)(2,1)}, u32[]{:S(2)}, u32[]{:S(2)}) async-start(bf16[8,14,32,1024]{3,2,1,0:T(8,128)(2,1)} %bitcast.225), calls=%async_computation | async-start | bytes 14680064 | tf_op jit(solution)/shard_map/all_to_all | solution.py:276
  101.0 181.3 %copy-start.81 = (f32[2,8,512]{2,1,0:T(8,128)}, f32[2,8,512]{2,1,0:T(8,128)S(1)}, u32[]{:S(2)}) copy-start(f32[2,8,512]{2,1,0:T(8,128)S(1)} %bitcast_reduce_fusion.1) | copy-start | bytes 98308
  101.7 173.8 %copy-start.151 = (f32[4,8]{1,0:T(4,128)}, f32[4,8]{1,0:T(4,128)S(1)}, u32[]{:S(2)}) copy-start(f32[4,8]{1,0:T(4,128)S(1)} %get-tuple-element.79) | copy-start | bytes 388
  265.7 53.6 %copy-start.4 = (f32[4,64,64]{2,1,0:T(8,128)}, f32[4,64,64]{2,1,0:T(8,128)S(1)}, u32[]{:S(2)}) copy-start(f32[4,64,64]{2,1,0:T(8,128)S(1)} %all_gather.21) | copy-start | bytes 196612
  449.2 32.4 %copy-start.48 = (f32[2048,512]{1,0:T(8,128)}, f32[2048,512]{1,0:T(8,128)S(1)}, u32[]{:S(2)}) copy-start(f32[2048,512]{1,0:T(8,128)S(1)} %get-tuple-element.91) | copy-start | bytes 12582916
  572.7 68.9 %copy-start.16 = (bf16[16,8,64,128]{3,2,1,0:T(8,128)(2,1)}, bf16[16,8,64,128]{3,2,1,0:T(8,128)(2,1)S(1)}, u32[]{:S(2)}) copy-start(bf16[16,8,64,128]{3,2,1,0:T(8,128)(2,1)S(1)} %multiply_convert_fusion.4) | copy-start | bytes 6291460
  581.4 53.1 %copy-start.29 = (bf16[32,32,8,64]{3,2,1,0:T(8,128)(2,1)S(1)}, bf16[32,32,8,64]{3,2,1,0:T(8,128)(2,1)}, u32[]{:S(2)}) copy-start(bf16[32,32,8,64]{3,2,1,0:T(8,128)(2,1)} %reshape.1266) | copy-start | bytes 3145732
  650.0 25.2 %copy-start.166 = (f32[2,64]{1,0:T(2,128)S(1)}, f32[2,64]{1,0:T(2,128)}, u32[]{:S(2)}) copy-start(f32[2,64]{1,0:T(2,128)} %copy-done.165) | copy-start | bytes 1540
  650.0 26.0 %copy-start.233 = (f32[2,64]{1,0:T(2,128)S(1)}, f32[2,64]{1,0:T(2,128)}, u32[]{:S(2)}) copy-start(f32[2,64]{1,0:T(2,128)} %copy-done.232) | copy-start | bytes 1540
  650.0 26.1 %copy-start.201 = (f32[2,64]{1,0:T(2,128)S(1)}, f32[2,64]{1,0:T(2,128)}, u32[]{:S(2)}) copy-start(f32[2,64]{1,0:T(2,128)} %copy-done.200) | copy-start | bytes 1540
  650.0 27.0 %copy-start.231 = (f32[2,64]{1,0:T(2,128)S(1)}, f32[2,64]{1,0:T(2,128)}, u32[]{:S(2)}) copy-start(f32[2,64]{1,0:T(2,128)} %copy-done.230) | copy-start | bytes 1540
  650.0 27.0 %copy-start.208 = (f32[2,64]{1,0:T(2,128)S(1)}, f32[2,64]{1,0:T(2,128)}, u32[]{:S(2)}) copy-start(f32[2,64]{1,0:T(2,128)} %copy-done.207) | copy-start | bytes 1540
  650.0 28.0 %copy-start.229 = (f32[2,64]{1,0:T(2,128)S(1)}, f32[2,64]{1,0:T(2,128)}, u32[]{:S(2)}) copy-start(f32[2,64]{1,0:T(2,128)} %copy-done.228) | copy-start | bytes 1540
  650.0 28.0 %copy-start.146 = (f32[2,64]{1,0:T(2,128)S(1)}, f32[2,64]{1,0:T(2,128)}, u32[]{:S(2)}) copy-start(f32[2,64]{1,0:T(2,128)} %copy-done.145) | copy-start | bytes 1540
  650.0 28.2 %copy-start.227 = (f32[2,64]{1,0:T(2,128)S(1)}, f32[2,64]{1,0:T(2,128)}, u32[]{:S(2)}) copy-start(f32[2,64]{1,0:T(2,128)} %copy-done.226) | copy-start | bytes 1540
  650.1 28.2 %copy-start.164 = (f32[2,64]{1,0:T(2,128)S(1)}, f32[2,64]{1,0:T(2,128)}, u32[]{:S(2)}) copy-start(f32[2,64]{1,0:T(2,128)} %copy-done.163) | copy-start | bytes 1540
  650.1 28.4 %copy-start.225 = (f32[2,64]{1,0:T(2,128)S(1)}, f32[2,64]{1,0:T(2,128)}, u32[]{:S(2)}) copy-start(f32[2,64]{1,0:T(2,128)} %copy-done.224) | copy-start | bytes 1540
  650.1 28.4 %copy-start.199 = (f32[2,64]{1,0:T(2,128)S(1)}, f32[2,64]{1,0:T(2,128)}, u32[]{:S(2)}) copy-start(f32[2,64]{1,0:T(2,128)} %copy-done.198) | copy-start | bytes 1540
  650.1 28.6 %copy-start.223 = (f32[2,64]{1,0:T(2,128)S(1)}, f32[2,64]{1,0:T(2,128)}, u32[]{:S(2)}) copy-start(f32[2,64]{1,0:T(2,128)} %copy-done.222) | copy-start | bytes 1540
  650.1 28.6 %copy-start.206 = (f32[2,64]{1,0:T(2,128)S(1)}, f32[2,64]{1,0:T(2,128)}, u32[]{:S(2)}) copy-start(f32[2,64]{1,0:T(2,128)} %copy-done.205) | copy-start | bytes 1540
  650.1 28.8 %copy-start.221 = (f32[2,64]{1,0:T(2,128)S(1)}, f32[2,64]{1,0:T(2,128)}, u32[]{:S(2)}) copy-start(f32[2,64]{1,0:T(2,128)} %copy-done.220) | copy-start | bytes 1540
  650.1 28.8 %copy-start.23 = (f32[2,64,64]{2,1,0:T(8,128)S(1)}, f32[2,64,64]{2,1,0:T(8,128)}, u32[]{:S(2)}) copy-start(f32[2,64,64]{2,1,0:T(8,128)} %copy-done.22) | copy-start | bytes 98308
  650.1 28.8 %copy-start.80 = (f32[2,64]{1,0:T(2,128)S(1)}, f32[2,64]{1,0:T(2,128)}, u32[]{:S(2)}) copy-start(f32[2,64]{1,0:T(2,128)} %copy-done.79) | copy-start | bytes 1540
  650.1 28.8 %copy-start.89 = (f32[2,64]{1,0:T(2,128)S(1)}, f32[2,64]{1,0:T(2,128)}, u32[]{:S(2)}) copy-start(f32[2,64]{1,0:T(2,128)} %copy-done.88) | copy-start | bytes 1540
  650.1 28.8 %copy-start.93 = (f32[2,64]{1,0:T(2,128)S(1)}, f32[2,64]{1,0:T(2,128)}, u32[]{:S(2)}) copy-start(f32[2,64]{1,0:T(2,128)} %copy-done.92) | copy-start | bytes 1540
  650.2 28.8 %copy-start.105 = (f32[2,64]{1,0:T(2,128)S(1)}, f32[2,64]{1,0:T(2,128)}, u32[]{:S(2)}) copy-start(f32[2,64]{1,0:T(2,128)} %copy-done.104) | copy-start | bytes 1540
  650.2 28.8 %copy-start.111 = (f32[2,64]{1,0:T(2,128)S(1)}, f32[2,64]{1,0:T(2,128)}, u32[]{:S(2)}) copy-start(f32[2,64]{1,0:T(2,128)} %copy-done.110) | copy-start | bytes 1540
  650.2 28.8 %copy-start.120 = (f32[2,64]{1,0:T(2,128)S(1)}, f32[2,64]{1,0:T(2,128)}, u32[]{:S(2)}) copy-start(f32[2,64]{1,0:T(2,128)} %copy-done.119) | copy-start | bytes 1540
  650.2 28.8 %copy-start.134 = (f32[2,64]{1,0:T(2,128)S(1)}, f32[2,64]{1,0:T(2,128)}, u32[]{:S(2)}) copy-start(f32[2,64]{1,0:T(2,128)} %copy-done.133) | copy-start | bytes 1540
  650.2 28.8 %copy-start.150 = (f32[2,64]{1,0:T(2,128)S(1)}, f32[2,64]{1,0:T(2,128)}, u32[]{:S(2)}) copy-start(f32[2,64]{1,0:T(2,128)} %copy-done.149) | copy-start | bytes 1540
  650.2 29.0 %copy-start.219 = (f32[2,64]{1,0:T(2,128)S(1)}, f32[2,64]{1,0:T(2,128)}, u32[]{:S(2)}) copy-start(f32[2,64]{1,0:T(2,128)} %copy-done.218) | copy-start | bytes 1540
  650.2 29.1 %copy-start.168 = (f32[2,64]{1,0:T(2,128)S(1)}, f32[2,64]{1,0:T(2,128)}, u32[]{:S(2)}) copy-start(f32[2,64]{1,0:T(2,128)} %copy-done.167) | copy-start | bytes 1540
  650.2 29.2 %copy-start.217 = (f32[2,64]{1,0:T(2,128)S(1)}, f32[2,64]{1,0:T(2,128)}, u32[]{:S(2)}) copy-start(f32[2,64]{1,0:T(2,128)} %copy-done.216) | copy-start | bytes 1540
  650.2 29.3 %copy-start.203 = (f32[2,64]{1,0:T(2,128)S(1)}, f32[2,64]{1,0:T(2,128)}, u32[]{:S(2)}) copy-start(f32[2,64]{1,0:T(2,128)} %copy-done.202) | copy-start | bytes 1540
  650.2 29.5 %copy-start.215 = (f32[2,64]{1,0:T(2,128)S(1)}, f32[2,64]{1,0:T(2,128)}, u32[]{:S(2)}) copy-start(f32[2,64]{1,0:T(2,128)} %copy-done.214) | copy-start | bytes 1540
  650.3 30.4 %copy-start.213 = (f32[2,64]{1,0:T(2,128)S(1)}, f32[2,64]{1,0:T(2,128)}, u32[]{:S(2)}) copy-start(f32[2,64]{1,0:T(2,128)} %copy-done.212) | copy-start | bytes 1540
  650.3 56.6 %copy-start.17 = (bf16[16,8,64,128]{3,2,1,0:T(8,128)(2,1)S(1)}, bf16[16,8,64,128]{3,2,1,0:T(8,128)(2,1)}, u32[]{:S(2)}) copy-start(bf16[16,8,64,128]{3,2,1,0:T(8,128)(2,1)} %copy-done.16) | copy-start | bytes 6291460
  810.0 143.9 %all-to-all-start.1 = ((bf16[8,14,32,1024]{3,2,1,0:T(8,128)(2,1)}), bf16[8,14,32,1024]{3,2,1,0:T(8,128)(2,1)}, u32[]{:S(2)}, u32[]{:S(2)}) async-start(bf16[8,14,32,1024]{3,2,1,0:T(8,128)(2,1)} %bitcast.226), calls=%async_computation.1 | async-start | bytes 14680064 | tf_op jit(solution)/shard_map/all_to_all | solution.py:362
  814.9 444.4 %all-reduce.4.cloned.1.call-start = ((), (), s32[]{:S(2)}) async-start(), calls=%async_computation.2 | async-start | bytes 25427968 | tf_op jit(solution)/shard_map/psum | solution.py:446
  856.8 23.8 %copy-start.178 = (f32[4,64]{1,0:T(4,128)S(1)}, f32[4,64]{1,0:T(4,128)}, u32[]{:S(2)}) copy-start(f32[4,64]{1,0:T(4,128)} %copy-done.177) | copy-start | bytes 3076
  856.8 23.8 %copy-start.170 = (f32[4,64]{1,0:T(4,128)S(1)}, f32[4,64]{1,0:T(4,128)}, u32[]{:S(2)}) copy-start(f32[4,64]{1,0:T(4,128)} %copy-done.169) | copy-start | bytes 3076
  856.8 24.1 %copy-start.176 = (f32[4,64]{1,0:T(4,128)S(1)}, f32[4,64]{1,0:T(4,128)}, u32[]{:S(2)}) copy-start(f32[4,64]{1,0:T(4,128)} %copy-done.175) | copy-start | bytes 3076
  856.8 24.2 %copy-start.82 = (f32[2,8,512]{2,1,0:T(8,128)S(1)}, f32[2,8,512]{2,1,0:T(8,128)}, u32[]{:S(2)}) copy-start(f32[2,8,512]{2,1,0:T(8,128)} %copy-done.81) | copy-start | bytes 98308
  861.8 24.4 %copy-start.8 = (f32[2048,512]{1,0:T(8,128)S(1)}, f32[2048,512]{1,0:T(8,128)}, u32[]{:S(2)}) copy-start(f32[2048,512]{1,0:T(8,128)} %copy-done.7) | copy-start | bytes 12582916
  (207 other events, 1435.0 us)
Sparse Core Ops, SparseCore 0:
  1021.7 237.5 all-reduce.3
where the time goes:
time: 1290 us; the launch traced here: 1280 us
  blocking collectives  326 us (25%)
  local copies, waits for them, and re-layouts  277 us (21%)
  other arithmetic  260 us (20%)
  waiting for transfers between devices  206 us (16%)
  matrix products  180 us (14%)
  between operations  18.2 us (1%)
    all_gather x1, blocking collectives, per_device(): lax.all_gather(logits_b, 'blk', axis=1, tiled=True)  164 us
    psum x1, waiting for transfers between devices, per_device(): lax.psum((grad_gain_one, grad_qkv, grad_w_out, grad_sort, grad_gain_two,...  162 us
    sub x2, other arithmetic, attend_back(): prob_grad - jnp.sum(probabilities * prob_grad, axis=-1, keepdims=True)  102 us
    reshape x14, local copies, waits for them, and re-layouts, split_heads(): return matrix.reshape(-1, block_size, HEADS, matrix.shape[-1] // HEADS)  51.8 us
    all_to_all x1, waiting for transfers between devices, per_device(): lax.all_to_all(placed.reshape(devices, capacity, length_right, pair_width...  44.1 us
    psum x1, blocking collectives, per_device(): lax.psum((grad_gain_one, grad_qkv, grad_w_out, grad_sort, grad_gain_two,...  39.2 us
    dot_general x4, matrix products, times_transpose(): lax.dot_general(left_side, right_side, (((1,), (1,)), ((), ())), preferre...  39.1 us
    unnamed x514, local copies, waits for them, and re-layouts  38.8 us
  transfers between devices with their start and end apart: 3, of which 2 were waited for; matrix products, arithmetic and copies ran while one was open for 15% of the time, Pallas kernels for 0%

commit v1 on v0

v1 whole, which is shorter than its diff:
```python
import functools

import jax
import jax.numpy as jnp
import numpy as np
from jax import lax
from jax.experimental import pallas as pl
from jax.experimental.pallas import tpu as pltpu
from jax.sharding import PartitionSpec as P

HEADS = 8
SINK_ITERS = 8
EPSILON = 1e-05
SOFTMAX_HEAT = 0.75
UNIT = 32
EXTRA = 256
GROUP = 64
TILE = 256
HALF = 256
PER_HALF = 4
VMEM_LIMIT = 58 * 1024 * 1024

F32 = jnp.float32
BF16 = jnp.bfloat16

NN = (((1,), (0,)), ((), ()))
NT = (((1,), (1,)), ((), ()))
TN = (((0,), (0,)), ((), ()))


def dot(a, b, dims=NN):
    return lax.dot_general(a, b, dims, preferred_element_type=F32)


def inverse_norm(values):
    return lax.rsqrt(jnp.mean(values * values, axis=-1, keepdims=True) + EPSILON)


def whole(shape):
    zeros = (0,) * len(shape)
    return pl.BlockSpec(shape, lambda *_: zeros, pipeline_mode=pl.Buffered(1))


def rows_of(tile, width):
    return pl.BlockSpec((tile, width), lambda i: (i, 0))


SMEM = pl.BlockSpec(memory_space=pltpu.SMEM)


def params():
    return pltpu.CompilerParams(
        dimension_semantics=("arbitrary",), vmem_limit_bytes=VMEM_LIMIT
    )


def cost(flops, nbytes):
    return pl.CostEstimate(flops=int(flops * 1e-3), bytes_accessed=int(nbytes * 1e-3), transcendentals=0)


ANY = pl.BlockSpec(memory_space=pl.ANY)
VMEM = pl.BlockSpec(memory_space=pltpu.VMEM)


def limit(mib):
    return pltpu.CompilerParams(vmem_limit_bytes=mib * 1024 * 1024)


def request_kernel(
    npl, seqs_a, seqs_b, devices, capacity, first, early, sizes, extra, spare_rows,
    sel_ref, table_ref, back_ref, far_ref, ret_ref, perm_ref, place_ref, kinds_ref, fill, begin, used,
):
    count_a = seqs_a * npl
    count_b = seqs_b * npl
    units_a = 2 * count_a
    width = sum(sizes)
    shift = npl.bit_length() - 1 if npl & (npl - 1) == 0 else -1

    def split(chosen):
        if shift >= 0:
            return lax.shift_right_logical(chosen, shift), lax.bitwise_and(chosen, npl - 1)
        return lax.div(chosen, npl), lax.rem(chosen, npl)

    def clear(ref):
        def body(i, carry):
            ref[i] = -1
            return carry

        return body

    lax.fori_loop(0, devices * capacity, clear(table_ref), 0)
    lax.fori_loop(0, devices * width, clear(back_ref), 0)
    for s in range(devices):
        fill[s] = 0
        used[s] = 0
        used[devices + s] = 0
    one = lambda flag: jnp.where(flag, 1, 0)
    ready_a, ready_b, must_a, must_b = (jnp.int32(0) for _ in range(4))
    for j in range(count_a + count_b):
        source, inner = split(sel_ref[j])
        slot = fill[source]
        begin[j] = slot
        size = 2 if j < count_a else 1
        fill[source] = slot + size
        if j < count_a:
            unit = inner * 2 + (j // npl) * npl * 2
            ready_a = ready_a + one(slot + 2 <= first)
            table_ref[source * capacity + slot + 1] = unit + 1
        else:
            unit = inner + (units_a + (j - count_a) // npl * npl)
            ready_b = ready_b + one(slot + 1 <= first)
        table_ref[source * capacity + slot] = unit

    two = early < count_a + count_b // 2

    def must(j):
        source, _ = split(sel_ref[j])
        if not two:
            return begin[j] < 0
        return begin[j] < fill[source] - 6

    for j in range(count_a):
        must_a = must_a + one(must(j))
    for j in range(count_b):
        must_b = must_b + one(must(count_a + j))
    even = jnp.logical_or(lax.bitwise_and(must_b, 1) == 0, ready_b > must_b)
    pairs = lax.shift_right_logical(must_b + one(even), 1)
    take_a = jnp.minimum(ready_a, early - pairs)
    if not two:
        take_a = jnp.int32(count_a)
    take_b = 2 * (early - take_a)
    late_b = 2 * (early + count_a - take_a)
    kinds_ref[0] = take_a
    kinds_ref[1] = early + count_a - take_a
    second = devices * first * UNIT

    def ret_row(phase, source, slot):
        chunks = list(enumerate(sizes))
        if two:
            chunks = chunks[:1] if phase == 0 else chunks[1:]
        row = jnp.int32(0)
        begin_slot, begin_row = 0, 0
        for index, size in chunks:
            height = size * UNIT + (extra if index == len(sizes) - 1 else 0)
            here = begin_row + source * height + (slot - begin_slot) * UNIT
            row = jnp.where(slot >= begin_slot, here, row)
            begin_slot += size
            begin_row += devices * height
        return row

    def put(pos, unit, inner, source, slot, late):
        near = (source * first + slot) * UNIT
        rest = second + source * ((capacity - first) * UNIT + spare_rows) + (slot - first) * UNIT
        far_ref[pos] = jnp.where(slot < first, near, rest)
        at = late * devices + source
        back = used[at]
        used[at] = back + 1
        if two:
            ret_ref[pos] = jnp.where(late == 0, ret_row(0, source, back), ret_row(1, source, back))
            back_ref[source * width + back + late * sizes[0]] = inner
        else:
            ret_ref[pos] = ret_row(0, source, back)
            back_ref[source * width + back] = inner
        perm_ref[pos] = unit
        place_ref[unit] = pos

    spare = take_a - must_a
    taken, other, free = (jnp.int32(0) for _ in range(3))
    for j in range(count_a):
        source, inner = split(sel_ref[j])
        slot = begin[j]
        need = must(j)
        pick = jnp.logical_and(jnp.logical_not(need), jnp.logical_and(slot + 2 <= first, free < spare))
        use = jnp.logical_or(need, pick)
        free = free + one(pick)
        pos = 2 * jnp.where(use, taken, early + other)
        inner = inner * 2 + (j // npl) * npl * 2
        put(pos, 2 * j, inner, source, slot, one(jnp.logical_not(use)))
        put(pos + 1, 2 * j + 1, inner + 1, source, slot + 1, one(jnp.logical_not(use)))
        taken = taken + one(use)
        other = other + one(jnp.logical_not(use))
    spare = take_b - must_b
    drop = one(spare < 0)
    taken, other, free = (jnp.int32(0) for _ in range(3))
    for j in range(count_b):
        source, inner = split(sel_ref[count_a + j])
        slot = begin[count_a + j]
        need = must(count_a + j)
        skip = jnp.logical_and(need, drop > 0)
        drop = drop - one(skip)
        pick = jnp.logical_and(jnp.logical_not(need), jnp.logical_and(slot + 1 <= first, free < spare))
        use = jnp.logical_or(jnp.logical_and(need, jnp.logical_not(skip)), pick)
        free = free + one(pick)
        pos = jnp.where(use, 2 * take_a + taken, late_b + other)
        inner = inner + (units_a + (j // npl) * npl)
        put(pos, units_a + j, inner, source, slot, one(jnp.logical_not(use)))
        taken = taken + one(use)
        other = other + one(jnp.logical_not(use))


def request(sel, npl, seqs_a, seqs_b, devices, capacity, first, early, sizes, extra, spare_rows):
    units = npl * (2 * seqs_a + seqs_b)
    counts = [devices * capacity, devices * sum(sizes), units, units, units, units, 2]
    return pl.pallas_call(
        functools.partial(
            request_kernel, npl, seqs_a, seqs_b, devices, capacity, first, early, sizes, extra,
            spare_rows,
        ),
        in_specs=[SMEM],
        out_specs=[SMEM] * len(counts),
        out_shape=[jax.ShapeDtypeStruct((n,), jnp.int32) for n in counts],
        scratch_shapes=[
            pltpu.SMEM((devices,), jnp.int32),
            pltpu.SMEM((npl * (seqs_a + seqs_b),), jnp.int32),
            pltpu.SMEM((2 * devices,), jnp.int32),
        ],
        cost_estimate=cost(1000, 2000),
        name="request",
    )(sel)


def digest_kernel(
    tiles_a, xa_ref, xb_ref, gain_ref, avg_ref, wsort_ref, x_ref, means_ref, logits_ref, sums
):
    step = pl.program_id(0)

    def take(src):
        x = src[...]
        x_ref[...] = x
        x = x.astype(F32)
        scaled = x * inverse_norm(x)
        units = x.shape[0] // UNIT
        at = pl.ds(pl.multiple_of(step * units, units), units)
        sums[at, :] = jnp.sum(scaled.reshape(units, UNIT, x.shape[1]), axis=1)

    pl.when(step < tiles_a)(lambda: take(xa_ref))
    pl.when(step >= tiles_a)(lambda: take(xb_ref))

    @pl.when(step == pl.num_programs(0) - 1)
    def _():
        means = lax.dot_general(
            avg_ref[...], sums[...], NN, precision=lax.Precision.HIGHEST, preferred_element_type=F32
        )
        means_ref[...] = means
        summary = means * gain_ref[...]
        unit = (summary * inverse_norm(summary)).astype(BF16)
        logits_ref[...] = dot(unit, wsort_ref[...]) * (1.0 / SOFTMAX_HEAT)


def digest(x_a, x_b, gain_row, average, w_sort):
    width = x_a.shape[1]
    tiles_a = x_a.shape[0] // TILE
    tiles_b = x_b.shape[0] // TILE
    rows = x_a.shape[0] + x_b.shape[0]
    picks = average.shape[0]
    return pl.pallas_call(
        functools.partial(digest_kernel, tiles_a),
        grid=(tiles_a + tiles_b,),
        in_specs=[
            pl.BlockSpec((TILE, width), lambda i: (jnp.minimum(i, tiles_a - 1), 0)),
            pl.BlockSpec((TILE, width), lambda i: (jnp.maximum(i - tiles_a, 0), 0)),
            whole((1, width)),
            whole(average.shape),
            whole(w_sort.shape),
        ],
        out_specs=[rows_of(TILE, width), whole((picks, width)), whole((picks, w_sort.shape[1]))],
        out_shape=[
            jax.ShapeDtypeStruct((rows, width), BF16),
            jax.ShapeDtypeStruct((picks, width), F32),
            jax.ShapeDtypeStruct((picks, w_sort.shape[1]), F32),
        ],
        scratch_shapes=[pltpu.VMEM((rows // UNIT, width), F32)],
        compiler_params=params(),
        cost_estimate=cost(rows * width * 10, rows * width * 4),
        name="digest",
    )(x_a, x_b, gain_row, average, w_sort)


def pack_kernel(devices, capacity, first, spare, table_ref, x_ref, *rest):
    outs = rest[: 1 if first == capacity else 2]
    held, sems = rest[len(outs) :]
    sizes = [first, capacity - first]
    copies = []
    for part, out_ref in enumerate(outs):
        size = sizes[part]
        base = part * devices * first
        for r in range(devices):
            for slot in range(size):
                unit = jnp.maximum(table_ref[r * capacity + part * first + slot], 0)
                src = pl.ds(pl.multiple_of(unit * UNIT, UNIT), UNIT)
                at = (base + r * size + slot) * UNIT
                held[at : at + UNIT, :] = x_ref[src, :]
            at = (base + r * size) * UNIT
            copy = pltpu.make_async_copy(
                held.at[pl.ds(at, size * UNIT)],
                out_ref.at[pl.ds(r * (size * UNIT + part * spare), size * UNIT)],
                sems.at[part * devices + r],
            )
            copy.start()
            copies.append(copy)
    for copy in copies:
        copy.wait()


def pack(table, x, devices, capacity, first, spare):
    width = x.shape[1]
    sizes = [first] if first == capacity else [first, capacity - first]
    return pl.pallas_call(
        functools.partial(pack_kernel, devices, capacity, first, spare),
        in_specs=[SMEM, VMEM],
        out_specs=[ANY] * len(sizes),
        out_shape=[
            jax.ShapeDtypeStruct((devices * (n * UNIT + i * spare), width), BF16)
            for i, n in enumerate(sizes)
        ],
        scratch_shapes=[
            pltpu.VMEM((devices * capacity * UNIT, width), BF16),
            pltpu.SemaphoreType.DMA((len(sizes) * devices,)),
        ],
        compiler_params=limit(12),
        cost_estimate=cost(0, x.size * 6),
        name="pack",
    )(table, x)


def arrange_kernel(units_a, perm_ref, x_ref, cota_ref, cotb_ref, xp_ref, cotp_ref):
    def body(pos, carry):
        unit = perm_ref[pos]
        at = pl.ds(pl.multiple_of(pos * UNIT, UNIT), UNIT)
        xp_ref[at, :] = x_ref[pl.ds(pl.multiple_of(unit * UNIT, UNIT), UNIT), :]

        @pl.when(unit < units_a)
        def _():
            cotp_ref[at, :] = cota_ref[pl.ds(pl.multiple_of(unit * UNIT, UNIT), UNIT), :]

        @pl.when(unit >= units_a)
        def _():
            src = pl.ds(pl.multiple_of((unit - units_a) * UNIT, UNIT), UNIT)
            cotp_ref[at, :] = cotb_ref[src, :]

        return carry

    lax.fori_loop(0, x_ref.shape[0] // UNIT, body, 0)


def arrange(perm, x, cot_a, cot_b):
    like = jax.ShapeDtypeStruct(x.shape, BF16)
    return pl.pallas_call(
        functools.partial(arrange_kernel, cot_a.shape[0] // UNIT),
        in_specs=[SMEM, VMEM, VMEM, VMEM],
        out_specs=[VMEM, VMEM],
        out_shape=[like, like],
        compiler_params=limit(16),
        cost_estimate=cost(0, x.size * 8),
        name="arrange",
    )(perm, x, cot_a, cot_b)


def restore_kernel(perm_ref, out_ref, outa_ref, outb_ref):
    units_a = outa_ref.shape[0] // UNIT

    def body(pos, carry):
        unit = perm_ref[pos]
        at = pl.ds(pl.multiple_of(pos * UNIT, UNIT), UNIT)

        @pl.when(unit < units_a)
        def _():
            outa_ref[pl.ds(pl.multiple_of(unit * UNIT, UNIT), UNIT), :] = out_ref[at, :]

        @pl.when(unit >= units_a)
        def _():
            dst = pl.ds(pl.multiple_of((unit - units_a) * UNIT, UNIT), UNIT)
            outb_ref[dst, :] = out_ref[at, :]

        return carry

    lax.fori_loop(0, out_ref.shape[0] // UNIT, body, 0)


def restore(perm, out, rows_a):
    rows, width = out.shape
    return pl.pallas_call(
        restore_kernel,
        in_specs=[SMEM, VMEM],
        out_specs=[VMEM, VMEM],
        out_shape=[
            jax.ShapeDtypeStruct((rows_a, width), BF16),
            jax.ShapeDtypeStruct((rows - rows_a, width), BF16),
        ],
        compiler_params=limit(16),
        cost_estimate=cost(0, out.size * 4),
        name="restore",
    )(perm, out)


def project_kernel(x_ref, gain_ref, w_ref, proj_ref):
    x = x_ref[...].astype(F32)
    proj_ref[...] = dot((x * inverse_norm(x) * gain_ref[...]).astype(BF16), w_ref[...]).astype(BF16)


def project(x, gain_row, w_qkv):
    rows, width = x.shape
    wide = w_qkv.shape[1]
    return pl.pallas_call(
        project_kernel,
        grid=(rows // TILE,),
        in_specs=[rows_of(TILE, width), whole((1, width)), whole((width, wide))],
        out_specs=rows_of(TILE, wide),
        out_shape=jax.ShapeDtypeStruct((rows, wide), BF16),
        compiler_params=params(),
        cost_estimate=cost(2 * rows * width * wide, rows * (width + wide) * 2),
        name="project",
    )(x, gain_row, w_qkv)


def log_sum(values, axis):
    top = jnp.max(values, axis=axis, keepdims=True)
    return top + jnp.log(jnp.sum(jnp.exp(values - top), axis=axis, keepdims=True))


def sinkhorn_kernel(logits_ref, picked_ref, weight_ref):
    state = logits_ref[...]
    for _ in range(SINK_ITERS):
        state = state - log_sum(state, 2)
        state = state - log_sum(state, 1)
    count = state.shape[1]
    weight = count * jnp.sum(jnp.exp(state) * picked_ref[...], axis=2, keepdims=True)
    weight_ref[...] = jnp.broadcast_to(weight, weight_ref.shape)


def sinkhorn(logits, picked):
    seqs, count, _ = logits.shape
    return pl.pallas_call(
        sinkhorn_kernel,
        out_shape=jax.ShapeDtypeStruct((seqs, count, 128), F32),
        cost_estimate=cost(logits.size * 100, logits.size * 32),
        name="sinkhorn",
    )(logits, picked)


def sinkhorn_back_kernel(logits_ref, picked_ref, gw_ref, out_ref, kept):
    state = logits_ref[...]
    for step in range(SINK_ITERS):
        state = state - log_sum(state, 2)
        kept[2 * step] = jnp.exp(state)
        state = state - log_sum(state, 1)
        kept[2 * step + 1] = jnp.exp(state)
    count = state.shape[1]
    grad = count * picked_ref[...] * gw_ref[...] * jnp.exp(state)
    for step in reversed(range(SINK_ITERS)):
        grad = grad - kept[2 * step + 1] * jnp.sum(grad, axis=1, keepdims=True)
        grad = grad - kept[2 * step] * jnp.sum(grad, axis=2, keepdims=True)
    out_ref[...] = grad


def sinkhorn_back(logits, picked, gw):
    return pl.pallas_call(
        sinkhorn_back_kernel,
        out_shape=jax.ShapeDtypeStruct(logits.shape, F32),
        scratch_shapes=[pltpu.VMEM((2 * SINK_ITERS,) + logits.shape, F32)],
        compiler_params=pltpu.CompilerParams(vmem_limit_bytes=VMEM_LIMIT),
        cost_estimate=cost(logits.size * 200, logits.size * 32),
        name="sinkhorn_back",
    )(logits, picked, gw)


def head_masks(rows):
    lane = lax.broadcasted_iota(jnp.int32, (rows, HALF), 1) // (HALF // PER_HALF)
    return [lane == h for h in range(PER_HALF)]


def stack_heads(values, masks):
    zero = jnp.zeros_like(values)
    return jnp.concatenate([jnp.where(m, values, zero) for m in masks], axis=0)


def unstack_heads(values, masks):
    total = None
    for h, m in enumerate(masks):
        part = jnp.where(m, values[h * GROUP : (h + 1) * GROUP], 0.0)
        total = part if total is None else total + part
    return total


def repeat_heads(values):
    return jnp.concatenate([values] * PER_HALF, axis=0)


def forward_kernel(first_group, recvs, prior, final, *refs):
    refs = list(refs)
    take = lambda n: [refs.pop(0) for _ in range(n)]
    far_ref, kinds_ref, core_ref = take(3)
    recv_refs = take(recvs)
    (
        x_ref, cot_ref, proj_ref, wrow_ref, mask_ref, gain1_ref, gain2_ref,
        wqkv_ref, wout_ref, wup_ref, wdown_ref,
    ) = take(11)
    take(1)
    prior_refs = take(3) if prior else []
    if prior:
        take(6)
    out_ref, gmid_ref, gatt_ref, prob_ref, farx_ref, farkv_ref = take(6)
    if final:
        keep_ref, give_ref, gain_ref = take(3)
    else:
        up_ref, down_ref, gain_ref = take(3)
    attended, up_acc, down_acc, wo_acc, gain_acc = take(5)
    if prior:
        up_prior, down_prior, sems = take(3)
    step = pl.program_id(0)
    steps = pl.num_programs(0)
    tile, width = x_ref.shape
    ff = wup_ref.shape[1]
    units = tile // UNIT
    groups = tile // GROUP
    base = first_group + step * groups
    rows_one = recv_refs[0].shape[0]
    for u in range(units):
        row = far_ref[2 * base + u]
        dst = pl.ds(u * UNIT, UNIT)
        if recvs == 1:
            farx_ref[dst, :] = recv_refs[0][pl.ds(pl.multiple_of(row, UNIT), UNIT), :]
        else:

            @pl.when(row < rows_one)
            def _():
                farx_ref[dst, :] = recv_refs[0][pl.ds(pl.multiple_of(row, 16), UNIT), :]

            @pl.when(row >= rows_one)
            def _():
                src = pl.ds(pl.multiple_of(row - rows_one, 16), UNIT)
                farx_ref[dst, :] = recv_refs[1][src, :]

    if prior:
        moves = [
            pltpu.make_async_copy(prior_refs[0], up_prior, sems.at[0]),
            pltpu.make_async_copy(prior_refs[1], down_prior, sems.at[1]),
        ]

        @pl.when(step == 0)
        def _():
            for move in moves:
                move.start()

    far = farx_ref[...].astype(F32)
    far = (far * inverse_norm(far) * gain1_ref[...]).astype(BF16)
    farkv_ref[...] = dot(far, wqkv_ref[:, width:]).astype(BF16)
    masks16 = head_masks(GROUP)
    head_scale = (width // HEADS) ** -0.5
    boundary = kinds_ref[1 if prior else 0]

    def group_step(i, carry):
        rows = pl.ds(pl.multiple_of(i * GROUP, GROUP), GROUP)
        which = jnp.where(base + i < boundary, 0, 1)
        barrier = repeat_heads(mask_ref[which])
        scale = repeat_heads(wrow_ref[rows, :])
        for half in range(width // HALF):
            lo = half * HALF
            q = proj_ref[rows, lo : lo + HALF] * jnp.asarray(head_scale, BF16)
            keys = jnp.concatenate(
                [proj_ref[rows, width + lo : width + lo + HALF], farkv_ref[rows, lo : lo + HALF]],
                axis=0,
            )
            vals = jnp.concatenate(
                [
                    proj_ref[rows, 2 * width + lo : 2 * width + lo + HALF],
                    farkv_ref[rows, width + lo : width + lo + HALF],
                ],
                axis=0,
            )
            scores = dot(stack_heads(q, masks16), keys, NT) + barrier
            top = jnp.max(scores, axis=1, keepdims=True)
            weight = jnp.exp(scores - top)
            prob = weight * (1.0 / jnp.sum(weight, axis=1, keepdims=True))
            prob_ref[i, half] = prob.astype(BF16)
            mixed = dot((prob * scale).astype(BF16), vals)
            attended[rows, lo : lo + HALF] = unstack_heads(mixed, masks16).astype(BF16)
        return carry

    lax.fori_loop(0, groups, group_step, 0, unroll=True)

    att = attended[...]
    middle = x_ref[...].astype(F32) + dot(att, wout_ref[...])
    r2 = inverse_norm(middle)
    scaled = middle * r2
    second = (scaled * gain2_ref[...]).astype(BF16)
    cot = cot_ref[...]
    cot_t = cot.T
    second_t = second.T

    @pl.when(step == 0)
    def _():
        up_acc[...] = jnp.zeros_like(up_acc)
        down_acc[...] = jnp.zeros_like(down_acc)
        wo_acc[...] = jnp.zeros_like(wo_acc)
        gain_acc[...] = prior_refs[2][...] if prior else jnp.zeros_like(gain_acc)

    result = middle
    back = jnp.zeros((tile, width), F32)
    c0 = 0.7978845608028654
    c1 = 0.044715
    chunk = 512
    for c in range(0, ff, chunk):
        hidden = dot(second, wup_ref[:, c : c + chunk])
        grad = dot(cot, wdown_ref[c : c + chunk, :], NT)
        square = hidden * hidden
        t = jnp.tanh(hidden * (c0 + (c0 * c1) * square))
        left = 0.5 + 0.5 * t
        active = (hidden * left).astype(BF16)
        slope = left + (0.5 * hidden) * (1.0 - t * t) * (c0 + (3.0 * c0 * c1) * square)
        grad = (grad * slope).astype(BF16)
        result = result + dot(active, wdown_ref[c : c + chunk, :])
        back = back + dot(grad, wup_ref[:, c : c + chunk], NT)
        down_acc[:, c : c + chunk] += dot(cot_t, active)
        up_acc[:, c : c + chunk] += dot(second_t, grad)
    out_ref[...] = result.astype(BF16)
    gain_acc[...] += jnp.sum(back * scaled, axis=0, keepdims=True)
    e = back * gain2_ref[...]
    inner = jnp.mean(e * scaled, axis=-1, keepdims=True)
    grad_middle = cot.astype(F32) + r2 * (e - scaled * inner)
    branch = grad_middle.astype(BF16)
    gmid_ref[...] = branch
    wo_acc[...] += dot(att.T, branch)
    gatt_ref[...] = dot(branch, wout_ref[...], NT).astype(BF16)

    @pl.when(step == steps - 1)
    def _():
        gain_ref[...] = gain_acc[...]
        if not final:
            up_ref[:, :ff] = up_acc[...].astype(BF16)
            up_ref[:, ff:] = wo_acc[...].astype(BF16)
            down_ref[...] = down_acc[...].astype(BF16)
            return
        if prior:
            for move in moves:
                move.wait()

        def total(acc, old, lanes):
            value = acc[:, lanes]
            return value + old[:, lanes].astype(F32) if prior else value

        def write(ref, half):
            at = 0
            for c in range(half * ff // 2, (half + 1) * ff // 2, width):
                value = total(up_acc, up_prior if prior else None, slice(c, c + width))
                ref[at : at + width, :] = value.astype(BF16)
                at += width
            lines = slice(half * width // 2, (half + 1) * width // 2)
            value = wo_acc[lines, :]
            if prior:
                value = value + up_prior[lines, ff:].astype(F32)
            ref[at : at + width // 2, :] = value.astype(BF16)
            at += width // 2
            for c in range(half * ff // 2, (half + 1) * ff // 2, width):
                value = total(down_acc, down_prior if prior else None, slice(c, c + width))
                ref[at : at + width, :] = value.T.astype(BF16)
                at += width

        @pl.when(core_ref[0] == 0)
        def _():
            write(keep_ref, 0)
            write(give_ref, 1)

        @pl.when(core_ref[0] == 1)
        def _():
            write(keep_ref, 1)
            write(give_ref, 0)


def forward(
    far_rows, kinds, core, recv, x, cot, proj, wrow, mask, gain1, gain2, w_qkv, w_out, w_up, w_down,
    first_group, groups, prior, final, token,
):
    rows, width = x.shape
    ff = w_up.shape[1]
    per = TILE // GROUP
    skip = first_group // per
    halves = width // HALF
    at = lambda wide: pl.BlockSpec((TILE, wide), lambda i: (i + skip, 0))
    like = lambda wide, kind=BF16: jax.ShapeDtypeStruct((rows, wide), kind)
    probs = jax.ShapeDtypeStruct((rows // GROUP, halves, PER_HALF * GROUP, 2 * GROUP), BF16)
    part = ff + width // 2
    if final:
        tail_shapes = [jax.ShapeDtypeStruct((part, width), BF16)] * 2
    else:
        tail_shapes = [
            jax.ShapeDtypeStruct((width, ff + width), BF16),
            jax.ShapeDtypeStruct((width, ff), BF16),
        ]
    tail_shapes = tail_shapes + [jax.ShapeDtypeStruct((1, width), F32)]
    in_specs = (
        [SMEM, SMEM, SMEM]
        + [whole(r.shape) for r in recv]
        + [at(width), at(width), at(3 * width), at(2 * GROUP)]
        + [whole(v.shape) for v in (mask, gain1, gain2, w_qkv, w_out, w_up, w_down)]
    )
    operands = [far_rows, kinds, core, *recv, x, cot, proj, wrow, mask, gain1, gain2]
    operands += [w_qkv, w_out, w_up, w_down]
    in_specs += [ANY]
    operands += [token]
    scratch = [
        pltpu.VMEM((TILE, width), BF16),
        pltpu.VMEM((width, ff), F32),
        pltpu.VMEM((width, ff), F32),
        pltpu.VMEM((width, width), F32),
        pltpu.VMEM((1, width), F32),
    ]
    aliases = {}
    if prior is not None:
        streams, sums = prior
        in_specs += [ANY, ANY, whole((1, width))] + [ANY] * 6
        operands += list(sums)
        aliases = {len(operands) + i: i for i in range(6)}
        operands += list(streams)
        scratch += [
            pltpu.VMEM((width, ff + width), BF16),
            pltpu.VMEM((width, ff), BF16),
            pltpu.SemaphoreType.DMA((2,)),
        ]
    out = pl.pallas_call(
        functools.partial(forward_kernel, first_group, len(recv), prior is not None, final),
        grid=(groups // per,),
        in_specs=in_specs,
        out_specs=[
            at(width),
            at(width),
            at(width),
            pl.BlockSpec((per,) + probs.shape[1:], lambda i: (i + skip, 0, 0, 0)),
            at(width),
            at(2 * width),
        ]
        + [whole(v.shape) for v in tail_shapes],
        out_shape=[like(width), like(width), like(width), probs, like(width), like(2 * width)]
        + tail_shapes,
        scratch_shapes=scratch,
        input_output_aliases=aliases,
        compiler_params=params(),
        cost_estimate=cost(1.0e9 * groups, 1e6 * groups),
        name="forward",
    )(*operands)
    return out[:6], out[6:]


def backward_kernel(first_group, prior, *refs):
    refs = list(refs)
    take = lambda n: [refs.pop(0) for _ in range(n)]
    (ret_rows,) = take(1)
    proj_ref, farx_ref, farkv_ref, gatt_ref, prob_ref, wrow_ref, wqkv_ref = take(7)
    if prior:
        (prior_gain,) = take(1)
        take(2)
    take(1)
    dproj_ref, dfar_ref, gw_ref, gain_ref = take(4)
    ret_refs = refs
    step = pl.program_id(0)
    tile, width = gatt_ref.shape
    units = tile // UNIT
    groups = tile // GROUP
    masks16 = head_masks(GROUP)
    head_scale = (width // HEADS) ** -0.5

    is_far = lax.broadcasted_iota(jnp.int32, (PER_HALF * GROUP, 2 * GROUP), 1) >= GROUP

    def group_step(i, carry):
        rows = pl.ds(pl.multiple_of(i * GROUP, GROUP), GROUP)
        scale = repeat_heads(wrow_ref[rows, :])
        weight_grad = jnp.zeros((GROUP, 1), F32)
        for half in range(width // HALF):
            lo = half * HALF
            q = proj_ref[rows, lo : lo + HALF] * jnp.asarray(head_scale, BF16)
            keys = jnp.concatenate(
                [proj_ref[rows, width + lo : width + lo + HALF], farkv_ref[rows, lo : lo + HALF]],
                axis=0,
            )
            vals = jnp.concatenate(
                [
                    proj_ref[rows, 2 * width + lo : 2 * width + lo + HALF],
                    farkv_ref[rows, width + lo : width + lo + HALF],
                ],
                axis=0,
            )
            q = stack_heads(q, masks16)
            up = stack_heads(gatt_ref[rows, lo : lo + HALF], masks16)
            prob = prob_ref[i, half].astype(F32)
            raw = dot(up, vals, NT)
            far_sum = jnp.sum(jnp.where(is_far, prob * raw, 0.0), axis=1, keepdims=True)
            mixed = prob * scale
            ds = mixed * raw
            total = jnp.sum(ds, axis=1, keepdims=True)
            ds = (ds - prob * total).astype(BF16)
            dq = unstack_heads(dot(ds, keys), masks16) * head_scale
            dk = dot(ds, q, TN).astype(BF16)
            dv = dot(mixed.astype(BF16), up, TN).astype(BF16)
            dproj_ref[rows, lo : lo + HALF] = dq.astype(BF16)
            dproj_ref[rows, width + lo : width + lo + HALF] = dk[:GROUP]
            dproj_ref[rows, 2 * width + lo : 2 * width + lo + HALF] = dv[:GROUP]
            dfar_ref[rows, lo : lo + HALF] = dk[GROUP:]
            dfar_ref[rows, width + lo : width + lo + HALF] = dv[GROUP:]
            for h in range(PER_HALF):
                weight_grad = weight_grad + far_sum[h * GROUP : (h + 1) * GROUP]
        pair = jnp.broadcast_to(weight_grad, (GROUP, 128)).reshape(GROUP // UNIT, UNIT, 128)
        gw_ref[i] = jnp.sum(pair, axis=1)
        return carry

    lax.fori_loop(0, groups, group_step, 0, unroll=True)

    def scatter(values, first_unit, count):
        for u in range(count):
            row = ret_rows[first_unit + u]
            edge = 0
            for ret_ref in ret_refs:
                inside = jnp.logical_and(row >= edge, row < edge + ret_ref.shape[0])

                @pl.when(inside)
                def _(ret_ref=ret_ref, edge=edge):
                    at = pl.ds(pl.multiple_of(row - edge, 16), UNIT)
                    ret_ref[at, :] = values(u)

                edge += ret_ref.shape[0]

    @pl.when(step == 0)
    def _():
        gain_ref[...] = prior_gain[...] if prior else jnp.zeros_like(gain_ref)

    grad = dot(dfar_ref[...], wqkv_ref[:, width:], NT)
    far = farx_ref[...].astype(F32)
    gain_ref[...] += jnp.sum(grad * (far * inverse_norm(far)), axis=0, keepdims=True)
    grad = grad.astype(BF16)
    scatter(
        lambda u: grad[u * UNIT : (u + 1) * UNIT],
        2 * first_group + step * units,
        units,
    )


def backward(
    ret_rows, proj, farx, farkv, gatt, prob, wrow, w_qkv, sizes, first_group, groups, prior, token
):
    rows, width = gatt.shape
    per = TILE // GROUP
    skip = first_group // per
    at = lambda wide: pl.BlockSpec((TILE, wide), lambda i: (i + skip, 0))
    in_specs = [
        SMEM,
        at(3 * width),
        at(width),
        at(2 * width),
        at(width),
        pl.BlockSpec((per,) + prob.shape[1:], lambda i: (i + skip, 0, 0, 0)),
        at(2 * GROUP),
        whole(w_qkv.shape),
    ]
    operands = [ret_rows, proj, farx, farkv, gatt, prob, wrow, w_qkv]
    aliases = {}
    if prior is not None:
        dproj, dfar, gain = prior
        in_specs += [whole(gain.shape), ANY, ANY]
        aliases = {len(operands) + 1: 0, len(operands) + 2: 1}
        operands += [gain, dproj, dfar]
    in_specs += [ANY]
    operands += [token]
    ret_specs = [whole((n, width)) for n in sizes]
    ret_shapes = [jax.ShapeDtypeStruct((n, width), BF16) for n in sizes]
    return pl.pallas_call(
        functools.partial(backward_kernel, first_group, prior is not None),
        grid=(groups // per,),
        in_specs=in_specs,
        out_specs=[
            at(3 * width),
            at(2 * width),
            pl.BlockSpec((per, GROUP // UNIT, 128), lambda i: (i, 0, 0)),
            whole((1, width)),
        ]
        + ret_specs,
        out_shape=[
            jax.ShapeDtypeStruct((rows, 3 * width), BF16),
            jax.ShapeDtypeStruct((rows, 2 * width), BF16),
            jax.ShapeDtypeStruct((groups, GROUP // UNIT, 128), F32),
            jax.ShapeDtypeStruct((1, width), F32),
        ]
        + ret_shapes,
        input_output_aliases=aliases,
        compiler_params=params(),
        cost_estimate=cost(0.4e9 * groups, 1e6 * groups),
        name="backward",
    )(*operands)


def qkv_kernel(
    extra, core_ref, x_ref, farx_ref, dproj_ref, dfar_ref, gain1_ref, wqkv_ref, gains_ref, token_ref,
    gn_ref, keep_ref, give_ref, acc, gain_acc,
):
    step = pl.program_id(0)
    steps = pl.num_programs(0)
    width = x_ref.shape[1]

    @pl.when(step == 0)
    def _():
        acc[...] = jnp.zeros_like(acc)
        gain_acc[...] = jnp.zeros_like(gain_acc)

    x = x_ref[...].astype(F32)
    scaled = x * inverse_norm(x)
    far = farx_ref[...].astype(F32)
    far = (far * inverse_norm(far) * gain1_ref[...]).astype(BF16)
    near = (scaled * gain1_ref[...]).astype(BF16)
    acc[...] += dot(near.T, dproj_ref[...])
    acc[:, width:] += dot(far.T, dfar_ref[...])
    grad = dot(dproj_ref[...], wqkv_ref[...], NT)
    gn_ref[...] = grad.astype(BF16)
    gain_acc[...] += jnp.sum(grad * scaled, axis=0, keepdims=True)

    @pl.when(step == steps - 1)
    def _():
        line = lax.broadcasted_iota(jnp.int32, (extra, width), 0)
        small = jnp.where(line == 0, gain_acc[...] + gains_ref[0:1, :], 0.0)
        small = jnp.where(line == 1, gains_ref[1:2, :], small)
        total = acc.shape[1] + extra
        half = total // 2

        def write(ref, which):
            at = which * half
            while at < (which + 1) * half:
                block, line = divmod(at, width)
                if at >= acc.shape[1]:
                    count = extra
                    value = small
                else:
                    count = min(width - line, (which + 1) * half - at)
                    value = acc[line : line + count, block * width : (block + 1) * width]
                ref[at - which * half : at - which * half + count, :] = value.astype(BF16)
                at += count

        @pl.when(core_ref[0] == 0)
        def _():
            write(keep_ref, 0)
            write(give_ref, 1)

        @pl.when(core_ref[0] == 1)
        def _():
            write(keep_ref, 1)
            write(give_ref, 0)


def qkv_grads(core, x, farx, dproj, dfar, gain1, w_qkv, gains, extra, token):
    rows, width = x.shape
    wide = w_qkv.shape[1]
    half = (wide + extra) // 2
    return pl.pallas_call(
        functools.partial(qkv_kernel, extra),
        grid=(rows // TILE,),
        in_specs=[
            SMEM,
            rows_of(TILE, width),
            rows_of(TILE, width),
            rows_of(TILE, wide),
            rows_of(TILE, 2 * width),
            whole((1, width)),
            whole(w_qkv.shape),
            whole(gains.shape),
            ANY,
        ],
        out_specs=[rows_of(TILE, width), whole((half, width)), whole((half, width))],
        out_shape=[
            jax.ShapeDtypeStruct((rows, width), BF16),
            jax.ShapeDtypeStruct((half, width), BF16),
            jax.ShapeDtypeStruct((half, width), BF16),
        ],
        scratch_shapes=[pltpu.VMEM((width, wide), F32), pltpu.VMEM((1, width), F32)],
        compiler_params=params(),
        cost_estimate=cost(10e9, 25e6),
        name="qkv_grads",
    )(core, x, farx, dproj, dfar, gain1, w_qkv, gains, token)


def row_gradient(f, x):
    r1 = inverse_norm(x)
    scaled = x * r1
    return r1 * (f - scaled * jnp.mean(f * scaled, axis=-1, keepdims=True))


def base_kernel(x_ref, gmid_ref, gn_ref, gs_ref, gain1_ref, out_ref):
    rows, width = x_ref.shape
    spread = jnp.broadcast_to(gs_ref[...][:, None, :], (rows // UNIT, UNIT, width))
    f = (gn_ref[...].astype(F32) + spread.reshape(rows, width)) * gain1_ref[...]
    grad = gmid_ref[...].astype(F32) + row_gradient(f, x_ref[...].astype(F32))
    out_ref[...] = grad.astype(BF16)


def base_rows(x, gmid, gn, gs, gain1):
    rows, width = x.shape
    return pl.pallas_call(
        base_kernel,
        grid=(rows // TILE,),
        in_specs=[
            rows_of(TILE, width),
            rows_of(TILE, width),
            rows_of(TILE, width),
            rows_of(TILE // UNIT, width),
            whole((1, width)),
        ],
        out_specs=rows_of(TILE, width),
        out_shape=jax.ShapeDtypeStruct((rows, width), BF16),
        compiler_params=params(),
        cost_estimate=cost(rows * width * 20, rows * width * 8),
        name="base",
    )(x, gmid, gn, gs, gain1)


def last_kernel(sizes, extra, capacity, table_ref, place_ref, *refs):
    ret_refs = refs[: len(sizes)]
    x_ref, base_ref, gain1_ref, outa_ref, outb_ref, acc = refs[len(sizes) :]
    rows_a = outa_ref.shape[0]
    acc[...] = jnp.zeros_like(acc)

    begin = 0
    for index, (size, ret_ref) in enumerate(zip(sizes, ret_refs)):
        height = size * UNIT + (extra if index == len(sizes) - 1 else 0)

        def add(r, carry, size=size, ret_ref=ret_ref, begin=begin, height=height):
            for slot in range(size):
                unit = table_ref[r * capacity + begin + slot]

                @pl.when(unit >= 0)
                def _():
                    at = pl.ds(pl.multiple_of(unit * UNIT, UNIT), UNIT)
                    src = pl.ds(pl.multiple_of(r * height + slot * UNIT, 16), UNIT)
                    acc[at, :] += ret_ref[src, :].astype(F32)

            return carry

        lax.fori_loop(0, ret_ref.shape[0] // height, add, 0)
        begin += size

    def finish(out_ref, first):
        def body(u, carry):
            at = pl.ds(pl.multiple_of(place_ref[first + u] * UNIT, UNIT), UNIT)
            own = pl.ds(pl.multiple_of((first + u) * UNIT, UNIT), UNIT)
            f = acc[own, :] * gain1_ref[...]
            grad = base_ref[at, :].astype(F32) + row_gradient(f, x_ref[own, :].astype(F32))
            out_ref[pl.ds(pl.multiple_of(u * UNIT, UNIT), UNIT), :] = grad.astype(BF16)
            return carry

        lax.fori_loop(0, out_ref.shape[0] // UNIT, body, 0, unroll=2)

    finish(outa_ref, 0)
    finish(outb_ref, rows_a // UNIT)


def last(table, place, ret, sizes, extra, capacity, x, base, gain1, rows_a):
    rows, width = x.shape
    return pl.pallas_call(
        functools.partial(last_kernel, sizes, extra, capacity),
        in_specs=[SMEM, SMEM] + [VMEM] * (len(ret) + 3),
        out_specs=[VMEM, VMEM],
        out_shape=[
            jax.ShapeDtypeStruct((rows_a, width), BF16),
            jax.ShapeDtypeStruct((rows - rows_a, width), BF16),
        ],
        scratch_shapes=[pltpu.VMEM((rows, width), F32)],
        compiler_params=limit(24),
        cost_estimate=cost(rows * width * 20, rows * width * 12),
        name="last",
    )(table, place, *ret, x, base, gain1)


def bits_of(size):
    count = 0
    while (1 << count) < size:
        count += 1
    return count


def bit_of(axis, bit):
    return (lax.axis_index(axis) >> bit) & 1


def swap(values, axis, bit):
    size = lax.axis_size(axis)
    return lax.ppermute(values, axis, [(i, i ^ (1 << bit)) for i in range(size)])


def halve(values, axis, bit):
    half = values.shape[0] // 2
    mine = bit_of(axis, bit)
    keep = lax.dynamic_slice_in_dim(values, mine * half, half, 0)
    give = lax.dynamic_slice_in_dim(values, (1 - mine) * half, half, 0)
    return keep, give


def double(values, axis, bit):
    got = swap(values, axis, bit)
    return jnp.where(
        bit_of(axis, bit) == 0,
        jnp.concatenate([values, got], axis=0),
        jnp.concatenate([got, values], axis=0),
    )


def add(one, two):
    return (one.astype(F32) + two.astype(F32)).astype(BF16)


def reduce_any(values, order):
    for axis, bit in order:
        keep, give = halve(values, axis, bit)
        values = add(keep, swap(give, axis, bit))
    for axis, bit in reversed(order):
        values = double(values, axis, bit)
    return values


def tie(values, *tokens):
    return pl.pallas_call(
        lambda *refs: None,
        in_specs=[ANY] * (1 + len(tokens)),
        out_specs=ANY,
        out_shape=jax.ShapeDtypeStruct(values.shape, values.dtype),
        input_output_aliases={0: 0},
        name="tie",
    )(values, *tokens)


def halve_kernel(ranges, sources, bits_ref, *refs):
    outs = refs[2 * sources + 1 :]
    for source, first, count, bit, out, there in ranges:
        own, came = refs[2 * source], refs[2 * source + 1]
        half = count // 2
        keep = pl.multiple_of(first + bits_ref[bit] * half, 16)
        give = pl.multiple_of(first + (1 - bits_ref[bit]) * half, 16)
        for ref, line in ((outs[2 * out], keep), (outs[2 * out + 1], give)):
            rows = pl.ds(line, half)
            total = own[rows, :].astype(F32) + came[rows, :].astype(F32)
            ref[there : there + half, :] = total.astype(BF16)


def halve_step(ranges, bits, pairs, token):
    width = pairs[0][0].shape[1]
    count = 1 + max(r[4] for r in ranges)
    heights = [max(r[5] + r[2] // 2 for r in ranges if r[4] == out) for out in range(count)]
    shapes = [jax.ShapeDtypeStruct((n, width), BF16) for n in heights for _ in range(2)]
    flat = [v for pair in pairs for v in pair]
    out = pl.pallas_call(
        functools.partial(halve_kernel, ranges, len(pairs)),
        in_specs=[SMEM] + [VMEM] * len(flat) + [ANY],
        out_specs=[VMEM] * len(shapes),
        out_shape=shapes,
        compiler_params=limit(24),
        cost_estimate=cost(0, 8 * sum(heights) * width),
        name="halve_step",
    )(jnp.stack([bit_of(*b) for b in bits]).astype(jnp.int32), *flat, token)
    return [(out[2 * i], out[2 * i + 1]) for i in range(count)]


def double_kernel(ranges, sources, tokens, bits_ref, *refs):
    outs = refs[2 * sources + tokens :]
    for source, first, count, bit, out, there in ranges:
        own, came = refs[2 * out], refs[2 * out + 1]
        half = count // 2
        keep = pl.multiple_of(first + bits_ref[bit] * half, 16)
        give = pl.multiple_of(first + (1 - bits_ref[bit]) * half, 16)
        outs[source][pl.ds(keep, half), :] = own[there : there + half, :]
        outs[source][pl.ds(give, half), :] = came[there : there + half, :]


def double_step(ranges, bits, pairs, *tokens):
    width = pairs[0][0].shape[1]
    count = 1 + max(r[0] for r in ranges)
    heights = [max(r[1] + r[2] for r in ranges if r[0] == source) for source in range(count)]
    flat = [v for pair in pairs for v in pair]
    return pl.pallas_call(
        functools.partial(double_kernel, ranges, len(pairs), len(tokens)),
        in_specs=[SMEM] + [VMEM] * len(flat) + [ANY] * len(tokens),
        out_specs=[VMEM] * count,
        out_shape=[jax.ShapeDtypeStruct((n, width), BF16) for n in heights],
        compiler_params=limit(24),
        cost_estimate=cost(0, 4 * sum(heights) * width),
        name="double_step",
    )(jnp.stack([bit_of(*b) for b in bits]).astype(jnp.int32), *flat, *tokens)


AXIS_X, AXIS_Y, AXIS_Z0, AXIS_Z1 = ("dp", 1), ("blk", 0), ("blk", 1), ("blk", 2)


def places(half, width, ff):
    up, down, out, qkv, gains = range(5)
    edge = ff // 2
    result = [
        (c, width, up, 0, half * edge + c) for c in range(0, edge, width)
    ]
    result.append((edge, width // 2, out, half * (width // 2), 0))
    result += [
        (edge + width // 2 + c, width, down, half * edge + c, 0) for c in range(0, edge, width)
    ]
    start = edge + width // 2 + edge
    total = 3 * width + EXTRA
    at = half * total // 2
    while at < (half + 1) * total // 2:
        block, line = divmod(at, width)
        if at >= 3 * width:
            result.append((start + at - half * total // 2, 16, gains, 0, 0))
            break
        count = min(width - line, (half + 1) * total // 2 - at)
        result.append((start + at - half * total // 2, count, qkv, line, block * width))
        at += count
    return result


def assemble_kernel(which, prior, width, ff, core_ref, values_ref, *refs):
    outs = refs[5 if prior else 0 :][:5]
    held, sems = refs[-2:]

    def write(half):
        copies = []
        for i, (first, count, out, line, column) in enumerate(places(half, width, ff)):
            held[first : first + count, :] = values_ref[first : first + count, :].astype(F32)
            copy = pltpu.make_async_copy(
                held.at[pl.ds(first, count)],
                outs[out].at[pl.ds(line, count), pl.ds(column, width)],
                sems.at[i],
            )
            copy.start()
            copies.append(copy)
        for copy in copies:
            copy.wait()

    @pl.when(core_ref[0] == which)
    def _():
        write(0)

    @pl.when(core_ref[0] != which)
    def _():
        write(1)


def assemble(core, which, values, width, ff, prior):
    shapes = [(width, ff), (ff, width), (width, width), (width, 3 * width), (16, width)]
    operands = [core, values] + (list(prior) if prior is not None else [])
    most = max(len(places(half, width, ff)) for half in (0, 1))
    return pl.pallas_call(
        functools.partial(assemble_kernel, which, prior is not None, width, ff),
        in_specs=[SMEM, VMEM] + [ANY] * (len(operands) - 2),
        out_specs=[ANY] * 5,
        out_shape=[jax.ShapeDtypeStruct(shape, F32) for shape in shapes],
        scratch_shapes=[pltpu.VMEM(values.shape, F32), pltpu.SemaphoreType.DMA((most,))],
        input_output_aliases={} if prior is None else {2 + i: i for i in range(5)},
        compiler_params=limit(16),
        cost_estimate=cost(0, values.size * 6),
        name="assemble",
    )(*operands)


def exchange(values, devices):
    shape = values.shape
    parts = values.reshape(devices, shape[0] // devices, *shape[1:])
    return lax.all_to_all(parts, "blk", split_axis=0, concat_axis=0, tiled=True).reshape(shape)


def per_device(
    x_a, x_b, sel_a, sel_b, gain_one, w_qkv, w_out, w_sort, gain_two, w_up, w_down, cot_a, cot_b
):
    devices = lax.axis_size("blk")
    me = lax.axis_index("blk")
    seqs_a, rows_a, width = x_a.shape
    seqs_b, rows_b, _ = x_b.shape
    npl = sel_a.shape[1]
    blocks = npl * devices
    len_a = rows_a // npl
    len_b = rows_b // npl
    total_a = seqs_a * rows_a
    total_b = seqs_b * rows_b
    rows = total_a + total_b
    units = rows // UNIT
    units_a = total_a // UNIT
    count_a = seqs_a * npl
    count_b = seqs_b * npl
    picks = count_a + count_b
    picks_up = -(-picks // 16) * 16
    groups = rows // GROUP
    per = TILE // GROUP
    capacity = 2 * max(1, (4 * units + 5 * devices - 1) // (5 * devices))
    send_rows = devices * capacity * UNIT
    ff = w_up.shape[1]
    gain1 = gain_one.astype(F32).reshape(1, width)
    gain2 = gain_two.astype(F32).reshape(1, width)

    first, early = capacity, groups
    if capacity > 8:
        full, left = divmod(units, capacity)
        sure = (full * 8 + min(left, 8)) // 2 // per * per
        if capacity == 14 and 0 < sure < groups:
            first, early = 8, sure

    sizes = [8, 7] if early < groups else [capacity]
    extra = 16
    sel = jnp.concatenate([sel_a.reshape(-1), sel_b.reshape(-1)])
    table, back_table, far_rows, ret_rows, perm, place, kinds = request(
        sel, npl, seqs_a, seqs_b, devices, capacity, first, early, sizes, extra, picks_up
    )

    average = np.zeros((picks, units), np.float32)
    for j in range(count_a):
        average[j, 2 * j : 2 * j + 2] = 1.0 / len_a
    for j in range(count_b):
        average[count_a + j, units_a + j] = 1.0 / len_b
    x, means, logits = digest(
        x_a.reshape(-1, width), x_b.reshape(-1, width), gain1, average, w_sort
    )
    spare = -(-picks // 8) * 8 + 8 - picks
    news = jnp.concatenate([logits, sel.astype(F32)[:, None]], axis=1)
    news = jnp.pad(news, ((0, spare), (0, 127 - blocks)))
    both = jnp.concatenate(
        [table.reshape(devices, capacity), back_table.reshape(devices, sum(sizes))], axis=1
    ).astype(F32)
    asked = jnp.pad(both[:, None], ((0, 0), (picks, spare - 1), (0, 128 - both.shape[1])))
    news = lax.all_to_all(news[None] + asked, "blk", split_axis=0, concat_axis=0, tiled=True)
    table = news[:, picks, :capacity].astype(jnp.int32).reshape(-1)
    back_table = news[:, picks, capacity : both.shape[1]].astype(jnp.int32).reshape(-1)
    news = news[:, :picks]
    parcels = pack(table, x, devices, capacity, first, picks_up)
    recv = [exchange(parcels[0], devices)]
    summary = means * gain1
    rs = inverse_norm(summary)
    unit_summary = (summary * rs).astype(BF16)
    all_summaries = jnp.broadcast_to(
        jnp.pad(unit_summary, ((0, picks_up - picks), (0, 0))), (devices, picks_up, width)
    )

    xp, cot = arrange(perm, x, cot_a.reshape(-1, width), cot_b.reshape(-1, width))
    proj = project(xp, gain1, w_qkv)

    def by_sequence(values):
        tail = values.shape[2:]
        one = values[:, :count_a].reshape((devices, seqs_a, npl) + tail)
        two = values[:, count_a:].reshape((devices, seqs_b, npl) + tail)
        both = jnp.concatenate([one, two], axis=1)
        return jnp.swapaxes(both, 0, 1).reshape((seqs_a + seqs_b, blocks) + tail)

    def own_rows(values):
        return lax.dynamic_slice_in_dim(values, me * npl, npl, 1).reshape((-1,) + values.shape[2:])

    def to_units(values):
        return jnp.concatenate(
            [jnp.repeat(values[:count_a], len_a // UNIT, axis=0), values[count_a:]], axis=0
        )

    news = by_sequence(news)
    logits = news[..., :blocks]
    picked = (news[..., blocks : blocks + 1] == jnp.arange(blocks, dtype=F32)).astype(F32)
    weights = jnp.take(to_units(own_rows(sinkhorn(logits, picked))), perm, axis=0)
    lane = jnp.arange(2 * GROUP) >= GROUP
    wrow = jnp.where(lane[None, :], jnp.repeat(weights, UNIT, axis=0), 1.0)
    if len(parcels) > 1:
        tall = (capacity - first) * UNIT
        parcel = lax.dynamic_update_slice(
            parcels[1].reshape(devices, -1, width), all_summaries, (0, tall, 0)
        )
        recv.append(exchange(tie(parcel.reshape(-1, width), wrow, proj), devices))
        units_all = recv[1].reshape(devices, -1, width)[:, tall:]
    else:
        units_all = exchange(all_summaries.reshape(-1, width), devices)
        units_all = units_all.reshape(devices, picks_up, width)
    units_all = by_sequence(units_all[:, :picks])
    block_of = np.arange(GROUP) // len_b
    cross = block_of[:, None] != block_of[None, :]
    mask = np.zeros((2, GROUP, 2 * GROUP), np.float32)
    mask[1] = np.where(np.concatenate([cross, cross], axis=1), -1e30, 0.0)

    core = bit_of("dp", 0).astype(jnp.int32).reshape(1)
    shared = (xp, cot, proj, wrow, mask, gain1, gain2, w_qkv, w_out, w_up, w_down)
    heights = [
        devices * (n * UNIT + (extra if i == len(sizes) - 1 else 0))
        for i, n in enumerate(sizes)
    ]

    def run_backward(streams, *rest):
        _, _, gatt, prob, farx, farkv = streams
        return backward(ret_rows, proj, farx, farkv, gatt, prob, wrow, w_qkv, *rest)

    fast = lax.axis_size("dp") == 4 and devices == 8 and early < groups
    part_x = ff // 2 + width // 2
    if early < groups:
        prior = forward(far_rows, kinds, core, recv[:1], *shared, 0, early, None, False, wrow)
        dproj, dfar, gw_one, gain, *ret = run_backward(
            prior[0], heights[:1], 0, early, None, prior[0][0]
        )
        back = [exchange(v, devices) for v in ret]
        streams, sums = forward(
            far_rows, kinds, core, recv, *shared, early, groups - early, prior, True, gain
        )
        keep, give, g_gain2 = sums
        out_a, out_b = restore(perm, streams[0], total_a)
        big_came = swap(give, "dp", 0)
        token = keep
        if fast:
            ranges_one = [(0, 0, part_x, 0, 0, 0), (0, part_x, keep.shape[0] - part_x, 1, 1, 0)]
            (bx, gx), (by, gy) = halve_step(
                ranges_one, [AXIS_X, AXIS_Y], [(keep, big_came)], out_a
            )
            bx_came, by_came = swap(gx, *AXIS_X), swap(gy, *AXIS_Y)
            token = bx
        dproj, dfar, gw_two, g_gain1_far, *ret = run_backward(
            streams, heights[1:], early, groups - early, (dproj, dfar, gain), token
        )
        gw = jnp.concatenate([gw_one, gw_two])
    else:
        streams, sums = forward(far_rows, kinds, core, recv, *shared, 0, groups, None, True, wrow)
        keep, give, g_gain2 = sums
        out_a, out_b = restore(perm, streams[0], total_a)
        big_came = swap(give, "dp", 0)
        back = []
        dproj, dfar, gw, g_gain1_far, *ret = run_backward(
            streams, heights, 0, groups, None, keep
        )
    _, gmid, _, _, farx, _ = streams

    gw = jnp.take(gw[:, :, 0].reshape(-1), place)
    gw = jnp.concatenate(
        [jnp.sum(gw[:units_a].reshape(-1, len_a // UNIT), axis=1), gw[units_a:]]
    )
    gw = jnp.pad(gw.astype(BF16)[None], ((0, extra - 1), (0, width - picks)))
    if fast:
        gw = tie(gw, bx_came, by_came, back[0])
    tall = sizes[len(back)] * UNIT
    parcel = lax.dynamic_update_slice(
        ret[0].reshape(devices, -1, width), jnp.broadcast_to(gw, (devices, extra, width)), (0, tall, 0)
    )
    arrived = exchange(parcel.reshape(-1, width), devices)
    back.append(arrived)
    gains = jnp.concatenate([g_gain1_far, g_gain2], axis=0)
    token = dproj
    gn, late_keep, late_give = qkv_grads(
        core, xp, farx, dproj, dfar, gain1, w_qkv, gains, EXTRA, token
    )
    late_came = swap(late_give, "dp", 0)
    part_late = 512
    gw = arrived.reshape(devices, -1, width)[:, tall:, :picks]
    if fast:
        late_rows = late_keep.shape[0]
        ranges_late = [(0, 0, part_late, 0, 0, 0), (0, part_late, late_rows - part_late, 1, 1, 0)]
        (lx, gx), (ly, gy) = halve_step(
            ranges_late, [AXIS_X, AXIS_Y], [(late_keep, late_came)], late_came
        )
        lx_came, ly_came = swap(gx, *AXIS_X), swap(gy, *AXIS_Y)
        nbx, nlx, nby, nly = (v.shape[0] for v in (bx, lx, by, ly))
        ranges_two = [
            (0, 0, nbx, 0, 0, 0),
            (1, 0, nlx, 0, 0, nbx // 2),
            (2, 0, nby, 1, 1, 0),
            (3, 0, nly, 1, 1, nby // 2),
        ]
        (vx, gx), (vy, gy) = halve_step(
            ranges_two,
            [AXIS_Y, AXIS_X],
            [(bx, bx_came), (lx, lx_came), (by, by_came), (ly, ly_came)],
            lx,
        )
        vx_came, vy_came = swap(gx, *AXIS_Y), swap(gy, *AXIS_X)
        cuts = [nbx // 2, nlx // 2, nby // 2, nly // 2]
        ranges_three = [
            (0, 0, cuts[0], 0, 0, 0),
            (0, cuts[0], cuts[1], 0, 0, cuts[0] // 2),
            (1, 0, cuts[2], 0, 0, (cuts[0] + cuts[1]) // 2),
            (1, cuts[2], cuts[3], 0, 0, (cuts[0] + cuts[1] + cuts[2]) // 2),
        ]
        ((total, gz),) = halve_step(
            ranges_three, [AXIS_Z0], [(vx, vx_came), (vy, vy_came)], arrived
        )
        gw = tie(gw, total)
        total = add(total, swap(gz, *AXIS_Z0))
    gw = by_sequence(gw[:, 0].astype(F32))
    g_logits = sinkhorn_back(logits, picked, jnp.broadcast_to(gw[..., None], logits.shape)) * (
        1.0 / SOFTMAX_HEAT
    )
    precise = lax.Precision.HIGHEST
    flat_logits = g_logits.reshape(-1, blocks)
    flat_units = units_all.reshape(-1, width).astype(F32)
    g_sort = lax.dot_general(
        flat_logits, flat_units, TN, precision=precise, preferred_element_type=F32
    )
    g_unit = lax.dot_general(
        flat_logits, w_sort.astype(F32), NT, precision=precise, preferred_element_type=F32
    )
    g_own = own_rows(g_unit.reshape(g_logits.shape[:2] + (width,)))
    g_summary = rs * (
        g_own - summary * rs * rs * jnp.mean(g_own * summary, axis=-1, keepdims=True)
    )
    both = g_unit * flat_units
    both = both - flat_units * flat_units * jnp.mean(both, axis=-1, keepdims=True)
    small = jnp.concatenate([g_sort, jnp.sum(both, axis=0, keepdims=True) / gain1], axis=0)
    spread = to_units(
        jnp.concatenate([g_summary[:count_a] / len_a, g_summary[count_a:] / len_b], axis=0)
    )
    base = base_rows(xp, gmid, gn, jnp.take(spread, perm, axis=0), gain1)

    gx_a, gx_b = last(back_table, place, back, sizes, extra, sum(sizes), x, base, gain1, total_a)
    if fast:
        for bit in (0, 1):
            small = small + swap(small, "dp", bit)
        total = add(total, tie(swap(total, *AXIS_Z1), gx_a, small))
        vx, vy = double_step(ranges_three, [AXIS_Z0], [(total, swap(total, *AXIS_Z0))])
        ranges_back = [
            (0, 0, nbx, 0, 0, 0),
            (0, nbx, nlx, 0, 0, cuts[0]),
            (1, 0, nby, 1, 1, 0),
            (1, nby, nly, 1, 1, cuts[2]),
        ]
        vx, vy = double_step(
            ranges_back,
            [AXIS_Y, AXIS_X],
            [(vx, swap(vx, *AXIS_Y)), (vy, swap(vy, *AXIS_X))],
        )
        big_rows = keep.shape[0]
        ranges_all = [
            (0, 0, part_x, 0, 0, 0),
            (0, big_rows, part_late, 0, 0, nbx),
            (0, part_x, big_rows - part_x, 1, 1, 0),
            (0, big_rows + part_late, late_rows - part_late, 1, 1, nby),
        ]
        (sums_own,) = double_step(
            ranges_all,
            [AXIS_X, AXIS_Y],
            [(vx, swap(vx, *AXIS_X)), (vy, swap(vy, *AXIS_Y))],
        )
    else:
        across = [("dp", bit) for bit in range(1, bits_of(lax.axis_size("dp")))]
        along = [("blk", bit) for bit in range(bits_of(devices))]
        sums_own = jnp.concatenate(
            [
                reduce_any(add(keep, big_came), across + along),
                reduce_any(add(late_keep, late_came), along + across),
            ],
            axis=0,
        )
    sums_came = swap(sums_own, "dp", 0)

    if not fast:
        small = lax.psum(small, "dp")
    written = assemble(core, 0, sums_own, width, ff, None)
    sum_up, sum_down, sum_out, sum_qkv, gains = assemble(core, 1, sums_came, width, ff, written)

    return (
        out_a.reshape(x_a.shape),
        out_b.reshape(x_b.shape),
        gx_a.reshape(x_a.shape),
        gx_b.reshape(x_b.shape),
        gains[0] + small[blocks],
        sum_qkv,
        sum_out,
        small[:blocks].T,
        gains[1],
        sum_up,
        sum_down,
    )


def solution(mesh):
    rows_spec = P("dp", "blk", None)
    in_specs = (
        (rows_spec, rows_spec, P("dp", "blk"), P("dp", "blk")) + (P(),) * 7 + (rows_spec, rows_spec)
    )
    out_specs = (rows_spec,) * 4 + (P(),) * 7
    return jax.shard_map(
        per_device, mesh=mesh, in_specs=in_specs, out_specs=out_specs, check_vma=False
    )
```

time: 1290 us -> 408 us (0.32)
  blocking collectives: 326 us -> 15.5 us
  other arithmetic: 260 us -> 16.9 us
  local copies, waits for them, and re-layouts: 277 us -> 46.3 us
  Pallas kernels: 0 us -> 193 us
  matrix products: 180 us -> 0.96 us
  waiting for transfers between devices: 206 us -> 92.7 us
  starting transfers between devices: 9.94 us -> 32.6 us
  between operations: 18.2 us -> 1.8 us
    all_gather x6 -> x0, blocking collectives: 286 us -> none  [the longest x1 164 us: per_device(): lax.all_gather(logits_b, 'blk', axis=1, tiled=True)]
    pallas_call x0 -> x28, Pallas kernels: none -> 193 us  [the longest x2 70.3 us: forward(): pl.pallas_call(functools.partial(forward_kernel, first_group, len(recv),...]
    dot_general x42 -> x2, matrix products: 180 us -> 0.96 us  [the longest x1 0.59 us: per_device(): lax.dot_general(flat_logits, w_sort.astype(F32), NT, precision=precise, p...]
    psum x1 -> x0, waiting for transfers between devices: 162 us -> none  [per_device(): lax.psum((grad_gain_one, grad_qkv, grad_w_out, grad_sort, grad_gain_two,...]
    sub x2 -> x0, other arithmetic: 102 us -> none  [attend_back(): prob_grad - jnp.sum(probabilities * prob_grad, axis=-1, keepdims=True)]
    reshape x29 -> x9, local copies, waits for them, and re-layouts: 95.2 us -> 3.63 us  [the longest x2 1.52 us: per_device(): sel = jnp.concatenate([sel_a.reshape(-1), sel_b.reshape(-1)])]
    ppermute x0 -> x18, waiting for transfers between devices: none -> 70 us  [swap(): return lax.ppermute(values, axis, [(i, i ^ 1 << bit) for i in range(size)])]
    mul x11 -> x0, local copies, waits for them, and re-layouts: 46.7 us -> none  [the longest x2 13.9 us: attend_back(): jnp.einsum('nhqk,nqhd->nkhd', near_ds, queries, preferred_element_type=jn...]
  transfers between devices with their start and end apart: 3 -> 22, of which waited for: 2 -> 12; matrix products, arithmetic and copies ran while one was open for 15% -> 5% of each run, Pallas kernels for 0% -> 42%
where the time goes in v1:
time: 408 us; the launch traced here: 400 us
  Pallas kernels  193 us (47%)
  waiting for transfers between devices  92.7 us (23%)
  local copies, waits for them, and re-layouts  46.3 us (11%)
  starting transfers between devices  32.6 us (8%)
  other arithmetic  16.9 us (4%)
  blocking collectives  15.5 us (4%)
    pallas_call x2, Pallas kernels, forward(): pl.pallas_call(functools.partial(forward_kernel, first_group, len(recv),...  70.3 us
    ppermute x18, waiting for transfers between devices, swap(): return lax.ppermute(values, axis, [(i, i ^ 1 << bit) for i in range(size)])  70 us
    pallas_call x2, Pallas kernels, backward(): pl.pallas_call(functools.partial(backward_kernel, first_group, prior is n...  36.2 us
    unnamed x107, local copies, waits for them, and re-layouts  29.4 us
    all_to_all x4, waiting for transfers between devices, exchange(): lax.all_to_all(parts, 'blk', split_axis=0, concat_axis=0, tiled=True)  22.8 us
    all_to_all x4, starting transfers between devices, exchange(): lax.all_to_all(parts, 'blk', split_axis=0, concat_axis=0, tiled=True)  20.2 us
    all_to_all x1, blocking collectives, per_device(): lax.all_to_all(news[None] + asked, 'blk', split_axis=0, concat_axis=0, ti...  15.5 us
    pallas_call x1, Pallas kernels, qkv_grads(): pl.pallas_call(functools.partial(qkv_kernel, extra), grid=(rows // TILE,)...  15.5 us
  transfers between devices with their start and end apart: 22, of which 12 were waited for; matrix products, arithmetic and copies ran while one was open for 5% of the time, Pallas kernels for 42%

profile of v1, /device:TPU:0, one launch (start us, length us, event | category | flops | bytes accessed | tf_op | source)
XLA Modules:
  0.0 400.1 jit_solution(16587899394625579094)
XLA Ops:
  4.9 1.6 copy.59.wsort_ref
  7.3 4.5 %request.1 = (s32[112]{0:T(128)}, s32[120]{0:T(128)}, s32[64]{0:T(128)}, s32[64]{0:T(128)}, s32[64]{0:T(128)}, /*index=5*/s32[64]{0:T(128)}, s32[2]{0:T(128)}) custom-call(s32[48]{0:T(128)} %pad_add_fusion.1.sel_ref), custom_call_target="tpu_custom_call" | custom-call | flops 1 | bytes 2 | tf_op jit(solution)/shard_map/request/pallas_call | solution.py:204
  13.2 6.8 %digest.1 = (bf16[2048,512]{1,0:T(8,128)(2,1)}, f32[48,512]{1,0:T(8,128)}, f32[48,64]{1,0:T(8,128)}) custom-call(bf16[1024,512]{1,0:T(8,128)(2,1)} %bitcast.100, bf16[1024,512]{1,0:T(8,128)(2,1)} %bitcast.101, f32[1,512]{1,0:T(1,128)} %bitcast.84, f32[48,64]{1,0:T(8,128)} %constant.86.clone.avg_ref, bf16[512,64]{1,0:T(8,128)(2,1)} %copy.59.wsort_ref), custom_call_target="tpu_custom_call" | custom-call | flops 10485 | bytes 4194 | tf_op jit(solution)/shard_map/digest/pallas_call | solution.py:256
  21.0 15.5 %all_to_all.25 = f32[8,56,128]{2,1,0:T(8,128)S(1)} all-to-all(f32[8,56,128]{2,1,0:T(8,128)S(1)} %copy.61), channel_id=1, replica_groups=mesh['dp'=4,'blk'=8] {'blk'}, dimensions={0} | all-to-all | bytes 458752 | tf_op jit(solution)/shard_map/all_to_all | solution.py:1316
  36.6 1.6 copy-done.2
  38.2 3.2 pack.1
  44.1 4.6 %all-to-all-start.1 = ((bf16[8,256,512]{2,1,0:T(8,128)(2,1)}), bf16[8,256,512]{2,1,0:T(8,128)(2,1)}, u32[]{:S(2)}, u32[]{:S(2)}) async-start(bf16[8,256,512]{2,1,0:T(8,128)(2,1)} %bitcast.80), calls=%async_computation.1 | async-start | bytes 4194304 | tf_op jit(solution)/shard_map/all_to_all | solution.py:1256
  50.0 1.9 arrange.1
  51.8 1.4 copy-done
  54.5 9.4 %project.1.refs_2_.refs_6_.refs_1_.refs_7_ = bf16[2048,1536]{1,0:T(8,128)(2,1)} custom-call(bf16[2048,512]{1,0:T(8,128)(2,1)} %copy-done, f32[1,512]{1,0:T(1,128)} %bitcast.85, bf16[512,1536]{1,0:T(8,128)(2,1)} %wqkv_ref.1), custom_call_target="tpu_custom_call" | custom-call | flops 3221225 | bytes 8388 | tf_op jit(solution)/shard_map/project/pallas_call | solution.py:404
  65.3 3.7 sinkhorn.1
  73.0 22.8 %all-to-all-done.1 = bf16[8,256,512]{2,1,0:T(8,128)(2,1)} async-done(((bf16[8,256,512]{2,1,0:T(8,128)(2,1)}), bf16[8,256,512]{2,1,0:T(8,128)(2,1)}, u32[]{:S(2)}, u32[]{:S(2)}) %all-to-all-start.1) | async-done | bytes 2097184 | tf_op jit(solution)/shard_map/all_to_all | solution.py:1256
  95.7 4.5 %all-to-all-start.2 = ((bf16[8,240,512]{2,1,0:T(8,128)(2,1)}), bf16[8,240,512]{2,1,0:T(8,128)(2,1)}, u32[]{:S(2)}, u32[]{:S(2)}) async-start(bf16[8,240,512]{2,1,0:T(8,128)(2,1)} %bitcast.79), calls=%async_computation.2 | async-start | bytes 3932160 | tf_op jit(solution)/shard_map/all_to_all | solution.py:1256
  100.9 40.6 %forward.2 = (bf16[2048,512]{1,0:T(8,128)(2,1)}, bf16[2048,512]{1,0:T(8,128)(2,1)}, bf16[2048,512]{1,0:T(8,128)(2,1)}, bf16[32,2,256,128]{3,2,1,0:T(8,128)(2,1)}...) custom-call(s32[64]{0:T(128)} %get-tuple-element.89.refs_0_, ...), custom_call_target="tpu_custom_call" | custom-call | flops 20000000 | bytes 20000 | tf_op jit(solution)/shard_map/forward/pallas_call | solution.py:720
  141.5 21.6 %backward.2 = (bf16[2048,1536]{1,0:T(8,128)(2,1)}, bf16[2048,1024]{1,0:T(8,128)(2,1)}, f32[20,2,128]{2,1,0:T(2,128)}, f32[1,512]{1,0:T(1,128)}, bf16[2048,512]{1,0:T(8,128)(2,1)}) custom-call(s32[64]{0:T(128)} %get-tuple-element.100.refs_0_, bf16[2048,1536]{1,0:T(8,128)(2,1)} %project.1.refs_2_.refs_6_.refs_1_.refs_7_, ...), custom_call_target="tpu_custom_call" | custom-call | flops 8000000 | bytes 20000 | tf_op jit(solution)/shard_map/backward/pallas_call | solution.py:864
  163.1 6.2 %all-to-all-start.3 = ((bf16[8,256,512]{2,1,0:T(8,128)(2,1)}), bf16[8,256,512]{2,1,0:T(8,128)(2,1)}, u32[]{:S(2)}, u32[]{:S(2)}) async-start(bf16[8,256,512]{2,1,0:T(8,128)(2,1)} %bitcast.96), calls=%async_computation.3 | async-start | bytes 4194304 | tf_op jit(solution)/shard_map/all_to_all | solution.py:1256
  169.4 29.7 %forward.3 = (bf16[2048,512]{1,0:T(8,128)(2,1)}, bf16[2048,512]{1,0:T(8,128)(2,1)}, bf16[2048,512]{1,0:T(8,128)(2,1)}, bf16[32,2,256,128]{3,2,1,0:T(8,128)(2,1)}...) custom-call(s32[64]{0:T(128)} %get-tuple-element.89.refs_0_, ...), custom_call_target="tpu_custom_call", output_to_operand_aliasing={{0}: (20, {}), {1}: (21, {}), {2}: (22, {}), {3}: (23, {}),... | custom-call | flops 12000000 | bytes 12000 | tf_op jit(solution)/shard_map/forward/pallas_call | solution.py:720
  199.3 1.6 copy-done.1
  200.9 3.1 restore.1
  204.1 1.7 copy-done.11
  207.0 3.1 halve_step.4
  211.8 1.5 collective-permute-start.1
  213.2 2.0 collective-permute-start.2
  215.3 14.6 %backward.3 = (bf16[2048,1536]{1,0:T(8,128)(2,1)}, bf16[2048,1024]{1,0:T(8,128)(2,1)}, f32[12,2,128]{2,1,0:T(2,128)}, f32[1,512]{1,0:T(1,128)}, bf16[1920,512]{1,0:T(8,128)(2,1)}) custom-call(s32[64]{0:T(128)} %get-tuple-element.100.refs_0_, ...), custom_call_target="tpu_custom_call", output_to_operand_aliasing={{0}: (9, {}), {1}: (10, {})} | custom-call | flops 4800000 | bytes 12000 | tf_op jit(solution)/shard_map/backward/pallas_call | solution.py:864
  233.6 1.4 broadcast_dynamic-update-slice_fusion.1
  235.0 4.8 %all-to-all-start.4 = ((bf16[8,240,512]{2,1,0:T(8,128)(2,1)}), bf16[8,240,512]{2,1,0:T(8,128)(2,1)}, u32[]{:S(2)}, u32[]{:S(2)}) async-start(bf16[8,240,512]{2,1,0:T(8,128)(2,1)} %broadcast_dynamic-update-slice_fusion.1), calls=%async_computation.4 | async-start | bytes 3932160 | tf_op jit(solution)/shard_map/all_to_all | solution.py:1256
  240.5 15.5 %qkv_grads.1 = (bf16[2048,512]{1,0:T(8,128)(2,1)}, bf16[896,512]{1,0:T(8,128)(2,1)}, bf16[896,512]{1,0:T(8,128)(2,1)}) custom-call(s32[1]{0:T(128)} %bitcast.refs_2_.core_ref, bf16[2048,512]{1,0:T(8,128)(2,1)} %copy-done, bf16[2048,512]{1,0:T(8,128)(2,1)} %get-tuple-element.116.refs_2_.farx_ref, bf16[2048,1536]{1,0:T(8,128)(2,1)} %get-tuple-element.131.dproj_ref.token_ref, ...), custom_call_target="tpu_custom_call" | custom-call | flops 10000000 | bytes 25000 | tf_op jit(solution)/shard_map/qkv_grads/pallas_call | solution.py:949
  256.1 2.7 collective-permute-done.3.refs_1_.refs_2_
  259.9 1.4 halve_step.5
  263.9 2.0 collective-permute-start.5
  267.0 8.4 %collective-permute-done.5.refs_7_ = bf16[192,512]{1,0:T(8,128)(2,1)} collective-permute-done((bf16[192,512]{1,0:T(8,128)(2,1)}, bf16[192,512]{1,0:T(8,128)(2,1)}, u32[]{:S(2)}, u32[]{:S(2)}) %collective-permute-start.5) | collective-permute-done | bytes 196640 | tf_op jit(solution)/shard_map/ppermute | solution.py:1080
  279.4 2.2 halve_step.6
  286.7 1.4 slice.124.refs_0_
  288.1 5.4 %collective-permute-done.7.refs_3_ = bf16[352,512]{1,0:T(8,128)(2,1)} collective-permute-done((bf16[352,512]{1,0:T(8,128)(2,1)}, bf16[352,512]{1,0:T(8,128)(2,1)}, u32[]{:S(2)}, u32[]{:S(2)}) %collective-permute-start.7) | collective-permute-done | bytes 360480 | tf_op jit(solution)/shard_map/ppermute | solution.py:1080
  293.5 2.0 collective-permute-done.6.refs_1_
  300.1 4.9 %sinkhorn_back.1 = f32[6,64,64]{2,1,0:T(8,128)} custom-call(f32[6,64,64]{2,1,0:T(8,128)} %bitcast.95, f32[6,64,64]{2,1,0:T(8,128)} %fusion.4.picked_ref, f32[6,64,64]{2,1,0:T(8,128)} %broadcast_in_dim.87.gw_ref), custom_call_target="tpu_custom_call" | custom-call | flops 4915 | bytes 786 | tf_op jit(solution)/shard_map/sinkhorn_back/pallas_call | solution.py:457
  309.0 10.9 %collective-permute-done.8 = bf16[400,512]{1,0:T(8,128)(2,1)} collective-permute-done((bf16[400,512]{1,0:T(8,128)(2,1)S(1)}, bf16[400,512]{1,0:T(8,128)(2,1)}, u32[]{:S(2)}, u32[]{:S(2)}) %collective-permute-start.8) | collective-permute-done | bytes 409632 | tf_op jit(solution)/shard_map/ppermute | solution.py:1080
  324.0 7.3 %base.1.refs_3_ = bf16[2048,512]{1,0:T(8,128)(2,1)} custom-call(bf16[2048,512]{1,0:T(8,128)(2,1)} %copy-done, bf16[2048,512]{1,0:T(8,128)(2,1)} %get-tuple-element.130.gmid_ref, bf16[2048,512]{1,0:T(8,128)(2,1)} %get-tuple-element.135.gn_ref, f32[64,512]{1,0:T(8,128)} %broadcast_select_fusion.gs_ref, f32[1,512]{1,0:T(1,128)} %bitcast.89), custom_call_target="tpu_custom_call" | custom-call | flops 20971 | bytes 8388 | tf_op jit(solution)/shard_map/base/pallas_call | solution.py:992
  331.4 1.6 copy-done.5
  333.0 11.4 %last.1 = (bf16[1024,512]{1,0:T(8,128)(2,1)}, bf16[1024,512]{1,0:T(8,128)(2,1)}) custom-call(s32[120]{0:T(128)S(1)} %convert_element_type.94.table_ref, s32[64]{0:T(128)S(1)} %copy-done.35, bf16[2048,512]{1,0:T(8,128)(2,1)} %bitcast.25.refs_3_.refs_0_, bf16[1920,512]{1,0:T(8,128)(2,1)} %bitcast.31.refs_4_.refs_1_, bf16[2048,512]{1,0:T(8,128)(2,1)S(1)} %copy-done.3, ...), custom_call_target="tpu_custom_call" | custom-call | flops 20971 | bytes 12582 | tf_op jit(solution)/shard_map/last/pallas_call | solution.py:1052
  347.4 10.5 %collective-permute-done.12.refs_1_ = bf16[400,512]{1,0:T(8,128)(2,1)S(1)} collective-permute-done((bf16[400,512]{1,0:T(8,128)(2,1)S(1)}, bf16[400,512]{1,0:T(8,128)(2,1)S(1)}, u32[]{:S(2)}, u32[]{:S(2)}) %collective-permute-start.12) | collective-permute-done | bytes 409632 | tf_op jit(solution)/shard_map/ppermute | solution.py:1080
  359.8 7.2 %collective-permute-done.14.refs_3_ = bf16[352,512]{1,0:T(8,128)(2,1)S(1)} collective-permute-done((bf16[352,512]{1,0:T(8,128)(2,1)S(1)}, bf16[352,512]{1,0:T(8,128)(2,1)S(1)}, u32[]{:S(2)}, u32[]{:S(2)}) %collective-permute-start.14) | collective-permute-done | bytes 360480 | tf_op jit(solution)/shard_map/ppermute | solution.py:1080
  367.0 2.0 collective-permute-done.13.refs_1_
  371.2 14.4 %collective-permute-done.16.refs_3_ = bf16[704,512]{1,0:T(8,128)(2,1)S(1)} collective-permute-done((bf16[704,512]{1,0:T(8,128)(2,1)S(1)}, bf16[704,512]{1,0:T(8,128)(2,1)S(1)}, u32[]{:S(2)}, u32[]{:S(2)}) %collective-permute-start.16) | collective-permute-done | bytes 720928 | tf_op jit(solution)/shard_map/ppermute | solution.py:1080
  385.6 4.1 %collective-permute-done.15.refs_1_ = bf16[896,512]{1,0:T(8,128)(2,1)S(1)} collective-permute-done((bf16[896,512]{1,0:T(8,128)(2,1)S(1)}, bf16[896,512]{1,0:T(8,128)(2,1)S(1)}, u32[]{:S(2)}, u32[]{:S(2)}) %collective-permute-start.15) | collective-permute-done | bytes 917536 | tf_op jit(solution)/shard_map/ppermute | solution.py:1080
  391.2 2.9 assemble.2
  394.1 2.3 collective-permute-done.17.values_ref
  396.4 2.7 assemble.3
  (221 shorter events, 61.5 us)
Async XLA Ops:
  36.5 27.7 %copy-start.46 = (f32[8,56,128]{2,1,0:T(8,128)}, f32[8,56,128]{2,1,0:T(8,128)S(1)}, u32[]{:S(2)}) copy-start(f32[8,56,128]{2,1,0:T(8,128)S(1)} %all_to_all.25) | copy-start | bytes 688132
  36.6 1.6 copy-start.2
  44.1 4.6 %copy-start.3 = (bf16[2048,512]{1,0:T(8,128)(2,1)S(1)}, bf16[2048,512]{1,0:T(8,128)(2,1)}, u32[]{:S(2)}) copy-start(bf16[2048,512]{1,0:T(8,128)(2,1)} %get-tuple-element.94.x_ref.refs_2_) | copy-start | bytes 6291460
  44.1 4.6 %copy-start.17 = (bf16[2,512,512]{2,1,0:T(8,128)(2,1)S(1)}, bf16[2,512,512]{2,1,0:T(8,128)(2,1)}, u32[]{:S(2)}) copy-start(bf16[2,512,512]{2,1,0:T(8,128)(2,1)} %param.26) | copy-start | bytes 3145732
  44.1 4.7 %copy-start.34 = (s32[64]{0:T(128)S(1)}, s32[64]{0:T(128)}, u32[]{:S(2)}) copy-start(s32[64]{0:T(128)} %get-tuple-element.88.perm_ref) | copy-start | bytes 772
  44.1 51.7 %all-to-all-start.1 = ((bf16[8,256,512]{2,1,0:T(8,128)(2,1)}), bf16[8,256,512]{2,1,0:T(8,128)(2,1)}, u32[]{:S(2)}, u32[]{:S(2)}) async-start(bf16[8,256,512]{2,1,0:T(8,128)(2,1)} %bitcast.80), calls=%async_computation.1 | async-start | bytes 4194304 | tf_op jit(solution)/shard_map/all_to_all | solution.py:1256
  54.5 9.4 %copy-start.29 = (f32[512]{0:T(512)S(1)}, f32[512]{0:T(512)}, u32[]{:S(2)}) copy-start(f32[512]{0:T(512)} %convert_element_type.86) | copy-start | bytes 6148
  54.5 9.4 %copy-start.42 = (f32[48,512]{1,0:T(8,128)S(1)}, f32[48,512]{1,0:T(8,128)}, u32[]{:S(2)}) copy-start(f32[48,512]{1,0:T(8,128)} %get-tuple-element.97) | copy-start | bytes 294916
  73.0 27.3 %copy-start.52 = (bf16[512]{0:T(512)(128)(2,1)S(1)}, bf16[512]{0:T(512)(128)(2,1)}, u32[]{:S(2)}) copy-start(bf16[512]{0:T(512)(128)(2,1)} %param.23) | copy-start | bytes 3076
  95.7 67.4 %all-to-all-start.2 = ((bf16[8,240,512]{2,1,0:T(8,128)(2,1)}), bf16[8,240,512]{2,1,0:T(8,128)(2,1)}, u32[]{:S(2)}, u32[]{:S(2)}) async-start(bf16[8,240,512]{2,1,0:T(8,128)(2,1)} %bitcast.79), calls=%async_computation.2 | async-start | bytes 3932160 | tf_op jit(solution)/shard_map/all_to_all | solution.py:1256
  163.1 69.5 %all-to-all-start.3 = ((bf16[8,256,512]{2,1,0:T(8,128)(2,1)}), bf16[8,256,512]{2,1,0:T(8,128)(2,1)}, u32[]{:S(2)}, u32[]{:S(2)}) async-start(bf16[8,256,512]{2,1,0:T(8,128)(2,1)} %bitcast.96), calls=%async_computation.3 | async-start | bytes 4194304 | tf_op jit(solution)/shard_map/all_to_all | solution.py:1256
  169.4 29.9 %copy-start.35 = (s32[64]{0:T(128)S(1)}, s32[64]{0:T(128)}, u32[]{:S(2)}) copy-start(s32[64]{0:T(128)} %get-tuple-element.114.place_ref) | copy-start | bytes 772
  199.1 4.9 %collective-permute-start = (bf16[2304,512]{1,0:T(8,128)(2,1)}, bf16[2304,512]{1,0:T(8,128)(2,1)}, u32[]{:S(2)}, u32[]{:S(2)}) collective-permute-start(bf16[2304,512]{1,0:T(8,128)(2,1)} %get-tuple-element.123), channel_id=1, source_target_pairs={{0,8},{8,0},{16,24},{24,16},{1,9},{9,1},{17,25},{25,17},{2,10},{10... | collective-permute-start | bytes 7077896 | tf_op jit(solution)/shard_map/ppermute | solution.py:1080
  204.1 1.7 copy-start.11
  211.8 20.8 %collective-permute-start.1 = (bf16[640,512]{1,0:T(8,128)(2,1)}, bf16[640,512]{1,0:T(8,128)(2,1)S(1)}, u32[]{:S(2)}, u32[]{:S(2)}) collective-permute-start(bf16[640,512]{1,0:T(8,128)(2,1)} %get-tuple-element.128), channel_id=1, source_target_pairs={{0,16},{8,24},{16,0},{24,8},{1,17},{9,25},{17,1},{25,9},{2,18},{10... | collective-permute-start | bytes 1966088 | tf_op jit(solution)/shard_map/ppermute | solution.py:1080
  213.2 19.4 %collective-permute-start.2 = (bf16[512,512]{1,0:T(8,128)(2,1)}, bf16[512,512]{1,0:T(8,128)(2,1)S(1)}, u32[]{:S(2)}, u32[]{:S(2)}) collective-permute-start(bf16[512,512]{1,0:T(8,128)(2,1)} %get-tuple-element.129), channel_id=1, source_target_pairs={{0,1},{1,0},{2,3},{3,2},{4,5},{5,4},{6,7},{7,6},{8,9},{9,8},{10,11... | collective-permute-start | bytes 1572872 | tf_op jit(solution)/shard_map/ppermute | solution.py:1080
  215.3 14.6 %copy-start.48 = (f32[20,2,128]{2,1,0:T(2,128)S(1)}, f32[20,2,128]{2,1,0:T(2,128)}, u32[]{:S(2)}) copy-start(f32[20,2,128]{2,1,0:T(2,128)} %get-tuple-element.126) | copy-start | bytes 61444
  233.6 6.3 %copy-start.50 = (f32[1,512]{1,0:T(1,128)S(1)}, f32[1,512]{1,0:T(1,128)}, u32[]{:S(2)}) copy-start(f32[1,512]{1,0:T(1,128)} %get-tuple-element.134) | copy-start | bytes 6148
  233.6 6.3 %copy-start.51 = (f32[1,512]{1,0:T(1,128)S(1)}, f32[1,512]{1,0:T(1,128)}, u32[]{:S(2)}) copy-start(f32[1,512]{1,0:T(1,128)} %get-tuple-element.133) | copy-start | bytes 6148
  235.0 51.7 %all-to-all-start.4 = ((bf16[8,240,512]{2,1,0:T(8,128)(2,1)}), bf16[8,240,512]{2,1,0:T(8,128)(2,1)}, u32[]{:S(2)}, u32[]{:S(2)}) async-start(bf16[8,240,512]{2,1,0:T(8,128)(2,1)} %broadcast_dynamic-update-slice_fusion.1), calls=%async_computation.4 | async-start | bytes 3932160 | tf_op jit(solution)/shard_map/all_to_all | solution.py:1256
  256.0 19.4 %copy-start.8 = (bf16[640,512]{1,0:T(8,128)(2,1)S(1)}, bf16[640,512]{1,0:T(8,128)(2,1)}, u32[]{:S(2)}) copy-start(bf16[640,512]{1,0:T(8,128)(2,1)} %copy-done.7) | copy-start | bytes 1966084
  256.0 19.4 %copy-start.10 = (bf16[640,512]{1,0:T(8,128)(2,1)S(1)}, bf16[640,512]{1,0:T(8,128)(2,1)}, u32[]{:S(2)}) copy-start(bf16[640,512]{1,0:T(8,128)(2,1)} %copy-done.9) | copy-start | bytes 1966084
  256.0 2.7 collective-permute-start.3
  263.4 12.0 %collective-permute-start.4 = (bf16[256,512]{1,0:T(8,128)(2,1)}, bf16[256,512]{1,0:T(8,128)(2,1)}, u32[]{:S(2)}, u32[]{:S(2)}) collective-permute-start(bf16[256,512]{1,0:T(8,128)(2,1)} %get-tuple-element.139), channel_id=1, source_target_pairs={{0,16},{8,24},{16,0},{24,8},{1,17},{9,25},{17,1},{25,9},{2,18},{10... | collective-permute-start | bytes 786440 | tf_op jit(solution)/shard_map/ppermute | solution.py:1080
  263.9 11.5 %collective-permute-start.5 = (bf16[192,512]{1,0:T(8,128)(2,1)}, bf16[192,512]{1,0:T(8,128)(2,1)}, u32[]{:S(2)}, u32[]{:S(2)}) collective-permute-start(bf16[192,512]{1,0:T(8,128)(2,1)} %copy-done.38), channel_id=1, source_target_pairs={{0,1},{1,0},{2,3},{3,2},{4,5},{5,4},{6,7},{7,6},{8,9},{9,8},{10,11... | collective-permute-start | bytes 589832 | tf_op jit(solution)/shard_map/ppermute | solution.py:1080
  283.1 12.4 %copy-start.26 = (bf16[448,512]{1,0:T(8,128)(2,1)S(1)}, bf16[448,512]{1,0:T(8,128)(2,1)}, u32[]{:S(2)}) copy-start(bf16[448,512]{1,0:T(8,128)(2,1)} %copy-done.25) | copy-start | bytes 1376260
  283.1 12.4 %copy-start.28 = (bf16[352,512]{1,0:T(8,128)(2,1)S(1)}, bf16[352,512]{1,0:T(8,128)(2,1)}, u32[]{:S(2)}) copy-start(bf16[352,512]{1,0:T(8,128)(2,1)} %copy-done.27) | copy-start | bytes 1081348
  283.1 12.4 %collective-permute-start.6 = (bf16[448,512]{1,0:T(8,128)(2,1)}, bf16[448,512]{1,0:T(8,128)(2,1)S(1)}, u32[]{:S(2)}, u32[]{:S(2)}) collective-permute-start(bf16[448,512]{1,0:T(8,128)(2,1)} %get-tuple-element.144), channel_id=1, source_target_pairs={{0,1},{1,0},{2,3},{3,2},{4,5},{5,4},{6,7},{7,6},{8,9},{9,8},{10,11... | collective-permute-start | bytes 1376264 | tf_op jit(solution)/shard_map/ppermute | solution.py:1080
  283.1 10.4 %collective-permute-start.7 = (bf16[352,512]{1,0:T(8,128)(2,1)}, bf16[352,512]{1,0:T(8,128)(2,1)}, u32[]{:S(2)}, u32[]{:S(2)}) collective-permute-start(bf16[352,512]{1,0:T(8,128)(2,1)} %get-tuple-element.146), channel_id=1, source_target_pairs={{0,16},{8,24},{16,0},{24,8},{1,17},{9,25},{17,1},{25,9},{2,18},{10... | collective-permute-start | bytes 1081352 | tf_op jit(solution)/shard_map/ppermute | solution.py:1080
  298.2 7.8 %copy-start.39 = (bf16[8,6,8,512]{3,2,0,1:T(8,128)(2,1)S(1)}, bf16[8,6,8,512]{3,2,0,1:T(8,128)(2,1)}, u32[]{:S(2)}) copy-start(bf16[8,6,8,512]{3,2,0,1:T(8,128)(2,1)} %copy.68) | copy-start | bytes 1179652
  298.2 7.8 %copy-start.47 = (bf16[512,64]{0,1:T(8,128)(2,1)S(1)}, bf16[512,64]{0,1:T(8,128)(2,1)}, u32[]{:S(2)}) copy-start(bf16[512,64]{0,1:T(8,128)(2,1)} %param.22) | copy-start | bytes 196612
  300.1 7.1 %copy-start.49 = (bf16[512]{0:T(512)(128)(2,1)S(1)}, bf16[512]{0:T(512)(128)(2,1)}, u32[]{:S(2)}) copy-start(bf16[512]{0:T(512)(128)(2,1)} %param.19) | copy-start | bytes 3076
  305.0 3.0 copy-start.37
  305.0 3.0 copy-start.30
  307.0 12.9 %copy-start.16 = (bf16[400,512]{1,0:T(8,128)(2,1)S(1)}, bf16[400,512]{1,0:T(8,128)(2,1)}, u32[]{:S(2)}) copy-start(bf16[400,512]{1,0:T(8,128)(2,1)} %copy-done.15) | copy-start | bytes 1228804
  307.9 13.2 %collective-permute-start.10 = (f32[65,512]{1,0:T(8,128)}, f32[65,512]{1,0:T(8,128)}, u32[]{:S(2)}, u32[]{:S(2)}) collective-permute-start(f32[65,512]{1,0:T(8,128)} %pad_maximum_fusion.2), channel_id=1, source_target_pairs={{0,8},{8,0},{16,24},{24,16},{1,9},{9,1},{17,25},{25,17},{2,10},{10... | collective-permute-start | bytes 399368 | tf_op jit(solution)/shard_map/ppermute | solution.py:1080
  307.9 12.0 %collective-permute-start.8 = (bf16[400,512]{1,0:T(8,128)(2,1)S(1)}, bf16[400,512]{1,0:T(8,128)(2,1)}, u32[]{:S(2)}, u32[]{:S(2)}) collective-permute-start(bf16[400,512]{1,0:T(8,128)(2,1)S(1)} %copy-done.37), channel_id=1, source_target_pairs={{0,2},{1,3},{2,0},{3,1},{4,6},{5,7},{6,4},{7,5},{8,10},{9,11},{10,... | collective-permute-start | bytes 1228808 | tf_op jit(solution)/shard_map/ppermute | solution.py:1080
  308.2 12.9 %copy-start.45 = (f32[64,512]{1,0:T(8,128)S(1)}, f32[64,512]{1,0:T(8,128)}, u32[]{:S(2)}) copy-start(f32[64,512]{1,0:T(8,128)} %copy-done.44) | copy-start | bytes 393220
  321.0 24.1 %collective-permute-start.9 = (bf16[400,512]{1,0:T(8,128)(2,1)S(1)}, bf16[400,512]{1,0:T(8,128)(2,1)S(1)}, u32[]{:S(2)}, u32[]{:S(2)}) collective-permute-start(bf16[400,512]{1,0:T(8,128)(2,1)S(1)} %add_convert_fusion.1), channel_id=1, source_target_pairs={{0,4},{1,5},{2,6},{3,7},{4,0},{5,1},{6,2},{7,3},{8,12},{9,13},{10,... | collective-permute-start | bytes 1228808 | tf_op jit(solution)/shard_map/ppermute | solution.py:1080
  322.0 22.3 %collective-permute-start.11 = (f32[65,512]{1,0:T(8,128)S(1)}, f32[65,512]{1,0:T(8,128)S(1)}, u32[]{:S(2)}, u32[]{:S(2)}) collective-permute-start(f32[65,512]{1,0:T(8,128)S(1)} %fusion.16), channel_id=1, source_target_pairs={{0,16},{8,24},{16,0},{24,8},{1,17},{9,25},{17,1},{25,9},{2,18},{10... | collective-permute-start | bytes 399368 | tf_op jit(solution)/shard_map/ppermute | solution.py:1080
  324.0 7.3 %copy-start.31 = (f32[512]{0:T(512)S(1)}, f32[512]{0:T(512)}, u32[]{:S(2)}) copy-start(f32[512]{0:T(512)} %convert_element_type.86) | copy-start | bytes 6148
  346.9 11.0 %collective-permute-start.12 = (bf16[400,512]{1,0:T(8,128)(2,1)S(1)}, bf16[400,512]{1,0:T(8,128)(2,1)S(1)}, u32[]{:S(2)}, u32[]{:S(2)}) collective-permute-start(bf16[400,512]{1,0:T(8,128)(2,1)S(1)} %add_convert_fusion.refs_0_), channel_id=1, source_target_pairs={{0,2},{1,3},{2,0},{3,1},{4,6},{5,7},{6,4},{7,5},{8,10},{9,11},{10,... | collective-permute-start | bytes 1228808 | tf_op jit(solution)/shard_map/ppermute | solution.py:1080
  357.9 11.1 %collective-permute-start.13 = (bf16[448,512]{1,0:T(8,128)(2,1)S(1)}, bf16[448,512]{1,0:T(8,128)(2,1)S(1)}, u32[]{:S(2)}, u32[]{:S(2)}) collective-permute-start(bf16[448,512]{1,0:T(8,128)(2,1)S(1)} %get-tuple-element.151.refs_0_), channel_id=1, source_target_pairs={{0,1},{1,0},{2,3},{3,2},{4,5},{5,4},{6,7},{7,6},{8,9},{9,8},{10,11... | collective-permute-start | bytes 1376264 | tf_op jit(solution)/shard_map/ppermute | solution.py:1080
  358.4 8.6 %collective-permute-start.14 = (bf16[352,512]{1,0:T(8,128)(2,1)S(1)}, bf16[352,512]{1,0:T(8,128)(2,1)S(1)}, u32[]{:S(2)}, u32[]{:S(2)}) collective-permute-start(bf16[352,512]{1,0:T(8,128)(2,1)S(1)} %get-tuple-element.152.refs_2_), channel_id=1, source_target_pairs={{0,16},{8,24},{16,0},{24,8},{1,17},{9,25},{17,1},{25,9},{2,18},{10... | collective-permute-start | bytes 1081352 | tf_op jit(solution)/shard_map/ppermute | solution.py:1080
  369.7 20.0 %collective-permute-start.15 = (bf16[896,512]{1,0:T(8,128)(2,1)S(1)}, bf16[896,512]{1,0:T(8,128)(2,1)S(1)}, u32[]{:S(2)}, u32[]{:S(2)}) collective-permute-start(bf16[896,512]{1,0:T(8,128)(2,1)S(1)} %get-tuple-element.153.refs_0_), channel_id=1, source_target_pairs={{0,16},{8,24},{16,0},{24,8},{1,17},{9,25},{17,1},{25,9},{2,18},{10... | collective-permute-start | bytes 2752520 | tf_op jit(solution)/shard_map/ppermute | solution.py:1080
  370.3 20.2 %copy-start.43 = (f32[65,512]{1,0:T(8,128)S(1)}, f32[65,512]{1,0:T(8,128)}, u32[]{:S(2)}) copy-start(f32[65,512]{1,0:T(8,128)} %add.75.refs_2_) | copy-start | bytes 399364
  370.3 15.3 %collective-permute-start.16 = (bf16[704,512]{1,0:T(8,128)(2,1)S(1)}, bf16[704,512]{1,0:T(8,128)(2,1)S(1)}, u32[]{:S(2)}, u32[]{:S(2)}) collective-permute-start(bf16[704,512]{1,0:T(8,128)(2,1)S(1)} %get-tuple-element.154.refs_2_), channel_id=1, source_target_pairs={{0,1},{1,0},{2,3},{3,2},{4,5},{5,4},{6,7},{7,6},{8,9},{9,8},{10,11... | collective-permute-start | bytes 2162696 | tf_op jit(solution)/shard_map/ppermute | solution.py:1080
  390.4 5.9 %collective-permute-start.17 = (bf16[3200,512]{1,0:T(8,128)(2,1)S(1)}, bf16[3200,512]{1,0:T(8,128)(2,1)S(1)}, u32[]{:S(2)}, u32[]{:S(2)}) collective-permute-start(bf16[3200,512]{1,0:T(8,128)(2,1)S(1)} %double_step.5.values_ref), channel_id=1, source_target_pairs={{0,8},{8,0},{16,24},{24,16},{1,9},{9,1},{17,25},{25,17},{2,10},{10... | collective-permute-start | bytes 9830408 | tf_op jit(solution)/shard_map/ppermute | solution.py:1080
  (27 other events, 27.6 us)

commit v2 on v1

--- a/solution.py
+++ b/solution.py
@@ -60,6 +60,7 @@
 
 ANY = pl.BlockSpec(memory_space=pl.ANY)
 VMEM = pl.BlockSpec(memory_space=pltpu.VMEM)
+HBM = pl.BlockSpec(memory_space=pltpu.HBM)
 
 
 def limit(mib):
@@ -68,13 +69,17 @@
 
 def request_kernel(
     npl, seqs_a, seqs_b, devices, capacity, first, early, sizes, extra, spare_rows,
-    sel_ref, table_ref, back_ref, far_ref, ret_ref, perm_ref, place_ref, kinds_ref, fill, begin, used,
+    sela_ref, selb_ref, table_ref, back_ref, far_ref, ret_ref, perm_ref, place_ref, kinds_ref, fill, begin, used,
 ):
     count_a = seqs_a * npl
     count_b = seqs_b * npl
     units_a = 2 * count_a
     width = sum(sizes)
     shift = npl.bit_length() - 1 if npl & (npl - 1) == 0 else -1
+
+    def choice(j):
+        ref, at = (sela_ref, j) if j < count_a else (selb_ref, j - count_a)
+        return ref[at // npl, at % npl]
 
     def split(chosen):
         if shift >= 0:
@@ -97,7 +102,7 @@
     one = lambda flag: jnp.where(flag, 1, 0)
     ready_a, ready_b, must_a, must_b = (jnp.int32(0) for _ in range(4))
     for j in range(count_a + count_b):
-        source, inner = split(sel_ref[j])
+        source, inner = split(choice(j))
         slot = fill[source]
         begin[j] = slot
         size = 2 if j < count_a else 1
@@ -114,7 +119,7 @@
     two = early < count_a + count_b // 2
 
     def must(j):
-        source, _ = split(sel_ref[j])
+        source, _ = split(choice(j))
         if not two:
             return begin[j] < 0
         return begin[j] < fill[source] - 6
@@ -167,7 +172,7 @@
     spare = take_a - must_a
     taken, other, free = (jnp.int32(0) for _ in range(3))
     for j in range(count_a):
-        source, inner = split(sel_ref[j])
+        source, inner = split(choice(j))
         slot = begin[j]
         need = must(j)
         pick = jnp.logical_and(jnp.logical_not(need), jnp.logical_and(slot + 2 <= first, free < spare))
@@ -183,7 +188,7 @@
     drop = one(spare < 0)
     taken, other, free = (jnp.int32(0) for _ in range(3))
     for j in range(count_b):
-        source, inner = split(sel_ref[count_a + j])
+        source, inner = split(choice(count_a + j))
         slot = begin[count_a + j]
         need = must(count_a + j)
         skip = jnp.logical_and(need, drop > 0)
@@ -198,31 +203,19 @@
         other = other + one(jnp.logical_not(use))
 
 
-def request(sel, npl, seqs_a, seqs_b, devices, capacity, first, early, sizes, extra, spare_rows):
-    units = npl * (2 * seqs_a + seqs_b)
-    counts = [devices * capacity, devices * sum(sizes), units, units, units, units, 2]
-    return pl.pallas_call(
-        functools.partial(
-            request_kernel, npl, seqs_a, seqs_b, devices, capacity, first, early, sizes, extra,
-            spare_rows,
-        ),
-        in_specs=[SMEM],
-        out_specs=[SMEM] * len(counts),
-        out_shape=[jax.ShapeDtypeStruct((n,), jnp.int32) for n in counts],
-        scratch_shapes=[
-            pltpu.SMEM((devices,), jnp.int32),
-            pltpu.SMEM((npl * (seqs_a + seqs_b),), jnp.int32),
-            pltpu.SMEM((2 * devices,), jnp.int32),
-        ],
-        cost_estimate=cost(1000, 2000),
-        name="request",
-    )(sel)
-
-
 def digest_kernel(
-    tiles_a, xa_ref, xb_ref, gain_ref, avg_ref, wsort_ref, x_ref, means_ref, logits_ref, sums
+    tiles_a, settings, sela_ref, selb_ref, xa_ref, xb_ref, gain_ref, avg_ref, wsort_ref,
+    x_ref, means_ref, news_ref, far_ref, ret_ref, perm_ref, place_ref, kinds_ref,
+    sums, table_ref, back_ref, fill, begin, used,
 ):
     step = pl.program_id(0)
+
+    @pl.when(step == 0)
+    def _():
+        request_kernel(
+            *settings, sela_ref, selb_ref, table_ref, back_ref, far_ref, ret_ref, perm_ref, place_ref,
+            kinds_ref, fill, begin, used,
+        )
 
     def take(src):
         x = src[...]
@@ -244,36 +237,75 @@
         means_ref[...] = means
         summary = means * gain_ref[...]
         unit = (summary * inverse_norm(summary)).astype(BF16)
-        logits_ref[...] = dot(unit, wsort_ref[...]) * (1.0 / SOFTMAX_HEAT)
-
-
-def digest(x_a, x_b, gain_row, average, w_sort):
+        logits = dot(unit, wsort_ref[...], NT) * (1.0 / SOFTMAX_HEAT)
+        picks, blocks = logits.shape
+        devices, height, lanes = news_ref.shape
+        line = lax.broadcasted_iota(jnp.int32, (picks, lanes - blocks), 0)
+        lane = lax.broadcasted_iota(jnp.int32, (picks, lanes - blocks), 1)
+        chosen = jnp.zeros((picks, lanes - blocks), jnp.int32)
+        count_a = sela_ref.shape[0] * sela_ref.shape[1]
+        for j in range(picks):
+            ref, at = (sela_ref, j) if j < count_a else (selb_ref, j - count_a)
+            npl = ref.shape[1]
+            chosen = jnp.where(line == j, ref[at // npl, at % npl], chosen)
+        chosen = jnp.where(lane == 0, chosen, 0).astype(F32)
+        message = jnp.concatenate([logits, chosen], axis=1)
+        lane = lax.broadcasted_iota(jnp.int32, (1, lanes), 1)
+        wanted = table_ref.shape[0] // devices
+        order = back_ref.shape[0] // devices
+        rest = lax.broadcasted_iota(jnp.int32, (height - picks, lanes), 0)
+        for d in range(devices):
+            row = jnp.zeros((1, lanes), jnp.int32)
+            for k in range(wanted):
+                row = jnp.where(lane == k, table_ref[d * wanted + k], row)
+            for k in range(order):
+                row = jnp.where(lane == wanted + k, back_ref[d * order + k], row)
+            news_ref[d, :picks, :] = message
+            news_ref[d, picks:, :] = jnp.where(rest == 0, row.astype(F32), 0.0)
+
+
+def digest(x_a, x_b, sel_a, sel_b, gain_row, average, w_sort_t, settings):
+    npl, seqs_a, seqs_b, devices, capacity, _, _, sizes, _, _ = settings
     width = x_a.shape[1]
     tiles_a = x_a.shape[0] // TILE
     tiles_b = x_b.shape[0] // TILE
     rows = x_a.shape[0] + x_b.shape[0]
     picks = average.shape[0]
+    height = -(-picks // 8) * 8 + 8
+    units = rows // UNIT
+    ints = lambda n: jax.ShapeDtypeStruct((n,), jnp.int32)
     return pl.pallas_call(
-        functools.partial(digest_kernel, tiles_a),
+        functools.partial(digest_kernel, tiles_a, settings),
         grid=(tiles_a + tiles_b,),
         in_specs=[
+            SMEM,
+            SMEM,
             pl.BlockSpec((TILE, width), lambda i: (jnp.minimum(i, tiles_a - 1), 0)),
             pl.BlockSpec((TILE, width), lambda i: (jnp.maximum(i - tiles_a, 0), 0)),
             whole((1, width)),
             whole(average.shape),
-            whole(w_sort.shape),
+            whole(w_sort_t.shape),
         ],
-        out_specs=[rows_of(TILE, width), whole((picks, width)), whole((picks, w_sort.shape[1]))],
+        out_specs=[rows_of(TILE, width), whole((picks, width)), whole((devices, height, 128))]
+        + [SMEM] * 5,
         out_shape=[
             jax.ShapeDtypeStruct((rows, width), BF16),
             jax.ShapeDtypeStruct((picks, width), F32),
-            jax.ShapeDtypeStruct((picks, w_sort.shape[1]), F32),
+            jax.ShapeDtypeStruct((devices, height, 128), F32),
+        ]
+        + [ints(n) for n in (units, units, units, units, 2)],
+        scratch_shapes=[
+            pltpu.VMEM((units, width), F32),
+            pltpu.SMEM((devices * capacity,), jnp.int32),
+            pltpu.SMEM((devices * sum(sizes),), jnp.int32),
+            pltpu.SMEM((devices,), jnp.int32),
+            pltpu.SMEM((picks,), jnp.int32),
+            pltpu.SMEM((2 * devices,), jnp.int32),
         ],
-        scratch_shapes=[pltpu.VMEM((rows // UNIT, width), F32)],
         compiler_params=params(),
         cost_estimate=cost(rows * width * 10, rows * width * 4),
         name="digest",
-    )(x_a, x_b, gain_row, average, w_sort)
+    )(sel_a, sel_b, x_a, x_b, gain_row, average, w_sort_t)
 
 
 def pack_kernel(devices, capacity, first, spare, table_ref, x_ref, *rest):
@@ -308,7 +340,7 @@
     return pl.pallas_call(
         functools.partial(pack_kernel, devices, capacity, first, spare),
         in_specs=[SMEM, VMEM],
-        out_specs=[ANY] * len(sizes),
+        out_specs=[HBM] * len(sizes),
         out_shape=[
             jax.ShapeDtypeStruct((devices * (n * UNIT + i * spare), width), BF16)
             for i, n in enumerate(sizes)
@@ -486,38 +518,76 @@
     return jnp.concatenate([values] * PER_HALF, axis=0)
 
 
-def forward_kernel(first_group, recvs, prior, final, *refs):
+class Mover:
+    def __init__(self, sems):
+        self.sems, self.used, self.out = sems, 0, []
+
+    def start(self, source, target):
+        copy = pltpu.make_async_copy(source, target, self.sems.at[self.used])
+        self.used += 1
+        copy.start()
+        return copy
+
+    def store(self, source, target):
+        self.out.append(self.start(source, target))
+
+    def finish(self):
+        for copy in self.out:
+            copy.wait()
+
+
+BATCH = 4
+
+
+def forward_kernel(first_group, groups, recvs, prior, final, *refs):
     refs = list(refs)
     take = lambda n: [refs.pop(0) for _ in range(n)]
     far_ref, kinds_ref, core_ref = take(3)
-    recv_refs = take(recvs)
-    (
-        x_ref, cot_ref, proj_ref, wrow_ref, mask_ref, gain1_ref, gain2_ref,
-        wqkv_ref, wout_ref, wup_ref, wdown_ref,
-    ) = take(11)
-    take(1)
+    recv_hbm = take(recvs)
+    x_hbm, cot_hbm, proj_hbm, wrow_hbm, mask_ref, gain1_ref, gain2_ref = take(7)
+    wqkv_hbm, wout_hbm, wup_hbm, wdown_hbm, _ = take(5)
     prior_refs = take(3) if prior else []
     if prior:
         take(6)
-    out_ref, gmid_ref, gatt_ref, prob_ref, farx_ref, farkv_ref = take(6)
+    out_hbm, gmid_hbm, gatt_hbm, prob_hbm, farx_hbm, farkv_hbm = take(6)
     if final:
-        keep_ref, give_ref, gain_ref = take(3)
+        keep_hbm, give_hbm, gain_ref = take(3)
     else:
-        up_ref, down_ref, gain_ref = take(3)
-    attended, up_acc, down_acc, wo_acc, gain_acc = take(5)
+        up_hbm, down_hbm, gain_ref = take(3)
+    recv_refs = take(recvs)
+    x_ref, cot_ref, proj_ref, wrow_ref, wqkv_ref, wout_ref, wup_ref, wdown_ref = take(8)
+    out_ref, gmid_ref, gatt_ref, prob_ref, farx_ref, farkv_ref, attended = take(7)
+    one_ref, two_ref = take(2)
     if prior:
-        up_prior, down_prior, sems = take(3)
-    step = pl.program_id(0)
-    steps = pl.num_programs(0)
-    tile, width = x_ref.shape
+        up_prior, down_prior = take(2)
+    (sems,) = take(1)
+    move = Mover(sems)
+    rows = groups * GROUP
+    width = x_ref.shape[1]
     ff = wup_ref.shape[1]
-    units = tile // UNIT
-    groups = tile // GROUP
-    base = first_group + step * groups
+    base = first_group
+    here = pl.ds(first_group * GROUP, rows)
+    got_recv = [move.start(a, b) for a, b in zip(recv_hbm, recv_refs)]
+    got_wqkv = move.start(wqkv_hbm, wqkv_ref)
+    got_proj = move.start(proj_hbm.at[here], proj_ref)
+    got_wrow = move.start(wrow_hbm.at[here], wrow_ref)
+    got_x = move.start(x_hbm.at[here], x_ref)
+    got_wout = move.start(wout_hbm, wout_ref)
+    got_cot = move.start(cot_hbm.at[here], cot_ref)
+    got_up = move.start(wup_hbm, wup_ref)
+    got_down = move.start(wdown_hbm, wdown_ref)
+    if prior:
+        got_prior = [
+            move.start(prior_refs[0], up_prior),
+            move.start(prior_refs[1], down_prior),
+        ]
+
+    for copy in got_recv:
+        copy.wait()
     rows_one = recv_refs[0].shape[0]
-    for u in range(units):
+    for u in range(rows // UNIT):
         row = far_ref[2 * base + u]
-        dst = pl.ds(u * UNIT, UNIT)
+        dst = slice(u * UNIT, (u + 1) * UNIT)
         if recvs == 1:
             farx_ref[dst, :] = recv_refs[0][pl.ds(pl.multiple_of(row, UNIT), UNIT), :]
         else:
@@ -531,140 +601,151 @@
                 src = pl.ds(pl.multiple_of(row - rows_one, 16), UNIT)
                 farx_ref[dst, :] = recv_refs[1][src, :]
 
-    if prior:
-        moves = [
-            pltpu.make_async_copy(prior_refs[0], up_prior, sems.at[0]),
-            pltpu.make_async_copy(prior_refs[1], down_prior, sems.at[1]),
-        ]
-
-        @pl.when(step == 0)
-        def _():
-            for move in moves:
-                move.start()
-
+    move.store(farx_ref, farx_hbm.at[here])
     far = farx_ref[...].astype(F32)
     far = (far * inverse_norm(far) * gain1_ref[...]).astype(BF16)
+    got_wqkv.wait()
     farkv_ref[...] = dot(far, wqkv_ref[:, width:]).astype(BF16)
+    move.store(farkv_ref, farkv_hbm.at[here])
     masks16 = head_masks(GROUP)
     head_scale = (width // HEADS) ** -0.5
     boundary = kinds_ref[1 if prior else 0]
-
-    def group_step(i, carry):
-        rows = pl.ds(pl.multiple_of(i * GROUP, GROUP), GROUP)
-        which = jnp.where(base + i < boundary, 0, 1)
-        barrier = repeat_heads(mask_ref[which])
-        scale = repeat_heads(wrow_ref[rows, :])
-        for half in range(width // HALF):
+    got_proj.wait()
+    got_wrow.wait()
+    for first in range(0, groups, BATCH):
+        work = [
+            (i, half) for i in range(first, min(first + BATCH, groups)) for half in range(width // HALF)
+        ]
+        scores, vals = [], []
+        for i, half in work:
+            at = slice(i * GROUP, (i + 1) * GROUP)
             lo = half * HALF
-            q = proj_ref[rows, lo : lo + HALF] * jnp.asarray(head_scale, BF16)
+            q = proj_ref[at, lo : lo + HALF] * jnp.asarray(head_scale, BF16)
             keys = jnp.concatenate(
-                [proj_ref[rows, width + lo : width + lo + HALF], farkv_ref[rows, lo : lo + HALF]],
-                axis=0,
+                [proj_ref[at, width + lo : width + lo + HALF], farkv_ref[at, lo : lo + HALF]], axis=0
             )
-            vals = jnp.concatenate(
-                [
-                    proj_ref[rows, 2 * width + lo : 2 * width + lo + HALF],
-                    farkv_ref[rows, width + lo : width + lo + HALF],
-                ],
-                axis=0,
+            vals.append(
+                jnp.concatenate(
+                    [
+                        proj_ref[at, 2 * width + lo : 2 * width + lo + HALF],
+                        farkv_ref[at, width + lo : width + lo + HALF],
+                    ],
+                    axis=0,
+                )
             )
-            scores = dot(stack_heads(q, masks16), keys, NT) + barrier
-            top = jnp.max(scores, axis=1, keepdims=True)
-            weight = jnp.exp(scores - top)
-            prob = weight * (1.0 / jnp.sum(weight, axis=1, keepdims=True))
+            which = jnp.where(base + i < boundary, 0, 1)
+            scores.append(dot(stack_heads(q, masks16), keys, NT) + repeat_heads(mask_ref[which]))
+        tops = [jnp.max(v, axis=1, keepdims=True) for v in scores]
+        weights = [jnp.exp(v - t) for v, t in zip(scores, tops)]
+        sums = [jnp.sum(v, axis=1, keepdims=True) for v in weights]
+        probs = [v * (1.0 / t) for v, t in zip(weights, sums)]
+        mixed = []
+        for (i, half), prob, value in zip(work, probs, vals):
+            at = slice(i * GROUP, (i + 1) * GROUP)
             prob_ref[i, half] = prob.astype(BF16)
-            mixed = dot((prob * scale).astype(BF16), vals)
-            attended[rows, lo : lo + HALF] = unstack_heads(mixed, masks16).astype(BF16)
-        return carry
-
-    lax.fori_loop(0, groups, group_step, 0, unroll=True)
-
+            mixed.append(dot((prob * repeat_heads(wrow_ref[at, :])).astype(BF16), value))
+        for (i, half), value in zip(work, mixed):
+            at = slice(i * GROUP, (i + 1) * GROUP)
+            lo = half * HALF
+            attended[at, lo : lo + HALF] = unstack_heads(value, masks16).astype(BF16)
+    move.store(prob_ref, prob_hbm.at[pl.ds(first_group, groups)])
+
+    got_x.wait()
+    got_wout.wait()
     att = attended[...]
     middle = x_ref[...].astype(F32) + dot(att, wout_ref[...])
     r2 = inverse_norm(middle)
     scaled = middle * r2
     second = (scaled * gain2_ref[...]).astype(BF16)
+    got_cot.wait()
     cot = cot_ref[...]
     cot_t = cot.T
     second_t = second.T
-
-    @pl.when(step == 0)
-    def _():
-        up_acc[...] = jnp.zeros_like(up_acc)
-        down_acc[...] = jnp.zeros_like(down_acc)
-        wo_acc[...] = jnp.zeros_like(wo_acc)
-        gain_acc[...] = prior_refs[2][...] if prior else jnp.zeros_like(gain_acc)
+    got_up.wait()
+    got_down.wait()
+    if prior:
+        for copy in got_prior:
+            copy.wait()
+
+    def total(value, old, lanes):
+        return value + old[:, lanes].astype(F32) if prior else value
+
+    edge = ff // 2
+
+    def put_up(c, value):
+        lanes = slice(c, c + width)
+        if not final:
+            one_ref[:, lanes] = value.astype(BF16)
+            return
+        ref, at = (one_ref, c) if c < edge else (two_ref, c - edge)
+        ref[at : at + width, :] = total(value, up_prior if prior else None, lanes).astype(BF16)
+
+    def put_down(c, value):
+        lanes = slice(c, c + width)
+        if not final:
+            two_ref[:, lanes] = value.astype(BF16)
+            return
+        ref, at = (one_ref, c) if c < edge else (two_ref, c - edge)
+        at += edge + width // 2
+        ref[at : at + width, :] = total(value, down_prior if prior else None, lanes).T.astype(BF16)
+
+    def put_out(value):
+        if not final:
+            one_ref[:, ff:] = value.astype(BF16)
+            return
+        value = total(value, up_prior if prior else None, slice(ff, ff + width)).astype(BF16)
+        one_ref[edge : edge + width // 2, :] = value[: width // 2]
+        two_ref[edge : edge + width // 2, :] = value[width // 2 :]
 
     result = middle
-    back = jnp.zeros((tile, width), F32)
+    back = jnp.zeros((rows, width), F32)
     c0 = 0.7978845608028654
     c1 = 0.044715
-    chunk = 512
-    for c in range(0, ff, chunk):
-        hidden = dot(second, wup_ref[:, c : c + chunk])
-        grad = dot(cot, wdown_ref[c : c + chunk, :], NT)
+    for c in range(0, ff, width):
+        hidden = dot(second, wup_ref[:, c : c + width])
+        grad = dot(cot, wdown_ref[c : c + width, :], NT)
         square = hidden * hidden
         t = jnp.tanh(hidden * (c0 + (c0 * c1) * square))
         left = 0.5 + 0.5 * t
         active = (hidden * left).astype(BF16)
         slope = left + (0.5 * hidden) * (1.0 - t * t) * (c0 + (3.0 * c0 * c1) * square)
         grad = (grad * slope).astype(BF16)
-        result = result + dot(active, wdown_ref[c : c + chunk, :])
-        back = back + dot(grad, wup_ref[:, c : c + chunk], NT)
-        down_acc[:, c : c + chunk] += dot(cot_t, active)
-        up_acc[:, c : c + chunk] += dot(second_t, grad)
+        result = result + dot(active, wdown_ref[c : c + width, :])
+        back = back + dot(grad, wup_ref[:, c : c + width], NT)
+        put_down(c, dot(cot_t, active))
+        put_up(c, dot(second_t, grad))
     out_ref[...] = result.astype(BF16)
-    gain_acc[...] += jnp.sum(back * scaled, axis=0, keepdims=True)
+    move.store(out_ref, out_hbm.at[here])
+    gain = jnp.sum(back * scaled, axis=0, keepdims=True)
+    gain_ref[...] = gain + prior_refs[2][...] if prior else gain
     e = back * gain2_ref[...]
     inner = jnp.mean(e * scaled, axis=-1, keepdims=True)
     grad_middle = cot.astype(F32) + r2 * (e - scaled * inner)
     branch = grad_middle.astype(BF16)
     gmid_ref[...] = branch
-    wo_acc[...] += dot(att.T, branch)
+    move.store(gmid_ref, gmid_hbm.at[here])
+    put_out(dot(att.T, branch))
+    if not final:
+        move.store(one_ref, up_hbm)
+        move.store(two_ref, down_hbm)
     gatt_ref[...] = dot(branch, wout_ref[...], NT).astype(BF16)
-
-    @pl.when(step == steps - 1)
-    def _():
-        gain_ref[...] = gain_acc[...]
-        if not final:
-            up_ref[:, :ff] = up_acc[...].astype(BF16)
-            up_ref[:, ff:] = wo_acc[...].astype(BF16)
-            down_ref[...] = down_acc[...].astype(BF16)
-            return
-        if prior:
-            for move in moves:
-                move.wait()
-
-        def total(acc, old, lanes):
-            value = acc[:, lanes]
-            return value + old[:, lanes].astype(F32) if prior else value
-
-        def write(ref, half):
-            at = 0
-            for c in range(half * ff // 2, (half + 1) * ff // 2, width):
-                value = total(up_acc, up_prior if prior else None, slice(c, c + width))
-                ref[at : at + width, :] = value.astype(BF16)
-                at += width
-            lines = slice(half * width // 2, (half + 1) * width // 2)
-            value = wo_acc[lines, :]
-            if prior:
-                value = value + up_prior[lines, ff:].astype(F32)
-            ref[at : at + width // 2, :] = value.astype(BF16)
-            at += width // 2
-            for c in range(half * ff // 2, (half + 1) * ff // 2, width):
-                value = total(down_acc, down_prior if prior else None, slice(c, c + width))
-                ref[at : at + width, :] = value.T.astype(BF16)
-                at += width
-
-        @pl.when(core_ref[0] == 0)
-        def _():
-            write(keep_ref, 0)
-            write(give_ref, 1)
-
-        @pl.when(core_ref[0] == 1)
-        def _():
-            write(keep_ref, 1)
-            write(give_ref, 0)
+    move.store(gatt_ref, gatt_hbm.at[here])
+    if final:
+        first, second_copy = move.used, move.used + 1
+        for which, (mine, other) in enumerate(((one_ref, two_ref), (two_ref, one_ref))):
+
+            @pl.when(core_ref[0] == which)
+            def _():
+                copies = [
+                    pltpu.make_async_copy(mine, keep_hbm, sems.at[first]),
+                    pltpu.make_async_copy(other, give_hbm, sems.at[second_copy]),
+                ]
+                for copy in copies:
+                    copy.start()
+                for copy in copies:
+                    copy.wait()
+
+    move.finish()
 
 
 def forward(
@@ -673,214 +754,258 @@
 ):
     rows, width = x.shape
     ff = w_up.shape[1]
-    per = TILE // GROUP
-    skip = first_group // per
     halves = width // HALF
-    at = lambda wide: pl.BlockSpec((TILE, wide), lambda i: (i + skip, 0))
+    count = groups * GROUP
     like = lambda wide, kind=BF16: jax.ShapeDtypeStruct((rows, wide), kind)
     probs = jax.ShapeDtypeStruct((rows // GROUP, halves, PER_HALF * GROUP, 2 * GROUP), BF16)
     part = ff + width // 2
     if final:
-        tail_shapes = [jax.ShapeDtypeStruct((part, width), BF16)] * 2
+        tails = [(part, width), (part, width)]
     else:
-        tail_shapes = [
-            jax.ShapeDtypeStruct((width, ff + width), BF16),
-            jax.ShapeDtypeStruct((width, ff), BF16),
-        ]
-    tail_shapes = tail_shapes + [jax.ShapeDtypeStruct((1, width), F32)]
-    in_specs = (
-        [SMEM, SMEM, SMEM]
-        + [whole(r.shape) for r in recv]
-        + [at(width), at(width), at(3 * width), at(2 * GROUP)]
-        + [whole(v.shape) for v in (mask, gain1, gain2, w_qkv, w_out, w_up, w_down)]
-    )
+        tails = [(width, ff + width), (width, ff)]
+    in_specs = [SMEM] * 3 + [ANY] * (len(recv) + 4) + [VMEM] * 3 + [ANY] * 5
     operands = [far_rows, kinds, core, *recv, x, cot, proj, wrow, mask, gain1, gain2]
-    operands += [w_qkv, w_out, w_up, w_down]
-    in_specs += [ANY]
-    operands += [token]
-    scratch = [
-        pltpu.VMEM((TILE, width), BF16),
-        pltpu.VMEM((width, ff), F32),
-        pltpu.VMEM((width, ff), F32),
-        pltpu.VMEM((width, width), F32),
-        pltpu.VMEM((1, width), F32),
+    operands += [w_qkv, w_out, w_up, w_down, token]
+    scratch = [pltpu.VMEM(r.shape, BF16) for r in recv]
+    scratch += [
+        pltpu.VMEM((count, width), BF16),
+        pltpu.VMEM((count, width), BF16),
+        pltpu.VMEM((count, 3 * width), BF16),
+        pltpu.VMEM((count, 2 * GROUP), F32),
     ]
+    scratch += [pltpu.VMEM(w.shape, BF16) for w in (w_qkv, w_out, w_up, w_down)]
+    scratch += [pltpu.VMEM((count, width), BF16)] * 3
+    scratch += [pltpu.VMEM((groups,) + probs.shape[1:], BF16)]
+    scratch += [pltpu.VMEM((count, n * width), BF16) for n in (1, 2, 1)]
+    scratch += [pltpu.VMEM(shape, BF16) for shape in tails]
     aliases = {}
     if prior is not None:
         streams, sums = prior
-        in_specs += [ANY, ANY, whole((1, width))] + [ANY] * 6
+        in_specs += [ANY, ANY, VMEM] + [ANY] * 6
         operands += list(sums)
         aliases = {len(operands) + i: i for i in range(6)}
         operands += list(streams)
-        scratch += [
-            pltpu.VMEM((width, ff + width), BF16),
-            pltpu.VMEM((width, ff), BF16),
-            pltpu.SemaphoreType.DMA((2,)),
-        ]
+        scratch += [pltpu.VMEM((width, ff + width), BF16), pltpu.VMEM((width, ff), BF16)]
+    scratch += [pltpu.SemaphoreType.DMA((24,))]
     out = pl.pallas_call(
-        functools.partial(forward_kernel, first_group, len(recv), prior is not None, final),
-        grid=(groups // per,),
+        functools.partial(
+            forward_kernel, first_group, groups, len(recv), prior is not None, final
+        ),
         in_specs=in_specs,
-        out_specs=[
-            at(width),
-            at(width),
-            at(width),
-            pl.BlockSpec((per,) + probs.shape[1:], lambda i: (i + skip, 0, 0, 0)),
-            at(width),
-            at(2 * width),
-        ]
-        + [whole(v.shape) for v in tail_shapes],
+        out_specs=[ANY] * 8 + [VMEM],
         out_shape=[like(width), like(width), like(width), probs, like(width), like(2 * width)]
-        + tail_shapes,
+        + [jax.ShapeDtypeStruct(shape, BF16) for shape in tails]
+        + [jax.ShapeDtypeStruct((1, width), F32)],
         scratch_shapes=scratch,
         input_output_aliases=aliases,
-        compiler_params=params(),
+        compiler_params=pltpu.CompilerParams(vmem_limit_bytes=VMEM_LIMIT),
         cost_estimate=cost(1.0e9 * groups, 1e6 * groups),
         name="forward",
     )(*operands)
     return out[:6], out[6:]
 
 
-def backward_kernel(first_group, prior, *refs):
+def backward_kernel(first_group, groups, prior, chunks, letter, *refs):
     refs = list(refs)
     take = lambda n: [refs.pop(0) for _ in range(n)]
-    (ret_rows,) = take(1)
-    proj_ref, farx_ref, farkv_ref, gatt_ref, prob_ref, wrow_ref, wqkv_ref = take(7)
+    ret_rows, place_ref = take(2)
+    proj_hbm, farx_hbm, farkv_hbm, gatt_hbm, prob_hbm, wrow_hbm, wqkv_hbm = take(7)
     if prior:
-        (prior_gain,) = take(1)
+        prior_gain, prior_gw = take(2)
         take(2)
     take(1)
-    dproj_ref, dfar_ref, gw_ref, gain_ref = take(4)
-    ret_refs = refs
-    step = pl.program_id(0)
-    tile, width = gatt_ref.shape
-    units = tile // UNIT
-    groups = tile // GROUP
+    dproj_hbm, dfar_hbm, gw_ref, gain_ref = take(4)
+    ret_hbm = take(chunks)
+    proj_ref, farx_ref, farkv_ref, gatt_ref, prob_ref, wrow_ref, wqkv_ref = take(7)
+    dproj_ref, dfar_ref = take(2)
+    ret_refs = take(chunks)
+    (sems,) = take(1)
+    move = Mover(sems)
+    rows = groups * GROUP
+    width = gatt_ref.shape[1]
+    start = first_group * GROUP
+    batches = [(first, min(first + BATCH, groups)) for first in range(0, groups, BATCH)]
+    loads = []
+    for low, high in batches:
+        at = pl.ds(low * GROUP, (high - low) * GROUP)
+        there = pl.ds(start + low * GROUP, (high - low) * GROUP)
+        loads.append(
+            [
+                move.start(hbm.at[there], ref.at[at])
+                for hbm, ref in (
+                    (proj_hbm, proj_ref),
+                    (farkv_hbm, farkv_ref),
+                    (gatt_hbm, gatt_ref),
+                    (wrow_hbm, wrow_ref),
+                )
+            ]
+            + [
+                move.start(
+                    prob_hbm.at[pl.ds(first_group + low, high - low)],
+                    prob_ref.at[pl.ds(low, high - low)],
+                )
+            ]
+        )
+    got_wqkv = move.start(wqkv_hbm, wqkv_ref)
+    got_farx = move.start(farx_hbm.at[pl.ds(start, rows)], farx_ref)
     masks16 = head_masks(GROUP)
     head_scale = (width // HEADS) ** -0.5
-
-    is_far = lax.broadcasted_iota(jnp.int32, (PER_HALF * GROUP, 2 * GROUP), 1) >= GROUP
-
-    def group_step(i, carry):
-        rows = pl.ds(pl.multiple_of(i * GROUP, GROUP), GROUP)
-        scale = repeat_heads(wrow_ref[rows, :])
-        weight_grad = jnp.zeros((GROUP, 1), F32)
-        for half in range(width // HALF):
+    far_lane = lax.broadcasted_iota(jnp.int32, (GROUP // UNIT, 2 * GROUP), 1) >= GROUP
+    for (low, high), copies in zip(batches, loads):
+        for copy in copies:
+            copy.wait()
+        work = [(i, half) for i in range(low, high) for half in range(width // HALF)]
+        stacks, products = [], []
+        for i, half in work:
+            at = slice(i * GROUP, (i + 1) * GROUP)
             lo = half * HALF
-            q = proj_ref[rows, lo : lo + HALF] * jnp.asarray(head_scale, BF16)
-            keys = jnp.concatenate(
-                [proj_ref[rows, width + lo : width + lo + HALF], farkv_ref[rows, lo : lo + HALF]],
-                axis=0,
-            )
             vals = jnp.concatenate(
                 [
-                    proj_ref[rows, 2 * width + lo : 2 * width + lo + HALF],
-                    farkv_ref[rows, width + lo : width + lo + HALF],
+                    proj_ref[at, 2 * width + lo : 2 * width + lo + HALF],
+                    farkv_ref[at, width + lo : width + lo + HALF],
                 ],
                 axis=0,
             )
-            q = stack_heads(q, masks16)
-            up = stack_heads(gatt_ref[rows, lo : lo + HALF], masks16)
+            up = stack_heads(gatt_ref[at, lo : lo + HALF], masks16)
+            stacks.append(up)
+            products.append(prob_ref[i, half].astype(F32) * dot(up, vals, NT))
+        for i in range(low, high):
+            summed = jnp.zeros((GROUP, 2 * GROUP), F32)
+            for (j, _), prod in zip(work, products):
+                if j == i:
+                    for h in range(PER_HALF):
+                        summed = summed + prod[h * GROUP : (h + 1) * GROUP]
+            pair = jnp.sum(summed.reshape(GROUP // UNIT, UNIT, 2 * GROUP), axis=1)
+            pair = jnp.sum(jnp.where(far_lane, pair, 0.0), axis=1, keepdims=True)
+            gw_ref[i] = jnp.broadcast_to(pair, (GROUP // UNIT, 128))
+        scales = [repeat_heads(wrow_ref[i * GROUP : (i + 1) * GROUP, :]) for i, _ in work]
+        products = [v * s for v, s in zip(products, scales)]
+        totals = [jnp.sum(v, axis=1, keepdims=True) for v in products]
+        for (i, half), up, prod, scale, total in zip(work, stacks, products, scales, totals):
+            at = slice(i * GROUP, (i + 1) * GROUP)
+            lo = half * HALF
             prob = prob_ref[i, half].astype(F32)
-            raw = dot(up, vals, NT)
-            far_sum = jnp.sum(jnp.where(is_far, prob * raw, 0.0), axis=1, keepdims=True)
-            mixed = prob * scale
-            ds = mixed * raw
-            total = jnp.sum(ds, axis=1, keepdims=True)
-            ds = (ds - prob * total).astype(BF16)
+            ds = (prod - prob * total).astype(BF16)
+            mixed = (prob * scale).astype(BF16)
+            q = stack_heads(
+                proj_ref[at, lo : lo + HALF] * jnp.asarray(head_scale, BF16), masks16
+            )
+            keys = jnp.concatenate(
+                [proj_ref[at, width + lo : width + lo + HALF], farkv_ref[at, lo : lo + HALF]], axis=0
+            )
             dq = unstack_heads(dot(ds, keys), masks16) * head_scale
             dk = dot(ds, q, TN).astype(BF16)
-            dv = dot(mixed.astype(BF16), up, TN).astype(BF16)
-            dproj_ref[rows, lo : lo + HALF] = dq.astype(BF16)
-            dproj_ref[rows, width + lo : width + lo + HALF] = dk[:GROUP]
-            dproj_ref[rows, 2 * width + lo : 2 * width + lo + HALF] = dv[:GROUP]
-            dfar_ref[rows, lo : lo + HALF] = dk[GROUP:]
-            dfar_ref[rows, width + lo : width + lo + HALF] = dv[GROUP:]
-            for h in range(PER_HALF):
-                weight_grad = weight_grad + far_sum[h * GROUP : (h + 1) * GROUP]
-        pair = jnp.broadcast_to(weight_grad, (GROUP, 128)).reshape(GROUP // UNIT, UNIT, 128)
-        gw_ref[i] = jnp.sum(pair, axis=1)
-        return carry
-
-    lax.fori_loop(0, groups, group_step, 0, unroll=True)
-
-    def scatter(values, first_unit, count):
-        for u in range(count):
-            row = ret_rows[first_unit + u]
-            edge = 0
-            for ret_ref in ret_refs:
-                inside = jnp.logical_and(row >= edge, row < edge + ret_ref.shape[0])
-
-                @pl.when(inside)
-                def _(ret_ref=ret_ref, edge=edge):
-                    at = pl.ds(pl.multiple_of(row - edge, 16), UNIT)
-                    ret_ref[at, :] = values(u)
-
-                edge += ret_ref.shape[0]
-
-    @pl.when(step == 0)
-    def _():
-        gain_ref[...] = prior_gain[...] if prior else jnp.zeros_like(gain_ref)
-
+            dv = dot(mixed, up, TN).astype(BF16)
+            dproj_ref[at, lo : lo + HALF] = dq.astype(BF16)
+            dproj_ref[at, width + lo : width + lo + HALF] = dk[:GROUP]
+            dproj_ref[at, 2 * width + lo : 2 * width + lo + HALF] = dv[:GROUP]
+            dfar_ref[at, lo : lo + HALF] = dk[GROUP:]
+            dfar_ref[at, width + lo : width + lo + HALF] = dv[GROUP:]
+        at = pl.ds(low * GROUP, (high - low) * GROUP)
+        there = pl.ds(start + low * GROUP, (high - low) * GROUP)
+        move.store(dproj_ref.at[at], dproj_hbm.at[there])
+        move.store(dfar_ref.at[at], dfar_hbm.at[there])
+
+    got_wqkv.wait()
+    got_farx.wait()
     grad = dot(dfar_ref[...], wqkv_ref[:, width:], NT)
     far = farx_ref[...].astype(F32)
-    gain_ref[...] += jnp.sum(grad * (far * inverse_norm(far)), axis=0, keepdims=True)
+    gain = jnp.sum(grad * (far * inverse_norm(far)), axis=0, keepdims=True)
+    gain_ref[...] = gain + prior_gain[...] if prior else gain
     grad = grad.astype(BF16)
-    scatter(
-        lambda u: grad[u * UNIT : (u + 1) * UNIT],
-        2 * first_group + step * units,
-        units,
-    )
+    for u in range(rows // UNIT):
+        row = ret_rows[2 * first_group + u]
+        edge = 0
+        for ret_ref in ret_refs:
+            value = grad[u * UNIT : (u + 1) * UNIT]
+
+            def put(ret_ref=ret_ref, edge=edge, value=value):
+                ret_ref[pl.ds(pl.multiple_of(row - edge, 16), UNIT), :] = value
+
+            if chunks == 1:
+                put()
+            else:
+                pl.when(jnp.logical_and(row >= edge, row < edge + ret_ref.shape[0]))(put)
+            edge += ret_ref.shape[0]
+    if letter:
+        count_a, count_b, devices, extra = letter
+        lane = lax.broadcasted_iota(jnp.int32, (1, 128), 1)
+        row = jnp.zeros((1, 128), F32)
+
+        def pair_at(at):
+            if not prior:
+                return gw_ref[at]
+            early = prior_gw.shape[0]
+            one = prior_gw[jnp.minimum(at, early - 1)]
+            two = gw_ref[jnp.maximum(at - early, 0)]
+            return jnp.where(at < early, one, two)
+
+        for j in range(count_a + count_b):
+            if j < count_a:
+                both = pair_at(lax.shift_right_logical(place_ref[2 * j], 1))
+                value = both[0:1] + both[1:2]
+            else:
+                pos = place_ref[count_a + j]
+                both = pair_at(lax.shift_right_logical(pos, 1))
+                value = jnp.where(lax.bitwise_and(pos, 1) == 0, both[0:1], both[1:2])
+            row = jnp.where(lane == j, value, row)
+        page = jnp.concatenate([row, jnp.zeros((1, width - 128), F32)], axis=1)
+        line = lax.broadcasted_iota(jnp.int32, (extra, width), 0)
+        page = jnp.where(line == 0, page, 0.0).astype(BF16)
+        ret_ref = ret_refs[-1]
+        height = ret_ref.shape[0] // devices
+        for d in range(devices):
+            ret_ref[(d + 1) * height - extra : (d + 1) * height, :] = page
+    for ret_ref, hbm in zip(ret_refs, ret_hbm):
+        move.store(ret_ref, hbm)
+    move.finish()
 
 
 def backward(
-    ret_rows, proj, farx, farkv, gatt, prob, wrow, w_qkv, sizes, first_group, groups, prior, token
+    ret_rows, place, proj, farx, farkv, gatt, prob, wrow, w_qkv, sizes, first_group, groups, prior, letter,
+    token,
 ):
     rows, width = gatt.shape
-    per = TILE // GROUP
-    skip = first_group // per
-    at = lambda wide: pl.BlockSpec((TILE, wide), lambda i: (i + skip, 0))
-    in_specs = [
-        SMEM,
-        at(3 * width),
-        at(width),
-        at(2 * width),
-        at(width),
-        pl.BlockSpec((per,) + prob.shape[1:], lambda i: (i + skip, 0, 0, 0)),
-        at(2 * GROUP),
-        whole(w_qkv.shape),
-    ]
-    operands = [ret_rows, proj, farx, farkv, gatt, prob, wrow, w_qkv]
+    count = groups * GROUP
+    in_specs = [SMEM, SMEM] + [ANY] * 7
+    operands = [ret_rows, place, proj, farx, farkv, gatt, prob, wrow, w_qkv]
     aliases = {}
     if prior is not None:
-        dproj, dfar, gain = prior
-        in_specs += [whole(gain.shape), ANY, ANY]
-        aliases = {len(operands) + 1: 0, len(operands) + 2: 1}
-        operands += [gain, dproj, dfar]
+        dproj, dfar, gw, gain = prior
+        in_specs += [VMEM, VMEM, ANY, ANY]
+        aliases = {len(operands) + 2: 0, len(operands) + 3: 1}
+        operands += [gain, gw, dproj, dfar]
     in_specs += [ANY]
     operands += [token]
-    ret_specs = [whole((n, width)) for n in sizes]
-    ret_shapes = [jax.ShapeDtypeStruct((n, width), BF16) for n in sizes]
+    batches = -(-groups // BATCH)
     return pl.pallas_call(
-        functools.partial(backward_kernel, first_group, prior is not None),
-        grid=(groups // per,),
+        functools.partial(
+            backward_kernel, first_group, groups, prior is not None, len(sizes), letter
+        ),
         in_specs=in_specs,
-        out_specs=[
-            at(3 * width),
-            at(2 * width),
-            pl.BlockSpec((per, GROUP // UNIT, 128), lambda i: (i, 0, 0)),
-            whole((1, width)),
-        ]
-        + ret_specs,
+        out_specs=[ANY, ANY, VMEM, VMEM] + [ANY] * len(sizes),
         out_shape=[
             jax.ShapeDtypeStruct((rows, 3 * width), BF16),
             jax.ShapeDtypeStruct((rows, 2 * width), BF16),
             jax.ShapeDtypeStruct((groups, GROUP // UNIT, 128), F32),
             jax.ShapeDtypeStruct((1, width), F32),
         ]
-        + ret_shapes,
+        + [jax.ShapeDtypeStruct((n, width), BF16) for n in sizes],
+        scratch_shapes=[
+            pltpu.VMEM((count, 3 * width), BF16),
+            pltpu.VMEM((count, width), BF16),
+            pltpu.VMEM((count, 2 * width), BF16),
+            pltpu.VMEM((count, width), BF16),
+            pltpu.VMEM((groups,) + prob.shape[1:], BF16),
+            pltpu.VMEM((count, 2 * GROUP), F32),
+            pltpu.VMEM(w_qkv.shape, BF16),
+            pltpu.VMEM((count, 3 * width), BF16),
+            pltpu.VMEM((count, 2 * width), BF16),
+        ]
+        + [pltpu.VMEM((n, width), BF16) for n in sizes]
+        + [pltpu.SemaphoreType.DMA((7 * batches + 2 + len(sizes),))],
         input_output_aliases=aliases,
-        compiler_params=params(),
+        compiler_params=pltpu.CompilerParams(vmem_limit_bytes=VMEM_LIMIT),
         cost_estimate=cost(0.4e9 * groups, 1e6 * groups),
         name="backward",
     )(*operands)
@@ -1121,8 +1246,23 @@
     )(values, *tokens)
 
 
+def fetch(sources, targets, sems):
+    copies = [
+        pltpu.make_async_copy(source, target, sems.at[i])
+        for i, (source, target) in enumerate(zip(sources, targets))
+    ]
+    for copy in copies:
+        copy.start()
+    for copy in copies:
+        copy.wait()
+
+
 def halve_kernel(ranges, sources, bits_ref, *refs):
-    outs = refs[2 * sources + 1 :]
+    count = 2 * (1 + max(r[4] for r in ranges))
+    outs = refs[2 * sources + 1 : 2 * sources + 1 + count]
+    held = refs[2 * sources + 1 + count : -1]
+    fetch(refs[: 2 * sources], held, refs[-1])
+    refs = held
     for source, first, count, bit, out, there in ranges:
         own, came = refs[2 * source], refs[2 * source + 1]
         half = count // 2
@@ -1142,9 +1282,11 @@
     flat = [v for pair in pairs for v in pair]
     out = pl.pallas_call(
         functools.partial(halve_kernel, ranges, len(pairs)),
-        in_specs=[SMEM] + [VMEM] * len(flat) + [ANY],
+        in_specs=[SMEM] + [ANY] * len(flat) + [ANY],
         out_specs=[VMEM] * len(shapes),
         out_shape=shapes,
+        scratch_shapes=[pltpu.VMEM(v.shape, BF16) for v in flat]
+        + [pltpu.SemaphoreType.DMA((len(flat),))],
         compiler_params=limit(24),
         cost_estimate=cost(0, 8 * sum(heights) * width),
         name="halve_step",
@@ -1153,7 +1295,11 @@
 
 
 def double_kernel(ranges, sources, tokens, bits_ref, *refs):
-    outs = refs[2 * sources + tokens :]
+    count = 1 + max(r[0] for r in ranges)
+    outs = refs[2 * sources + tokens : 2 * sources + tokens + count]
+    held = refs[2 * sources + tokens + count : -1]
+    fetch(refs[: 2 * sources], held, refs[-1])
+    refs = held
     for source, first, count, bit, out, there in ranges:
         own, came = refs[2 * out], refs[2 * out + 1]
         half = count // 2
@@ -1170,9 +1316,11 @@
     flat = [v for pair in pairs for v in pair]
     return pl.pallas_call(
         functools.partial(double_kernel, ranges, len(pairs), len(tokens)),
-        in_specs=[SMEM] + [VMEM] * len(flat) + [ANY] * len(tokens),
+        in_specs=[SMEM] + [ANY] * len(flat) + [ANY] * len(tokens),
         out_specs=[VMEM] * count,
         out_shape=[jax.ShapeDtypeStruct((n, width), BF16) for n in heights],
+        scratch_shapes=[pltpu.VMEM(v.shape, BF16) for v in flat]
+        + [pltpu.SemaphoreType.DMA((len(flat),))],
         compiler_params=limit(24),
         cost_estimate=cost(0, 4 * sum(heights) * width),
         name="double_step",
@@ -1293,29 +1441,19 @@
 
     sizes = [8, 7] if early < groups else [capacity]
     extra = 16
-    sel = jnp.concatenate([sel_a.reshape(-1), sel_b.reshape(-1)])
-    table, back_table, far_rows, ret_rows, perm, place, kinds = request(
-        sel, npl, seqs_a, seqs_b, devices, capacity, first, early, sizes, extra, picks_up
-    )
-
     average = np.zeros((picks, units), np.float32)
     for j in range(count_a):
         average[j, 2 * j : 2 * j + 2] = 1.0 / len_a
     for j in range(count_b):
         average[count_a + j, units_a + j] = 1.0 / len_b
-    x, means, logits = digest(
-        x_a.reshape(-1, width), x_b.reshape(-1, width), gain1, average, w_sort
+    settings = (npl, seqs_a, seqs_b, devices, capacity, first, early, sizes, extra, picks_up)
+    w_sort_t = w_sort.T
+    x, means, news, far_rows, ret_rows, perm, place, kinds = digest(
+        x_a.reshape(-1, width), x_b.reshape(-1, width), sel_a, sel_b, gain1, average, w_sort_t, settings
     )
-    spare = -(-picks // 8) * 8 + 8 - picks
-    news = jnp.concatenate([logits, sel.astype(F32)[:, None]], axis=1)
-    news = jnp.pad(news, ((0, spare), (0, 127 - blocks)))
-    both = jnp.concatenate(
-        [table.reshape(devices, capacity), back_table.reshape(devices, sum(sizes))], axis=1
-    ).astype(F32)
-    asked = jnp.pad(both[:, None], ((0, 0), (picks, spare - 1), (0, 128 - both.shape[1])))
-    news = lax.all_to_all(news[None] + asked, "blk", split_axis=0, concat_axis=0, tiled=True)
+    news = lax.all_to_all(news, "blk", split_axis=0, concat_axis=0, tiled=True)
     table = news[:, picks, :capacity].astype(jnp.int32).reshape(-1)
-    back_table = news[:, picks, capacity : both.shape[1]].astype(jnp.int32).reshape(-1)
+    back_table = news[:, picks, capacity : capacity + sum(sizes)].astype(jnp.int32).reshape(-1)
     news = news[:, :picks]
     parcels = pack(table, x, devices, capacity, first, picks_up)
     recv = [exchange(parcels[0], devices)]
@@ -1373,16 +1511,18 @@
         for i, n in enumerate(sizes)
     ]
 
+    letter = (count_a, count_b, devices, extra)
+
     def run_backward(streams, *rest):
         _, _, gatt, prob, farx, farkv = streams
-        return backward(ret_rows, proj, farx, farkv, gatt, prob, wrow, w_qkv, *rest)
+        return backward(ret_rows, place, proj, farx, farkv, gatt, prob, wrow, w_qkv, *rest)
 
     fast = lax.axis_size("dp") == 4 and devices == 8 and early < groups
     part_x = ff // 2 + width // 2
     if early < groups:
         prior = forward(far_rows, kinds, core, recv[:1], *shared, 0, early, None, False, wrow)
         dproj, dfar, gw_one, gain, *ret = run_backward(
-            prior[0], heights[:1], 0, early, None, prior[0][0]
+            prior[0], heights[:1], 0, early, None, None, prior[0][0]
         )
         back = [exchange(v, devices) for v in ret]
         streams, sums = forward(
@@ -1399,33 +1539,23 @@
             )
             bx_came, by_came = swap(gx, *AXIS_X), swap(gy, *AXIS_Y)
             token = bx
-        dproj, dfar, gw_two, g_gain1_far, *ret = run_backward(
-            streams, heights[1:], early, groups - early, (dproj, dfar, gain), token
+        dproj, dfar, _, g_gain1_far, *ret = run_backward(
+            streams, heights[1:], early, groups - early, (dproj, dfar, gw_one, gain), letter, token
         )
-        gw = jnp.concatenate([gw_one, gw_two])
     else:
         streams, sums = forward(far_rows, kinds, core, recv, *shared, 0, groups, None, True, wrow)
         keep, give, g_gain2 = sums
         out_a, out_b = restore(perm, streams[0], total_a)
         big_came = swap(give, "dp", 0)
         back = []
-        dproj, dfar, gw, g_gain1_far, *ret = run_backward(
-            streams, heights, 0, groups, None, keep
+        dproj, dfar, _, g_gain1_far, *ret = run_backward(
+            streams, heights, 0, groups, None, letter, keep
         )
     _, gmid, _, _, farx, _ = streams
 
-    gw = jnp.take(gw[:, :, 0].reshape(-1), place)
-    gw = jnp.concatenate(
-        [jnp.sum(gw[:units_a].reshape(-1, len_a // UNIT), axis=1), gw[units_a:]]
-    )
-    gw = jnp.pad(gw.astype(BF16)[None], ((0, extra - 1), (0, width - picks)))
-    if fast:
-        gw = tie(gw, bx_came, by_came, back[0])
-    tall = sizes[len(back)] * UNIT
-    parcel = lax.dynamic_update_slice(
-        ret[0].reshape(devices, -1, width), jnp.broadcast_to(gw, (devices, extra, width)), (0, tall, 0)
-    )
-    arrived = exchange(parcel.reshape(-1, width), devices)
+    parcel = tie(ret[0], bx_came, by_came, back[0]) if fast else ret[0]
+    tall = sizes[-1] * UNIT
+    arrived = exchange(parcel, devices)
     back.append(arrived)
     gains = jnp.concatenate([g_gain1_far, g_gain2], axis=0)
     token = dproj
@@ -1479,7 +1609,7 @@
         flat_logits, flat_units, TN, precision=precise, preferred_element_type=F32
     )
     g_unit = lax.dot_general(
-        flat_logits, w_sort.astype(F32), NT, precision=precise, preferred_element_type=F32
+        flat_logits, w_sort_t.astype(F32), NN, precision=precise, preferred_element_type=F32
     )
     g_own = own_rows(g_unit.reshape(g_logits.shape[:2] + (width,)))
     g_summary = rs * (

time: 408 us -> 375 us (0.919)
  Pallas kernels: 193 us -> 169 us
  local copies, waits for them, and re-layouts: 46.3 us -> 34.7 us
    pallas_call x6 -> x5, Pallas kernels: 118 us -> 91.4 us  [the longest x2 60.4 us: forward(): pl.pallas_call(functools.partial(forward_kernel, first_group, groups, len...]
    unnamed x107 -> x102, local copies, waits for them, and re-layouts: 29.4 us -> 25.7 us
  transfers between devices with their start and end apart: 22 -> 22, of which waited for: 12 -> 14; matrix products, arithmetic and copies ran while one was open for 5% -> 5% of each run, Pallas kernels for 42% -> 39%
where the time goes in v2:
time: 375 us; the launch traced here: 368 us
  Pallas kernels  169 us (45%)
  waiting for transfers between devices  95.5 us (25%)
  starting transfers between devices  35.3 us (9%)
  local copies, waits for them, and re-layouts  34.7 us (9%)
  blocking collectives  15.7 us (4%)
  other arithmetic  15.3 us (4%)
    ppermute x18, waiting for transfers between devices, swap(): return lax.ppermute(values, axis, [(i, i ^ 1 << bit) for i in range(size)])  72.6 us
    pallas_call x2, Pallas kernels, forward(): pl.pallas_call(functools.partial(forward_kernel, first_group, groups, len...  60.4 us
    unnamed x102, local copies, waits for them, and re-layouts  25.7 us
    all_to_all x4, waiting for transfers between devices, exchange(): lax.all_to_all(parts, 'blk', split_axis=0, concat_axis=0, tiled=True)  22.9 us
    pallas_call x2, Pallas kernels, backward(): pl.pallas_call(functools.partial(backward_kernel, first_group, groups, pr...  21 us
    all_to_all x4, starting transfers between devices, exchange(): lax.all_to_all(parts, 'blk', split_axis=0, concat_axis=0, tiled=True)  20.8 us
    all_to_all x1, blocking collectives, per_device(): news = lax.all_to_all(news, 'blk', split_axis=0, concat_axis=0, tiled=True)  15.7 us
    pallas_call x1, Pallas kernels, qkv_grads(): pl.pallas_call(functools.partial(qkv_kernel, extra), grid=(rows // TILE,)...  15.5 us
  transfers between devices with their start and end apart: 22, of which 14 were waited for; matrix products, arithmetic and copies ran while one was open for 5% of the time, Pallas kernels for 39%

profile of v2, /device:TPU:0, one launch (start us, length us, event | category | flops | bytes accessed | tf_op | source)
XLA Modules:
  0.0 367.8 jit_solution(4205424948577031900)
XLA Ops:
  1.9 9.9 %digest.1 = (bf16[2048,512]{1,0:T(8,128)(2,1)}, f32[48,512]{1,0:T(8,128)}, f32[8,56,128]{2,1,0:T(8,128)}, s32[64]{0:T(128)}, s32[64]{0:T(128)}, /*index=5*/s32[64]{0:T(128)}, s32[64]{0:T(128)}, s32[2]{0:T(128)}) custom-call(s32[2,8]{1,0:T(2,128)} %sela_ref.1, s32[4,8]{1,0:T(4,128)} %selb_ref.1, bf16[1024,512]{1,0:T(8,128)(2,1)} %bitcast.97, ...), custom_call_target="tpu_custom_call" | custom-call | flops 10485 | bytes 4194 | tf_op jit(solution)/shard_map/digest/pallas_call | solution.py:277
  11.9 15.7 %all_to_all.25 = f32[8,56,128]{2,1,0:T(8,128)S(1)} all-to-all(f32[8,56,128]{2,1,0:T(8,128)} %get-tuple-element.88), channel_id=1, replica_groups=mesh['dp'=4,'blk'=8] {'blk'}, dimensions={0} | all-to-all | bytes 458752 | tf_op jit(solution)/shard_map/all_to_all | solution.py:1454
  27.7 1.6 copy-done.4
  29.3 2.2 pack.1
  32.8 4.6 %all-to-all-start.1 = ((bf16[8,256,512]{2,1,0:T(8,128)(2,1)}), bf16[8,256,512]{2,1,0:T(8,128)(2,1)}, u32[]{:S(2)}, u32[]{:S(2)}) async-start(bf16[8,256,512]{2,1,0:T(8,128)(2,1)} %bitcast.76), calls=%async_computation.1 | async-start | bytes 4194304 | tf_op jit(solution)/shard_map/all_to_all | solution.py:1404
  38.7 1.9 arrange.1
  43.2 9.4 %project.1.refs_2_.refs_6_.refs_7_ = bf16[2048,1536]{1,0:T(8,128)(2,1)} custom-call(bf16[2048,512]{1,0:T(8,128)(2,1)} %copy-done, f32[1,512]{1,0:T(1,128)} %bitcast.81, bf16[512,1536]{1,0:T(8,128)(2,1)} %wqkv_ref.1), custom_call_target="tpu_custom_call" | custom-call | flops 3221225 | bytes 8388 | tf_op jit(solution)/shard_map/project/pallas_call | solution.py:436
  54.0 3.7 %sinkhorn.1 = f32[6,64,128]{2,1,0:T(8,128)} custom-call(f32[6,64,64]{2,1,0:T(8,128)} %bitcast.92, f32[6,64,64]{2,1,0:T(8,128)} %fusion.4.picked_ref), custom_call_target="tpu_custom_call" | custom-call | flops 2457 | bytes 786 | tf_op jit(solution)/shard_map/sinkhorn/pallas_call | solution.py:465
  61.6 22.9 %all-to-all-done.1 = bf16[8,256,512]{2,1,0:T(8,128)(2,1)} async-done(((bf16[8,256,512]{2,1,0:T(8,128)(2,1)}), bf16[8,256,512]{2,1,0:T(8,128)(2,1)}, u32[]{:S(2)}, u32[]{:S(2)}) %all-to-all-start.1) | async-done | bytes 2097184 | tf_op jit(solution)/shard_map/all_to_all | solution.py:1404
  84.5 3.8 %all-to-all-start.2 = ((bf16[8,240,512]{2,1,0:T(8,128)(2,1)}), bf16[8,240,512]{2,1,0:T(8,128)(2,1)S(1)}, u32[]{:S(2)}, u32[]{:S(2)}) async-start(bf16[8,240,512]{2,1,0:T(8,128)(2,1)} %bitcast.20), calls=%async_computation.2 | async-start | bytes 3932160 | tf_op jit(solution)/shard_map/all_to_all | solution.py:1404
  88.9 35.3 %forward.2 = (bf16[2048,512]{1,0:T(8,128)(2,1)}, bf16[2048,512]{1,0:T(8,128)(2,1)}, bf16[2048,512]{1,0:T(8,128)(2,1)}, bf16[32,2,256,128]{3,2,1,0:T(8,128)(2,1)}...) custom-call(s32[64]{0:T(128)} %get-tuple-element.86.refs_0_, ...), custom_call_target="tpu_custom_call" | custom-call | flops 20000000 | bytes 20000 | tf_op jit(solution)/shard_map/forward/pallas_call | solution.py:790
  124.3 11.9 %backward.2 = (bf16[2048,1536]{1,0:T(8,128)(2,1)}, bf16[2048,1024]{1,0:T(8,128)(2,1)}, f32[20,2,128]{2,1,0:T(2,128)}, f32[1,512]{1,0:T(1,128)}, bf16[2048,512]{1,0:T(8,128)(2,1)}) custom-call(s32[64]{0:T(128)} %get-tuple-element.95.refs_0_, s32[64]{0:T(128)} %get-tuple-element.96.refs_1_.place_ref, bf16[2048,1536]{1,0:T(8,128)(2,1)} %project.1.refs_2_.refs_6_.refs_7_, ...), custom_call_target="tpu_custom_call" | custom-call | flops 8000000 | bytes 20000 | tf_op jit(solution)/shard_map/backward/pallas_call | solution.py:981
  137.5 6.0 %all-to-all-start.3 = ((bf16[8,256,512]{2,1,0:T(8,128)(2,1)}), bf16[8,256,512]{2,1,0:T(8,128)(2,1)S(1)}, u32[]{:S(2)}, u32[]{:S(2)}) async-start(bf16[8,256,512]{2,1,0:T(8,128)(2,1)} %bitcast.94), calls=%async_computation.3 | async-start | bytes 4194304 | tf_op jit(solution)/shard_map/all_to_all | solution.py:1404
  143.5 25.1 %forward.3 = (bf16[2048,512]{1,0:T(8,128)(2,1)}, bf16[2048,512]{1,0:T(8,128)(2,1)}, bf16[2048,512]{1,0:T(8,128)(2,1)}, bf16[32,2,256,128]{3,2,1,0:T(8,128)(2,1)}...) custom-call(s32[64]{0:T(128)} %get-tuple-element.86.refs_0_, ...), custom_call_target="tpu_custom_call", output_to_operand_aliasing={{0}: (20, {}), {1}: (21, {}), {2}: (22, {}), {3}: (23, {}),... | custom-call | flops 12000000 | bytes 12000 | tf_op jit(solution)/shard_map/forward/pallas_call | solution.py:790
  168.7 1.6 copy-done.3
  170.3 3.1 restore.1
  173.5 1.7 copy-done.13
  176.4 2.9 halve_step.4
  182.4 2.0 collective-permute-start.2
  184.5 9.1 %backward.3 = (bf16[2048,1536]{1,0:T(8,128)(2,1)}, bf16[2048,1024]{1,0:T(8,128)(2,1)}, f32[12,2,128]{2,1,0:T(2,128)}, f32[1,512]{1,0:T(1,128)}, bf16[1920,512]{1,0:T(8,128)(2,1)}) custom-call(s32[64]{0:T(128)} %get-tuple-element.95.refs_0_, s32[64]{0:T(128)} %get-tuple-element.96.refs_1_.place_ref, ...), custom_call_target="tpu_custom_call", output_to_operand_aliasing={{0}: (11, {}), {1}: (12, {})} | custom-call | flops 4800000 | bytes 12000 | tf_op jit(solution)/shard_map/backward/pallas_call | solution.py:981
  193.6 3.3 collective-permute-done.2.refs_2_.refs_5_
  199.6 6.4 %all-to-all-start.4 = ((bf16[8,240,512]{2,1,0:T(8,128)(2,1)}), bf16[8,240,512]{2,1,0:T(8,128)(2,1)S(1)}, u32[]{:S(2)}, u32[]{:S(2)}) async-start(bf16[8,240,512]{2,1,0:T(8,128)(2,1)} %bitcast.88), calls=%async_computation.4 | async-start | bytes 3932160 | tf_op jit(solution)/shard_map/all_to_all | solution.py:1404
  206.6 15.5 %qkv_grads.1 = (bf16[2048,512]{1,0:T(8,128)(2,1)}, bf16[896,512]{1,0:T(8,128)(2,1)}, bf16[896,512]{1,0:T(8,128)(2,1)}) custom-call(s32[1]{0:T(128)} %bitcast.4.refs_2_.core_ref, bf16[2048,512]{1,0:T(8,128)(2,1)} %copy-done, bf16[2048,512]{1,0:T(8,128)(2,1)} %get-tuple-element.111.refs_3_.farx_ref, bf16[2048,1536]{1,0:T(8,128)(2,1)} %get-tuple-element.125.dproj_ref.token_ref, ...), custom_call_target="tpu_custom_call" | custom-call | flops 10000000 | bytes 25000 | tf_op jit(solution)/shard_map/qkv_grads/pallas_call | solution.py:1074
  222.2 2.7 collective-permute-done.3.refs_1_.refs_2_
  226.1 1.8 halve_step.5
  230.8 2.0 collective-permute-start.5
  233.9 7.8 %collective-permute-done.5.refs_7_ = bf16[192,512]{1,0:T(8,128)(2,1)} collective-permute-done((bf16[192,512]{1,0:T(8,128)(2,1)}, bf16[192,512]{1,0:T(8,128)(2,1)}, u32[]{:S(2)}, u32[]{:S(2)}) %collective-permute-start.5) | collective-permute-done | bytes 196640 | tf_op jit(solution)/shard_map/ppermute | solution.py:1205
  244.7 3.5 halve_step.6
  252.8 6.2 %collective-permute-done.7.refs_3_ = bf16[352,512]{1,0:T(8,128)(2,1)S(1)} collective-permute-done((bf16[352,512]{1,0:T(8,128)(2,1)}, bf16[352,512]{1,0:T(8,128)(2,1)S(1)}, u32[]{:S(2)}, u32[]{:S(2)}) %collective-permute-start.7) | collective-permute-done | bytes 360480 | tf_op jit(solution)/shard_map/ppermute | solution.py:1205
  259.0 2.0 collective-permute-done.6.refs_1_
  266.7 4.9 %sinkhorn_back.1 = f32[6,64,64]{2,1,0:T(8,128)} custom-call(f32[6,64,64]{2,1,0:T(8,128)} %bitcast.93, f32[6,64,64]{2,1,0:T(8,128)} %fusion.4.picked_ref, f32[6,64,64]{2,1,0:T(8,128)} %broadcast_in_dim.69.gw_ref), custom_call_target="tpu_custom_call" | custom-call | flops 4915 | bytes 786 | tf_op jit(solution)/shard_map/sinkhorn_back/pallas_call | solution.py:489
  275.6 10.9 %collective-permute-done.8 = bf16[400,512]{1,0:T(8,128)(2,1)} collective-permute-done((bf16[400,512]{1,0:T(8,128)(2,1)S(1)}, bf16[400,512]{1,0:T(8,128)(2,1)}, u32[]{:S(2)}, u32[]{:S(2)}) %collective-permute-start.8) | collective-permute-done | bytes 409632 | tf_op jit(solution)/shard_map/ppermute | solution.py:1205
  286.5 1.9 add_convert_fusion.1
  290.5 7.7 %base.1.refs_3_ = bf16[2048,512]{1,0:T(8,128)(2,1)} custom-call(bf16[2048,512]{1,0:T(8,128)(2,1)} %copy-done, bf16[2048,512]{1,0:T(8,128)(2,1)} %get-tuple-element.124.gmid_ref, bf16[2048,512]{1,0:T(8,128)(2,1)} %get-tuple-element.129.gn_ref, f32[64,512]{1,0:T(8,128)} %broadcast_select_fusion.gs_ref, f32[1,512]{1,0:T(1,128)} %bitcast.85), custom_call_target="tpu_custom_call" | custom-call | flops 20971 | bytes 8388 | tf_op jit(solution)/shard_map/base/pallas_call | solution.py:1117
  298.3 1.6 copy-done.8
  299.8 10.0 %last.1 = (bf16[1024,512]{1,0:T(8,128)(2,1)}, bf16[1024,512]{1,0:T(8,128)(2,1)}) custom-call(s32[120]{0:T(128)S(1)} %convert_element_type.58.table_ref, s32[64]{0:T(128)S(1)} %copy-done.34, bf16[2048,512]{1,0:T(8,128)(2,1)S(1)} %bitcast.73, bf16[1920,512]{1,0:T(8,128)(2,1)S(1)} %bitcast.75, bf16[2048,512]{1,0:T(8,128)(2,1)S(1)} %copy-done.6, ...), custom_call_target="tpu_custom_call" | custom-call | flops 20971 | bytes 12582 | tf_op jit(solution)/shard_map/last/pallas_call | solution.py:1177
  309.8 1.7 add.52.refs_2_
  312.7 1.7 collective-permute-start.12
  314.4 9.2 %collective-permute-done.12.refs_1_ = bf16[400,512]{1,0:T(8,128)(2,1)S(1)} collective-permute-done((bf16[400,512]{1,0:T(8,128)(2,1)S(1)}, bf16[400,512]{1,0:T(8,128)(2,1)S(1)}, u32[]{:S(2)}, u32[]{:S(2)}) %collective-permute-start.12) | collective-permute-done | bytes 409632 | tf_op jit(solution)/shard_map/ppermute | solution.py:1205
  325.9 7.0 %collective-permute-done.14.refs_3_ = bf16[352,512]{1,0:T(8,128)(2,1)S(1)} collective-permute-done((bf16[352,512]{1,0:T(8,128)(2,1)S(1)}, bf16[352,512]{1,0:T(8,128)(2,1)S(1)}, u32[]{:S(2)}, u32[]{:S(2)}) %collective-permute-start.14) | collective-permute-done | bytes 360480 | tf_op jit(solution)/shard_map/ppermute | solution.py:1205
  333.0 2.0 collective-permute-done.13.refs_1_
  334.9 1.5 double_step.4
  338.3 15.1 %collective-permute-done.16.refs_3_ = bf16[704,512]{1,0:T(8,128)(2,1)S(1)} collective-permute-done((bf16[704,512]{1,0:T(8,128)(2,1)S(1)}, bf16[704,512]{1,0:T(8,128)(2,1)S(1)}, u32[]{:S(2)}, u32[]{:S(2)}) %collective-permute-start.16) | collective-permute-done | bytes 720928 | tf_op jit(solution)/shard_map/ppermute | solution.py:1205
  353.4 2.9 collective-permute-done.15.refs_1_
  356.3 1.8 double_step.5.values_ref
  358.9 2.9 assemble.2
  361.8 2.3 collective-permute-done.17.values_ref
  364.1 2.7 assemble.3
  (191 shorter events, 52.5 us)
Async XLA Ops:
  27.6 25.3 %copy-start.45 = (f32[8,56,128]{2,1,0:T(8,128)}, f32[8,56,128]{2,1,0:T(8,128)S(1)}, u32[]{:S(2)}) copy-start(f32[8,56,128]{2,1,0:T(8,128)S(1)} %all_to_all.25) | copy-start | bytes 688132
  32.8 4.6 %copy-start.5 = (bf16[2048,512]{1,0:T(8,128)(2,1)S(1)}, bf16[2048,512]{1,0:T(8,128)(2,1)}, u32[]{:S(2)}) copy-start(bf16[2048,512]{1,0:T(8,128)(2,1)} %get-tuple-element.89.x_ref.refs_2_) | copy-start | bytes 6291460
  32.8 4.6 %copy-start.19 = (bf16[2,512,512]{2,1,0:T(8,128)(2,1)S(1)}, bf16[2,512,512]{2,1,0:T(8,128)(2,1)}, u32[]{:S(2)}) copy-start(bf16[2,512,512]{2,1,0:T(8,128)(2,1)} %param.26) | copy-start | bytes 3145732
  32.8 4.7 %copy-start.35 = (s32[64]{0:T(128)S(1)}, s32[64]{0:T(128)}, u32[]{:S(2)}) copy-start(s32[64]{0:T(128)} %get-tuple-element.85.perm_ref) | copy-start | bytes 772
  32.8 51.7 %all-to-all-start.1 = ((bf16[8,256,512]{2,1,0:T(8,128)(2,1)}), bf16[8,256,512]{2,1,0:T(8,128)(2,1)}, u32[]{:S(2)}, u32[]{:S(2)}) async-start(bf16[8,256,512]{2,1,0:T(8,128)(2,1)} %bitcast.76), calls=%async_computation.1 | async-start | bytes 4194304 | tf_op jit(solution)/shard_map/all_to_all | solution.py:1404
  43.2 9.4 %copy-start.31 = (f32[512]{0:T(512)S(1)}, f32[512]{0:T(512)}, u32[]{:S(2)}) copy-start(f32[512]{0:T(512)} %convert_element_type.52) | copy-start | bytes 6148
  43.2 9.4 %copy-start.40 = (f32[48,512]{1,0:T(8,128)S(1)}, f32[48,512]{1,0:T(8,128)}, u32[]{:S(2)}) copy-start(f32[48,512]{1,0:T(8,128)} %get-tuple-element.92) | copy-start | bytes 294916
  61.6 26.7 %copy-start.50 = (bf16[512]{0:T(512)(128)(2,1)S(1)}, bf16[512]{0:T(512)(128)(2,1)}, u32[]{:S(2)}) copy-start(bf16[512]{0:T(512)(128)(2,1)} %param.23) | copy-start | bytes 3076
  84.5 51.7 %all-to-all-start.2 = ((bf16[8,240,512]{2,1,0:T(8,128)(2,1)}), bf16[8,240,512]{2,1,0:T(8,128)(2,1)S(1)}, u32[]{:S(2)}, u32[]{:S(2)}) async-start(bf16[8,240,512]{2,1,0:T(8,128)(2,1)} %bitcast.20), calls=%async_computation.2 | async-start | bytes 3932160 | tf_op jit(solution)/shard_map/all_to_all | solution.py:1404
  137.5 60.6 %all-to-all-start.3 = ((bf16[8,256,512]{2,1,0:T(8,128)(2,1)}), bf16[8,256,512]{2,1,0:T(8,128)(2,1)S(1)}, u32[]{:S(2)}, u32[]{:S(2)}) async-start(bf16[8,256,512]{2,1,0:T(8,128)(2,1)} %bitcast.94), calls=%async_computation.3 | async-start | bytes 4194304 | tf_op jit(solution)/shard_map/all_to_all | solution.py:1404
  168.6 4.9 %collective-permute-start = (bf16[2304,512]{1,0:T(8,128)(2,1)}, bf16[2304,512]{1,0:T(8,128)(2,1)}, u32[]{:S(2)}, u32[]{:S(2)}) collective-permute-start(bf16[2304,512]{1,0:T(8,128)(2,1)} %get-tuple-element.119), channel_id=1, source_target_pairs={{0,8},{8,0},{16,24},{24,16},{1,9},{9,1},{17,25},{25,17},{2,10},{10... | collective-permute-start | bytes 7077896 | tf_op jit(solution)/shard_map/ppermute | solution.py:1205
  173.5 1.7 copy-start.13
  181.0 17.1 %collective-permute-start.1 = (bf16[640,512]{1,0:T(8,128)(2,1)S(1)}, bf16[640,512]{1,0:T(8,128)(2,1)S(1)}, u32[]{:S(2)}, u32[]{:S(2)}) collective-permute-start(bf16[640,512]{1,0:T(8,128)(2,1)S(1)} %get-tuple-element.122), channel_id=1, source_target_pairs={{0,16},{8,24},{16,0},{24,8},{1,17},{9,25},{17,1},{25,9},{2,18},{10... | collective-permute-start | bytes 1966088 | tf_op jit(solution)/shard_map/ppermute | solution.py:1205
  182.4 14.4 %collective-permute-start.2 = (bf16[512,512]{1,0:T(8,128)(2,1)S(1)}, bf16[512,512]{1,0:T(8,128)(2,1)S(1)}, u32[]{:S(2)}, u32[]{:S(2)}) collective-permute-start(bf16[512,512]{1,0:T(8,128)(2,1)S(1)} %get-tuple-element.123), channel_id=1, source_target_pairs={{0,1},{1,0},{2,3},{3,2},{4,5},{5,4},{6,7},{7,6},{8,9},{9,8},{10,11... | collective-permute-start | bytes 1572872 | tf_op jit(solution)/shard_map/ppermute | solution.py:1205
  199.6 6.4 %copy-start.48 = (f32[1,512]{1,0:T(1,128)S(1)}, f32[1,512]{1,0:T(1,128)}, u32[]{:S(2)}) copy-start(f32[1,512]{1,0:T(1,128)} %get-tuple-element.128) | copy-start | bytes 6148
  199.6 6.4 %copy-start.49 = (f32[1,512]{1,0:T(1,128)S(1)}, f32[1,512]{1,0:T(1,128)}, u32[]{:S(2)}) copy-start(f32[1,512]{1,0:T(1,128)} %get-tuple-element.127) | copy-start | bytes 6148
  199.6 52.6 %all-to-all-start.4 = ((bf16[8,240,512]{2,1,0:T(8,128)(2,1)}), bf16[8,240,512]{2,1,0:T(8,128)(2,1)S(1)}, u32[]{:S(2)}, u32[]{:S(2)}) async-start(bf16[8,240,512]{2,1,0:T(8,128)(2,1)} %bitcast.88), calls=%async_computation.4 | async-start | bytes 3932160 | tf_op jit(solution)/shard_map/all_to_all | solution.py:1404
  222.1 19.6 %copy-start.10 = (bf16[640,512]{1,0:T(8,128)(2,1)S(1)}, bf16[640,512]{1,0:T(8,128)(2,1)}, u32[]{:S(2)}) copy-start(bf16[640,512]{1,0:T(8,128)(2,1)} %copy-done.9) | copy-start | bytes 1966084
  222.1 19.6 %copy-start.12 = (bf16[640,512]{1,0:T(8,128)(2,1)S(1)}, bf16[640,512]{1,0:T(8,128)(2,1)}, u32[]{:S(2)}) copy-start(bf16[640,512]{1,0:T(8,128)(2,1)} %copy-done.11) | copy-start | bytes 1966084
  222.1 2.7 collective-permute-start.3
  229.3 12.3 %collective-permute-start.4 = (bf16[256,512]{1,0:T(8,128)(2,1)}, bf16[256,512]{1,0:T(8,128)(2,1)}, u32[]{:S(2)}, u32[]{:S(2)}) collective-permute-start(bf16[256,512]{1,0:T(8,128)(2,1)} %get-tuple-element.133), channel_id=1, source_target_pairs={{0,16},{8,24},{16,0},{24,8},{1,17},{9,25},{17,1},{25,9},{2,18},{10... | collective-permute-start | bytes 786440 | tf_op jit(solution)/shard_map/ppermute | solution.py:1205
  230.8 10.8 %collective-permute-start.5 = (bf16[192,512]{1,0:T(8,128)(2,1)}, bf16[192,512]{1,0:T(8,128)(2,1)}, u32[]{:S(2)}, u32[]{:S(2)}) collective-permute-start(bf16[192,512]{1,0:T(8,128)(2,1)} %copy-done.36), channel_id=1, source_target_pairs={{0,1},{1,0},{2,3},{3,2},{4,5},{5,4},{6,7},{7,6},{8,9},{9,8},{10,11... | collective-permute-start | bytes 589832 | tf_op jit(solution)/shard_map/ppermute | solution.py:1205
  248.2 3.1 copy-start.27
  248.2 3.1 copy-start.29
  248.3 12.7 %collective-permute-start.6 = (bf16[448,512]{1,0:T(8,128)(2,1)}, bf16[448,512]{1,0:T(8,128)(2,1)S(1)}, u32[]{:S(2)}, u32[]{:S(2)}) collective-permute-start(bf16[448,512]{1,0:T(8,128)(2,1)} %get-tuple-element.138), channel_id=1, source_target_pairs={{0,1},{1,0},{2,3},{3,2},{4,5},{5,4},{6,7},{7,6},{8,9},{9,8},{10,11... | collective-permute-start | bytes 1376264 | tf_op jit(solution)/shard_map/ppermute | solution.py:1205
  248.3 10.6 %collective-permute-start.7 = (bf16[352,512]{1,0:T(8,128)(2,1)}, bf16[352,512]{1,0:T(8,128)(2,1)S(1)}, u32[]{:S(2)}, u32[]{:S(2)}) collective-permute-start(bf16[352,512]{1,0:T(8,128)(2,1)} %get-tuple-element.140), channel_id=1, source_target_pairs={{0,16},{8,24},{16,0},{24,8},{1,17},{9,25},{17,1},{25,9},{2,18},{10... | collective-permute-start | bytes 1081352 | tf_op jit(solution)/shard_map/ppermute | solution.py:1205
  264.8 7.8 %copy-start.38 = (bf16[8,6,8,512]{3,2,0,1:T(8,128)(2,1)S(1)}, bf16[8,6,8,512]{3,2,0,1:T(8,128)(2,1)}, u32[]{:S(2)}) copy-start(bf16[8,6,8,512]{3,2,0,1:T(8,128)(2,1)} %copy.54) | copy-start | bytes 1179652
  264.8 7.8 %copy-start.46 = (bf16[512,64]{0,1:T(8,128)(2,1)S(1)}, bf16[512,64]{0,1:T(8,128)(2,1)}, u32[]{:S(2)}) copy-start(bf16[512,64]{0,1:T(8,128)(2,1)} %param.22) | copy-start | bytes 196612
  266.7 7.1 %copy-start.47 = (bf16[512]{0:T(512)(128)(2,1)S(1)}, bf16[512]{0:T(512)(128)(2,1)}, u32[]{:S(2)}) copy-start(bf16[512]{0:T(512)(128)(2,1)} %param.19) | copy-start | bytes 3076
  271.6 2.9 copy-start.32
  271.6 2.9 copy-start.41
  273.6 12.9 %copy-start.18 = (bf16[400,512]{1,0:T(8,128)(2,1)S(1)}, bf16[400,512]{1,0:T(8,128)(2,1)}, u32[]{:S(2)}) copy-start(bf16[400,512]{1,0:T(8,128)(2,1)} %copy-done.17) | copy-start | bytes 1228804
  274.5 13.9 %collective-permute-start.10 = (f32[65,512]{1,0:T(8,128)}, f32[65,512]{1,0:T(8,128)S(1)}, u32[]{:S(2)}, u32[]{:S(2)}) collective-permute-start(f32[65,512]{1,0:T(8,128)} %pad_maximum_fusion.2), channel_id=1, source_target_pairs={{0,8},{8,0},{16,24},{24,16},{1,9},{9,1},{17,25},{25,17},{2,10},{10... | collective-permute-start | bytes 399368 | tf_op jit(solution)/shard_map/ppermute | solution.py:1205
  274.5 12.0 %collective-permute-start.8 = (bf16[400,512]{1,0:T(8,128)(2,1)S(1)}, bf16[400,512]{1,0:T(8,128)(2,1)}, u32[]{:S(2)}, u32[]{:S(2)}) collective-permute-start(bf16[400,512]{1,0:T(8,128)(2,1)S(1)} %get-tuple-element.144), channel_id=1, source_target_pairs={{0,2},{1,3},{2,0},{3,1},{4,6},{5,7},{6,4},{7,5},{8,10},{9,11},{10,... | collective-permute-start | bytes 1228808 | tf_op jit(solution)/shard_map/ppermute | solution.py:1205
  274.8 13.6 %copy-start.44 = (f32[64,512]{1,0:T(8,128)S(1)}, f32[64,512]{1,0:T(8,128)}, u32[]{:S(2)}) copy-start(f32[64,512]{1,0:T(8,128)} %copy-done.43) | copy-start | bytes 393220
  288.4 23.1 %collective-permute-start.9 = (bf16[400,512]{1,0:T(8,128)(2,1)}, bf16[400,512]{1,0:T(8,128)(2,1)}, u32[]{:S(2)}, u32[]{:S(2)}) collective-permute-start(bf16[400,512]{1,0:T(8,128)(2,1)} %add_convert_fusion.1), channel_id=1, source_target_pairs={{0,4},{1,5},{2,6},{3,7},{4,0},{5,1},{6,2},{7,3},{8,12},{9,13},{10,... | collective-permute-start | bytes 1228808 | tf_op jit(solution)/shard_map/ppermute | solution.py:1205
  289.1 20.8 %collective-permute-start.11 = (f32[65,512]{1,0:T(8,128)}, f32[65,512]{1,0:T(8,128)}, u32[]{:S(2)}, u32[]{:S(2)}) collective-permute-start(f32[65,512]{1,0:T(8,128)} %fusion.9), channel_id=1, source_target_pairs={{0,16},{8,24},{16,0},{24,8},{1,17},{9,25},{17,1},{25,9},{2,18},{10... | collective-permute-start | bytes 399368 | tf_op jit(solution)/shard_map/ppermute | solution.py:1205
  290.5 7.7 %copy-start.2 = (bf16[8,256,512]{2,1,0:T(8,128)(2,1)S(1)}, bf16[8,256,512]{2,1,0:T(8,128)(2,1)}, u32[]{:S(2)}) copy-start(bf16[8,256,512]{2,1,0:T(8,128)(2,1)} %copy-done.1) | copy-start | bytes 6291460
  290.5 7.7 %copy-start.6 = (bf16[2048,512]{1,0:T(8,128)(2,1)S(1)}, bf16[2048,512]{1,0:T(8,128)(2,1)}, u32[]{:S(2)}) copy-start(bf16[2048,512]{1,0:T(8,128)(2,1)} %get-tuple-element.89.x_ref.refs_2_) | copy-start | bytes 6291460
  290.5 7.8 %copy-start.33 = (f32[512]{0:T(512)S(1)}, f32[512]{0:T(512)}, u32[]{:S(2)}) copy-start(f32[512]{0:T(512)} %convert_element_type.52) | copy-start | bytes 6148
  290.5 7.8 %copy-start.34 = (s32[64]{0:T(128)S(1)}, s32[64]{0:T(128)}, u32[]{:S(2)}) copy-start(s32[64]{0:T(128)} %get-tuple-element.96.refs_1_.place_ref) | copy-start | bytes 772
  312.7 10.8 %collective-permute-start.12 = (bf16[400,512]{1,0:T(8,128)(2,1)S(1)}, bf16[400,512]{1,0:T(8,128)(2,1)S(1)}, u32[]{:S(2)}, u32[]{:S(2)}) collective-permute-start(bf16[400,512]{1,0:T(8,128)(2,1)S(1)} %add_convert_fusion.refs_0_), channel_id=1, source_target_pairs={{0,2},{1,3},{2,0},{3,1},{4,6},{5,7},{6,4},{7,5},{8,10},{9,11},{10,... | collective-permute-start | bytes 1228808 | tf_op jit(solution)/shard_map/ppermute | solution.py:1205
  324.0 10.9 %collective-permute-start.13 = (bf16[448,512]{1,0:T(8,128)(2,1)S(1)}, bf16[448,512]{1,0:T(8,128)(2,1)S(1)}, u32[]{:S(2)}, u32[]{:S(2)}) collective-permute-start(bf16[448,512]{1,0:T(8,128)(2,1)S(1)} %get-tuple-element.145.refs_0_), channel_id=1, source_target_pairs={{0,1},{1,0},{2,3},{3,2},{4,5},{5,4},{6,7},{7,6},{8,9},{9,8},{10,11... | collective-permute-start | bytes 1376264 | tf_op jit(solution)/shard_map/ppermute | solution.py:1205
  324.9 8.1 %collective-permute-start.14 = (bf16[352,512]{1,0:T(8,128)(2,1)S(1)}, bf16[352,512]{1,0:T(8,128)(2,1)S(1)}, u32[]{:S(2)}, u32[]{:S(2)}) collective-permute-start(bf16[352,512]{1,0:T(8,128)(2,1)S(1)} %get-tuple-element.146.refs_2_), channel_id=1, source_target_pairs={{0,16},{8,24},{16,0},{24,8},{1,17},{9,25},{17,1},{25,9},{2,18},{10... | collective-permute-start | bytes 1081352 | tf_op jit(solution)/shard_map/ppermute | solution.py:1205
  336.5 19.8 %collective-permute-start.15 = (bf16[896,512]{1,0:T(8,128)(2,1)S(1)}, bf16[896,512]{1,0:T(8,128)(2,1)S(1)}, u32[]{:S(2)}, u32[]{:S(2)}) collective-permute-start(bf16[896,512]{1,0:T(8,128)(2,1)S(1)} %get-tuple-element.147.refs_0_), channel_id=1, source_target_pairs={{0,16},{8,24},{16,0},{24,8},{1,17},{9,25},{17,1},{25,9},{2,18},{10... | collective-permute-start | bytes 2752520 | tf_op jit(solution)/shard_map/ppermute | solution.py:1205
  338.0 20.3 %copy-start.42 = (f32[65,512]{1,0:T(8,128)S(1)}, f32[65,512]{1,0:T(8,128)}, u32[]{:S(2)}) copy-start(f32[65,512]{1,0:T(8,128)} %add.52.refs_2_) | copy-start | bytes 399364
  338.0 15.4 %collective-permute-start.16 = (bf16[704,512]{1,0:T(8,128)(2,1)S(1)}, bf16[704,512]{1,0:T(8,128)(2,1)S(1)}, u32[]{:S(2)}, u32[]{:S(2)}) collective-permute-start(bf16[704,512]{1,0:T(8,128)(2,1)S(1)} %get-tuple-element.148.refs_2_), channel_id=1, source_target_pairs={{0,1},{1,0},{2,3},{3,2},{4,5},{5,4},{6,7},{7,6},{8,9},{9,8},{10,11... | collective-permute-start | bytes 2162696 | tf_op jit(solution)/shard_map/ppermute | solution.py:1205
  358.1 5.9 %collective-permute-start.17 = (bf16[3200,512]{1,0:T(8,128)(2,1)S(1)}, bf16[3200,512]{1,0:T(8,128)(2,1)S(1)}, u32[]{:S(2)}, u32[]{:S(2)}) collective-permute-start(bf16[3200,512]{1,0:T(8,128)(2,1)S(1)} %double_step.5.values_ref), channel_id=1, source_target_pairs={{0,8},{8,0},{16,24},{24,16},{1,9},{9,1},{17,25},{25,17},{2,10},{10... | collective-permute-start | bytes 9830408 | tf_op jit(solution)/shard_map/ppermute | solution.py:1205
  (25 other events, 28.3 us)

commit v3 on v2

--- a/solution.py
+++ b/solution.py
@@ -18,7 +18,7 @@
 TILE = 256
 HALF = 256
 PER_HALF = 4
-VMEM_LIMIT = 58 * 1024 * 1024
+VMEM_LIMIT = 62 * 1024 * 1024
 
 F32 = jnp.float32
 BF16 = jnp.bfloat16
@@ -267,8 +267,9 @@
 def digest(x_a, x_b, sel_a, sel_b, gain_row, average, w_sort_t, settings):
     npl, seqs_a, seqs_b, devices, capacity, _, _, sizes, _, _ = settings
     width = x_a.shape[1]
-    tiles_a = x_a.shape[0] // TILE
-    tiles_b = x_b.shape[0] // TILE
+    tile = 2 * TILE if x_a.shape[0] % (2 * TILE) == 0 and x_b.shape[0] % (2 * TILE) == 0 else TILE
+    tiles_a = x_a.shape[0] // tile
+    tiles_b = x_b.shape[0] // tile
     rows = x_a.shape[0] + x_b.shape[0]
     picks = average.shape[0]
     height = -(-picks // 8) * 8 + 8
@@ -280,13 +281,13 @@
         in_specs=[
             SMEM,
             SMEM,
-            pl.BlockSpec((TILE, width), lambda i: (jnp.minimum(i, tiles_a - 1), 0)),
-            pl.BlockSpec((TILE, width), lambda i: (jnp.maximum(i - tiles_a, 0), 0)),
+            pl.BlockSpec((tile, width), lambda i: (jnp.minimum(i, tiles_a - 1), 0)),
+            pl.BlockSpec((tile, width), lambda i: (jnp.maximum(i - tiles_a, 0), 0)),
             whole((1, width)),
             whole(average.shape),
             whole(w_sort_t.shape),
         ],
-        out_specs=[rows_of(TILE, width), whole((picks, width)), whole((devices, height, 128))]
+        out_specs=[rows_of(tile, width), whole((picks, width)), whole((devices, height, 128))]
         + [SMEM] * 5,
         out_shape=[
             jax.ShapeDtypeStruct((rows, width), BF16),
@@ -349,7 +350,7 @@
             pltpu.VMEM((devices * capacity * UNIT, width), BF16),
             pltpu.SemaphoreType.DMA((len(sizes) * devices,)),
         ],
-        compiler_params=limit(12),
+        compiler_params=limit(62),
         cost_estimate=cost(0, x.size * 6),
         name="pack",
     )(table, x)
@@ -470,30 +471,100 @@
     )(logits, picked)
 
 
-def sinkhorn_back_kernel(logits_ref, picked_ref, gw_ref, out_ref, kept):
+def exact(a, b, dims=NN):
+    return lax.dot_general(
+        a, b, dims, precision=lax.Precision.HIGHEST, preferred_element_type=F32
+    )
+
+
+def sort_back_kernel(
+    npl, seqs_a, lengths, tall, me_ref, perm_ref, logits_ref, picked_ref, units_ref, wsort_ref, gain_ref,
+    means_ref, arrived, token_ref, small_ref, spread_ref, kept, letters, sems,
+):
+    seqs, blocks, _ = logits_ref.shape
+    devices = blocks // npl
+    picks = means_ref.shape[0]
+    extra = letters.shape[1]
+    height = arrived.shape[0] // devices
+    copies = []
+    for d in range(devices):
+        source = arrived.at[pl.ds(d * height + tall, extra), pl.ds(0, 128)]
+        copies.append(pltpu.make_async_copy(source, letters.at[d], sems.at[d]))
+    for copy in copies:
+        copy.start()
     state = logits_ref[...]
     for step in range(SINK_ITERS):
         state = state - log_sum(state, 2)
         kept[2 * step] = jnp.exp(state)
         state = state - log_sum(state, 1)
         kept[2 * step + 1] = jnp.exp(state)
-    count = state.shape[1]
-    grad = count * picked_ref[...] * gw_ref[...] * jnp.exp(state)
+    for copy in copies:
+        copy.wait()
+    rows = seqs * blocks
+    line = lax.broadcasted_iota(jnp.int32, (rows, 128), 0)
+    lane = lax.broadcasted_iota(jnp.int32, (rows, 128), 1)
+    own_lane = line // blocks * npl + line % npl
+    device = (line // npl) % devices
+    table = jnp.zeros((rows, 128), F32)
+    for d in range(devices):
+        table = jnp.where(device == d, letters[d, 0:1, :].astype(F32), table)
+    gw = jnp.sum(jnp.where(lane == own_lane, table, 0.0), axis=1, keepdims=True)
+    grad = blocks * picked_ref[...] * gw.reshape(seqs, blocks, 1) * kept[2 * SINK_ITERS - 1]
     for step in reversed(range(SINK_ITERS)):
         grad = grad - kept[2 * step + 1] * jnp.sum(grad, axis=1, keepdims=True)
         grad = grad - kept[2 * step] * jnp.sum(grad, axis=2, keepdims=True)
-    out_ref[...] = grad
-
-
-def sinkhorn_back(logits, picked, gw):
+    grad = (grad * (1.0 / SOFTMAX_HEAT)).reshape(rows, blocks)
+    units = units_ref[...].astype(F32)
+    small_ref[:blocks, :] = exact(grad, units, TN)
+    g_unit = exact(grad, wsort_ref[...].astype(F32))
+    both = g_unit * units
+    both = both - units * units * jnp.mean(both, axis=-1, keepdims=True)
+    row = jnp.sum(both, axis=0, keepdims=True) / gain_ref[...]
+    first = lax.broadcasted_iota(jnp.int32, (small_ref.shape[0] - blocks, units.shape[1]), 0) == 0
+    small_ref[blocks:, :] = jnp.where(first, row, 0.0)
+    line = lax.broadcasted_iota(jnp.int32, (picks, rows), 0)
+    lane = lax.broadcasted_iota(jnp.int32, (picks, rows), 1)
+    mine = lane == line // npl * blocks + me_ref[0] * npl + line % npl
+    g_own = exact(jnp.where(mine, 1.0, 0.0), g_unit)
+    summary = means_ref[...] * gain_ref[...]
+    rs = inverse_norm(summary)
+    g_summary = rs * (
+        g_own - summary * (rs * rs) * jnp.mean(g_own * summary, axis=-1, keepdims=True)
+    )
+    count_a = seqs_a * npl
+    places = spread_ref.shape[0]
+    line = lax.broadcasted_iota(jnp.int32, (places, picks), 0)
+    lane = lax.broadcasted_iota(jnp.int32, (places, picks), 1)
+    unit = jnp.zeros((places, picks), jnp.int32)
+    for pos in range(places):
+        unit = jnp.where(line == pos, perm_ref[pos], unit)
+    block = jnp.where(unit < 2 * count_a, unit // 2, unit - count_a)
+    share = jnp.where(lane < count_a, 1.0 / lengths[0], 1.0 / lengths[1])
+    spread_ref[...] = exact(jnp.where(lane == block, share, 0.0), g_summary)
+
+
+def sort_back(
+    me, perm, logits, picked, units, w_sort_t, gain, means, arrived, npl, seqs_a, lengths, tall, extra, token
+):
+    seqs, blocks, _ = logits.shape
+    width = means.shape[1]
     return pl.pallas_call(
-        sinkhorn_back_kernel,
-        out_shape=jax.ShapeDtypeStruct(logits.shape, F32),
-        scratch_shapes=[pltpu.VMEM((2 * SINK_ITERS,) + logits.shape, F32)],
-        compiler_params=pltpu.CompilerParams(vmem_limit_bytes=VMEM_LIMIT),
+        functools.partial(sort_back_kernel, npl, seqs_a, lengths, tall),
+        in_specs=[SMEM, SMEM] + [VMEM] * 6 + [ANY, ANY],
+        out_specs=[VMEM, VMEM],
+        out_shape=[
+            jax.ShapeDtypeStruct((blocks + 8, width), F32),
+            jax.ShapeDtypeStruct((perm.shape[0], width), F32),
+        ],
+        scratch_shapes=[
+            pltpu.VMEM((2 * SINK_ITERS,) + logits.shape, F32),
+            pltpu.VMEM((blocks // npl, extra, 128), BF16),
+            pltpu.SemaphoreType.DMA((blocks // npl,)),
+        ],
+        compiler_params=limit(24),
         cost_estimate=cost(logits.size * 200, logits.size * 32),
-        name="sinkhorn_back",
-    )(logits, picked, gw)
+        name="sort_back",
+    )(me, perm, logits, picked, units, w_sort_t, gain, means, arrived, token)
 
 
 def head_masks(rows):
@@ -554,7 +625,6 @@
         keep_hbm, give_hbm, gain_ref = take(3)
     else:
         up_hbm, down_hbm, gain_ref = take(3)
-    recv_refs = take(recvs)
     x_ref, cot_ref, proj_ref, wrow_ref, wqkv_ref, wout_ref, wup_ref, wdown_ref = take(8)
     out_ref, gmid_ref, gatt_ref, prob_ref, farx_ref, farkv_ref, attended = take(7)
     one_ref, two_ref = take(2)
@@ -567,7 +637,21 @@
     ff = wup_ref.shape[1]
     base = first_group
     here = pl.ds(first_group * GROUP, rows)
-    got_recv = [move.start(a, b) for a, b in zip(recv_hbm, recv_refs)]
+    rows_one = recv_hbm[0].shape[0]
+    far_sem = sems.at[sems.shape[0] - 1]
+    for u in range(rows // UNIT):
+        row = far_ref[2 * base + u]
+        dst = farx_ref.at[pl.ds(u * UNIT, UNIT)]
+
+        def bring(ref, row, dst=dst):
+            src = ref.at[pl.ds(pl.multiple_of(row, 16), UNIT)]
+            pltpu.make_async_copy(src, dst, far_sem).start()
+
+        if recvs == 1:
+            bring(recv_hbm[0], row)
+        else:
+            pl.when(row < rows_one)(lambda row=row, bring=bring: bring(recv_hbm[0], row))
+            pl.when(row >= rows_one)(lambda row=row, bring=bring: bring(recv_hbm[1], row - rows_one))
     got_wqkv = move.start(wqkv_hbm, wqkv_ref)
     got_proj = move.start(proj_hbm.at[here], proj_ref)
     got_wrow = move.start(wrow_hbm.at[here], wrow_ref)
@@ -582,25 +666,7 @@
             move.start(prior_refs[1], down_prior),
         ]
 
-    for copy in got_recv:
-        copy.wait()
-    rows_one = recv_refs[0].shape[0]
-    for u in range(rows // UNIT):
-        row = far_ref[2 * base + u]
-        dst = slice(u * UNIT, (u + 1) * UNIT)
-        if recvs == 1:
-            farx_ref[dst, :] = recv_refs[0][pl.ds(pl.multiple_of(row, UNIT), UNIT), :]
-        else:
-
-            @pl.when(row < rows_one)
-            def _():
-                farx_ref[dst, :] = recv_refs[0][pl.ds(pl.multiple_of(row, 16), UNIT), :]
-
-            @pl.when(row >= rows_one)
-            def _():
-                src = pl.ds(pl.multiple_of(row - rows_one, 16), UNIT)
-                farx_ref[dst, :] = recv_refs[1][src, :]
-
+    pltpu.make_async_copy(farx_ref, farx_ref, far_sem).wait()
     move.store(farx_ref, farx_hbm.at[here])
     far = farx_ref[...].astype(F32)
     far = (far * inverse_norm(far) * gain1_ref[...]).astype(BF16)
@@ -672,30 +738,51 @@
 
     edge = ff // 2
 
+    pending = []
+
+    def send(ref, half, lines):
+        sem = sems.at[move.used]
+        move.used += 1
+        for which, hbm in ((half, keep_hbm), (1 - half, give_hbm)):
+            copy = pltpu.make_async_copy(ref.at[lines], hbm.at[lines], sem)
+            pl.when(core_ref[0] == which)(copy.start)
+        pending.append(copy)
+
     def put_up(c, value):
         lanes = slice(c, c + width)
         if not final:
             one_ref[:, lanes] = value.astype(BF16)
+            at = (slice(None), pl.ds(c, width))
+            move.store(one_ref.at[at], up_hbm.at[at])
             return
         ref, at = (one_ref, c) if c < edge else (two_ref, c - edge)
         ref[at : at + width, :] = total(value, up_prior if prior else None, lanes).astype(BF16)
+        send(ref, 0 if c < edge else 1, pl.ds(at, width))
 
     def put_down(c, value):
         lanes = slice(c, c + width)
         if not final:
             two_ref[:, lanes] = value.astype(BF16)
+            at = (slice(None), pl.ds(c, width))
+            move.store(two_ref.at[at], down_hbm.at[at])
             return
         ref, at = (one_ref, c) if c < edge else (two_ref, c - edge)
         at += edge + width // 2
         ref[at : at + width, :] = total(value, down_prior if prior else None, lanes).T.astype(BF16)
+        send(ref, 0 if c < edge else 1, pl.ds(at, width))
 
     def put_out(value):
         if not final:
             one_ref[:, ff:] = value.astype(BF16)
+            at = (slice(None), pl.ds(ff, width))
+            move.store(one_ref.at[at], up_hbm.at[at])
             return
         value = total(value, up_prior if prior else None, slice(ff, ff + width)).astype(BF16)
-        one_ref[edge : edge + width // 2, :] = value[: width // 2]
-        two_ref[edge : edge + width // 2, :] = value[width // 2 :]
+        lines = slice(edge, edge + width // 2)
+        one_ref[lines, :] = value[: width // 2]
+        two_ref[lines, :] = value[width // 2 :]
+        send(one_ref, 0, pl.ds(edge, width // 2))
+        send(two_ref, 1, pl.ds(edge, width // 2))
 
     result = middle
     back = jnp.zeros((rows, width), F32)
@@ -725,26 +812,10 @@
     gmid_ref[...] = branch
     move.store(gmid_ref, gmid_hbm.at[here])
     put_out(dot(att.T, branch))
-    if not final:
-        move.store(one_ref, up_hbm)
-        move.store(two_ref, down_hbm)
     gatt_ref[...] = dot(branch, wout_ref[...], NT).astype(BF16)
     move.store(gatt_ref, gatt_hbm.at[here])
-    if final:
-        first, second_copy = move.used, move.used + 1
-        for which, (mine, other) in enumerate(((one_ref, two_ref), (two_ref, one_ref))):
-
-            @pl.when(core_ref[0] == which)
-            def _():
-                copies = [
-                    pltpu.make_async_copy(mine, keep_hbm, sems.at[first]),
-                    pltpu.make_async_copy(other, give_hbm, sems.at[second_copy]),
-                ]
-                for copy in copies:
-                    copy.start()
-                for copy in copies:
-                    copy.wait()
-
+    for copy in pending:
+        copy.wait()
     move.finish()
 
 
@@ -766,8 +837,7 @@
     in_specs = [SMEM] * 3 + [ANY] * (len(recv) + 4) + [VMEM] * 3 + [ANY] * 5
     operands = [far_rows, kinds, core, *recv, x, cot, proj, wrow, mask, gain1, gain2]
     operands += [w_qkv, w_out, w_up, w_down, token]
-    scratch = [pltpu.VMEM(r.shape, BF16) for r in recv]
-    scratch += [
+    scratch = [
         pltpu.VMEM((count, width), BF16),
         pltpu.VMEM((count, width), BF16),
         pltpu.VMEM((count, 3 * width), BF16),
@@ -786,7 +856,7 @@
         aliases = {len(operands) + i: i for i in range(6)}
         operands += list(streams)
         scratch += [pltpu.VMEM((width, ff + width), BF16), pltpu.VMEM((width, ff), BF16)]
-    scratch += [pltpu.SemaphoreType.DMA((24,))]
+    scratch += [pltpu.SemaphoreType.DMA((40,))]
     out = pl.pallas_call(
         functools.partial(
             forward_kernel, first_group, groups, len(recv), prior is not None, final
@@ -1012,87 +1082,108 @@
 
 
 def qkv_kernel(
-    extra, core_ref, x_ref, farx_ref, dproj_ref, dfar_ref, gain1_ref, wqkv_ref, gains_ref, token_ref,
-    gn_ref, keep_ref, give_ref, acc, gain_acc,
+    extra, core_ref, x_hbm, farx_hbm, dproj_hbm, dfar_hbm, gain1_ref, wqkv_hbm, gains_ref, token_ref,
+    gn_hbm, keep_ref, give_ref, x_ref, farx_ref, dproj_ref, dfar_ref, wqkv_ref, gn_ref, near_t, far_t, sems,
 ):
-    step = pl.program_id(0)
-    steps = pl.num_programs(0)
-    width = x_ref.shape[1]
-
-    @pl.when(step == 0)
+    move = Mover(sems)
+    rows, width = x_ref.shape
+    wide = wqkv_ref.shape[1]
+    size = min(512, rows)
+    got_w = move.start(wqkv_hbm, wqkv_ref)
+    loads = []
+    for low in range(0, rows, size):
+        at = pl.ds(low, size)
+        loads.append(
+            [
+                move.start(hbm.at[at], ref.at[at])
+                for hbm, ref in (
+                    (x_hbm, x_ref),
+                    (dproj_hbm, dproj_ref),
+                    (farx_hbm, farx_ref),
+                    (dfar_hbm, dfar_ref),
+                )
+            ]
+        )
+    got_w.wait()
+    gain = jnp.zeros((1, width), F32)
+    for low, copies in zip(range(0, rows, size), loads):
+        at = slice(low, low + size)
+        for copy in copies:
+            copy.wait()
+        x = x_ref[at, :].astype(F32)
+        scaled = x * inverse_norm(x)
+        near_t[:, at] = (scaled * gain1_ref[...]).astype(BF16).T
+        far = farx_ref[at, :].astype(F32)
+        far_t[:, at] = (far * inverse_norm(far) * gain1_ref[...]).astype(BF16).T
+        grad = dot(dproj_ref[at, :], wqkv_ref[...], NT)
+        gn_ref[at, :] = grad.astype(BF16)
+        move.store(gn_ref.at[pl.ds(low, size)], gn_hbm.at[pl.ds(low, size)])
+        gain = gain + jnp.sum(grad * scaled, axis=0, keepdims=True)
+    grads = []
+    for c in range(0, wide, width):
+        value = dot(near_t[...], dproj_ref[:, c : c + width])
+        if c:
+            value = value + dot(far_t[...], dfar_ref[:, c - width : c])
+        grads.append(value)
+
+    line = lax.broadcasted_iota(jnp.int32, (extra, width), 0)
+    small = jnp.where(line == 0, gain + gains_ref[0:1, :], 0.0)
+    small = jnp.where(line == 1, gains_ref[1:2, :], small)
+    total = wide + extra
+    half = total // 2
+
+    def write(ref, which):
+        at = which * half
+        while at < (which + 1) * half:
+            block, line = divmod(at, width)
+            if at >= wide:
+                count = extra
+                value = small
+            else:
+                count = min(width - line, (which + 1) * half - at)
+                value = grads[block][line : line + count]
+            ref[at - which * half : at - which * half + count, :] = value.astype(BF16)
+            at += count
+
+    @pl.when(core_ref[0] == 0)
     def _():
-        acc[...] = jnp.zeros_like(acc)
-        gain_acc[...] = jnp.zeros_like(gain_acc)
-
-    x = x_ref[...].astype(F32)
-    scaled = x * inverse_norm(x)
-    far = farx_ref[...].astype(F32)
-    far = (far * inverse_norm(far) * gain1_ref[...]).astype(BF16)
-    near = (scaled * gain1_ref[...]).astype(BF16)
-    acc[...] += dot(near.T, dproj_ref[...])
-    acc[:, width:] += dot(far.T, dfar_ref[...])
-    grad = dot(dproj_ref[...], wqkv_ref[...], NT)
-    gn_ref[...] = grad.astype(BF16)
-    gain_acc[...] += jnp.sum(grad * scaled, axis=0, keepdims=True)
-
-    @pl.when(step == steps - 1)
+        write(keep_ref, 0)
+        write(give_ref, 1)
+
+    @pl.when(core_ref[0] == 1)
     def _():
-        line = lax.broadcasted_iota(jnp.int32, (extra, width), 0)
-        small = jnp.where(line == 0, gain_acc[...] + gains_ref[0:1, :], 0.0)
-        small = jnp.where(line == 1, gains_ref[1:2, :], small)
-        total = acc.shape[1] + extra
-        half = total // 2
-
-        def write(ref, which):
-            at = which * half
-            while at < (which + 1) * half:
-                block, line = divmod(at, width)
-                if at >= acc.shape[1]:
-                    count = extra
-                    value = small
-                else:
-                    count = min(width - line, (which + 1) * half - at)
-                    value = acc[line : line + count, block * width : (block + 1) * width]
-                ref[at - which * half : at - which * half + count, :] = value.astype(BF16)
-                at += count
-
-        @pl.when(core_ref[0] == 0)
-        def _():
-            write(keep_ref, 0)
-            write(give_ref, 1)
-
-        @pl.when(core_ref[0] == 1)
-        def _():
-            write(keep_ref, 1)
-            write(give_ref, 0)
+        write(keep_ref, 1)
+        write(give_ref, 0)
+
+    move.finish()
 
 
 def qkv_grads(core, x, farx, dproj, dfar, gain1, w_qkv, gains, extra, token):
     rows, width = x.shape
     wide = w_qkv.shape[1]
     half = (wide + extra) // 2
+    tall = lambda size: pltpu.VMEM((rows, size), BF16)
     return pl.pallas_call(
         functools.partial(qkv_kernel, extra),
-        grid=(rows // TILE,),
-        in_specs=[
-            SMEM,
-            rows_of(TILE, width),
-            rows_of(TILE, width),
-            rows_of(TILE, wide),
-            rows_of(TILE, 2 * width),
-            whole((1, width)),
-            whole(w_qkv.shape),
-            whole(gains.shape),
-            ANY,
-        ],
-        out_specs=[rows_of(TILE, width), whole((half, width)), whole((half, width))],
+        in_specs=[SMEM] + [ANY] * 4 + [VMEM, ANY, VMEM, ANY],
+        out_specs=[ANY, VMEM, VMEM],
         out_shape=[
             jax.ShapeDtypeStruct((rows, width), BF16),
             jax.ShapeDtypeStruct((half, width), BF16),
             jax.ShapeDtypeStruct((half, width), BF16),
         ],
-        scratch_shapes=[pltpu.VMEM((width, wide), F32), pltpu.VMEM((1, width), F32)],
-        compiler_params=params(),
+        scratch_shapes=[
+            tall(width),
+            tall(width),
+            tall(wide),
+            tall(2 * width),
+            pltpu.VMEM(w_qkv.shape, BF16),
+            tall(width),
+            pltpu.VMEM((width, rows), BF16),
+            pltpu.VMEM((width, rows), BF16),
+            pltpu.SemaphoreType.DMA((5 * (rows // min(512, rows)) + 1,)),
+        ],
+        compiler_params=limit(62),
         cost_estimate=cost(10e9, 25e6),
         name="qkv_grads",
     )(core, x, farx, dproj, dfar, gain1, w_qkv, gains, token)
@@ -1259,19 +1350,22 @@
 
 def halve_kernel(ranges, sources, bits_ref, *refs):
     count = 2 * (1 + max(r[4] for r in ranges))
+    sems = refs[-1]
     outs = refs[2 * sources + 1 : 2 * sources + 1 + count]
-    held = refs[2 * sources + 1 + count : -1]
-    fetch(refs[: 2 * sources], held, refs[-1])
+    held = refs[2 * sources + 1 + count : -2]
+    made = held[2 * sources :]
+    fetch(refs[: 2 * sources], held, refs[-2])
     refs = held
     for source, first, count, bit, out, there in ranges:
         own, came = refs[2 * source], refs[2 * source + 1]
         half = count // 2
         keep = pl.multiple_of(first + bits_ref[bit] * half, 16)
         give = pl.multiple_of(first + (1 - bits_ref[bit]) * half, 16)
-        for ref, line in ((outs[2 * out], keep), (outs[2 * out + 1], give)):
+        for ref, line in ((made[2 * out], keep), (made[2 * out + 1], give)):
             rows = pl.ds(line, half)
             total = own[rows, :].astype(F32) + came[rows, :].astype(F32)
             ref[there : there + half, :] = total.astype(BF16)
+    fetch(made, outs, sems)
 
 
 def halve_step(ranges, bits, pairs, token):
@@ -1282,12 +1376,12 @@
     flat = [v for pair in pairs for v in pair]
     out = pl.pallas_call(
         functools.partial(halve_kernel, ranges, len(pairs)),
-        in_specs=[SMEM] + [ANY] * len(flat) + [ANY],
-        out_specs=[VMEM] * len(shapes),
+        in_specs=[SMEM] + [HBM] * len(flat) + [ANY],
+        out_specs=[HBM] * len(shapes),
         out_shape=shapes,
-        scratch_shapes=[pltpu.VMEM(v.shape, BF16) for v in flat]
-        + [pltpu.SemaphoreType.DMA((len(flat),))],
-        compiler_params=limit(24),
+        scratch_shapes=[pltpu.VMEM(v.shape, BF16) for v in flat + shapes]
+        + [pltpu.SemaphoreType.DMA((len(flat),)), pltpu.SemaphoreType.DMA((len(shapes),))],
+        compiler_params=limit(62),
         cost_estimate=cost(0, 8 * sum(heights) * width),
         name="halve_step",
     )(jnp.stack([bit_of(*b) for b in bits]).astype(jnp.int32), *flat, token)
@@ -1563,8 +1657,7 @@
         core, xp, farx, dproj, dfar, gain1, w_qkv, gains, EXTRA, token
     )
     late_came = swap(late_give, "dp", 0)
-    part_late = 512
-    gw = arrived.reshape(devices, -1, width)[:, tall:, :picks]
+    part_late = 384
     if fast:
         late_rows = late_keep.shape[0]
         ranges_late = [(0, 0, part_late, 0, 0, 0), (0, part_late, late_rows - part_late, 1, 1, 0)]
@@ -1586,6 +1679,11 @@
             lx,
         )
         vx_came, vy_came = swap(gx, *AXIS_Y), swap(gy, *AXIS_X)
+    small, spread = sort_back(
+        me.reshape(1), perm, logits, picked, units_all.reshape(-1, width), w_sort_t, gain1, means,
+        arrived, npl, seqs_a, (len_a, len_b), tall, extra, vx if fast else arrived,
+    )
+    if fast:
         cuts = [nbx // 2, nlx // 2, nby // 2, nly // 2]
         ranges_three = [
             (0, 0, cuts[0], 0, 0, 0),
@@ -1594,34 +1692,11 @@
             (1, cuts[2], cuts[3], 0, 0, (cuts[0] + cuts[1] + cuts[2]) // 2),
         ]
         ((total, gz),) = halve_step(
-            ranges_three, [AXIS_Z0], [(vx, vx_came), (vy, vy_came)], arrived
+            ranges_three, [AXIS_Z0], [(vx, vx_came), (vy, vy_came)], spread
         )
-        gw = tie(gw, total)
-        total = add(total, swap(gz, *AXIS_Z0))
-    gw = by_sequence(gw[:, 0].astype(F32))
-    g_logits = sinkhorn_back(logits, picked, jnp.broadcast_to(gw[..., None], logits.shape)) * (
-        1.0 / SOFTMAX_HEAT
-    )
-    precise = lax.Precision.HIGHEST
-    flat_logits = g_logits.reshape(-1, blocks)
-    flat_units = units_all.reshape(-1, width).astype(F32)
-    g_sort = lax.dot_general(
-        flat_logits, flat_units, TN, precision=precise, preferred_element_type=F32
-    )
-    g_unit = lax.dot_general(
-        flat_logits, w_sort_t.astype(F32), NN, precision=precise, preferred_element_type=F32
-    )
-    g_own = own_rows(g_unit.reshape(g_logits.shape[:2] + (width,)))
-    g_summary = rs * (
-        g_own - summary * rs * rs * jnp.mean(g_own * summary, axis=-1, keepdims=True)
-    )
-    both = g_unit * flat_units
-    both = both - flat_units * flat_units * jnp.mean(both, axis=-1, keepdims=True)
-    small = jnp.concatenate([g_sort, jnp.sum(both, axis=0, keepdims=True) / gain1], axis=0)
-    spread = to_units(
-        jnp.concatenate([g_summary[:count_a] / len_a, g_summary[count_a:] / len_b], axis=0)
-    )
-    base = base_rows(xp, gmid, gn, jnp.take(spread, perm, axis=0), gain1)
+    base = base_rows(xp, gmid, gn, spread, gain1)
+    if fast:
+        total = add(total, tie(swap(gz, *AXIS_Z0), base))
 
     gx_a, gx_b = last(back_table, place, back, sizes, extra, sum(sizes), x, base, gain1, total_a)
     if fast:

time: 375 us -> 348 us (0.928)
  local copies, waits for them, and re-layouts: 34.7 us -> 19.5 us
  waiting for transfers between devices: 95.5 us -> 83.6 us
  other arithmetic: 15.3 us -> 10.2 us
  starting transfers between devices: 35.3 us -> 40.3 us
    ppermute x18, waiting for transfers between devices: 72.6 us -> 59.3 us  [swap(): return lax.ppermute(values, axis, [(i, i ^ 1 << bit) for i in range(size)])]
    unnamed x102 -> x80, local copies, waits for them, and re-layouts: 25.7 us -> 13.1 us
    pallas_call x4, Pallas kernels: 9.31 us -> 14.2 us  [halve_step(): pl.pallas_call(functools.partial(halve_kernel, ranges, len(pairs)), in_sp...]
    ppermute x18, starting transfers between devices: 14.5 us -> 19 us  [swap(): return lax.ppermute(values, axis, [(i, i ^ 1 << bit) for i in range(size)])]
  transfers between devices with their start and end apart: 22 -> 22, of which waited for: 14 -> 14; matrix products, arithmetic and copies ran while one was open for 5% -> 3% of each run, Pallas kernels for 39% -> 44%
where the time goes in v3:
time: 348 us; the launch traced here: 342 us
  Pallas kernels  171 us (49%)
  waiting for transfers between devices  83.6 us (24%)
  starting transfers between devices  40.3 us (12%)
  local copies, waits for them, and re-layouts  19.5 us (6%)
  blocking collectives  15.7 us (5%)
  other arithmetic  10.2 us (3%)
    ppermute x18, waiting for transfers between devices, swap(): return lax.ppermute(values, axis, [(i, i ^ 1 << bit) for i in range(size)])  59.3 us
    pallas_call x2, Pallas kernels, forward(): pl.pallas_call(functools.partial(forward_kernel, first_group, groups, len...  57.9 us
    all_to_all x4, waiting for transfers between devices, exchange(): lax.all_to_all(parts, 'blk', split_axis=0, concat_axis=0, tiled=True)  24.3 us
    all_to_all x4, starting transfers between devices, exchange(): lax.all_to_all(parts, 'blk', split_axis=0, concat_axis=0, tiled=True)  21.3 us
    pallas_call x2, Pallas kernels, backward(): pl.pallas_call(functools.partial(backward_kernel, first_group, groups, pr...  21 us
    ppermute x18, starting transfers between devices, swap(): return lax.ppermute(values, axis, [(i, i ^ 1 << bit) for i in range(size)])  19 us
    all_to_all x1, blocking collectives, per_device(): news = lax.all_to_all(news, 'blk', split_axis=0, concat_axis=0, tiled=True)  15.7 us
    pallas_call x1, Pallas kernels, qkv_grads(): pl.pallas_call(functools.partial(qkv_kernel, extra), in_specs=[SMEM] + [A...  14.9 us
  transfers between devices with their start and end apart: 22, of which 14 were waited for; matrix products, arithmetic and copies ran while one was open for 3% of the time, Pallas kernels for 44%

profile of v3, /device:TPU:0, one launch (start us, length us, event | category | flops | bytes accessed | tf_op | source)
XLA Modules:
  0.0 341.6 jit_solution(16143793454400039675)
XLA Ops:
  1.9 8.1 %digest.1 = (bf16[2048,512]{1,0:T(8,128)(2,1)}, f32[48,512]{1,0:T(8,128)}, f32[8,56,128]{2,1,0:T(8,128)}, s32[64]{0:T(128)}, s32[64]{0:T(128)}, /*index=5*/s32[64]{0:T(128)}, s32[64]{0:T(128)}, s32[2]{0:T(128)}) custom-call(s32[2,8]{1,0:T(2,128)} %sela_ref.1, s32[4,8]{1,0:T(4,128)} %selb_ref.1, bf16[1024,512]{1,0:T(8,128)(2,1)} %bitcast.73, ...), custom_call_target="tpu_custom_call" | custom-call | flops 10485 | bytes 4194 | tf_op jit(solution)/shard_map/digest/pallas_call | solution.py:278
  10.0 15.7 %all_to_all.25 = f32[8,56,128]{2,1,0:T(8,128)S(1)} all-to-all(f32[8,56,128]{2,1,0:T(8,128)} %get-tuple-element.90), channel_id=1, replica_groups=mesh['dp'=4,'blk'=8] {'blk'}, dimensions={0} | all-to-all | bytes 458752 | tf_op jit(solution)/shard_map/all_to_all | solution.py:1548
  26.3 3.6 %pack.1 = (bf16[2048,512]{1,0:T(8,128)(2,1)}, bf16[1920,512]{1,0:T(8,128)(2,1)}) custom-call(s32[112]{0:T(128)} %convert_element_type.44.table_ref, bf16[2048,512]{1,0:T(8,128)(2,1)} %get-tuple-element.91.x_ref.refs_2_), custom_call_target="tpu_custom_call" | custom-call | bytes 6291 | tf_op jit(solution)/shard_map/pack/pallas_call | solution.py:341
  29.9 4.6 %all-to-all-start.1 = ((bf16[8,256,512]{2,1,0:T(8,128)(2,1)}), bf16[8,256,512]{2,1,0:T(8,128)(2,1)}, u32[]{:S(2)}, u32[]{:S(2)}) async-start(bf16[8,256,512]{2,1,0:T(8,128)(2,1)} %bitcast.72), calls=%async_computation.1 | async-start | bytes 4194304 | tf_op jit(solution)/shard_map/all_to_all | solution.py:1498
  35.8 1.9 arrange.1
  40.3 9.4 %project.1.refs_2_.refs_6_.refs_7_ = bf16[2048,1536]{1,0:T(8,128)(2,1)} custom-call(bf16[2048,512]{1,0:T(8,128)(2,1)} %copy-done, f32[1,512]{1,0:T(1,128)} %bitcast.63, bf16[512,1536]{1,0:T(8,128)(2,1)} %wqkv_hbm.1), custom_call_target="tpu_custom_call" | custom-call | flops 3221225 | bytes 8388 | tf_op jit(solution)/shard_map/project/pallas_call | solution.py:437
  51.0 3.7 %sinkhorn.1 = f32[6,64,128]{2,1,0:T(8,128)} custom-call(f32[6,64,64]{2,1,0:T(8,128)} %bitcast.55, f32[6,64,64]{2,1,0:T(8,128)} %fusion.picked_ref), custom_call_target="tpu_custom_call" | custom-call | flops 2457 | bytes 786 | tf_op jit(solution)/shard_map/sinkhorn/pallas_call | solution.py:466
  58.7 22.9 %all-to-all-done.1 = bf16[8,256,512]{2,1,0:T(8,128)(2,1)} async-done(((bf16[8,256,512]{2,1,0:T(8,128)(2,1)}), bf16[8,256,512]{2,1,0:T(8,128)(2,1)}, u32[]{:S(2)}, u32[]{:S(2)}) %all-to-all-start.1) | async-done | bytes 2097184 | tf_op jit(solution)/shard_map/all_to_all | solution.py:1498
  81.6 4.8 %all-to-all-start.2 = ((bf16[8,240,512]{2,1,0:T(8,128)(2,1)}), bf16[8,240,512]{2,1,0:T(8,128)(2,1)}, u32[]{:S(2)}, u32[]{:S(2)}) async-start(bf16[8,240,512]{2,1,0:T(8,128)(2,1)} %bitcast.20), calls=%async_computation.2 | async-start | bytes 3932160 | tf_op jit(solution)/shard_map/all_to_all | solution.py:1498
  87.0 34.3 %forward.2 = (bf16[2048,512]{1,0:T(8,128)(2,1)}, bf16[2048,512]{1,0:T(8,128)(2,1)}, bf16[2048,512]{1,0:T(8,128)(2,1)}, bf16[32,2,256,128]{3,2,1,0:T(8,128)(2,1)}...) custom-call(s32[64]{0:T(128)} %get-tuple-element.88.refs_0_, ...), custom_call_target="tpu_custom_call" | custom-call | flops 20000000 | bytes 20000 | tf_op jit(solution)/shard_map/forward/pallas_call | solution.py:860
  121.3 11.9 %backward.2 = (bf16[2048,1536]{1,0:T(8,128)(2,1)}, bf16[2048,1024]{1,0:T(8,128)(2,1)}, f32[20,2,128]{2,1,0:T(2,128)}, f32[1,512]{1,0:T(1,128)}, bf16[2048,512]{1,0:T(8,128)(2,1)}) custom-call(s32[64]{0:T(128)} %get-tuple-element.97.refs_0_, s32[64]{0:T(128)} %get-tuple-element.98.refs_1_.place_ref, bf16[2048,1536]{1,0:T(8,128)(2,1)} %project.1.refs_2_.refs_6_.refs_7_, ...), custom_call_target="tpu_custom_call" | custom-call | flops 8000000 | bytes 20000 | tf_op jit(solution)/shard_map/backward/pallas_call | solution.py:1051
  133.2 6.4 %all-to-all-start.3 = ((bf16[8,256,512]{2,1,0:T(8,128)(2,1)}), bf16[8,256,512]{2,1,0:T(8,128)(2,1)}, u32[]{:S(2)}, u32[]{:S(2)}) async-start(bf16[8,256,512]{2,1,0:T(8,128)(2,1)} %bitcast.71), calls=%async_computation.3 | async-start | bytes 4194304 | tf_op jit(solution)/shard_map/all_to_all | solution.py:1498
  139.6 23.7 %forward.3 = (bf16[2048,512]{1,0:T(8,128)(2,1)}, bf16[2048,512]{1,0:T(8,128)(2,1)}, bf16[2048,512]{1,0:T(8,128)(2,1)}, bf16[32,2,256,128]{3,2,1,0:T(8,128)(2,1)}...) custom-call(s32[64]{0:T(128)} %get-tuple-element.88.refs_0_, ...), custom_call_target="tpu_custom_call", output_to_operand_aliasing={{0}: (20, {}), {1}: (21, {}), {2}: (22, {}), {3}: (23, {}),... | custom-call | flops 12000000 | bytes 12000 | tf_op jit(solution)/shard_map/forward/pallas_call | solution.py:860
  164.0 1.6 copy-done.2
  165.6 3.1 restore.1
  168.7 4.6 %halve_step.4 = (bf16[640,512]{1,0:T(8,128)(2,1)}, bf16[640,512]{1,0:T(8,128)(2,1)}, bf16[512,512]{1,0:T(8,128)(2,1)}, bf16[512,512]{1,0:T(8,128)(2,1)}) custom-call(s32[2]{0:T(128)} %pad_add_fusion.bits_ref, bf16[2304,512]{1,0:T(8,128)(2,1)} %get-tuple-element.120.refs_0_, bf16[2304,512]{1,0:T(8,128)(2,1)} %collective-permute-done.refs_1_, ...), custom_call_target="tpu_custom_call" | custom-call | bytes 4718 | tf_op jit(solution)/shard_map/halve_step/pallas_call | solution.py:1377
  173.3 1.6 collective-permute-start.1
  174.9 2.0 collective-permute-start.2
  176.9 9.1 %backward.3 = (bf16[2048,1536]{1,0:T(8,128)(2,1)}, bf16[2048,1024]{1,0:T(8,128)(2,1)}, f32[12,2,128]{2,1,0:T(2,128)}, f32[1,512]{1,0:T(1,128)}, bf16[1920,512]{1,0:T(8,128)(2,1)}) custom-call(s32[64]{0:T(128)} %get-tuple-element.97.refs_0_, s32[64]{0:T(128)} %get-tuple-element.98.refs_1_.place_ref, ...), custom_call_target="tpu_custom_call", output_to_operand_aliasing={{0}: (11, {}), {1}: (12, {})} | custom-call | flops 4800000 | bytes 12000 | tf_op jit(solution)/shard_map/backward/pallas_call | solution.py:1051
  186.0 5.2 %collective-permute-done.2.refs_2_.refs_5_ = bf16[512,512]{1,0:T(8,128)(2,1)S(1)} collective-permute-done((bf16[512,512]{1,0:T(8,128)(2,1)}, bf16[512,512]{1,0:T(8,128)(2,1)S(1)}, u32[]{:S(2)}, u32[]{:S(2)}) %collective-permute-start.2) | collective-permute-done | bytes 524320 | tf_op jit(solution)/shard_map/ppermute | solution.py:1296
  192.2 5.5 %all-to-all-start.4 = ((bf16[8,240,512]{2,1,0:T(8,128)(2,1)}), bf16[8,240,512]{2,1,0:T(8,128)(2,1)S(1)}, u32[]{:S(2)}, u32[]{:S(2)}) async-start(bf16[8,240,512]{2,1,0:T(8,128)(2,1)} %bitcast.70), calls=%async_computation.4 | async-start | bytes 3932160 | tf_op jit(solution)/shard_map/all_to_all | solution.py:1498
  198.3 14.9 %qkv_grads.1 = (bf16[2048,512]{1,0:T(8,128)(2,1)}, bf16[896,512]{1,0:T(8,128)(2,1)}, bf16[896,512]{1,0:T(8,128)(2,1)}) custom-call(s32[1]{0:T(128)} %bitcast.4.refs_2_.core_ref, bf16[2048,512]{1,0:T(8,128)(2,1)} %copy-done, bf16[2048,512]{1,0:T(8,128)(2,1)} %get-tuple-element.113.refs_3_.farx_hbm, bf16[2048,1536]{1,0:T(8,128)(2,1)} %get-tuple-element.127.dproj_hbm.token_ref, ...), custom_call_target="tpu_custom_call" | custom-call | flops 10000000 | bytes 25000 | tf_op jit(solution)/shard_map/qkv_grads/pallas_call | solution.py:1166
  213.3 2.8 collective-permute-done.3.refs_1_.refs_2_
  216.1 3.1 halve_step.5
  219.2 2.1 collective-permute-start.5
  221.3 1.5 collective-permute-start.4
  223.4 4.8 %collective-permute-done.4.refs_3_ = bf16[192,512]{1,0:T(8,128)(2,1)S(1)} collective-permute-done((bf16[192,512]{1,0:T(8,128)(2,1)}, bf16[192,512]{1,0:T(8,128)(2,1)S(1)}, u32[]{:S(2)}, u32[]{:S(2)}) %collective-permute-start.4) | collective-permute-done | bytes 196640 | tf_op jit(solution)/shard_map/ppermute | solution.py:1296
  228.2 5.1 %collective-permute-done.5.refs_7_ = bf16[256,512]{1,0:T(8,128)(2,1)S(1)} collective-permute-done((bf16[256,512]{1,0:T(8,128)(2,1)}, bf16[256,512]{1,0:T(8,128)(2,1)S(1)}, u32[]{:S(2)}, u32[]{:S(2)}) %collective-permute-start.5) | collective-permute-done | bytes 262176 | tf_op jit(solution)/shard_map/ppermute | solution.py:1296
  234.0 4.0 %halve_step.6 = (bf16[416,512]{1,0:T(8,128)(2,1)}, bf16[416,512]{1,0:T(8,128)(2,1)}, bf16[384,512]{1,0:T(8,128)(2,1)}, bf16[384,512]{1,0:T(8,128)(2,1)}) custom-call(s32[2]{0:T(128)} %pad_add_fusion.1.bits_ref, bf16[640,512]{1,0:T(8,128)(2,1)} %get-tuple-element.122.refs_13_.refs_0_, bf16[640,512]{1,0:T(8,128)(2,1)} %copy-done.28, ...), custom_call_target="tpu_custom_call" | custom-call | bytes 3276 | tf_op jit(solution)/shard_map/halve_step/pallas_call | solution.py:1377
  238.1 1.6 collective-permute-start.7
  243.1 6.0 %sort_back.1 = (f32[72,512]{1,0:T(8,128)S(1)}, f32[64,512]{1,0:T(8,128)S(1)}) custom-call(s32[1]{0:T(128)} %bitcast.31.me_ref, s32[64]{0:T(128)S(1)} %copy-done.25, f32[6,64,64]{2,1,0:T(8,128)S(1)} %bitcast.56, f32[6,64,64]{2,1,0:T(8,128)S(1)} %copy-done.10, bf16[384,512]{1,0:T(8,128)(2,1)S(1)} %bitcast.57, bf16[64,512]{1,0:T(8,128)(2,1)S(1)} %bitcast.61, ...), custom_call_target="tpu_custom_call" | custom-call | flops 4915 | bytes 786 | tf_op jit(solution)/shard_map/sort_back/pallas_call | solution.py:551
  250.4 2.4 halve_step.7
  253.7 7.3 %base.1.refs_3_.refs_1_ = bf16[2048,512]{1,0:T(8,128)(2,1)} custom-call(bf16[2048,512]{1,0:T(8,128)(2,1)} %copy-done, bf16[2048,512]{1,0:T(8,128)(2,1)} %get-tuple-element.126.gmid_ref, bf16[2048,512]{1,0:T(8,128)(2,1)} %get-tuple-element.131.gn_ref, f32[64,512]{1,0:T(8,128)} %copy-done.16, f32[1,512]{1,0:T(1,128)} %bitcast.67), custom_call_target="tpu_custom_call" | custom-call | flops 20971 | bytes 8388 | tf_op jit(solution)/shard_map/base/pallas_call | solution.py:1208
  261.1 1.9 collective-permute-done.8.refs_0_
  264.9 2.6 collective-permute-start.9
  267.5 1.4 collective-permute-done.10
  268.9 1.6 collective-permute-start.11
  271.4 1.6 copy-done.4
  273.0 1.5 copy-done.6
  274.5 10.9 %last.1 = (bf16[1024,512]{1,0:T(8,128)(2,1)}, bf16[1024,512]{1,0:T(8,128)(2,1)}) custom-call(s32[120]{0:T(128)S(1)} %convert_element_type.48.table_ref, s32[64]{0:T(128)S(1)} %copy-done.23, bf16[2048,512]{1,0:T(8,128)(2,1)} %bitcast.26.refs_3_.refs_0_, bf16[1920,512]{1,0:T(8,128)(2,1)S(1)} %bitcast.54, bf16[2048,512]{1,0:T(8,128)(2,1)S(1)} %copy-done.4, ...), custom_call_target="tpu_custom_call" | custom-call | flops 20971 | bytes 12582 | tf_op jit(solution)/shard_map/last/pallas_call | solution.py:1268
  288.0 1.8 collective-permute-start.12
  289.8 9.4 %collective-permute-done.12.refs_1_ = bf16[400,512]{1,0:T(8,128)(2,1)S(1)} collective-permute-done((bf16[400,512]{1,0:T(8,128)(2,1)S(1)}, bf16[400,512]{1,0:T(8,128)(2,1)S(1)}, u32[]{:S(2)}, u32[]{:S(2)}) %collective-permute-start.12) | collective-permute-done | bytes 409632 | tf_op jit(solution)/shard_map/ppermute | solution.py:1296
  301.0 9.2 %collective-permute-done.14.refs_3_ = bf16[384,512]{1,0:T(8,128)(2,1)S(1)} collective-permute-done((bf16[384,512]{1,0:T(8,128)(2,1)S(1)}, bf16[384,512]{1,0:T(8,128)(2,1)S(1)}, u32[]{:S(2)}, u32[]{:S(2)}) %collective-permute-start.14) | collective-permute-done | bytes 393248 | tf_op jit(solution)/shard_map/ppermute | solution.py:1296
  310.4 1.5 double_step.4
  313.8 16.3 %collective-permute-done.16.refs_3_ = bf16[768,512]{1,0:T(8,128)(2,1)S(1)} collective-permute-done((bf16[768,512]{1,0:T(8,128)(2,1)S(1)}, bf16[768,512]{1,0:T(8,128)(2,1)S(1)}, u32[]{:S(2)}, u32[]{:S(2)}) %collective-permute-start.16) | collective-permute-done | bytes 786464 | tf_op jit(solution)/shard_map/ppermute | solution.py:1296
  332.8 2.9 assemble.2
  335.7 2.3 collective-permute-done.17.values_ref
  338.0 2.7 assemble.3
  (143 shorter events, 33.3 us)
Async XLA Ops:
  25.7 24.2 %copy-start.33 = (f32[8,56,128]{2,1,0:T(8,128)}, f32[8,56,128]{2,1,0:T(8,128)S(1)}, u32[]{:S(2)}) copy-start(f32[8,56,128]{2,1,0:T(8,128)S(1)} %all_to_all.25) | copy-start | bytes 688132
  29.9 4.7 %copy-start.3 = (bf16[2048,512]{1,0:T(8,128)(2,1)S(1)}, bf16[2048,512]{1,0:T(8,128)(2,1)}, u32[]{:S(2)}) copy-start(bf16[2048,512]{1,0:T(8,128)(2,1)} %get-tuple-element.91.x_ref.refs_2_) | copy-start | bytes 6291460
  29.9 4.7 %copy-start.12 = (bf16[2,512,512]{2,1,0:T(8,128)(2,1)S(1)}, bf16[2,512,512]{2,1,0:T(8,128)(2,1)}, u32[]{:S(2)}) copy-start(bf16[2,512,512]{2,1,0:T(8,128)(2,1)} %param.26) | copy-start | bytes 3145732
  29.9 4.7 %copy-start.24 = (s32[64]{0:T(128)S(1)}, s32[64]{0:T(128)}, u32[]{:S(2)}) copy-start(s32[64]{0:T(128)} %get-tuple-element.87.perm_ref) | copy-start | bytes 772
  29.9 51.7 %all-to-all-start.1 = ((bf16[8,256,512]{2,1,0:T(8,128)(2,1)}), bf16[8,256,512]{2,1,0:T(8,128)(2,1)}, u32[]{:S(2)}, u32[]{:S(2)}) async-start(bf16[8,256,512]{2,1,0:T(8,128)(2,1)} %bitcast.72), calls=%async_computation.1 | async-start | bytes 4194304 | tf_op jit(solution)/shard_map/all_to_all | solution.py:1498
  40.3 9.4 %copy-start.14 = (f32[48,512]{1,0:T(8,128)S(1)}, f32[48,512]{1,0:T(8,128)}, u32[]{:S(2)}) copy-start(f32[48,512]{1,0:T(8,128)} %get-tuple-element.94.means_ref) | copy-start | bytes 294916
  40.3 9.4 %copy-start.18 = (f32[512]{0:T(512)S(1)}, f32[512]{0:T(512)}, u32[]{:S(2)}) copy-start(f32[512]{0:T(512)} %convert_element_type.42) | copy-start | bytes 6148
  58.7 27.7 %copy-start.39 = (bf16[512]{0:T(512)(128)(2,1)S(1)}, bf16[512]{0:T(512)(128)(2,1)}, u32[]{:S(2)}) copy-start(bf16[512]{0:T(512)(128)(2,1)} %param.23) | copy-start | bytes 3076
  81.6 51.6 %all-to-all-start.2 = ((bf16[8,240,512]{2,1,0:T(8,128)(2,1)}), bf16[8,240,512]{2,1,0:T(8,128)(2,1)}, u32[]{:S(2)}, u32[]{:S(2)}) async-start(bf16[8,240,512]{2,1,0:T(8,128)(2,1)} %bitcast.20), calls=%async_computation.2 | async-start | bytes 3932160 | tf_op jit(solution)/shard_map/all_to_all | solution.py:1498
  133.2 57.9 %all-to-all-start.3 = ((bf16[8,256,512]{2,1,0:T(8,128)(2,1)}), bf16[8,256,512]{2,1,0:T(8,128)(2,1)}, u32[]{:S(2)}, u32[]{:S(2)}) async-start(bf16[8,256,512]{2,1,0:T(8,128)(2,1)} %bitcast.71), calls=%async_computation.3 | async-start | bytes 4194304 | tf_op jit(solution)/shard_map/all_to_all | solution.py:1498
  163.2 5.5 %collective-permute-start = (bf16[2304,512]{1,0:T(8,128)(2,1)}, bf16[2304,512]{1,0:T(8,128)(2,1)}, u32[]{:S(2)}, u32[]{:S(2)}) collective-permute-start(bf16[2304,512]{1,0:T(8,128)(2,1)} %get-tuple-element.121), channel_id=1, source_target_pairs={{0,8},{8,0},{16,24},{24,16},{1,9},{9,1},{17,25},{25,17},{2,10},{10... | collective-permute-start | bytes 7077896 | tf_op jit(solution)/shard_map/ppermute | solution.py:1296
  173.3 17.8 %collective-permute-start.1 = (bf16[640,512]{1,0:T(8,128)(2,1)}, bf16[640,512]{1,0:T(8,128)(2,1)S(1)}, u32[]{:S(2)}, u32[]{:S(2)}) collective-permute-start(bf16[640,512]{1,0:T(8,128)(2,1)} %get-tuple-element.124), channel_id=1, source_target_pairs={{0,16},{8,24},{16,0},{24,8},{1,17},{9,25},{17,1},{25,9},{2,18},{10... | collective-permute-start | bytes 1966088 | tf_op jit(solution)/shard_map/ppermute | solution.py:1296
  174.9 16.2 %collective-permute-start.2 = (bf16[512,512]{1,0:T(8,128)(2,1)}, bf16[512,512]{1,0:T(8,128)(2,1)S(1)}, u32[]{:S(2)}, u32[]{:S(2)}) collective-permute-start(bf16[512,512]{1,0:T(8,128)(2,1)} %get-tuple-element.125), channel_id=1, source_target_pairs={{0,1},{1,0},{2,3},{3,2},{4,5},{5,4},{6,7},{7,6},{8,9},{9,8},{10,11... | collective-permute-start | bytes 1572872 | tf_op jit(solution)/shard_map/ppermute | solution.py:1296
  192.2 5.6 %copy-start.37 = (f32[1,512]{1,0:T(1,128)S(1)}, f32[1,512]{1,0:T(1,128)}, u32[]{:S(2)}) copy-start(f32[1,512]{1,0:T(1,128)} %get-tuple-element.130) | copy-start | bytes 6148
  192.2 5.6 %copy-start.38 = (f32[1,512]{1,0:T(1,128)S(1)}, f32[1,512]{1,0:T(1,128)}, u32[]{:S(2)}) copy-start(f32[1,512]{1,0:T(1,128)} %get-tuple-element.129) | copy-start | bytes 6148
  192.2 50.9 %all-to-all-start.4 = ((bf16[8,240,512]{2,1,0:T(8,128)(2,1)}), bf16[8,240,512]{2,1,0:T(8,128)(2,1)S(1)}, u32[]{:S(2)}, u32[]{:S(2)}) async-start(bf16[8,240,512]{2,1,0:T(8,128)(2,1)} %bitcast.70), calls=%async_computation.4 | async-start | bytes 3932160 | tf_op jit(solution)/shard_map/all_to_all | solution.py:1498
  213.2 2.9 collective-permute-start.3
  219.2 14.0 %collective-permute-start.5 = (bf16[256,512]{1,0:T(8,128)(2,1)}, bf16[256,512]{1,0:T(8,128)(2,1)S(1)}, u32[]{:S(2)}, u32[]{:S(2)}) collective-permute-start(bf16[256,512]{1,0:T(8,128)(2,1)} %get-tuple-element.138), channel_id=1, source_target_pairs={{0,1},{1,0},{2,3},{3,2},{4,5},{5,4},{6,7},{7,6},{8,9},{9,8},{10,11... | collective-permute-start | bytes 786440 | tf_op jit(solution)/shard_map/ppermute | solution.py:1296
  221.3 6.9 %collective-permute-start.4 = (bf16[192,512]{1,0:T(8,128)(2,1)}, bf16[192,512]{1,0:T(8,128)(2,1)S(1)}, u32[]{:S(2)}, u32[]{:S(2)}) collective-permute-start(bf16[192,512]{1,0:T(8,128)(2,1)} %get-tuple-element.135), channel_id=1, source_target_pairs={{0,16},{8,24},{16,0},{24,8},{1,17},{9,25},{17,1},{25,9},{2,18},{10... | collective-permute-start | bytes 589832 | tf_op jit(solution)/shard_map/ppermute | solution.py:1296
  228.2 5.1 %copy-start.36 = (bf16[192,512]{1,0:T(8,128)(2,1)}, bf16[192,512]{1,0:T(8,128)(2,1)S(1)}, u32[]{:S(2)}) copy-start(bf16[192,512]{1,0:T(8,128)(2,1)S(1)} %collective-permute-done.4.refs_3_) | copy-start | bytes 589828
  234.0 9.1 %copy-start.17 = (bf16[512,64]{0,1:T(8,128)(2,1)S(1)}, bf16[512,64]{0,1:T(8,128)(2,1)}, u32[]{:S(2)}) copy-start(bf16[512,64]{0,1:T(8,128)(2,1)} %param.22) | copy-start | bytes 196612
  238.0 5.0 %copy-start.9 = (f32[6,64,128]{2,1,0:T(8,128)S(1)}, f32[6,64,128]{2,1,0:T(8,128)}, u32[]{:S(2)}) copy-start(f32[6,64,128]{2,1,0:T(8,128)} %copy-done.8) | copy-start | bytes 589828
  238.0 5.0 %copy-start.10 = (f32[6,64,64]{2,1,0:T(8,128)S(1)}, f32[6,64,64]{2,1,0:T(8,128)}, u32[]{:S(2)}) copy-start(f32[6,64,64]{2,1,0:T(8,128)} %fusion.picked_ref) | copy-start | bytes 294916
  238.0 5.0 %copy-start.11 = (bf16[416,512]{1,0:T(8,128)(2,1)S(1)}, bf16[416,512]{1,0:T(8,128)(2,1)}, u32[]{:S(2)}) copy-start(bf16[416,512]{1,0:T(8,128)(2,1)} %get-tuple-element.139.token_ref.refs_0_) | copy-start | bytes 1277956
  238.0 5.0 %copy-start.15 = (f32[48,512]{1,0:T(8,128)S(1)}, f32[48,512]{1,0:T(8,128)}, u32[]{:S(2)}) copy-start(f32[48,512]{1,0:T(8,128)} %get-tuple-element.94.means_ref) | copy-start | bytes 294916
  238.0 5.0 %copy-start.19 = (f32[512]{0:T(512)S(1)}, f32[512]{0:T(512)}, u32[]{:S(2)}) copy-start(f32[512]{0:T(512)} %convert_element_type.42) | copy-start | bytes 6148
  238.0 5.0 %copy-start.25 = (s32[64]{0:T(128)S(1)}, s32[64]{0:T(128)}, u32[]{:S(2)}) copy-start(s32[64]{0:T(128)} %get-tuple-element.87.perm_ref) | copy-start | bytes 772
  238.1 12.3 %collective-permute-start.6 = (bf16[416,512]{1,0:T(8,128)(2,1)}, bf16[416,512]{1,0:T(8,128)(2,1)}, u32[]{:S(2)}, u32[]{:S(2)}) collective-permute-start(bf16[416,512]{1,0:T(8,128)(2,1)} %get-tuple-element.143), channel_id=1, source_target_pairs={{0,1},{1,0},{2,3},{3,2},{4,5},{5,4},{6,7},{7,6},{8,9},{9,8},{10,11... | collective-permute-start | bytes 1277960 | tf_op jit(solution)/shard_map/ppermute | solution.py:1296
  238.1 12.3 %collective-permute-start.7 = (bf16[384,512]{1,0:T(8,128)(2,1)}, bf16[384,512]{1,0:T(8,128)(2,1)}, u32[]{:S(2)}, u32[]{:S(2)}) collective-permute-start(bf16[384,512]{1,0:T(8,128)(2,1)} %get-tuple-element.145), channel_id=1, source_target_pairs={{0,16},{8,24},{16,0},{24,8},{1,17},{9,25},{17,1},{25,9},{2,18},{10... | collective-permute-start | bytes 1179656 | tf_op jit(solution)/shard_map/ppermute | solution.py:1296
  243.0 9.8 %copy-start.5 = (bf16[8,240,512]{2,1,0:T(8,128)(2,1)}, bf16[8,240,512]{2,1,0:T(8,128)(2,1)S(1)}, u32[]{:S(2)}) copy-start(bf16[8,240,512]{2,1,0:T(8,128)(2,1)S(1)} %all-to-all-done.4) | copy-start | bytes 5898244
  252.8 10.2 %collective-permute-start.8 = (bf16[400,512]{1,0:T(8,128)(2,1)}, bf16[400,512]{1,0:T(8,128)(2,1)S(1)}, u32[]{:S(2)}, u32[]{:S(2)}) collective-permute-start(bf16[400,512]{1,0:T(8,128)(2,1)} %get-tuple-element.147), channel_id=1, source_target_pairs={{0,2},{1,3},{2,0},{3,1},{4,6},{5,7},{6,4},{7,5},{8,10},{9,11},{10,... | collective-permute-start | bytes 1228808 | tf_op jit(solution)/shard_map/ppermute | solution.py:1296
  261.1 2.7 copy-start.34
  261.1 6.4 %copy-start.22 = (f32[72,512]{1,0:T(8,128)S(1)}, f32[72,512]{1,0:T(8,128)}, u32[]{:S(2)}) copy-start(f32[72,512]{1,0:T(8,128)} %copy-done.21) | copy-start | bytes 442372
  261.1 10.3 %copy-start.1 = (bf16[2048,512]{1,0:T(8,128)(2,1)S(1)}, bf16[2048,512]{1,0:T(8,128)(2,1)}, u32[]{:S(2)}) copy-start(bf16[2048,512]{1,0:T(8,128)(2,1)} %base.1.refs_3_.refs_1_) | copy-start | bytes 6291460
  261.1 10.3 %copy-start.20 = (f32[512]{0:T(512)S(1)}, f32[512]{0:T(512)}, u32[]{:S(2)}) copy-start(f32[512]{0:T(512)} %convert_element_type.42) | copy-start | bytes 6148
  261.1 10.3 %copy-start.23 = (s32[64]{0:T(128)S(1)}, s32[64]{0:T(128)}, u32[]{:S(2)}) copy-start(s32[64]{0:T(128)} %get-tuple-element.98.refs_1_.place_ref) | copy-start | bytes 772
  264.9 21.2 %collective-permute-start.9 = (bf16[400,512]{1,0:T(8,128)(2,1)S(1)}, bf16[400,512]{1,0:T(8,128)(2,1)S(1)}, u32[]{:S(2)}, u32[]{:S(2)}) collective-permute-start(bf16[400,512]{1,0:T(8,128)(2,1)S(1)} %add_convert_fusion.1), channel_id=1, source_target_pairs={{0,4},{1,5},{2,6},{3,7},{4,0},{5,1},{6,2},{7,3},{8,12},{9,13},{10,... | collective-permute-start | bytes 1228808 | tf_op jit(solution)/shard_map/ppermute | solution.py:1296
  267.5 1.4 collective-permute-start.10
  268.9 16.5 %collective-permute-start.11 = (f32[72,512]{1,0:T(8,128)S(1)}, f32[72,512]{1,0:T(8,128)S(1)}, u32[]{:S(2)}, u32[]{:S(2)}) collective-permute-start(f32[72,512]{1,0:T(8,128)S(1)} %add.46), channel_id=1, source_target_pairs={{0,16},{8,24},{16,0},{24,8},{1,17},{9,25},{17,1},{25,9},{2,18},{10... | collective-permute-start | bytes 442376 | tf_op jit(solution)/shard_map/ppermute | solution.py:1296
  286.1 24.3 %copy-start.27 = (s32[2]{0:T(128)S(1)}, s32[2]{0:T(128)}, u32[]{:S(2)}) copy-start(s32[2]{0:T(128)} %pad_add_fusion.1.bits_ref) | copy-start | bytes 28
  286.9 44.0 %copy-start.26 = (s32[2]{0:T(128)S(1)}, s32[2]{0:T(128)}, u32[]{:S(2)}) copy-start(s32[2]{0:T(128)} %pad_add_fusion.bits_ref) | copy-start | bytes 28
  288.0 11.2 %collective-permute-start.12 = (bf16[400,512]{1,0:T(8,128)(2,1)S(1)}, bf16[400,512]{1,0:T(8,128)(2,1)S(1)}, u32[]{:S(2)}, u32[]{:S(2)}) collective-permute-start(bf16[400,512]{1,0:T(8,128)(2,1)S(1)} %add_convert_fusion.refs_0_), channel_id=1, source_target_pairs={{0,2},{1,3},{2,0},{3,1},{4,6},{5,7},{6,4},{7,5},{8,10},{9,11},{10,... | collective-permute-start | bytes 1228808 | tf_op jit(solution)/shard_map/ppermute | solution.py:1296
  299.7 10.7 %collective-permute-start.13 = (bf16[416,512]{1,0:T(8,128)(2,1)S(1)}, bf16[416,512]{1,0:T(8,128)(2,1)S(1)}, u32[]{:S(2)}, u32[]{:S(2)}) collective-permute-start(bf16[416,512]{1,0:T(8,128)(2,1)S(1)} %get-tuple-element.149.refs_0_), channel_id=1, source_target_pairs={{0,1},{1,0},{2,3},{3,2},{4,5},{5,4},{6,7},{7,6},{8,9},{9,8},{10,11... | collective-permute-start | bytes 1277960 | tf_op jit(solution)/shard_map/ppermute | solution.py:1296
  300.5 9.8 %collective-permute-start.14 = (bf16[384,512]{1,0:T(8,128)(2,1)S(1)}, bf16[384,512]{1,0:T(8,128)(2,1)S(1)}, u32[]{:S(2)}, u32[]{:S(2)}) collective-permute-start(bf16[384,512]{1,0:T(8,128)(2,1)S(1)} %get-tuple-element.150.refs_2_), channel_id=1, source_target_pairs={{0,16},{8,24},{16,0},{24,8},{1,17},{9,25},{17,1},{25,9},{2,18},{10... | collective-permute-start | bytes 1179656 | tf_op jit(solution)/shard_map/ppermute | solution.py:1296
  312.0 18.9 %collective-permute-start.15 = (bf16[832,512]{1,0:T(8,128)(2,1)S(1)}, bf16[832,512]{1,0:T(8,128)(2,1)S(1)}, u32[]{:S(2)}, u32[]{:S(2)}) collective-permute-start(bf16[832,512]{1,0:T(8,128)(2,1)S(1)} %get-tuple-element.151.refs_0_), channel_id=1, source_target_pairs={{0,16},{8,24},{16,0},{24,8},{1,17},{9,25},{17,1},{25,9},{2,18},{10... | collective-permute-start | bytes 2555912 | tf_op jit(solution)/shard_map/ppermute | solution.py:1296
  312.8 19.4 %copy-start.32 = (f32[72,512]{1,0:T(8,128)S(1)}, f32[72,512]{1,0:T(8,128)}, u32[]{:S(2)}) copy-start(f32[72,512]{1,0:T(8,128)} %add.47.refs_2_) | copy-start | bytes 442372
  312.8 17.3 %collective-permute-start.16 = (bf16[768,512]{1,0:T(8,128)(2,1)S(1)}, bf16[768,512]{1,0:T(8,128)(2,1)S(1)}, u32[]{:S(2)}, u32[]{:S(2)}) collective-permute-start(bf16[768,512]{1,0:T(8,128)(2,1)S(1)} %get-tuple-element.152.refs_2_), channel_id=1, source_target_pairs={{0,1},{1,0},{2,3},{3,2},{4,5},{5,4},{6,7},{7,6},{8,9},{9,8},{10,11... | collective-permute-start | bytes 2359304 | tf_op jit(solution)/shard_map/ppermute | solution.py:1296
  332.1 5.9 %collective-permute-start.17 = (bf16[3200,512]{1,0:T(8,128)(2,1)S(1)}, bf16[3200,512]{1,0:T(8,128)(2,1)S(1)}, u32[]{:S(2)}, u32[]{:S(2)}) collective-permute-start(bf16[3200,512]{1,0:T(8,128)(2,1)S(1)} %double_step.5.values_ref), channel_id=1, source_target_pairs={{0,8},{8,0},{16,24},{24,16},{1,9},{9,1},{17,25},{25,17},{2,10},{10... | collective-permute-start | bytes 9830408 | tf_op jit(solution)/shard_map/ppermute | solution.py:1296
  (14 other events, 14.9 us)

commit v4 on v3

--- a/solution.py
+++ b/solution.py
@@ -13,7 +13,6 @@
 EPSILON = 1e-05
 SOFTMAX_HEAT = 0.75
 UNIT = 32
-EXTRA = 256
 GROUP = 64
 TILE = 256
 HALF = 256
@@ -617,14 +616,14 @@
     recv_hbm = take(recvs)
     x_hbm, cot_hbm, proj_hbm, wrow_hbm, mask_ref, gain1_ref, gain2_ref = take(7)
     wqkv_hbm, wout_hbm, wup_hbm, wdown_hbm, _ = take(5)
-    prior_refs = take(3) if prior else []
+    prior_refs = take(2) if prior else []
     if prior:
         take(6)
     out_hbm, gmid_hbm, gatt_hbm, prob_hbm, farx_hbm, farkv_hbm = take(6)
     if final:
-        keep_hbm, give_hbm, gain_ref = take(3)
+        keep_hbm, give_hbm = take(2)
     else:
-        up_hbm, down_hbm, gain_ref = take(3)
+        up_hbm, down_hbm = take(2)
     x_ref, cot_ref, proj_ref, wrow_ref, wqkv_ref, wout_ref, wup_ref, wdown_ref = take(8)
     out_ref, gmid_ref, gatt_ref, prob_ref, farx_ref, farkv_ref, attended = take(7)
     one_ref, two_ref = take(2)
@@ -803,8 +802,6 @@
         put_up(c, dot(second_t, grad))
     out_ref[...] = result.astype(BF16)
     move.store(out_ref, out_hbm.at[here])
-    gain = jnp.sum(back * scaled, axis=0, keepdims=True)
-    gain_ref[...] = gain + prior_refs[2][...] if prior else gain
     e = back * gain2_ref[...]
     inner = jnp.mean(e * scaled, axis=-1, keepdims=True)
     grad_middle = cot.astype(F32) + r2 * (e - scaled * inner)
@@ -851,7 +848,7 @@
     aliases = {}
     if prior is not None:
         streams, sums = prior
-        in_specs += [ANY, ANY, VMEM] + [ANY] * 6
+        in_specs += [ANY, ANY] + [ANY] * 6
         operands += list(sums)
         aliases = {len(operands) + i: i for i in range(6)}
         operands += list(streams)
@@ -862,10 +859,9 @@
             forward_kernel, first_group, groups, len(recv), prior is not None, final
         ),
         in_specs=in_specs,
-        out_specs=[ANY] * 8 + [VMEM],
+        out_specs=[ANY] * 8,
         out_shape=[like(width), like(width), like(width), probs, like(width), like(2 * width)]
-        + [jax.ShapeDtypeStruct(shape, BF16) for shape in tails]
-        + [jax.ShapeDtypeStruct((1, width), F32)],
+        + [jax.ShapeDtypeStruct(shape, BF16) for shape in tails],
         scratch_shapes=scratch,
         input_output_aliases=aliases,
         compiler_params=pltpu.CompilerParams(vmem_limit_bytes=VMEM_LIMIT),
@@ -879,14 +875,14 @@
     refs = list(refs)
     take = lambda n: [refs.pop(0) for _ in range(n)]
     ret_rows, place_ref = take(2)
-    proj_hbm, farx_hbm, farkv_hbm, gatt_hbm, prob_hbm, wrow_hbm, wqkv_hbm = take(7)
+    proj_hbm, farkv_hbm, gatt_hbm, prob_hbm, wrow_hbm, wqkv_hbm = take(6)
     if prior:
-        prior_gain, prior_gw = take(2)
+        (prior_gw,) = take(1)
         take(2)
     take(1)
-    dproj_hbm, dfar_hbm, gw_ref, gain_ref = take(4)
+    dproj_hbm, dfar_hbm, gw_ref = take(3)
     ret_hbm = take(chunks)
-    proj_ref, farx_ref, farkv_ref, gatt_ref, prob_ref, wrow_ref, wqkv_ref = take(7)
+    proj_ref, farkv_ref, gatt_ref, prob_ref, wrow_ref, wqkv_ref = take(6)
     dproj_ref, dfar_ref = take(2)
     ret_refs = take(chunks)
     (sems,) = take(1)
@@ -917,7 +913,6 @@
             ]
         )
     got_wqkv = move.start(wqkv_hbm, wqkv_ref)
-    got_farx = move.start(farx_hbm.at[pl.ds(start, rows)], farx_ref)
     masks16 = head_masks(GROUP)
     head_scale = (width // HEADS) ** -0.5
     far_lane = lax.broadcasted_iota(jnp.int32, (GROUP // UNIT, 2 * GROUP), 1) >= GROUP
@@ -977,12 +972,7 @@
         move.store(dfar_ref.at[at], dfar_hbm.at[there])
 
     got_wqkv.wait()
-    got_farx.wait()
-    grad = dot(dfar_ref[...], wqkv_ref[:, width:], NT)
-    far = farx_ref[...].astype(F32)
-    gain = jnp.sum(grad * (far * inverse_norm(far)), axis=0, keepdims=True)
-    gain_ref[...] = gain + prior_gain[...] if prior else gain
-    grad = grad.astype(BF16)
+    grad = dot(dfar_ref[...], wqkv_ref[:, width:], NT).astype(BF16)
     for u in range(rows // UNIT):
         row = ret_rows[2 * first_group + u]
         edge = 0
@@ -1032,19 +1022,19 @@
 
 
 def backward(
-    ret_rows, place, proj, farx, farkv, gatt, prob, wrow, w_qkv, sizes, first_group, groups, prior, letter,
+    ret_rows, place, proj, farkv, gatt, prob, wrow, w_qkv, sizes, first_group, groups, prior, letter,
     token,
 ):
     rows, width = gatt.shape
     count = groups * GROUP
-    in_specs = [SMEM, SMEM] + [ANY] * 7
-    operands = [ret_rows, place, proj, farx, farkv, gatt, prob, wrow, w_qkv]
+    in_specs = [SMEM, SMEM] + [ANY] * 6
+    operands = [ret_rows, place, proj, farkv, gatt, prob, wrow, w_qkv]
     aliases = {}
     if prior is not None:
-        dproj, dfar, gw, gain = prior
-        in_specs += [VMEM, VMEM, ANY, ANY]
-        aliases = {len(operands) + 2: 0, len(operands) + 3: 1}
-        operands += [gain, gw, dproj, dfar]
+        dproj, dfar, gw = prior
+        in_specs += [VMEM, ANY, ANY]
+        aliases = {len(operands) + 1: 0, len(operands) + 2: 1}
+        operands += [gw, dproj, dfar]
     in_specs += [ANY]
     operands += [token]
     batches = -(-groups // BATCH)
@@ -1053,17 +1043,15 @@
             backward_kernel, first_group, groups, prior is not None, len(sizes), letter
         ),
         in_specs=in_specs,
-        out_specs=[ANY, ANY, VMEM, VMEM] + [ANY] * len(sizes),
+        out_specs=[ANY, ANY, VMEM] + [ANY] * len(sizes),
         out_shape=[
             jax.ShapeDtypeStruct((rows, 3 * width), BF16),
             jax.ShapeDtypeStruct((rows, 2 * width), BF16),
             jax.ShapeDtypeStruct((groups, GROUP // UNIT, 128), F32),
-            jax.ShapeDtypeStruct((1, width), F32),
         ]
         + [jax.ShapeDtypeStruct((n, width), BF16) for n in sizes],
         scratch_shapes=[
             pltpu.VMEM((count, 3 * width), BF16),
-            pltpu.VMEM((count, width), BF16),
             pltpu.VMEM((count, 2 * width), BF16),
             pltpu.VMEM((count, width), BF16),
             pltpu.VMEM((groups,) + prob.shape[1:], BF16),
@@ -1082,7 +1070,7 @@
 
 
 def qkv_kernel(
-    extra, core_ref, x_hbm, farx_hbm, dproj_hbm, dfar_hbm, gain1_ref, wqkv_hbm, gains_ref, token_ref,
+    core_ref, x_hbm, farx_hbm, dproj_hbm, dfar_hbm, gain1_ref, wqkv_hbm, token_ref,
     gn_hbm, keep_ref, give_ref, x_ref, farx_ref, dproj_ref, dfar_ref, wqkv_ref, gn_ref, near_t, far_t, sems,
 ):
     move = Mover(sems)
@@ -1105,7 +1093,6 @@
             ]
         )
     got_w.wait()
-    gain = jnp.zeros((1, width), F32)
     for low, copies in zip(range(0, rows, size), loads):
         at = slice(low, low + size)
         for copy in copies:
@@ -1118,7 +1105,6 @@
         grad = dot(dproj_ref[at, :], wqkv_ref[...], NT)
         gn_ref[at, :] = grad.astype(BF16)
         move.store(gn_ref.at[pl.ds(low, size)], gn_hbm.at[pl.ds(low, size)])
-        gain = gain + jnp.sum(grad * scaled, axis=0, keepdims=True)
     grads = []
     for c in range(0, wide, width):
         value = dot(near_t[...], dproj_ref[:, c : c + width])
@@ -1126,22 +1112,14 @@
             value = value + dot(far_t[...], dfar_ref[:, c - width : c])
         grads.append(value)
 
-    line = lax.broadcasted_iota(jnp.int32, (extra, width), 0)
-    small = jnp.where(line == 0, gain + gains_ref[0:1, :], 0.0)
-    small = jnp.where(line == 1, gains_ref[1:2, :], small)
-    total = wide + extra
-    half = total // 2
+    half = wide // 2
 
     def write(ref, which):
         at = which * half
         while at < (which + 1) * half:
             block, line = divmod(at, width)
-            if at >= wide:
-                count = extra
-                value = small
-            else:
-                count = min(width - line, (which + 1) * half - at)
-                value = grads[block][line : line + count]
+            count = min(width - line, (which + 1) * half - at)
+            value = grads[block][line : line + count]
             ref[at - which * half : at - which * half + count, :] = value.astype(BF16)
             at += count
 
@@ -1158,14 +1136,14 @@
     move.finish()
 
 
-def qkv_grads(core, x, farx, dproj, dfar, gain1, w_qkv, gains, extra, token):
+def qkv_grads(core, x, farx, dproj, dfar, gain1, w_qkv, token):
     rows, width = x.shape
     wide = w_qkv.shape[1]
-    half = (wide + extra) // 2
+    half = wide // 2
     tall = lambda size: pltpu.VMEM((rows, size), BF16)
     return pl.pallas_call(
-        functools.partial(qkv_kernel, extra),
-        in_specs=[SMEM] + [ANY] * 4 + [VMEM, ANY, VMEM, ANY],
+        qkv_kernel,
+        in_specs=[SMEM] + [ANY] * 4 + [VMEM, ANY, ANY],
         out_specs=[ANY, VMEM, VMEM],
         out_shape=[
             jax.ShapeDtypeStruct((rows, width), BF16),
@@ -1186,7 +1164,7 @@
         compiler_params=limit(62),
         cost_estimate=cost(10e9, 25e6),
         name="qkv_grads",
-    )(core, x, farx, dproj, dfar, gain1, w_qkv, gains, token)
+    )(core, x, farx, dproj, dfar, gain1, w_qkv, token)
 
 
 def row_gradient(f, x):
@@ -1205,17 +1183,18 @@
 
 def base_rows(x, gmid, gn, gs, gain1):
     rows, width = x.shape
+    tile = 2 * TILE
     return pl.pallas_call(
         base_kernel,
-        grid=(rows // TILE,),
+        grid=(rows // tile,),
         in_specs=[
-            rows_of(TILE, width),
-            rows_of(TILE, width),
-            rows_of(TILE, width),
-            rows_of(TILE // UNIT, width),
+            rows_of(tile, width),
+            rows_of(tile, width),
+            rows_of(tile, width),
+            rows_of(tile // UNIT, width),
             whole((1, width)),
         ],
-        out_specs=rows_of(TILE, width),
+        out_specs=rows_of(tile, width),
         out_shape=jax.ShapeDtypeStruct((rows, width), BF16),
         compiler_params=params(),
         cost_estimate=cost(rows * width * 20, rows * width * 8),
@@ -1425,7 +1404,7 @@
 
 
 def places(half, width, ff):
-    up, down, out, qkv, gains = range(5)
+    up, down, out, qkv = range(4)
     edge = ff // 2
     result = [
         (c, width, up, 0, half * edge + c) for c in range(0, edge, width)
@@ -1435,27 +1414,27 @@
         (edge + width // 2 + c, width, down, half * edge + c, 0) for c in range(0, edge, width)
     ]
     start = edge + width // 2 + edge
-    total = 3 * width + EXTRA
+    total = 3 * width
     at = half * total // 2
     while at < (half + 1) * total // 2:
         block, line = divmod(at, width)
-        if at >= 3 * width:
-            result.append((start + at - half * total // 2, 16, gains, 0, 0))
-            break
         count = min(width - line, (half + 1) * total // 2 - at)
         result.append((start + at - half * total // 2, count, qkv, line, block * width))
         at += count
     return result
 
 
-def assemble_kernel(which, prior, width, ff, core_ref, values_ref, *refs):
+def assemble_kernel(which, prior, width, ff, core_ref, values_ref, wup_ref, wqkv_ref, *refs):
     outs = refs[5 if prior else 0 :][:5]
-    held, sems = refs[-2:]
+    held, products, sems = refs[-3:]
+    ones = jnp.ones((8, width), BF16)
 
     def write(half):
         copies = []
+        seen = set()
         for i, (first, count, out, line, column) in enumerate(places(half, width, ff)):
-            held[first : first + count, :] = values_ref[first : first + count, :].astype(F32)
+            value = values_ref[first : first + count, :].astype(F32)
+            held[first : first + count, :] = value
             copy = pltpu.make_async_copy(
                 held.at[pl.ds(first, count)],
                 outs[out].at[pl.ds(line, count), pl.ds(column, width)],
@@ -1463,8 +1442,27 @@
             )
             copy.start()
             copies.append(copy)
+            if out in (0, 3):
+                weights = (wup_ref if out == 0 else wqkv_ref)[line : line + count, column : column + width]
+                part = weights.astype(F32) * value
+                if out in seen:
+                    products[out // 3, line : line + count, :] += part
+                else:
+                    products[out // 3, line : line + count, :] = part
+                    if count < width:
+                        rest = slice(0, line) if line else slice(count, width)
+                        products[out // 3, rest, :] = jnp.zeros((width - count, width), F32)
+                    seen.add(out)
+        for out, at in ((3, 0), (0, 1)):
+            value = products[out // 3]
+            high = value.astype(BF16)
+            low = (value - high.astype(F32)).astype(BF16)
+            row = (dot(ones, high, NT) + dot(ones, low, NT))[0:1]
+            outs[4][at : at + 1, :] = row + refs[0][at : at + 1, :] if prior else row
         for copy in copies:
             copy.wait()
+
+    outs[4][...] = jnp.zeros_like(outs[4])
 
     @pl.when(core_ref[0] == which)
     def _():
@@ -1475,18 +1473,24 @@
         write(1)
 
 
-def assemble(core, which, values, width, ff, prior):
-    shapes = [(width, ff), (ff, width), (width, width), (width, 3 * width), (16, width)]
-    operands = [core, values] + (list(prior) if prior is not None else [])
+def assemble(core, which, values, w_up, w_qkv, width, ff, prior):
+    shapes = [(width, ff), (ff, width), (width, width), (width, 3 * width), (8, width)]
+    operands = [core, values, w_up, w_qkv]
+    if prior is not None:
+        operands += [prior[4], *prior[:4]]
     most = max(len(places(half, width, ff)) for half in (0, 1))
     return pl.pallas_call(
         functools.partial(assemble_kernel, which, prior is not None, width, ff),
-        in_specs=[SMEM, VMEM] + [ANY] * (len(operands) - 2),
-        out_specs=[ANY] * 5,
+        in_specs=[SMEM] + [VMEM] * (3 if prior is None else 4) + [ANY] * (0 if prior is None else 4),
+        out_specs=[ANY] * 4 + [VMEM],
         out_shape=[jax.ShapeDtypeStruct(shape, F32) for shape in shapes],
-        scratch_shapes=[pltpu.VMEM(values.shape, F32), pltpu.SemaphoreType.DMA((most,))],
-        input_output_aliases={} if prior is None else {2 + i: i for i in range(5)},
-        compiler_params=limit(16),
+        scratch_shapes=[
+            pltpu.VMEM(values.shape, F32),
+            pltpu.VMEM((2, width, width), F32),
+            pltpu.SemaphoreType.DMA((most,)),
+        ],
+        input_output_aliases={} if prior is None else {5 + i: i for i in range(4)},
+        compiler_params=limit(20),
         cost_estimate=cost(0, values.size * 6),
         name="assemble",
     )(*operands)
@@ -1608,21 +1612,21 @@
     letter = (count_a, count_b, devices, extra)
 
     def run_backward(streams, *rest):
-        _, _, gatt, prob, farx, farkv = streams
-        return backward(ret_rows, place, proj, farx, farkv, gatt, prob, wrow, w_qkv, *rest)
+        _, _, gatt, prob, _, farkv = streams
+        return backward(ret_rows, place, proj, farkv, gatt, prob, wrow, w_qkv, *rest)
 
     fast = lax.axis_size("dp") == 4 and devices == 8 and early < groups
     part_x = ff // 2 + width // 2
     if early < groups:
         prior = forward(far_rows, kinds, core, recv[:1], *shared, 0, early, None, False, wrow)
-        dproj, dfar, gw_one, gain, *ret = run_backward(
+        dproj, dfar, gw_one, *ret = run_backward(
             prior[0], heights[:1], 0, early, None, None, prior[0][0]
         )
         back = [exchange(v, devices) for v in ret]
         streams, sums = forward(
-            far_rows, kinds, core, recv, *shared, early, groups - early, prior, True, gain
+            far_rows, kinds, core, recv, *shared, early, groups - early, prior, True, dproj
         )
-        keep, give, g_gain2 = sums
+        keep, give = sums
         out_a, out_b = restore(perm, streams[0], total_a)
         big_came = swap(give, "dp", 0)
         token = keep
@@ -1633,16 +1637,16 @@
             )
             bx_came, by_came = swap(gx, *AXIS_X), swap(gy, *AXIS_Y)
             token = bx
-        dproj, dfar, _, g_gain1_far, *ret = run_backward(
-            streams, heights[1:], early, groups - early, (dproj, dfar, gw_one, gain), letter, token
+        dproj, dfar, _, *ret = run_backward(
+            streams, heights[1:], early, groups - early, (dproj, dfar, gw_one), letter, token
         )
     else:
         streams, sums = forward(far_rows, kinds, core, recv, *shared, 0, groups, None, True, wrow)
-        keep, give, g_gain2 = sums
+        keep, give = sums
         out_a, out_b = restore(perm, streams[0], total_a)
         big_came = swap(give, "dp", 0)
         back = []
-        dproj, dfar, _, g_gain1_far, *ret = run_backward(
+        dproj, dfar, _, *ret = run_backward(
             streams, heights, 0, groups, None, letter, keep
         )
     _, gmid, _, _, farx, _ = streams
@@ -1651,13 +1655,12 @@
     tall = sizes[-1] * UNIT
     arrived = exchange(parcel, devices)
     back.append(arrived)
-    gains = jnp.concatenate([g_gain1_far, g_gain2], axis=0)
     token = dproj
     gn, late_keep, late_give = qkv_grads(
-        core, xp, farx, dproj, dfar, gain1, w_qkv, gains, EXTRA, token
+        core, xp, farx, dproj, dfar, gain1, w_qkv, token
     )
     late_came = swap(late_give, "dp", 0)
-    part_late = 384
+    part_late = 256
     if fast:
         late_rows = late_keep.shape[0]
         ranges_late = [(0, 0, part_late, 0, 0, 0), (0, part_late, late_rows - part_late, 1, 1, 0)]
@@ -1741,19 +1744,21 @@
 
     if not fast:
         small = lax.psum(small, "dp")
-    written = assemble(core, 0, sums_own, width, ff, None)
-    sum_up, sum_down, sum_out, sum_qkv, gains = assemble(core, 1, sums_came, width, ff, written)
+    written = assemble(core, 0, sums_own, w_up, w_qkv, width, ff, None)
+    sum_up, sum_down, sum_out, sum_qkv, gains = assemble(
+        core, 1, sums_came, w_up, w_qkv, width, ff, written
+    )
 
     return (
         out_a.reshape(x_a.shape),
         out_b.reshape(x_b.shape),
         gx_a.reshape(x_a.shape),
         gx_b.reshape(x_b.shape),
-        gains[0] + small[blocks],
+        gains[0] / gain1[0] + small[blocks],
         sum_qkv,
         sum_out,
         small[:blocks].T,
-        gains[1],
+        gains[1] / gain2[0],
         sum_up,
         sum_down,
     )

time: 348 us -> 345 us (level)
    unnamed x80 -> x84, local copies, waits for them, and re-layouts: 13.1 us -> 13.2 us
where the time goes in v4:
time: 345 us; the launch traced here: 338 us
  Pallas kernels  168 us (49%)
  waiting for transfers between devices  85.2 us (25%)
  starting transfers between devices  38.7 us (11%)
  local copies, waits for them, and re-layouts  19.5 us (6%)
  blocking collectives  15.7 us (5%)
  other arithmetic  9.7 us (3%)
    ppermute x18, waiting for transfers between devices, swap(): return lax.ppermute(values, axis, [(i, i ^ 1 << bit) for i in range(size)])  60.4 us
    pallas_call x2, Pallas kernels, forward(): pl.pallas_call(functools.partial(forward_kernel, first_group, groups, len...  56.6 us
    all_to_all x4, waiting for transfers between devices, exchange(): lax.all_to_all(parts, 'blk', split_axis=0, concat_axis=0, tiled=True)  24.8 us
    pallas_call x2, Pallas kernels, backward(): pl.pallas_call(functools.partial(backward_kernel, first_group, groups, pr...  20.6 us
    all_to_all x4, starting transfers between devices, exchange(): lax.all_to_all(parts, 'blk', split_axis=0, concat_axis=0, tiled=True)  20.1 us
    ppermute x18, starting transfers between devices, swap(): return lax.ppermute(values, axis, [(i, i ^ 1 << bit) for i in range(size)])  18.6 us
    all_to_all x1, blocking collectives, per_device(): news = lax.all_to_all(news, 'blk', split_axis=0, concat_axis=0, tiled=True)  15.7 us
    pallas_call x1, Pallas kernels, qkv_grads(): pl.pallas_call(qkv_kernel, in_specs=[SMEM] + [ANY] * 4 + [VMEM, ANY, ANY]...  14.8 us
  transfers between devices with their start and end apart: 22, of which 14 were waited for; matrix products, arithmetic and copies ran while one was open for 3% of the time, Pallas kernels for 44%

profile of v4, /device:TPU:0, one launch (start us, length us, event | category | flops | bytes accessed | tf_op | source)
XLA Modules:
  0.0 338.4 jit_solution(8925252621743368434)
XLA Ops:
  1.9 8.1 %digest.1 = (bf16[2048,512]{1,0:T(8,128)(2,1)}, f32[48,512]{1,0:T(8,128)}, f32[8,56,128]{2,1,0:T(8,128)}, s32[64]{0:T(128)}, s32[64]{0:T(128)}, /*index=5*/s32[64]{0:T(128)}, s32[64]{0:T(128)}, s32[2]{0:T(128)}) custom-call(s32[2,8]{1,0:T(2,128)} %sela_ref.1, s32[4,8]{1,0:T(4,128)} %selb_ref.1, bf16[1024,512]{1,0:T(8,128)(2,1)} %bitcast.75, ...), custom_call_target="tpu_custom_call" | custom-call | flops 10485 | bytes 4194 | tf_op jit(solution)/shard_map/digest/pallas_call | solution.py:277
  10.0 15.7 %all_to_all.25 = f32[8,56,128]{2,1,0:T(8,128)S(1)} all-to-all(f32[8,56,128]{2,1,0:T(8,128)} %get-tuple-element.86), channel_id=1, replica_groups=mesh['dp'=4,'blk'=8] {'blk'}, dimensions={0} | all-to-all | bytes 458752 | tf_op jit(solution)/shard_map/all_to_all | solution.py:1552
  26.3 3.6 %pack.1 = (bf16[2048,512]{1,0:T(8,128)(2,1)}, bf16[1920,512]{1,0:T(8,128)(2,1)}) custom-call(s32[112]{0:T(128)} %convert_element_type.46.table_ref, bf16[2048,512]{1,0:T(8,128)(2,1)} %get-tuple-element.87.x_ref.refs_2_), custom_call_target="tpu_custom_call" | custom-call | bytes 6291 | tf_op jit(solution)/shard_map/pack/pallas_call | solution.py:340
  29.9 4.6 %all-to-all-start.1 = ((bf16[8,256,512]{2,1,0:T(8,128)(2,1)}), bf16[8,256,512]{2,1,0:T(8,128)(2,1)}, u32[]{:S(2)}, u32[]{:S(2)}) async-start(bf16[8,256,512]{2,1,0:T(8,128)(2,1)} %bitcast.73), calls=%async_computation.1 | async-start | bytes 4194304 | tf_op jit(solution)/shard_map/all_to_all | solution.py:1502
  35.8 1.9 arrange.1
  40.3 9.4 %project.1.refs_2_.refs_6_.refs_7_ = bf16[2048,1536]{1,0:T(8,128)(2,1)} custom-call(bf16[2048,512]{1,0:T(8,128)(2,1)} %copy-done.1, f32[1,512]{1,0:T(1,128)} %bitcast.64, bf16[512,1536]{1,0:T(8,128)(2,1)} %wqkv_ref.3), custom_call_target="tpu_custom_call" | custom-call | flops 3221225 | bytes 8388 | tf_op jit(solution)/shard_map/project/pallas_call | solution.py:436
  51.0 3.7 %sinkhorn.1 = f32[6,64,128]{2,1,0:T(8,128)} custom-call(f32[6,64,64]{2,1,0:T(8,128)} %bitcast.56, f32[6,64,64]{2,1,0:T(8,128)} %fusion.picked_ref), custom_call_target="tpu_custom_call" | custom-call | flops 2457 | bytes 786 | tf_op jit(solution)/shard_map/sinkhorn/pallas_call | solution.py:465
  58.7 22.9 %all-to-all-done.1 = bf16[8,256,512]{2,1,0:T(8,128)(2,1)} async-done(((bf16[8,256,512]{2,1,0:T(8,128)(2,1)}), bf16[8,256,512]{2,1,0:T(8,128)(2,1)}, u32[]{:S(2)}, u32[]{:S(2)}) %all-to-all-start.1) | async-done | bytes 2097184 | tf_op jit(solution)/shard_map/all_to_all | solution.py:1502
  81.6 4.5 %all-to-all-start.2 = ((bf16[8,240,512]{2,1,0:T(8,128)(2,1)}), bf16[8,240,512]{2,1,0:T(8,128)(2,1)}, u32[]{:S(2)}, u32[]{:S(2)}) async-start(bf16[8,240,512]{2,1,0:T(8,128)(2,1)} %bitcast.20), calls=%async_computation.2 | async-start | bytes 3932160 | tf_op jit(solution)/shard_map/all_to_all | solution.py:1502
  86.7 33.8 %forward.2 = (bf16[2048,512]{1,0:T(8,128)(2,1)}, bf16[2048,512]{1,0:T(8,128)(2,1)}, bf16[2048,512]{1,0:T(8,128)(2,1)}, bf16[32,2,256,128]{3,2,1,0:T(8,128)(2,1)}...) custom-call(s32[64]{0:T(128)} %get-tuple-element.84.refs_0_, ...), custom_call_target="tpu_custom_call" | custom-call | flops 20000000 | bytes 20000 | tf_op jit(solution)/shard_map/forward/pallas_call | solution.py:857
  120.5 11.6 %backward.2 = (bf16[2048,1536]{1,0:T(8,128)(2,1)}, bf16[2048,1024]{1,0:T(8,128)(2,1)}, f32[20,2,128]{2,1,0:T(2,128)}, bf16[2048,512]{1,0:T(8,128)(2,1)}) custom-call(s32[64]{0:T(128)} %get-tuple-element.93.refs_0_, s32[64]{0:T(128)} %get-tuple-element.94.refs_1_.place_ref, bf16[2048,1536]{1,0:T(8,128)(2,1)} %project.1.refs_2_.refs_6_.refs_7_, ...), custom_call_target="tpu_custom_call" | custom-call | flops 8000000 | bytes 20000 | tf_op jit(solution)/shard_map/backward/pallas_call | solution.py:1041
  132.2 6.3 %all-to-all-start.3 = ((bf16[8,256,512]{2,1,0:T(8,128)(2,1)}), bf16[8,256,512]{2,1,0:T(8,128)(2,1)}, u32[]{:S(2)}, u32[]{:S(2)}) async-start(bf16[8,256,512]{2,1,0:T(8,128)(2,1)} %bitcast.72), calls=%async_computation.3 | async-start | bytes 4194304 | tf_op jit(solution)/shard_map/all_to_all | solution.py:1502
  138.5 22.8 %forward.3 = (bf16[2048,512]{1,0:T(8,128)(2,1)}, bf16[2048,512]{1,0:T(8,128)(2,1)}, bf16[2048,512]{1,0:T(8,128)(2,1)}, bf16[32,2,256,128]{3,2,1,0:T(8,128)(2,1)}...) custom-call(s32[64]{0:T(128)} %get-tuple-element.84.refs_0_, ...), custom_call_target="tpu_custom_call", output_to_operand_aliasing={{0}: (19, {}), {1}: (20, {}), {2}: (21, {}), {3}: (22, {}),... | custom-call | flops 12000000 | bytes 12000 | tf_op jit(solution)/shard_map/forward/pallas_call | solution.py:857
  162.0 1.6 copy-done.6
  163.6 3.1 restore.1
  166.7 4.6 %halve_step.4 = (bf16[640,512]{1,0:T(8,128)(2,1)}, bf16[640,512]{1,0:T(8,128)(2,1)}, bf16[512,512]{1,0:T(8,128)(2,1)}, bf16[512,512]{1,0:T(8,128)(2,1)}) custom-call(s32[2]{0:T(128)} %pad_add_fusion.bits_ref, bf16[2304,512]{1,0:T(8,128)(2,1)} %get-tuple-element.113.refs_0_, bf16[2304,512]{1,0:T(8,128)(2,1)} %collective-permute-done.refs_1_, ...), custom_call_target="tpu_custom_call" | custom-call | bytes 4718 | tf_op jit(solution)/shard_map/halve_step/pallas_call | solution.py:1356
  171.4 1.6 collective-permute-start.1
  172.9 2.0 collective-permute-start.2
  175.0 8.9 %backward.3 = (bf16[2048,1536]{1,0:T(8,128)(2,1)}, bf16[2048,1024]{1,0:T(8,128)(2,1)}, f32[12,2,128]{2,1,0:T(2,128)}, bf16[1920,512]{1,0:T(8,128)(2,1)}) custom-call(s32[64]{0:T(128)} %get-tuple-element.93.refs_0_, s32[64]{0:T(128)} %get-tuple-element.94.refs_1_.place_ref, ...), custom_call_target="tpu_custom_call", output_to_operand_aliasing={{0}: (9, {}), {1}: (10, {})} | custom-call | flops 4800000 | bytes 12000 | tf_op jit(solution)/shard_map/backward/pallas_call | solution.py:1041
  183.9 6.1 %collective-permute-done.2.refs_2_.refs_5_ = bf16[512,512]{1,0:T(8,128)(2,1)S(1)} collective-permute-done((bf16[512,512]{1,0:T(8,128)(2,1)}, bf16[512,512]{1,0:T(8,128)(2,1)S(1)}, u32[]{:S(2)}, u32[]{:S(2)}) %collective-permute-start.2) | collective-permute-done | bytes 524320 | tf_op jit(solution)/shard_map/ppermute | solution.py:1275
  191.0 4.6 %all-to-all-start.4 = ((bf16[8,240,512]{2,1,0:T(8,128)(2,1)}), bf16[8,240,512]{2,1,0:T(8,128)(2,1)S(1)}, u32[]{:S(2)}, u32[]{:S(2)}) async-start(bf16[8,240,512]{2,1,0:T(8,128)(2,1)} %bitcast.71), calls=%async_computation.4 | async-start | bytes 3932160 | tf_op jit(solution)/shard_map/all_to_all | solution.py:1502
  195.7 14.8 %qkv_grads.1 = (bf16[2048,512]{1,0:T(8,128)(2,1)}, bf16[768,512]{1,0:T(8,128)(2,1)}, bf16[768,512]{1,0:T(8,128)(2,1)}) custom-call(s32[1]{0:T(128)} %bitcast.4.refs_2_.core_ref, bf16[2048,512]{1,0:T(8,128)(2,1)} %copy-done.1, bf16[2048,512]{1,0:T(8,128)(2,1)} %get-tuple-element.120.farx_hbm, bf16[2048,1536]{1,0:T(8,128)(2,1)} %get-tuple-element.121.dproj_hbm.token_ref, ...), custom_call_target="tpu_custom_call" | custom-call | flops 10000000 | bytes 25000 | tf_op jit(solution)/shard_map/qkv_grads/pallas_call | solution.py:1144
  210.6 2.6 collective-permute-done.3.refs_1_.refs_2_
  213.2 3.0 halve_step.5
  216.2 2.1 collective-permute-start.5
  218.3 1.5 collective-permute-start.4
  220.4 3.3 collective-permute-done.4.refs_3_
  223.7 7.4 %collective-permute-done.5.refs_7_ = bf16[256,512]{1,0:T(8,128)(2,1)S(1)} collective-permute-done((bf16[256,512]{1,0:T(8,128)(2,1)}, bf16[256,512]{1,0:T(8,128)(2,1)S(1)}, u32[]{:S(2)}, u32[]{:S(2)}) %collective-permute-start.5) | collective-permute-done | bytes 262176 | tf_op jit(solution)/shard_map/ppermute | solution.py:1275
  231.8 3.9 %halve_step.6 = (bf16[384,512]{1,0:T(8,128)(2,1)}, bf16[384,512]{1,0:T(8,128)(2,1)}, bf16[384,512]{1,0:T(8,128)(2,1)}, bf16[384,512]{1,0:T(8,128)(2,1)}) custom-call(s32[2]{0:T(128)} %pad_add_fusion.1.bits_ref, bf16[640,512]{1,0:T(8,128)(2,1)} %get-tuple-element.115.refs_11_.refs_0_, bf16[640,512]{1,0:T(8,128)(2,1)} %copy-done.30, ...), custom_call_target="tpu_custom_call" | custom-call | bytes 3145 | tf_op jit(solution)/shard_map/halve_step/pallas_call | solution.py:1356
  235.9 1.6 collective-permute-start.7
  239.4 1.9 all-to-all-done.4
  241.4 6.0 %sort_back.1 = (f32[72,512]{1,0:T(8,128)S(1)}, f32[64,512]{1,0:T(8,128)S(1)}) custom-call(s32[1]{0:T(128)} %bitcast.31.me_ref, s32[64]{0:T(128)S(1)} %copy-done.28, f32[6,64,64]{2,1,0:T(8,128)S(1)} %bitcast.57, f32[6,64,64]{2,1,0:T(8,128)S(1)} %copy-done.12, bf16[384,512]{1,0:T(8,128)(2,1)S(1)} %bitcast.58, bf16[64,512]{1,0:T(8,128)(2,1)S(1)} %bitcast.62, ...), custom_call_target="tpu_custom_call" | custom-call | flops 4915 | bytes 786 | tf_op jit(solution)/shard_map/sort_back/pallas_call | solution.py:550
  248.7 2.4 halve_step.7
  251.5 5.7 %base.1.refs_3_.refs_1_ = bf16[2048,512]{1,0:T(8,128)(2,1)} custom-call(bf16[2048,512]{1,0:T(8,128)(2,1)} %copy-done.1, bf16[2048,512]{1,0:T(8,128)(2,1)} %get-tuple-element.119.gmid_ref, bf16[2048,512]{1,0:T(8,128)(2,1)} %get-tuple-element.123.gn_ref, f32[64,512]{1,0:T(8,128)} %copy-done.18, f32[1,512]{1,0:T(1,128)} %bitcast.68), custom_call_target="tpu_custom_call" | custom-call | flops 20971 | bytes 8388 | tf_op jit(solution)/shard_map/base/pallas_call | solution.py:1187
  257.2 4.1 %collective-permute-done.8.refs_0_ = bf16[384,512]{1,0:T(8,128)(2,1)S(1)} collective-permute-done((bf16[384,512]{1,0:T(8,128)(2,1)}, bf16[384,512]{1,0:T(8,128)(2,1)S(1)}, u32[]{:S(2)}, u32[]{:S(2)}) %collective-permute-start.8) | collective-permute-done | bytes 393248 | tf_op jit(solution)/shard_map/ppermute | solution.py:1275
  263.2 2.3 collective-permute-start.9
  266.8 1.6 collective-permute-start.11
  269.3 1.6 copy-done.5
  270.9 1.5 copy-done.8
  272.5 10.8 %last.1 = (bf16[1024,512]{1,0:T(8,128)(2,1)}, bf16[1024,512]{1,0:T(8,128)(2,1)}) custom-call(s32[120]{0:T(128)S(1)} %convert_element_type.51.table_ref, s32[64]{0:T(128)S(1)} %copy-done.25, bf16[2048,512]{1,0:T(8,128)(2,1)} %bitcast.26.refs_3_.refs_0_, bf16[1920,512]{1,0:T(8,128)(2,1)S(1)} %bitcast.55, bf16[2048,512]{1,0:T(8,128)(2,1)S(1)} %copy-done.5, ...), custom_call_target="tpu_custom_call" | custom-call | flops 20971 | bytes 12582 | tf_op jit(solution)/shard_map/last/pallas_call | solution.py:1247
  285.9 1.8 collective-permute-start.12
  287.7 9.2 %collective-permute-done.12.refs_1_ = bf16[384,512]{1,0:T(8,128)(2,1)S(1)} collective-permute-done((bf16[384,512]{1,0:T(8,128)(2,1)S(1)}, bf16[384,512]{1,0:T(8,128)(2,1)S(1)}, u32[]{:S(2)}, u32[]{:S(2)}) %collective-permute-start.12) | collective-permute-done | bytes 393248 | tf_op jit(solution)/shard_map/ppermute | solution.py:1275
  298.5 8.9 %collective-permute-done.13.refs_1_ = bf16[384,512]{1,0:T(8,128)(2,1)S(1)} collective-permute-done((bf16[384,512]{1,0:T(8,128)(2,1)S(1)}, bf16[384,512]{1,0:T(8,128)(2,1)S(1)}, u32[]{:S(2)}, u32[]{:S(2)}) %collective-permute-start.13) | collective-permute-done | bytes 393248 | tf_op jit(solution)/shard_map/ppermute | solution.py:1275
  309.8 1.7 collective-permute-start.16
  311.4 15.0 %collective-permute-done.15.refs_1_ = bf16[768,512]{1,0:T(8,128)(2,1)S(1)} collective-permute-done((bf16[768,512]{1,0:T(8,128)(2,1)S(1)}, bf16[768,512]{1,0:T(8,128)(2,1)S(1)}, u32[]{:S(2)}, u32[]{:S(2)}) %collective-permute-start.15) | collective-permute-done | bytes 786464 | tf_op jit(solution)/shard_map/ppermute | solution.py:1275
  328.9 3.4 %assemble.2 = (f32[512,2048]{1,0:T(8,128)}, f32[2048,512]{1,0:T(8,128)}, f32[512,512]{1,0:T(8,128)}, f32[512,1536]{1,0:T(8,128)}, f32[8,512]{1,0:T(8,128)S(1)}) custom-call(s32[1]{0:T(128)} %bitcast.4.refs_2_.core_ref, bf16[3072,512]{1,0:T(8,128)(2,1)S(1)} %double_step.5.values_ref, bf16[512,2048]{1,0:T(8,128)(2,1)S(1)} %copy-done.2, ...), custom_call_target="tpu_custom_call" | custom-call | bytes 9437 | tf_op jit(solution)/shard_map/assemble/pallas_call | solution.py:1482
  332.3 1.5 collective-permute-done.17.values_ref
  333.9 3.4 %assemble.3 = (f32[512,2048]{1,0:T(8,128)}, f32[2048,512]{1,0:T(8,128)}, f32[512,512]{1,0:T(8,128)}, f32[512,1536]{1,0:T(8,128)}, f32[8,512]{1,0:T(8,128)S(1)}) custom-call(s32[1]{0:T(128)} %bitcast.4.refs_2_.core_ref, ...), custom_call_target="tpu_custom_call", output_to_operand_aliasing={{0}: (5, {}), {1}: (6, {}), {2}: (7, {}), {3}: (8, {})} | custom-call | bytes 9437 | tf_op jit(solution)/shard_map/assemble/pallas_call | solution.py:1482
  (149 shorter events, 32.3 us)
Async XLA Ops:
  25.7 24.3 %copy-start.35 = (f32[8,56,128]{2,1,0:T(8,128)}, f32[8,56,128]{2,1,0:T(8,128)S(1)}, u32[]{:S(2)}) copy-start(f32[8,56,128]{2,1,0:T(8,128)S(1)} %all_to_all.25) | copy-start | bytes 688132
  29.9 4.7 %copy-start.4 = (bf16[2048,512]{1,0:T(8,128)(2,1)S(1)}, bf16[2048,512]{1,0:T(8,128)(2,1)}, u32[]{:S(2)}) copy-start(bf16[2048,512]{1,0:T(8,128)(2,1)} %get-tuple-element.87.x_ref.refs_2_) | copy-start | bytes 6291460
  29.9 4.7 %copy-start.14 = (bf16[2,512,512]{2,1,0:T(8,128)(2,1)S(1)}, bf16[2,512,512]{2,1,0:T(8,128)(2,1)}, u32[]{:S(2)}) copy-start(bf16[2,512,512]{2,1,0:T(8,128)(2,1)} %param.26) | copy-start | bytes 3145732
  29.9 4.7 %copy-start.27 = (s32[64]{0:T(128)S(1)}, s32[64]{0:T(128)}, u32[]{:S(2)}) copy-start(s32[64]{0:T(128)} %get-tuple-element.83.perm_ref) | copy-start | bytes 772
  29.9 51.7 %all-to-all-start.1 = ((bf16[8,256,512]{2,1,0:T(8,128)(2,1)}), bf16[8,256,512]{2,1,0:T(8,128)(2,1)}, u32[]{:S(2)}, u32[]{:S(2)}) async-start(bf16[8,256,512]{2,1,0:T(8,128)(2,1)} %bitcast.73), calls=%async_computation.1 | async-start | bytes 4194304 | tf_op jit(solution)/shard_map/all_to_all | solution.py:1502
  40.3 9.4 %copy-start.16 = (f32[48,512]{1,0:T(8,128)S(1)}, f32[48,512]{1,0:T(8,128)}, u32[]{:S(2)}) copy-start(f32[48,512]{1,0:T(8,128)} %get-tuple-element.90.means_ref) | copy-start | bytes 294916
  40.3 9.4 %copy-start.20 = (f32[512]{0:T(512)S(1)}, f32[512]{0:T(512)}, u32[]{:S(2)}) copy-start(f32[512]{0:T(512)} %convert_element_type.44) | copy-start | bytes 6148
  58.7 27.5 %copy-start.40 = (bf16[512]{0:T(512)(128)(2,1)S(1)}, bf16[512]{0:T(512)(128)(2,1)}, u32[]{:S(2)}) copy-start(bf16[512]{0:T(512)(128)(2,1)} %param.23) | copy-start | bytes 3076
  81.6 50.6 %all-to-all-start.2 = ((bf16[8,240,512]{2,1,0:T(8,128)(2,1)}), bf16[8,240,512]{2,1,0:T(8,128)(2,1)}, u32[]{:S(2)}, u32[]{:S(2)}) async-start(bf16[8,240,512]{2,1,0:T(8,128)(2,1)} %bitcast.20), calls=%async_computation.2 | async-start | bytes 3932160 | tf_op jit(solution)/shard_map/all_to_all | solution.py:1502
  132.2 57.9 %all-to-all-start.3 = ((bf16[8,256,512]{2,1,0:T(8,128)(2,1)}), bf16[8,256,512]{2,1,0:T(8,128)(2,1)}, u32[]{:S(2)}, u32[]{:S(2)}) async-start(bf16[8,256,512]{2,1,0:T(8,128)(2,1)} %bitcast.72), calls=%async_computation.3 | async-start | bytes 4194304 | tf_op jit(solution)/shard_map/all_to_all | solution.py:1502
  161.3 5.5 %collective-permute-start = (bf16[2304,512]{1,0:T(8,128)(2,1)}, bf16[2304,512]{1,0:T(8,128)(2,1)}, u32[]{:S(2)}, u32[]{:S(2)}) collective-permute-start(bf16[2304,512]{1,0:T(8,128)(2,1)} %get-tuple-element.114), channel_id=1, source_target_pairs={{0,8},{8,0},{16,24},{24,16},{1,9},{9,1},{17,25},{25,17},{2,10},{10... | collective-permute-start | bytes 7077896 | tf_op jit(solution)/shard_map/ppermute | solution.py:1275
  171.4 18.6 %collective-permute-start.1 = (bf16[640,512]{1,0:T(8,128)(2,1)}, bf16[640,512]{1,0:T(8,128)(2,1)S(1)}, u32[]{:S(2)}, u32[]{:S(2)}) collective-permute-start(bf16[640,512]{1,0:T(8,128)(2,1)} %get-tuple-element.117), channel_id=1, source_target_pairs={{0,16},{8,24},{16,0},{24,8},{1,17},{9,25},{17,1},{25,9},{2,18},{10... | collective-permute-start | bytes 1966088 | tf_op jit(solution)/shard_map/ppermute | solution.py:1275
  172.9 17.1 %collective-permute-start.2 = (bf16[512,512]{1,0:T(8,128)(2,1)}, bf16[512,512]{1,0:T(8,128)(2,1)S(1)}, u32[]{:S(2)}, u32[]{:S(2)}) collective-permute-start(bf16[512,512]{1,0:T(8,128)(2,1)} %get-tuple-element.118), channel_id=1, source_target_pairs={{0,1},{1,0},{2,3},{3,2},{4,5},{5,4},{6,7},{7,6},{8,9},{9,8},{10,11... | collective-permute-start | bytes 1572872 | tf_op jit(solution)/shard_map/ppermute | solution.py:1275
  191.0 50.3 %all-to-all-start.4 = ((bf16[8,240,512]{2,1,0:T(8,128)(2,1)}), bf16[8,240,512]{2,1,0:T(8,128)(2,1)S(1)}, u32[]{:S(2)}, u32[]{:S(2)}) async-start(bf16[8,240,512]{2,1,0:T(8,128)(2,1)} %bitcast.71), calls=%async_computation.4 | async-start | bytes 3932160 | tf_op jit(solution)/shard_map/all_to_all | solution.py:1502
  210.5 2.7 collective-permute-start.3
  216.2 14.9 %collective-permute-start.5 = (bf16[256,512]{1,0:T(8,128)(2,1)}, bf16[256,512]{1,0:T(8,128)(2,1)S(1)}, u32[]{:S(2)}, u32[]{:S(2)}) collective-permute-start(bf16[256,512]{1,0:T(8,128)(2,1)} %get-tuple-element.130), channel_id=1, source_target_pairs={{0,1},{1,0},{2,3},{3,2},{4,5},{5,4},{6,7},{7,6},{8,9},{9,8},{10,11... | collective-permute-start | bytes 786440 | tf_op jit(solution)/shard_map/ppermute | solution.py:1275
  218.3 5.5 %collective-permute-start.4 = (bf16[128,512]{1,0:T(8,128)(2,1)}, bf16[128,512]{1,0:T(8,128)(2,1)S(1)}, u32[]{:S(2)}, u32[]{:S(2)}) collective-permute-start(bf16[128,512]{1,0:T(8,128)(2,1)} %get-tuple-element.127), channel_id=1, source_target_pairs={{0,16},{8,24},{16,0},{24,8},{1,17},{9,25},{17,1},{25,9},{2,18},{10... | collective-permute-start | bytes 393224 | tf_op jit(solution)/shard_map/ppermute | solution.py:1275
  223.7 7.4 %copy-start.38 = (bf16[128,512]{1,0:T(8,128)(2,1)}, bf16[128,512]{1,0:T(8,128)(2,1)S(1)}, u32[]{:S(2)}) copy-start(bf16[128,512]{1,0:T(8,128)(2,1)S(1)} %collective-permute-done.4.refs_3_) | copy-start | bytes 393220
  231.8 9.5 %copy-start.19 = (bf16[512,64]{0,1:T(8,128)(2,1)S(1)}, bf16[512,64]{0,1:T(8,128)(2,1)}, u32[]{:S(2)}) copy-start(bf16[512,64]{0,1:T(8,128)(2,1)} %param.22) | copy-start | bytes 196612
  235.7 5.6 %copy-start.11 = (f32[6,64,128]{2,1,0:T(8,128)S(1)}, f32[6,64,128]{2,1,0:T(8,128)}, u32[]{:S(2)}) copy-start(f32[6,64,128]{2,1,0:T(8,128)} %copy-done.10) | copy-start | bytes 589828
  235.8 5.6 %copy-start.12 = (f32[6,64,64]{2,1,0:T(8,128)S(1)}, f32[6,64,64]{2,1,0:T(8,128)}, u32[]{:S(2)}) copy-start(f32[6,64,64]{2,1,0:T(8,128)} %fusion.picked_ref) | copy-start | bytes 294916
  235.8 5.6 %copy-start.13 = (bf16[384,512]{1,0:T(8,128)(2,1)S(1)}, bf16[384,512]{1,0:T(8,128)(2,1)}, u32[]{:S(2)}) copy-start(bf16[384,512]{1,0:T(8,128)(2,1)} %get-tuple-element.131.token_ref.refs_0_) | copy-start | bytes 1179652
  235.8 5.6 %copy-start.17 = (f32[48,512]{1,0:T(8,128)S(1)}, f32[48,512]{1,0:T(8,128)}, u32[]{:S(2)}) copy-start(f32[48,512]{1,0:T(8,128)} %get-tuple-element.90.means_ref) | copy-start | bytes 294916
  235.8 5.6 %copy-start.21 = (f32[512]{0:T(512)S(1)}, f32[512]{0:T(512)}, u32[]{:S(2)}) copy-start(f32[512]{0:T(512)} %convert_element_type.44) | copy-start | bytes 6148
  235.8 5.6 %copy-start.28 = (s32[64]{0:T(128)S(1)}, s32[64]{0:T(128)}, u32[]{:S(2)}) copy-start(s32[64]{0:T(128)} %get-tuple-element.83.perm_ref) | copy-start | bytes 772
  235.8 12.9 %collective-permute-start.6 = (bf16[384,512]{1,0:T(8,128)(2,1)}, bf16[384,512]{1,0:T(8,128)(2,1)}, u32[]{:S(2)}, u32[]{:S(2)}) collective-permute-start(bf16[384,512]{1,0:T(8,128)(2,1)} %get-tuple-element.135), channel_id=1, source_target_pairs={{0,1},{1,0},{2,3},{3,2},{4,5},{5,4},{6,7},{7,6},{8,9},{9,8},{10,11... | collective-permute-start | bytes 1179656 | tf_op jit(solution)/shard_map/ppermute | solution.py:1275
  235.9 12.8 %collective-permute-start.7 = (bf16[384,512]{1,0:T(8,128)(2,1)}, bf16[384,512]{1,0:T(8,128)(2,1)}, u32[]{:S(2)}, u32[]{:S(2)}) collective-permute-start(bf16[384,512]{1,0:T(8,128)(2,1)} %get-tuple-element.137), channel_id=1, source_target_pairs={{0,16},{8,24},{16,0},{24,8},{1,17},{9,25},{17,1},{25,9},{2,18},{10... | collective-permute-start | bytes 1179656 | tf_op jit(solution)/shard_map/ppermute | solution.py:1275
  241.3 9.8 %copy-start.7 = (bf16[8,240,512]{2,1,0:T(8,128)(2,1)}, bf16[8,240,512]{2,1,0:T(8,128)(2,1)S(1)}, u32[]{:S(2)}) copy-start(bf16[8,240,512]{2,1,0:T(8,128)(2,1)S(1)} %all-to-all-done.4) | copy-start | bytes 5898244
  251.1 10.2 %collective-permute-start.8 = (bf16[384,512]{1,0:T(8,128)(2,1)}, bf16[384,512]{1,0:T(8,128)(2,1)S(1)}, u32[]{:S(2)}, u32[]{:S(2)}) collective-permute-start(bf16[384,512]{1,0:T(8,128)(2,1)} %get-tuple-element.139), channel_id=1, source_target_pairs={{0,2},{1,3},{2,0},{3,1},{4,6},{5,7},{6,4},{7,5},{8,10},{9,11},{10,... | collective-permute-start | bytes 1179656 | tf_op jit(solution)/shard_map/ppermute | solution.py:1275
  257.2 4.9 %copy-start.36 = (bf16[384,512]{1,0:T(8,128)(2,1)S(1)}, bf16[384,512]{1,0:T(8,128)(2,1)}, u32[]{:S(2)}) copy-start(bf16[384,512]{1,0:T(8,128)(2,1)} %get-tuple-element.138) | copy-start | bytes 1179652
  257.2 8.3 %copy-start.24 = (f32[72,512]{1,0:T(8,128)S(1)}, f32[72,512]{1,0:T(8,128)}, u32[]{:S(2)}) copy-start(f32[72,512]{1,0:T(8,128)} %copy-done.23) | copy-start | bytes 442372
  257.2 12.1 %copy-start.3 = (bf16[2048,512]{1,0:T(8,128)(2,1)S(1)}, bf16[2048,512]{1,0:T(8,128)(2,1)}, u32[]{:S(2)}) copy-start(bf16[2048,512]{1,0:T(8,128)(2,1)} %base.1.refs_3_.refs_1_) | copy-start | bytes 6291460
  257.2 12.1 %copy-start.22 = (f32[512]{0:T(512)S(1)}, f32[512]{0:T(512)}, u32[]{:S(2)}) copy-start(f32[512]{0:T(512)} %convert_element_type.44) | copy-start | bytes 6148
  257.2 12.1 %copy-start.25 = (s32[64]{0:T(128)S(1)}, s32[64]{0:T(128)}, u32[]{:S(2)}) copy-start(s32[64]{0:T(128)} %get-tuple-element.94.refs_1_.place_ref) | copy-start | bytes 772
  263.2 20.8 %collective-permute-start.9 = (bf16[384,512]{1,0:T(8,128)(2,1)S(1)}, bf16[384,512]{1,0:T(8,128)(2,1)S(1)}, u32[]{:S(2)}, u32[]{:S(2)}) collective-permute-start(bf16[384,512]{1,0:T(8,128)(2,1)S(1)} %add_convert_fusion.1), channel_id=1, source_target_pairs={{0,4},{1,5},{2,6},{3,7},{4,0},{5,1},{6,2},{7,3},{8,12},{9,13},{10,... | collective-permute-start | bytes 1179656 | tf_op jit(solution)/shard_map/ppermute | solution.py:1275
  265.4 1.4 collective-permute-start.10
  266.8 16.5 %collective-permute-start.11 = (f32[72,512]{1,0:T(8,128)S(1)}, f32[72,512]{1,0:T(8,128)S(1)}, u32[]{:S(2)}, u32[]{:S(2)}) collective-permute-start(f32[72,512]{1,0:T(8,128)S(1)} %add.43), channel_id=1, source_target_pairs={{0,16},{8,24},{16,0},{24,8},{1,17},{9,25},{17,1},{25,9},{2,18},{10... | collective-permute-start | bytes 442376 | tf_op jit(solution)/shard_map/ppermute | solution.py:1275
  283.3 24.3 %copy-start.29 = (s32[2]{0:T(128)S(1)}, s32[2]{0:T(128)}, u32[]{:S(2)}) copy-start(s32[2]{0:T(128)} %pad_add_fusion.1.bits_ref) | copy-start | bytes 28
  284.8 42.4 %copy-start.26 = (s32[2]{0:T(128)S(1)}, s32[2]{0:T(128)}, u32[]{:S(2)}) copy-start(s32[2]{0:T(128)} %pad_add_fusion.bits_ref) | copy-start | bytes 28
  285.9 11.0 %collective-permute-start.12 = (bf16[384,512]{1,0:T(8,128)(2,1)S(1)}, bf16[384,512]{1,0:T(8,128)(2,1)S(1)}, u32[]{:S(2)}, u32[]{:S(2)}) collective-permute-start(bf16[384,512]{1,0:T(8,128)(2,1)S(1)} %add_convert_fusion.refs_0_), channel_id=1, source_target_pairs={{0,2},{1,3},{2,0},{3,1},{4,6},{5,7},{6,4},{7,5},{8,10},{9,11},{10,... | collective-permute-start | bytes 1179656 | tf_op jit(solution)/shard_map/ppermute | solution.py:1275
  297.3 10.1 %collective-permute-start.13 = (bf16[384,512]{1,0:T(8,128)(2,1)S(1)}, bf16[384,512]{1,0:T(8,128)(2,1)S(1)}, u32[]{:S(2)}, u32[]{:S(2)}) collective-permute-start(bf16[384,512]{1,0:T(8,128)(2,1)S(1)} %get-tuple-element.141.refs_0_), channel_id=1, source_target_pairs={{0,1},{1,0},{2,3},{3,2},{4,5},{5,4},{6,7},{7,6},{8,9},{9,8},{10,11... | collective-permute-start | bytes 1179656 | tf_op jit(solution)/shard_map/ppermute | solution.py:1275
  297.9 9.7 %collective-permute-start.14 = (bf16[384,512]{1,0:T(8,128)(2,1)S(1)}, bf16[384,512]{1,0:T(8,128)(2,1)S(1)}, u32[]{:S(2)}, u32[]{:S(2)}) collective-permute-start(bf16[384,512]{1,0:T(8,128)(2,1)S(1)} %get-tuple-element.142.refs_2_), channel_id=1, source_target_pairs={{0,16},{8,24},{16,0},{24,8},{1,17},{9,25},{17,1},{25,9},{2,18},{10... | collective-permute-start | bytes 1179656 | tf_op jit(solution)/shard_map/ppermute | solution.py:1275
  309.1 17.3 %collective-permute-start.15 = (bf16[768,512]{1,0:T(8,128)(2,1)S(1)}, bf16[768,512]{1,0:T(8,128)(2,1)S(1)}, u32[]{:S(2)}, u32[]{:S(2)}) collective-permute-start(bf16[768,512]{1,0:T(8,128)(2,1)S(1)} %get-tuple-element.143.refs_0_), channel_id=1, source_target_pairs={{0,16},{8,24},{16,0},{24,8},{1,17},{9,25},{17,1},{25,9},{2,18},{10... | collective-permute-start | bytes 2359304 | tf_op jit(solution)/shard_map/ppermute | solution.py:1275
  309.8 18.5 %copy-start.34 = (f32[72,512]{1,0:T(8,128)S(1)}, f32[72,512]{1,0:T(8,128)}, u32[]{:S(2)}) copy-start(f32[72,512]{1,0:T(8,128)} %add.44.refs_2_) | copy-start | bytes 442372
  309.8 19.1 %copy-start = (bf16[512,1536]{1,0:T(8,128)(2,1)S(1)}, bf16[512,1536]{1,0:T(8,128)(2,1)}, u32[]{:S(2)}) copy-start(bf16[512,1536]{1,0:T(8,128)(2,1)} %wqkv_ref.3) | copy-start | bytes 4718596
  309.8 19.1 %copy-start.2 = (bf16[512,2048]{1,0:T(8,128)(2,1)S(1)}, bf16[512,2048]{1,0:T(8,128)(2,1)}, u32[]{:S(2)}) copy-start(bf16[512,2048]{1,0:T(8,128)(2,1)} %wup_ref.3) | copy-start | bytes 6291460
  309.8 17.4 %collective-permute-start.16 = (bf16[768,512]{1,0:T(8,128)(2,1)S(1)}, bf16[768,512]{1,0:T(8,128)(2,1)S(1)}, u32[]{:S(2)}, u32[]{:S(2)}) collective-permute-start(bf16[768,512]{1,0:T(8,128)(2,1)S(1)} %get-tuple-element.144.refs_2_), channel_id=1, source_target_pairs={{0,1},{1,0},{2,3},{3,2},{4,5},{5,4},{6,7},{7,6},{8,9},{9,8},{10,11... | collective-permute-start | bytes 2359304 | tf_op jit(solution)/shard_map/ppermute | solution.py:1275
  328.2 5.7 %collective-permute-start.17 = (bf16[3072,512]{1,0:T(8,128)(2,1)S(1)}, bf16[3072,512]{1,0:T(8,128)(2,1)S(1)}, u32[]{:S(2)}, u32[]{:S(2)}) collective-permute-start(bf16[3072,512]{1,0:T(8,128)(2,1)S(1)} %double_step.5.values_ref), channel_id=1, source_target_pairs={{0,8},{8,0},{16,24},{24,16},{1,9},{9,1},{17,25},{25,17},{2,10},{10... | collective-permute-start | bytes 9437192 | tf_op jit(solution)/shard_map/ppermute | solution.py:1275
  (17 other events, 25.4 us)

commit v5 on v4

--- a/solution.py
+++ b/solution.py
@@ -1691,22 +1691,30 @@
         ranges_three = [
             (0, 0, cuts[0], 0, 0, 0),
             (0, cuts[0], cuts[1], 0, 0, cuts[0] // 2),
-            (1, 0, cuts[2], 0, 0, (cuts[0] + cuts[1]) // 2),
-            (1, cuts[2], cuts[3], 0, 0, (cuts[0] + cuts[1] + cuts[2]) // 2),
+            (1, 0, cuts[2], 0, 1, 0),
+            (1, cuts[2], cuts[3], 0, 1, cuts[2] // 2),
         ]
-        ((total, gz),) = halve_step(
+        (zx, gx), (zy, gy) = halve_step(
             ranges_three, [AXIS_Z0], [(vx, vx_came), (vy, vy_came)], spread
         )
     base = base_rows(xp, gmid, gn, spread, gain1)
     if fast:
-        total = add(total, tie(swap(gz, *AXIS_Z0), base))
+        zx_came, zy_came = swap(gx, *AXIS_Z0), swap(gy, *AXIS_Z0)
+        zx = add(zx, tie(zx_came, base, zy_came))
+        zx_came = swap(zx, *AXIS_Z1)
+        zy = add(zy, zy_came)
+        zy_came = swap(zy, *AXIS_Z1)
 
     gx_a, gx_b = last(back_table, place, back, sizes, extra, sum(sizes), x, base, gain1, total_a)
     if fast:
         for bit in (0, 1):
             small = small + swap(small, "dp", bit)
-        total = add(total, tie(swap(total, *AXIS_Z1), gx_a, small))
-        vx, vy = double_step(ranges_three, [AXIS_Z0], [(total, swap(total, *AXIS_Z0))])
+        zx, zy = add(zx, tie(zx_came, small)), add(zy, zy_came)
+        vx, vy = double_step(
+            ranges_three,
+            [AXIS_Z0],
+            [(zx, swap(zx, *AXIS_Z0)), (zy, swap(zy, *AXIS_Z0))],
+        )
         ranges_back = [
             (0, 0, nbx, 0, 0, 0),
             (0, nbx, nlx, 0, 0, cuts[0]),
@@ -1729,6 +1737,7 @@
             ranges_all,
             [AXIS_X, AXIS_Y],
             [(vx, swap(vx, *AXIS_X)), (vy, swap(vy, *AXIS_Y))],
+            gx_a,
         )
     else:
         across = [("dp", bit) for bit in range(1, bits_of(lax.axis_size("dp")))]

time: 345 us -> 343 us (level)
  waiting for transfers between devices: 85.2 us -> 78.2 us
    ppermute x18 -> x21, waiting for transfers between devices: 60.4 us -> 53.4 us  [swap(): return lax.ppermute(values, axis, [(i, i ^ 1 << bit) for i in range(size)])]
    unnamed x84 -> x90, local copies, waits for them, and re-layouts: 13.2 us -> 14.3 us
    ppermute x18 -> x21, starting transfers between devices: 18.6 us -> 19.1 us  [swap(): return lax.ppermute(values, axis, [(i, i ^ 1 << bit) for i in range(size)])]
  transfers between devices with their start and end apart: 22 -> 25, of which waited for: 14 -> 15; matrix products, arithmetic and copies ran while one was open for 3% -> 4% of each run, Pallas kernels for 44% -> 44%
where the time goes in v5:
time: 343 us; the launch traced here: 336 us
  Pallas kernels  171 us (50%)
  waiting for transfers between devices  78.2 us (23%)
  starting transfers between devices  39.2 us (11%)
  local copies, waits for them, and re-layouts  20.6 us (6%)
  blocking collectives  15.7 us (5%)
  other arithmetic  9.44 us (3%)
    pallas_call x2, Pallas kernels, forward(): pl.pallas_call(functools.partial(forward_kernel, first_group, groups, len...  56.6 us
    ppermute x21, waiting for transfers between devices, swap(): return lax.ppermute(values, axis, [(i, i ^ 1 << bit) for i in range(size)])  53.4 us
    all_to_all x4, waiting for transfers between devices, exchange(): lax.all_to_all(parts, 'blk', split_axis=0, concat_axis=0, tiled=True)  24.8 us
    pallas_call x2, Pallas kernels, backward(): pl.pallas_call(functools.partial(backward_kernel, first_group, groups, pr...  20.5 us
    all_to_all x4, starting transfers between devices, exchange(): lax.all_to_all(parts, 'blk', split_axis=0, concat_axis=0, tiled=True)  20.1 us
    ppermute x21, starting transfers between devices, swap(): return lax.ppermute(values, axis, [(i, i ^ 1 << bit) for i in range(size)])  19.1 us
    all_to_all x1, blocking collectives, per_device(): news = lax.all_to_all(news, 'blk', split_axis=0, concat_axis=0, tiled=True)  15.7 us
    pallas_call x1, Pallas kernels, qkv_grads(): pl.pallas_call(qkv_kernel, in_specs=[SMEM] + [ANY] * 4 + [VMEM, ANY, ANY]...  14.8 us
  transfers between devices with their start and end apart: 25, of which 15 were waited for; matrix products, arithmetic and copies ran while one was open for 4% of the time, Pallas kernels for 44%

profile of v5, /device:TPU:0, one launch (start us, length us, event | category | flops | bytes accessed | tf_op | source)
XLA Modules:
  0.0 336.1 jit_solution(6004758582360772090)
XLA Ops:
  1.9 8.0 %digest.1 = (bf16[2048,512]{1,0:T(8,128)(2,1)}, f32[48,512]{1,0:T(8,128)}, f32[8,56,128]{2,1,0:T(8,128)}, s32[64]{0:T(128)}, s32[64]{0:T(128)}, /*index=5*/s32[64]{0:T(128)}, s32[64]{0:T(128)}, s32[2]{0:T(128)}) custom-call(s32[2,8]{1,0:T(2,128)} %sela_ref.1, s32[4,8]{1,0:T(4,128)} %selb_ref.1, bf16[1024,512]{1,0:T(8,128)(2,1)} %bitcast.76, ...), custom_call_target="tpu_custom_call" | custom-call | flops 10485 | bytes 4194 | tf_op jit(solution)/shard_map/digest/pallas_call | solution.py:277
  9.9 15.7 %all_to_all.25 = f32[8,56,128]{2,1,0:T(8,128)S(1)} all-to-all(f32[8,56,128]{2,1,0:T(8,128)} %get-tuple-element.88), channel_id=1, replica_groups=mesh['dp'=4,'blk'=8] {'blk'}, dimensions={0} | all-to-all | bytes 458752 | tf_op jit(solution)/shard_map/all_to_all | solution.py:1552
  26.3 3.6 %pack.1 = (bf16[2048,512]{1,0:T(8,128)(2,1)}, bf16[1920,512]{1,0:T(8,128)(2,1)}) custom-call(s32[112]{0:T(128)} %convert_element_type.64.table_ref, bf16[2048,512]{1,0:T(8,128)(2,1)} %get-tuple-element.89.x_ref.refs_2_), custom_call_target="tpu_custom_call" | custom-call | bytes 6291 | tf_op jit(solution)/shard_map/pack/pallas_call | solution.py:340
  29.9 4.6 %all-to-all-start.1 = ((bf16[8,256,512]{2,1,0:T(8,128)(2,1)}), bf16[8,256,512]{2,1,0:T(8,128)(2,1)}, u32[]{:S(2)}, u32[]{:S(2)}) async-start(bf16[8,256,512]{2,1,0:T(8,128)(2,1)} %bitcast.74), calls=%async_computation.1 | async-start | bytes 4194304 | tf_op jit(solution)/shard_map/all_to_all | solution.py:1502
  35.8 1.9 arrange.1
  40.3 9.4 %project.1.refs_2_.refs_6_.refs_7_ = bf16[2048,1536]{1,0:T(8,128)(2,1)} custom-call(bf16[2048,512]{1,0:T(8,128)(2,1)} %copy-done.1, f32[1,512]{1,0:T(1,128)} %bitcast.65, bf16[512,1536]{1,0:T(8,128)(2,1)} %wqkv_ref.3), custom_call_target="tpu_custom_call" | custom-call | flops 3221225 | bytes 8388 | tf_op jit(solution)/shard_map/project/pallas_call | solution.py:436
  51.1 3.7 %sinkhorn.1 = f32[6,64,128]{2,1,0:T(8,128)} custom-call(f32[6,64,64]{2,1,0:T(8,128)} %bitcast.56, f32[6,64,64]{2,1,0:T(8,128)} %fusion.picked_ref), custom_call_target="tpu_custom_call" | custom-call | flops 2457 | bytes 786 | tf_op jit(solution)/shard_map/sinkhorn/pallas_call | solution.py:465
  58.7 22.9 %all-to-all-done.1 = bf16[8,256,512]{2,1,0:T(8,128)(2,1)} async-done(((bf16[8,256,512]{2,1,0:T(8,128)(2,1)}), bf16[8,256,512]{2,1,0:T(8,128)(2,1)}, u32[]{:S(2)}, u32[]{:S(2)}) %all-to-all-start.1) | async-done | bytes 2097184 | tf_op jit(solution)/shard_map/all_to_all | solution.py:1502
  81.6 4.6 %all-to-all-start.2 = ((bf16[8,240,512]{2,1,0:T(8,128)(2,1)}), bf16[8,240,512]{2,1,0:T(8,128)(2,1)}, u32[]{:S(2)}, u32[]{:S(2)}) async-start(bf16[8,240,512]{2,1,0:T(8,128)(2,1)} %bitcast.20), calls=%async_computation.2 | async-start | bytes 3932160 | tf_op jit(solution)/shard_map/all_to_all | solution.py:1502
  86.8 33.7 %forward.2 = (bf16[2048,512]{1,0:T(8,128)(2,1)}, bf16[2048,512]{1,0:T(8,128)(2,1)}, bf16[2048,512]{1,0:T(8,128)(2,1)}, bf16[32,2,256,128]{3,2,1,0:T(8,128)(2,1)}...) custom-call(s32[64]{0:T(128)} %get-tuple-element.86.refs_0_, ...), custom_call_target="tpu_custom_call" | custom-call | flops 20000000 | bytes 20000 | tf_op jit(solution)/shard_map/forward/pallas_call | solution.py:857
  120.5 11.6 %backward.2 = (bf16[2048,1536]{1,0:T(8,128)(2,1)}, bf16[2048,1024]{1,0:T(8,128)(2,1)}, f32[20,2,128]{2,1,0:T(2,128)}, bf16[2048,512]{1,0:T(8,128)(2,1)}) custom-call(s32[64]{0:T(128)} %get-tuple-element.95.refs_0_, s32[64]{0:T(128)} %get-tuple-element.96.refs_1_.place_ref, bf16[2048,1536]{1,0:T(8,128)(2,1)} %project.1.refs_2_.refs_6_.refs_7_, ...), custom_call_target="tpu_custom_call" | custom-call | flops 8000000 | bytes 20000 | tf_op jit(solution)/shard_map/backward/pallas_call | solution.py:1041
  132.2 6.3 %all-to-all-start.3 = ((bf16[8,256,512]{2,1,0:T(8,128)(2,1)}), bf16[8,256,512]{2,1,0:T(8,128)(2,1)}, u32[]{:S(2)}, u32[]{:S(2)}) async-start(bf16[8,256,512]{2,1,0:T(8,128)(2,1)} %bitcast.73), calls=%async_computation.3 | async-start | bytes 4194304 | tf_op jit(solution)/shard_map/all_to_all | solution.py:1502
  138.5 22.8 %forward.3 = (bf16[2048,512]{1,0:T(8,128)(2,1)}, bf16[2048,512]{1,0:T(8,128)(2,1)}, bf16[2048,512]{1,0:T(8,128)(2,1)}, bf16[32,2,256,128]{3,2,1,0:T(8,128)(2,1)}...) custom-call(s32[64]{0:T(128)} %get-tuple-element.86.refs_0_, ...), custom_call_target="tpu_custom_call", output_to_operand_aliasing={{0}: (19, {}), {1}: (20, {}), {2}: (21, {}), {3}: (22, {}),... | custom-call | flops 12000000 | bytes 12000 | tf_op jit(solution)/shard_map/forward/pallas_call | solution.py:857
  161.9 1.6 copy-done.6
  163.5 3.1 restore.1
  166.7 4.6 %halve_step.4 = (bf16[640,512]{1,0:T(8,128)(2,1)}, bf16[640,512]{1,0:T(8,128)(2,1)}, bf16[512,512]{1,0:T(8,128)(2,1)}, bf16[512,512]{1,0:T(8,128)(2,1)}) custom-call(s32[2]{0:T(128)} %pad_add_fusion.bits_ref, bf16[2304,512]{1,0:T(8,128)(2,1)} %get-tuple-element.115.refs_0_, bf16[2304,512]{1,0:T(8,128)(2,1)} %collective-permute-done.refs_1_, ...), custom_call_target="tpu_custom_call" | custom-call | bytes 4718 | tf_op jit(solution)/shard_map/halve_step/pallas_call | solution.py:1356
  171.3 1.6 collective-permute-start.1
  172.9 2.0 collective-permute-start.2
  174.9 8.9 %backward.3 = (bf16[2048,1536]{1,0:T(8,128)(2,1)}, bf16[2048,1024]{1,0:T(8,128)(2,1)}, f32[12,2,128]{2,1,0:T(2,128)}, bf16[1920,512]{1,0:T(8,128)(2,1)}) custom-call(s32[64]{0:T(128)} %get-tuple-element.95.refs_0_, s32[64]{0:T(128)} %get-tuple-element.96.refs_1_.place_ref, ...), custom_call_target="tpu_custom_call", output_to_operand_aliasing={{0}: (9, {}), {1}: (10, {})} | custom-call | flops 4800000 | bytes 12000 | tf_op jit(solution)/shard_map/backward/pallas_call | solution.py:1041
  183.9 6.1 %collective-permute-done.2.refs_2_.refs_5_ = bf16[512,512]{1,0:T(8,128)(2,1)S(1)} collective-permute-done((bf16[512,512]{1,0:T(8,128)(2,1)}, bf16[512,512]{1,0:T(8,128)(2,1)S(1)}, u32[]{:S(2)}, u32[]{:S(2)}) %collective-permute-start.2) | collective-permute-done | bytes 524320 | tf_op jit(solution)/shard_map/ppermute | solution.py:1275
  191.0 4.6 %all-to-all-start.4 = ((bf16[8,240,512]{2,1,0:T(8,128)(2,1)}), bf16[8,240,512]{2,1,0:T(8,128)(2,1)S(1)}, u32[]{:S(2)}, u32[]{:S(2)}) async-start(bf16[8,240,512]{2,1,0:T(8,128)(2,1)} %bitcast.72), calls=%async_computation.4 | async-start | bytes 3932160 | tf_op jit(solution)/shard_map/all_to_all | solution.py:1502
  195.7 14.8 %qkv_grads.1 = (bf16[2048,512]{1,0:T(8,128)(2,1)}, bf16[768,512]{1,0:T(8,128)(2,1)}, bf16[768,512]{1,0:T(8,128)(2,1)}) custom-call(s32[1]{0:T(128)} %bitcast.4.refs_2_.core_ref, bf16[2048,512]{1,0:T(8,128)(2,1)} %copy-done.1, bf16[2048,512]{1,0:T(8,128)(2,1)} %get-tuple-element.122.farx_hbm, bf16[2048,1536]{1,0:T(8,128)(2,1)} %get-tuple-element.123.dproj_hbm.token_ref, ...), custom_call_target="tpu_custom_call" | custom-call | flops 10000000 | bytes 25000 | tf_op jit(solution)/shard_map/qkv_grads/pallas_call | solution.py:1144
  210.5 2.6 collective-permute-done.3.refs_1_.refs_2_
  213.2 3.0 halve_step.5
  216.2 2.1 collective-permute-start.5
  220.3 3.4 collective-permute-done.4.refs_3_
  223.7 7.4 %collective-permute-done.5.refs_7_ = bf16[256,512]{1,0:T(8,128)(2,1)S(1)} collective-permute-done((bf16[256,512]{1,0:T(8,128)(2,1)}, bf16[256,512]{1,0:T(8,128)(2,1)S(1)}, u32[]{:S(2)}, u32[]{:S(2)}) %collective-permute-start.5) | collective-permute-done | bytes 262176 | tf_op jit(solution)/shard_map/ppermute | solution.py:1275
  231.8 3.9 %halve_step.6 = (bf16[384,512]{1,0:T(8,128)(2,1)}, bf16[384,512]{1,0:T(8,128)(2,1)}, bf16[384,512]{1,0:T(8,128)(2,1)}, bf16[384,512]{1,0:T(8,128)(2,1)}) custom-call(s32[2]{0:T(128)} %pad_add_fusion.1.bits_ref, bf16[640,512]{1,0:T(8,128)(2,1)} %get-tuple-element.117.refs_11_.refs_0_, bf16[640,512]{1,0:T(8,128)(2,1)} %copy-done.31, ...), custom_call_target="tpu_custom_call" | custom-call | bytes 3145 | tf_op jit(solution)/shard_map/halve_step/pallas_call | solution.py:1356
  239.4 1.9 all-to-all-done.4
  241.4 6.0 %sort_back.1 = (f32[72,512]{1,0:T(8,128)S(1)}, f32[64,512]{1,0:T(8,128)S(1)}) custom-call(s32[1]{0:T(128)} %bitcast.31.me_ref, s32[64]{0:T(128)S(1)} %copy-done.28, f32[6,64,64]{2,1,0:T(8,128)S(1)} %bitcast.57, f32[6,64,64]{2,1,0:T(8,128)S(1)} %copy-done.12, bf16[384,512]{1,0:T(8,128)(2,1)S(1)} %bitcast.58, bf16[64,512]{1,0:T(8,128)(2,1)S(1)} %bitcast.63, ...), custom_call_target="tpu_custom_call" | custom-call | flops 4915 | bytes 786 | tf_op jit(solution)/shard_map/sort_back/pallas_call | solution.py:550
  248.7 2.4 halve_step.7
  251.4 1.8 collective-permute-start.8
  253.2 5.7 %base.1.refs_3_.refs_1_ = bf16[2048,512]{1,0:T(8,128)(2,1)} custom-call(bf16[2048,512]{1,0:T(8,128)(2,1)} %copy-done.1, bf16[2048,512]{1,0:T(8,128)(2,1)} %get-tuple-element.121.gmid_ref, bf16[2048,512]{1,0:T(8,128)(2,1)} %get-tuple-element.125.gn_ref, f32[64,512]{1,0:T(8,128)} %copy-done.19, f32[1,512]{1,0:T(1,128)} %bitcast.69), custom_call_target="tpu_custom_call" | custom-call | flops 20971 | bytes 8388 | tf_op jit(solution)/shard_map/base/pallas_call | solution.py:1187
  259.0 1.5 collective-permute-start.12
  263.3 2.0 collective-permute-start.10
  266.0 10.5 %collective-permute-done.14 = bf16[192,512]{1,0:T(8,128)(2,1)S(1)} collective-permute-done((bf16[192,512]{1,0:T(8,128)(2,1)S(1)}, bf16[192,512]{1,0:T(8,128)(2,1)S(1)}, u32[]{:S(2)}, u32[]{:S(2)}) %collective-permute-start.14) | collective-permute-done | bytes 196640 | tf_op jit(solution)/shard_map/ppermute | solution.py:1275
  276.7 4.1 %collective-permute-done.10.refs_0_ = bf16[192,512]{1,0:T(8,128)(2,1)S(1)} collective-permute-done((bf16[192,512]{1,0:T(8,128)(2,1)S(1)}, bf16[192,512]{1,0:T(8,128)(2,1)S(1)}, u32[]{:S(2)}, u32[]{:S(2)}) %collective-permute-start.10) | collective-permute-done | bytes 196640 | tf_op jit(solution)/shard_map/ppermute | solution.py:1275
  282.5 2.4 collective-permute-done.15.refs_3_
  284.9 4.3 %collective-permute-done.13.refs_1_ = bf16[192,512]{1,0:T(8,128)(2,1)S(1)} collective-permute-done((bf16[192,512]{1,0:T(8,128)(2,1)S(1)}, bf16[192,512]{1,0:T(8,128)(2,1)S(1)}, u32[]{:S(2)}, u32[]{:S(2)}) %collective-permute-start.13) | collective-permute-done | bytes 196640 | tf_op jit(solution)/shard_map/ppermute | solution.py:1275
  292.4 8.1 %collective-permute-done.16.refs_1_ = bf16[384,512]{1,0:T(8,128)(2,1)S(1)} collective-permute-done((bf16[384,512]{1,0:T(8,128)(2,1)S(1)}, bf16[384,512]{1,0:T(8,128)(2,1)S(1)}, u32[]{:S(2)}, u32[]{:S(2)}) %collective-permute-start.16) | collective-permute-done | bytes 393248 | tf_op jit(solution)/shard_map/ppermute | solution.py:1275
  301.6 2.3 double_step.4
  306.1 1.6 copy-done.5
  307.7 1.5 copy-done.8
  309.2 10.9 %last.1 = (bf16[1024,512]{1,0:T(8,128)(2,1)}, bf16[1024,512]{1,0:T(8,128)(2,1)}) custom-call(s32[120]{0:T(128)S(1)} %convert_element_type.69.table_ref, s32[64]{0:T(128)S(1)} %copy-done.26, bf16[2048,512]{1,0:T(8,128)(2,1)} %bitcast.26.refs_3_.refs_0_, bf16[1920,512]{1,0:T(8,128)(2,1)S(1)} %bitcast.55, bf16[2048,512]{1,0:T(8,128)(2,1)S(1)} %copy-done.5, ...), custom_call_target="tpu_custom_call" | custom-call | flops 20971 | bytes 12582 | tf_op jit(solution)/shard_map/last/pallas_call | solution.py:1247
  323.1 2.8 double_step.5.values_ref
  326.6 3.4 %assemble.2 = (f32[512,2048]{1,0:T(8,128)}, f32[2048,512]{1,0:T(8,128)}, f32[512,512]{1,0:T(8,128)}, f32[512,1536]{1,0:T(8,128)}, f32[8,512]{1,0:T(8,128)S(1)}) custom-call(s32[1]{0:T(128)} %bitcast.4.refs_2_.core_ref, bf16[3072,512]{1,0:T(8,128)(2,1)S(1)} %double_step.5.values_ref, bf16[512,2048]{1,0:T(8,128)(2,1)S(1)} %copy-done.2, ...), custom_call_target="tpu_custom_call" | custom-call | bytes 9437 | tf_op jit(solution)/shard_map/assemble/pallas_call | solution.py:1482
  330.0 1.6 collective-permute-done.20.values_ref
  331.6 3.4 %assemble.3 = (f32[512,2048]{1,0:T(8,128)}, f32[2048,512]{1,0:T(8,128)}, f32[512,512]{1,0:T(8,128)}, f32[512,1536]{1,0:T(8,128)}, f32[8,512]{1,0:T(8,128)S(1)}) custom-call(s32[1]{0:T(128)} %bitcast.4.refs_2_.core_ref, ...), custom_call_target="tpu_custom_call", output_to_operand_aliasing={{0}: (5, {}), {1}: (6, {}), {2}: (7, {}), {3}: (8, {})} | custom-call | bytes 9437 | tf_op jit(solution)/shard_map/assemble/pallas_call | solution.py:1482
  (163 shorter events, 37.5 us)
Async XLA Ops:
  25.7 24.3 %copy-start.34 = (f32[8,56,128]{2,1,0:T(8,128)}, f32[8,56,128]{2,1,0:T(8,128)S(1)}, u32[]{:S(2)}) copy-start(f32[8,56,128]{2,1,0:T(8,128)S(1)} %all_to_all.25) | copy-start | bytes 688132
  29.9 4.7 %copy-start.4 = (bf16[2048,512]{1,0:T(8,128)(2,1)S(1)}, bf16[2048,512]{1,0:T(8,128)(2,1)}, u32[]{:S(2)}) copy-start(bf16[2048,512]{1,0:T(8,128)(2,1)} %get-tuple-element.89.x_ref.refs_2_) | copy-start | bytes 6291460
  29.9 4.7 %copy-start.14 = (bf16[2,512,512]{2,1,0:T(8,128)(2,1)S(1)}, bf16[2,512,512]{2,1,0:T(8,128)(2,1)}, u32[]{:S(2)}) copy-start(bf16[2,512,512]{2,1,0:T(8,128)(2,1)} %param.26) | copy-start | bytes 3145732
  29.9 4.7 %copy-start.27 = (s32[64]{0:T(128)S(1)}, s32[64]{0:T(128)}, u32[]{:S(2)}) copy-start(s32[64]{0:T(128)} %get-tuple-element.85.perm_ref) | copy-start | bytes 772
  29.9 51.7 %all-to-all-start.1 = ((bf16[8,256,512]{2,1,0:T(8,128)(2,1)}), bf16[8,256,512]{2,1,0:T(8,128)(2,1)}, u32[]{:S(2)}, u32[]{:S(2)}) async-start(bf16[8,256,512]{2,1,0:T(8,128)(2,1)} %bitcast.74), calls=%async_computation.1 | async-start | bytes 4194304 | tf_op jit(solution)/shard_map/all_to_all | solution.py:1502
  40.3 9.4 %copy-start.17 = (f32[48,512]{1,0:T(8,128)S(1)}, f32[48,512]{1,0:T(8,128)}, u32[]{:S(2)}) copy-start(f32[48,512]{1,0:T(8,128)} %get-tuple-element.92.means_ref) | copy-start | bytes 294916
  40.3 9.4 %copy-start.21 = (f32[512]{0:T(512)S(1)}, f32[512]{0:T(512)}, u32[]{:S(2)}) copy-start(f32[512]{0:T(512)} %convert_element_type.62) | copy-start | bytes 6148
  58.7 27.5 %copy-start.43 = (bf16[512]{0:T(512)(128)(2,1)S(1)}, bf16[512]{0:T(512)(128)(2,1)}, u32[]{:S(2)}) copy-start(bf16[512]{0:T(512)(128)(2,1)} %param.23) | copy-start | bytes 3076
  81.6 50.6 %all-to-all-start.2 = ((bf16[8,240,512]{2,1,0:T(8,128)(2,1)}), bf16[8,240,512]{2,1,0:T(8,128)(2,1)}, u32[]{:S(2)}, u32[]{:S(2)}) async-start(bf16[8,240,512]{2,1,0:T(8,128)(2,1)} %bitcast.20), calls=%async_computation.2 | async-start | bytes 3932160 | tf_op jit(solution)/shard_map/all_to_all | solution.py:1502
  132.2 57.8 %all-to-all-start.3 = ((bf16[8,256,512]{2,1,0:T(8,128)(2,1)}), bf16[8,256,512]{2,1,0:T(8,128)(2,1)}, u32[]{:S(2)}, u32[]{:S(2)}) async-start(bf16[8,256,512]{2,1,0:T(8,128)(2,1)} %bitcast.73), calls=%async_computation.3 | async-start | bytes 4194304 | tf_op jit(solution)/shard_map/all_to_all | solution.py:1502
  161.3 5.4 %collective-permute-start = (bf16[2304,512]{1,0:T(8,128)(2,1)}, bf16[2304,512]{1,0:T(8,128)(2,1)}, u32[]{:S(2)}, u32[]{:S(2)}) collective-permute-start(bf16[2304,512]{1,0:T(8,128)(2,1)} %get-tuple-element.116), channel_id=1, source_target_pairs={{0,8},{8,0},{16,24},{24,16},{1,9},{9,1},{17,25},{25,17},{2,10},{10... | collective-permute-start | bytes 7077896 | tf_op jit(solution)/shard_map/ppermute | solution.py:1275
  171.3 18.7 %collective-permute-start.1 = (bf16[640,512]{1,0:T(8,128)(2,1)}, bf16[640,512]{1,0:T(8,128)(2,1)S(1)}, u32[]{:S(2)}, u32[]{:S(2)}) collective-permute-start(bf16[640,512]{1,0:T(8,128)(2,1)} %get-tuple-element.119), channel_id=1, source_target_pairs={{0,16},{8,24},{16,0},{24,8},{1,17},{9,25},{17,1},{25,9},{2,18},{10... | collective-permute-start | bytes 1966088 | tf_op jit(solution)/shard_map/ppermute | solution.py:1275
  172.9 17.1 %collective-permute-start.2 = (bf16[512,512]{1,0:T(8,128)(2,1)}, bf16[512,512]{1,0:T(8,128)(2,1)S(1)}, u32[]{:S(2)}, u32[]{:S(2)}) collective-permute-start(bf16[512,512]{1,0:T(8,128)(2,1)} %get-tuple-element.120), channel_id=1, source_target_pairs={{0,1},{1,0},{2,3},{3,2},{4,5},{5,4},{6,7},{7,6},{8,9},{9,8},{10,11... | collective-permute-start | bytes 1572872 | tf_op jit(solution)/shard_map/ppermute | solution.py:1275
  191.0 50.3 %all-to-all-start.4 = ((bf16[8,240,512]{2,1,0:T(8,128)(2,1)}), bf16[8,240,512]{2,1,0:T(8,128)(2,1)S(1)}, u32[]{:S(2)}, u32[]{:S(2)}) async-start(bf16[8,240,512]{2,1,0:T(8,128)(2,1)} %bitcast.72), calls=%async_computation.4 | async-start | bytes 3932160 | tf_op jit(solution)/shard_map/all_to_all | solution.py:1502
  210.5 2.7 collective-permute-start.3
  216.2 14.9 %collective-permute-start.5 = (bf16[256,512]{1,0:T(8,128)(2,1)}, bf16[256,512]{1,0:T(8,128)(2,1)S(1)}, u32[]{:S(2)}, u32[]{:S(2)}) collective-permute-start(bf16[256,512]{1,0:T(8,128)(2,1)} %get-tuple-element.132), channel_id=1, source_target_pairs={{0,1},{1,0},{2,3},{3,2},{4,5},{5,4},{6,7},{7,6},{8,9},{9,8},{10,11... | collective-permute-start | bytes 786440 | tf_op jit(solution)/shard_map/ppermute | solution.py:1275
  218.2 5.5 %collective-permute-start.4 = (bf16[128,512]{1,0:T(8,128)(2,1)}, bf16[128,512]{1,0:T(8,128)(2,1)S(1)}, u32[]{:S(2)}, u32[]{:S(2)}) collective-permute-start(bf16[128,512]{1,0:T(8,128)(2,1)} %get-tuple-element.129), channel_id=1, source_target_pairs={{0,16},{8,24},{16,0},{24,8},{1,17},{9,25},{17,1},{25,9},{2,18},{10... | collective-permute-start | bytes 393224 | tf_op jit(solution)/shard_map/ppermute | solution.py:1275
  223.7 7.4 %copy-start.41 = (bf16[128,512]{1,0:T(8,128)(2,1)}, bf16[128,512]{1,0:T(8,128)(2,1)S(1)}, u32[]{:S(2)}) copy-start(bf16[128,512]{1,0:T(8,128)(2,1)S(1)} %collective-permute-done.4.refs_3_) | copy-start | bytes 393220
  231.8 9.5 %copy-start.20 = (bf16[512,64]{0,1:T(8,128)(2,1)S(1)}, bf16[512,64]{0,1:T(8,128)(2,1)}, u32[]{:S(2)}) copy-start(bf16[512,64]{0,1:T(8,128)(2,1)} %param.22) | copy-start | bytes 196612
  235.7 5.6 %copy-start.11 = (f32[6,64,128]{2,1,0:T(8,128)S(1)}, f32[6,64,128]{2,1,0:T(8,128)}, u32[]{:S(2)}) copy-start(f32[6,64,128]{2,1,0:T(8,128)} %copy-done.10) | copy-start | bytes 589828
  235.7 5.6 %copy-start.12 = (f32[6,64,64]{2,1,0:T(8,128)S(1)}, f32[6,64,64]{2,1,0:T(8,128)}, u32[]{:S(2)}) copy-start(f32[6,64,64]{2,1,0:T(8,128)} %fusion.picked_ref) | copy-start | bytes 294916
  235.7 5.6 %copy-start.13 = (bf16[384,512]{1,0:T(8,128)(2,1)S(1)}, bf16[384,512]{1,0:T(8,128)(2,1)}, u32[]{:S(2)}) copy-start(bf16[384,512]{1,0:T(8,128)(2,1)} %get-tuple-element.133.token_ref.refs_0_) | copy-start | bytes 1179652
  235.8 5.6 %copy-start.18 = (f32[48,512]{1,0:T(8,128)S(1)}, f32[48,512]{1,0:T(8,128)}, u32[]{:S(2)}) copy-start(f32[48,512]{1,0:T(8,128)} %get-tuple-element.92.means_ref) | copy-start | bytes 294916
  235.8 5.6 %copy-start.22 = (f32[512]{0:T(512)S(1)}, f32[512]{0:T(512)}, u32[]{:S(2)}) copy-start(f32[512]{0:T(512)} %convert_element_type.62) | copy-start | bytes 6148
  235.8 5.6 %copy-start.28 = (s32[64]{0:T(128)S(1)}, s32[64]{0:T(128)}, u32[]{:S(2)}) copy-start(s32[64]{0:T(128)} %get-tuple-element.85.perm_ref) | copy-start | bytes 772
  235.8 12.9 %collective-permute-start.6 = (bf16[384,512]{1,0:T(8,128)(2,1)}, bf16[384,512]{1,0:T(8,128)(2,1)}, u32[]{:S(2)}, u32[]{:S(2)}) collective-permute-start(bf16[384,512]{1,0:T(8,128)(2,1)} %get-tuple-element.137), channel_id=1, source_target_pairs={{0,1},{1,0},{2,3},{3,2},{4,5},{5,4},{6,7},{7,6},{8,9},{9,8},{10,11... | collective-permute-start | bytes 1179656 | tf_op jit(solution)/shard_map/ppermute | solution.py:1275
  235.9 12.8 %collective-permute-start.7 = (bf16[384,512]{1,0:T(8,128)(2,1)}, bf16[384,512]{1,0:T(8,128)(2,1)}, u32[]{:S(2)}, u32[]{:S(2)}) collective-permute-start(bf16[384,512]{1,0:T(8,128)(2,1)} %get-tuple-element.139), channel_id=1, source_target_pairs={{0,16},{8,24},{16,0},{24,8},{1,17},{9,25},{17,1},{25,9},{2,18},{10... | collective-permute-start | bytes 1179656 | tf_op jit(solution)/shard_map/ppermute | solution.py:1275
  241.3 9.8 %copy-start.7 = (bf16[8,240,512]{2,1,0:T(8,128)(2,1)}, bf16[8,240,512]{2,1,0:T(8,128)(2,1)S(1)}, u32[]{:S(2)}) copy-start(bf16[8,240,512]{2,1,0:T(8,128)(2,1)S(1)} %all-to-all-done.4) | copy-start | bytes 5898244
  251.1 9.4 %collective-permute-start.9 = (bf16[192,512]{1,0:T(8,128)(2,1)}, bf16[192,512]{1,0:T(8,128)(2,1)S(1)}, u32[]{:S(2)}, u32[]{:S(2)}) collective-permute-start(bf16[192,512]{1,0:T(8,128)(2,1)} %get-tuple-element.142), channel_id=1, source_target_pairs={{0,2},{1,3},{2,0},{3,1},{4,6},{5,7},{6,4},{7,5},{8,10},{9,11},{10,... | collective-permute-start | bytes 589832 | tf_op jit(solution)/shard_map/ppermute | solution.py:1275
  251.4 7.5 %collective-permute-start.11 = (f32[72,512]{1,0:T(8,128)}, f32[72,512]{1,0:T(8,128)S(1)}, u32[]{:S(2)}, u32[]{:S(2)}) collective-permute-start(f32[72,512]{1,0:T(8,128)} %copy-done.24), channel_id=1, source_target_pairs={{0,8},{8,0},{16,24},{24,16},{1,9},{9,1},{17,25},{25,17},{2,10},{10... | collective-permute-start | bytes 442376 | tf_op jit(solution)/shard_map/ppermute | solution.py:1275
  251.4 10.2 %collective-permute-start.8 = (bf16[192,512]{1,0:T(8,128)(2,1)}, bf16[192,512]{1,0:T(8,128)(2,1)S(1)}, u32[]{:S(2)}, u32[]{:S(2)}) collective-permute-start(bf16[192,512]{1,0:T(8,128)(2,1)} %get-tuple-element.141), channel_id=1, source_target_pairs={{0,2},{1,3},{2,0},{3,1},{4,6},{5,7},{6,4},{7,5},{8,10},{9,11},{10,... | collective-permute-start | bytes 589832 | tf_op jit(solution)/shard_map/ppermute | solution.py:1275
  253.2 5.7 %copy-start.25 = (f32[72,512]{1,0:T(8,128)S(1)}, f32[72,512]{1,0:T(8,128)}, u32[]{:S(2)}) copy-start(f32[72,512]{1,0:T(8,128)} %copy-done.24) | copy-start | bytes 442372
  253.2 7.3 %copy-start.40 = (bf16[192,512]{1,0:T(8,128)(2,1)S(1)}, bf16[192,512]{1,0:T(8,128)(2,1)}, u32[]{:S(2)}) copy-start(bf16[192,512]{1,0:T(8,128)(2,1)} %get-tuple-element.144) | copy-start | bytes 589828
  259.0 6.3 %collective-permute-start.12 = (f32[72,512]{1,0:T(8,128)S(1)}, f32[72,512]{1,0:T(8,128)S(1)}, u32[]{:S(2)}, u32[]{:S(2)}) collective-permute-start(f32[72,512]{1,0:T(8,128)S(1)} %add.49), channel_id=1, source_target_pairs={{0,16},{8,24},{16,0},{24,8},{1,17},{9,25},{17,1},{25,9},{2,18},{10... | collective-permute-start | bytes 442376 | tf_op jit(solution)/shard_map/ppermute | solution.py:1275
  260.6 16.0 %collective-permute-start.14 = (bf16[192,512]{1,0:T(8,128)(2,1)S(1)}, bf16[192,512]{1,0:T(8,128)(2,1)S(1)}, u32[]{:S(2)}, u32[]{:S(2)}) collective-permute-start(bf16[192,512]{1,0:T(8,128)(2,1)S(1)} %add_convert_fusion.1), channel_id=1, source_target_pairs={{0,4},{1,5},{2,6},{3,7},{4,0},{5,1},{6,2},{7,3},{8,12},{9,13},{10,... | collective-permute-start | bytes 589832 | tf_op jit(solution)/shard_map/ppermute | solution.py:1275
  262.3 39.3 %copy-start.30 = (s32[2]{0:T(128)S(1)}, s32[2]{0:T(128)}, u32[]{:S(2)}) copy-start(s32[2]{0:T(128)} %pad_add_fusion.1.bits_ref) | copy-start | bytes 28
  263.3 17.5 %collective-permute-start.10 = (bf16[192,512]{1,0:T(8,128)(2,1)S(1)}, bf16[192,512]{1,0:T(8,128)(2,1)S(1)}, u32[]{:S(2)}, u32[]{:S(2)}) collective-permute-start(bf16[192,512]{1,0:T(8,128)(2,1)S(1)} %add_convert_fusion.3), channel_id=1, source_target_pairs={{0,4},{1,5},{2,6},{3,7},{4,0},{5,1},{6,2},{7,3},{8,12},{9,13},{10,... | collective-permute-start | bytes 589832 | tf_op jit(solution)/shard_map/ppermute | solution.py:1275
  266.0 40.1 %copy-start.3 = (bf16[2048,512]{1,0:T(8,128)(2,1)S(1)}, bf16[2048,512]{1,0:T(8,128)(2,1)}, u32[]{:S(2)}) copy-start(bf16[2048,512]{1,0:T(8,128)(2,1)} %base.1.refs_3_.refs_1_) | copy-start | bytes 6291460
  266.0 40.1 %copy-start.23 = (f32[512]{0:T(512)S(1)}, f32[512]{0:T(512)}, u32[]{:S(2)}) copy-start(f32[512]{0:T(512)} %convert_element_type.62) | copy-start | bytes 6148
  266.0 40.1 %copy-start.26 = (s32[64]{0:T(128)S(1)}, s32[64]{0:T(128)}, u32[]{:S(2)}) copy-start(s32[64]{0:T(128)} %get-tuple-element.96.refs_1_.place_ref) | copy-start | bytes 772
  276.6 8.3 %collective-permute-start.15 = (bf16[192,512]{1,0:T(8,128)(2,1)S(1)}, bf16[192,512]{1,0:T(8,128)(2,1)S(1)}, u32[]{:S(2)}, u32[]{:S(2)}) collective-permute-start(bf16[192,512]{1,0:T(8,128)(2,1)S(1)} %add_convert_fusion.refs_2_), channel_id=1, source_target_pairs={{0,2},{1,3},{2,0},{3,1},{4,6},{5,7},{6,4},{7,5},{8,10},{9,11},{10,... | collective-permute-start | bytes 589832 | tf_op jit(solution)/shard_map/ppermute | solution.py:1275
  282.4 6.8 %collective-permute-start.13 = (bf16[192,512]{1,0:T(8,128)(2,1)S(1)}, bf16[192,512]{1,0:T(8,128)(2,1)S(1)}, u32[]{:S(2)}, u32[]{:S(2)}) collective-permute-start(bf16[192,512]{1,0:T(8,128)(2,1)S(1)} %add_convert_fusion.2.refs_0_), channel_id=1, source_target_pairs={{0,2},{1,3},{2,0},{3,1},{4,6},{5,7},{6,4},{7,5},{8,10},{9,11},{10,... | collective-permute-start | bytes 589832 | tf_op jit(solution)/shard_map/ppermute | solution.py:1275
  290.3 10.1 %collective-permute-start.16 = (bf16[384,512]{1,0:T(8,128)(2,1)S(1)}, bf16[384,512]{1,0:T(8,128)(2,1)S(1)}, u32[]{:S(2)}, u32[]{:S(2)}) collective-permute-start(bf16[384,512]{1,0:T(8,128)(2,1)S(1)} %get-tuple-element.145.refs_0_), channel_id=1, source_target_pairs={{0,1},{1,0},{2,3},{3,2},{4,5},{5,4},{6,7},{7,6},{8,9},{9,8},{10,11... | collective-permute-start | bytes 1179656 | tf_op jit(solution)/shard_map/ppermute | solution.py:1275
  291.8 9.8 %collective-permute-start.17 = (bf16[384,512]{1,0:T(8,128)(2,1)S(1)}, bf16[384,512]{1,0:T(8,128)(2,1)S(1)}, u32[]{:S(2)}, u32[]{:S(2)}) collective-permute-start(bf16[384,512]{1,0:T(8,128)(2,1)S(1)} %get-tuple-element.146.refs_2_), channel_id=1, source_target_pairs={{0,16},{8,24},{16,0},{24,8},{1,17},{9,25},{17,1},{25,9},{2,18},{10... | collective-permute-start | bytes 1179656 | tf_op jit(solution)/shard_map/ppermute | solution.py:1275
  303.9 17.5 %collective-permute-start.18 = (bf16[768,512]{1,0:T(8,128)(2,1)S(1)}, bf16[768,512]{1,0:T(8,128)(2,1)}, u32[]{:S(2)}, u32[]{:S(2)}) collective-permute-start(bf16[768,512]{1,0:T(8,128)(2,1)S(1)} %get-tuple-element.147.refs_0_), channel_id=1, source_target_pairs={{0,16},{8,24},{16,0},{24,8},{1,17},{9,25},{17,1},{25,9},{2,18},{10... | collective-permute-start | bytes 2359304 | tf_op jit(solution)/shard_map/ppermute | solution.py:1275
  304.5 17.3 %collective-permute-start.19 = (bf16[768,512]{1,0:T(8,128)(2,1)}, bf16[768,512]{1,0:T(8,128)(2,1)}, u32[]{:S(2)}, u32[]{:S(2)}) collective-permute-start(bf16[768,512]{1,0:T(8,128)(2,1)} %get-tuple-element.148.refs_2_), channel_id=1, source_target_pairs={{0,1},{1,0},{2,3},{3,2},{4,5},{5,4},{6,7},{7,6},{8,9},{9,8},{10,11... | collective-permute-start | bytes 2359304 | tf_op jit(solution)/shard_map/ppermute | solution.py:1275
  309.2 12.6 %copy-start.29 = (s32[2]{0:T(128)S(1)}, s32[2]{0:T(128)}, u32[]{:S(2)}) copy-start(s32[2]{0:T(128)} %pad_add_fusion.bits_ref) | copy-start | bytes 28
  325.9 5.7 %collective-permute-start.20 = (bf16[3072,512]{1,0:T(8,128)(2,1)S(1)}, bf16[3072,512]{1,0:T(8,128)(2,1)S(1)}, u32[]{:S(2)}, u32[]{:S(2)}) collective-permute-start(bf16[3072,512]{1,0:T(8,128)(2,1)S(1)} %double_step.5.values_ref), channel_id=1, source_target_pairs={{0,8},{8,0},{16,24},{24,16},{1,9},{9,1},{17,25},{25,17},{2,10},{10... | collective-permute-start | bytes 9437192 | tf_op jit(solution)/shard_map/ppermute | solution.py:1275
  (23 other events, 40.9 us)

commit v6 on v5

--- a/solution.py
+++ b/solution.py
@@ -1253,7 +1253,7 @@
             jax.ShapeDtypeStruct((rows - rows_a, width), BF16),
         ],
         scratch_shapes=[pltpu.VMEM((rows, width), F32)],
-        compiler_params=limit(24),
+        compiler_params=limit(62),
         cost_estimate=cost(rows * width * 20, rows * width * 12),
         name="last",
     )(table, place, *ret, x, base, gain1)

time: 343 us -> 341 us (level)
    unnamed x90 -> x80, local copies, waits for them, and re-layouts: 14.3 us -> 11.2 us
  transfers between devices with their start and end apart: 25 -> 25, of which waited for: 15 -> 15; matrix products, arithmetic and copies ran while one was open for 4% -> 4% of each run, Pallas kernels for 44% -> 45%
where the time goes in v6:
time: 341 us; the launch traced here: 335 us
  Pallas kernels  172 us (50%)
  waiting for transfers between devices  78.8 us (23%)
  starting transfers between devices  39.2 us (11%)
  local copies, waits for them, and re-layouts  18 us (5%)
  blocking collectives  15.7 us (5%)
  other arithmetic  9.53 us (3%)
    pallas_call x2, Pallas kernels, forward(): pl.pallas_call(functools.partial(forward_kernel, first_group, groups, len...  56.6 us
    ppermute x21, waiting for transfers between devices, swap(): return lax.ppermute(values, axis, [(i, i ^ 1 << bit) for i in range(size)])  54 us
    all_to_all x4, waiting for transfers between devices, exchange(): lax.all_to_all(parts, 'blk', split_axis=0, concat_axis=0, tiled=True)  24.8 us
    pallas_call x2, Pallas kernels, backward(): pl.pallas_call(functools.partial(backward_kernel, first_group, groups, pr...  20.6 us
    all_to_all x4, starting transfers between devices, exchange(): lax.all_to_all(parts, 'blk', split_axis=0, concat_axis=0, tiled=True)  20.1 us
    ppermute x21, starting transfers between devices, swap(): return lax.ppermute(values, axis, [(i, i ^ 1 << bit) for i in range(size)])  19.1 us
    all_to_all x1, blocking collectives, per_device(): news = lax.all_to_all(news, 'blk', split_axis=0, concat_axis=0, tiled=True)  15.7 us
    pallas_call x1, Pallas kernels, qkv_grads(): pl.pallas_call(qkv_kernel, in_specs=[SMEM] + [ANY] * 4 + [VMEM, ANY, ANY]...  14.8 us
  transfers between devices with their start and end apart: 25, of which 15 were waited for; matrix products, arithmetic and copies ran while one was open for 4% of the time, Pallas kernels for 45%

profile of v6, /device:TPU:0, one launch (start us, length us, event | category | flops | bytes accessed | tf_op | source)
XLA Modules:
  0.0 334.8 jit_solution(13158449606717011629)
XLA Ops:
  1.9 8.0 %digest.1 = (bf16[2048,512]{1,0:T(8,128)(2,1)}, f32[48,512]{1,0:T(8,128)}, f32[8,56,128]{2,1,0:T(8,128)}, s32[64]{0:T(128)}, s32[64]{0:T(128)}, /*index=5*/s32[64]{0:T(128)}, s32[64]{0:T(128)}, s32[2]{0:T(128)}) custom-call(s32[2,8]{1,0:T(2,128)} %sela_ref.1, s32[4,8]{1,0:T(4,128)} %selb_ref.1, bf16[1024,512]{1,0:T(8,128)(2,1)} %bitcast.76, ...), custom_call_target="tpu_custom_call" | custom-call | flops 10485 | bytes 4194 | tf_op jit(solution)/shard_map/digest/pallas_call | solution.py:277
  10.0 15.7 %all_to_all.25 = f32[8,56,128]{2,1,0:T(8,128)S(1)} all-to-all(f32[8,56,128]{2,1,0:T(8,128)} %get-tuple-element.88), channel_id=1, replica_groups=mesh['dp'=4,'blk'=8] {'blk'}, dimensions={0} | all-to-all | bytes 458752 | tf_op jit(solution)/shard_map/all_to_all | solution.py:1552
  26.3 3.6 %pack.1 = (bf16[2048,512]{1,0:T(8,128)(2,1)}, bf16[1920,512]{1,0:T(8,128)(2,1)}) custom-call(s32[112]{0:T(128)} %convert_element_type.64.table_ref, bf16[2048,512]{1,0:T(8,128)(2,1)} %get-tuple-element.89.x_ref.refs_2_), custom_call_target="tpu_custom_call" | custom-call | bytes 6291 | tf_op jit(solution)/shard_map/pack/pallas_call | solution.py:340
  29.9 4.6 %all-to-all-start.1 = ((bf16[8,256,512]{2,1,0:T(8,128)(2,1)}), bf16[8,256,512]{2,1,0:T(8,128)(2,1)}, u32[]{:S(2)}, u32[]{:S(2)}) async-start(bf16[8,256,512]{2,1,0:T(8,128)(2,1)} %bitcast.74), calls=%async_computation.1 | async-start | bytes 4194304 | tf_op jit(solution)/shard_map/all_to_all | solution.py:1502
  35.8 1.9 arrange.1
  40.3 9.4 %project.1.refs_2_.refs_6_.refs_7_ = bf16[2048,1536]{1,0:T(8,128)(2,1)} custom-call(bf16[2048,512]{1,0:T(8,128)(2,1)} %copy-done.1, f32[1,512]{1,0:T(1,128)} %bitcast.65, bf16[512,1536]{1,0:T(8,128)(2,1)} %wqkv_ref.3), custom_call_target="tpu_custom_call" | custom-call | flops 3221225 | bytes 8388 | tf_op jit(solution)/shard_map/project/pallas_call | solution.py:436
  51.1 3.7 %sinkhorn.1 = f32[6,64,128]{2,1,0:T(8,128)} custom-call(f32[6,64,64]{2,1,0:T(8,128)} %bitcast.56, f32[6,64,64]{2,1,0:T(8,128)} %fusion.picked_ref), custom_call_target="tpu_custom_call" | custom-call | flops 2457 | bytes 786 | tf_op jit(solution)/shard_map/sinkhorn/pallas_call | solution.py:465
  58.7 22.9 %all-to-all-done.1 = bf16[8,256,512]{2,1,0:T(8,128)(2,1)} async-done(((bf16[8,256,512]{2,1,0:T(8,128)(2,1)}), bf16[8,256,512]{2,1,0:T(8,128)(2,1)}, u32[]{:S(2)}, u32[]{:S(2)}) %all-to-all-start.1) | async-done | bytes 2097184 | tf_op jit(solution)/shard_map/all_to_all | solution.py:1502
  81.6 4.5 %all-to-all-start.2 = ((bf16[8,240,512]{2,1,0:T(8,128)(2,1)}), bf16[8,240,512]{2,1,0:T(8,128)(2,1)}, u32[]{:S(2)}, u32[]{:S(2)}) async-start(bf16[8,240,512]{2,1,0:T(8,128)(2,1)} %bitcast.20), calls=%async_computation.2 | async-start | bytes 3932160 | tf_op jit(solution)/shard_map/all_to_all | solution.py:1502
  86.7 33.8 %forward.2 = (bf16[2048,512]{1,0:T(8,128)(2,1)}, bf16[2048,512]{1,0:T(8,128)(2,1)}, bf16[2048,512]{1,0:T(8,128)(2,1)}, bf16[32,2,256,128]{3,2,1,0:T(8,128)(2,1)}...) custom-call(s32[64]{0:T(128)} %get-tuple-element.86.refs_0_, ...), custom_call_target="tpu_custom_call" | custom-call | flops 20000000 | bytes 20000 | tf_op jit(solution)/shard_map/forward/pallas_call | solution.py:857
  120.5 11.6 %backward.2 = (bf16[2048,1536]{1,0:T(8,128)(2,1)}, bf16[2048,1024]{1,0:T(8,128)(2,1)}, f32[20,2,128]{2,1,0:T(2,128)}, bf16[2048,512]{1,0:T(8,128)(2,1)}) custom-call(s32[64]{0:T(128)} %get-tuple-element.95.refs_0_, s32[64]{0:T(128)} %get-tuple-element.96.refs_1_.place_ref, bf16[2048,1536]{1,0:T(8,128)(2,1)} %project.1.refs_2_.refs_6_.refs_7_, ...), custom_call_target="tpu_custom_call" | custom-call | flops 8000000 | bytes 20000 | tf_op jit(solution)/shard_map/backward/pallas_call | solution.py:1041
  132.2 6.3 %all-to-all-start.3 = ((bf16[8,256,512]{2,1,0:T(8,128)(2,1)}), bf16[8,256,512]{2,1,0:T(8,128)(2,1)}, u32[]{:S(2)}, u32[]{:S(2)}) async-start(bf16[8,256,512]{2,1,0:T(8,128)(2,1)} %bitcast.73), calls=%async_computation.3 | async-start | bytes 4194304 | tf_op jit(solution)/shard_map/all_to_all | solution.py:1502
  138.5 22.9 %forward.3 = (bf16[2048,512]{1,0:T(8,128)(2,1)}, bf16[2048,512]{1,0:T(8,128)(2,1)}, bf16[2048,512]{1,0:T(8,128)(2,1)}, bf16[32,2,256,128]{3,2,1,0:T(8,128)(2,1)}...) custom-call(s32[64]{0:T(128)} %get-tuple-element.86.refs_0_, ...), custom_call_target="tpu_custom_call", output_to_operand_aliasing={{0}: (19, {}), {1}: (20, {}), {2}: (21, {}), {3}: (22, {}),... | custom-call | flops 12000000 | bytes 12000 | tf_op jit(solution)/shard_map/forward/pallas_call | solution.py:857
  162.0 1.6 copy-done.4
  163.6 3.1 restore.1
  166.8 4.6 %halve_step.4 = (bf16[640,512]{1,0:T(8,128)(2,1)}, bf16[640,512]{1,0:T(8,128)(2,1)}, bf16[512,512]{1,0:T(8,128)(2,1)}, bf16[512,512]{1,0:T(8,128)(2,1)}) custom-call(s32[2]{0:T(128)} %pad_add_fusion.bits_ref, bf16[2304,512]{1,0:T(8,128)(2,1)} %get-tuple-element.115.refs_0_, bf16[2304,512]{1,0:T(8,128)(2,1)} %collective-permute-done.refs_1_, ...), custom_call_target="tpu_custom_call" | custom-call | bytes 4718 | tf_op jit(solution)/shard_map/halve_step/pallas_call | solution.py:1356
  171.4 1.5 collective-permute-start.1
  172.9 2.0 collective-permute-start.2
  175.0 8.9 %backward.3 = (bf16[2048,1536]{1,0:T(8,128)(2,1)}, bf16[2048,1024]{1,0:T(8,128)(2,1)}, f32[12,2,128]{2,1,0:T(2,128)}, bf16[1920,512]{1,0:T(8,128)(2,1)}) custom-call(s32[64]{0:T(128)} %get-tuple-element.95.refs_0_, s32[64]{0:T(128)} %get-tuple-element.96.refs_1_.place_ref, ...), custom_call_target="tpu_custom_call", output_to_operand_aliasing={{0}: (9, {}), {1}: (10, {})} | custom-call | flops 4800000 | bytes 12000 | tf_op jit(solution)/shard_map/backward/pallas_call | solution.py:1041
  183.9 6.1 %collective-permute-done.2.refs_2_.refs_5_ = bf16[512,512]{1,0:T(8,128)(2,1)S(1)} collective-permute-done((bf16[512,512]{1,0:T(8,128)(2,1)}, bf16[512,512]{1,0:T(8,128)(2,1)S(1)}, u32[]{:S(2)}, u32[]{:S(2)}) %collective-permute-start.2) | collective-permute-done | bytes 524320 | tf_op jit(solution)/shard_map/ppermute | solution.py:1275
  191.1 4.7 %all-to-all-start.4 = ((bf16[8,240,512]{2,1,0:T(8,128)(2,1)}), bf16[8,240,512]{2,1,0:T(8,128)(2,1)S(1)}, u32[]{:S(2)}, u32[]{:S(2)}) async-start(bf16[8,240,512]{2,1,0:T(8,128)(2,1)} %bitcast.72), calls=%async_computation.4 | async-start | bytes 3932160 | tf_op jit(solution)/shard_map/all_to_all | solution.py:1502
  195.7 14.8 %qkv_grads.1 = (bf16[2048,512]{1,0:T(8,128)(2,1)}, bf16[768,512]{1,0:T(8,128)(2,1)}, bf16[768,512]{1,0:T(8,128)(2,1)}) custom-call(s32[1]{0:T(128)} %bitcast.4.refs_2_.core_ref, bf16[2048,512]{1,0:T(8,128)(2,1)} %copy-done.1, bf16[2048,512]{1,0:T(8,128)(2,1)} %get-tuple-element.122.farx_hbm, bf16[2048,1536]{1,0:T(8,128)(2,1)} %get-tuple-element.123.dproj_hbm.token_ref, ...), custom_call_target="tpu_custom_call" | custom-call | flops 10000000 | bytes 25000 | tf_op jit(solution)/shard_map/qkv_grads/pallas_call | solution.py:1144
  210.6 2.6 collective-permute-done.3.refs_1_.refs_2_
  213.2 3.0 halve_step.5
  216.2 2.1 collective-permute-start.5
  220.4 3.4 %collective-permute-done.4.refs_3_ = bf16[128,512]{1,0:T(8,128)(2,1)S(1)} collective-permute-done((bf16[128,512]{1,0:T(8,128)(2,1)}, bf16[128,512]{1,0:T(8,128)(2,1)S(1)}, u32[]{:S(2)}, u32[]{:S(2)}) %collective-permute-start.4) | collective-permute-done | bytes 131104 | tf_op jit(solution)/shard_map/ppermute | solution.py:1275
  223.8 7.4 %collective-permute-done.5.refs_7_ = bf16[256,512]{1,0:T(8,128)(2,1)S(1)} collective-permute-done((bf16[256,512]{1,0:T(8,128)(2,1)}, bf16[256,512]{1,0:T(8,128)(2,1)S(1)}, u32[]{:S(2)}, u32[]{:S(2)}) %collective-permute-start.5) | collective-permute-done | bytes 262176 | tf_op jit(solution)/shard_map/ppermute | solution.py:1275
  231.9 3.9 %halve_step.6 = (bf16[384,512]{1,0:T(8,128)(2,1)}, bf16[384,512]{1,0:T(8,128)(2,1)}, bf16[384,512]{1,0:T(8,128)(2,1)}, bf16[384,512]{1,0:T(8,128)(2,1)}) custom-call(s32[2]{0:T(128)} %pad_add_fusion.1.bits_ref, bf16[640,512]{1,0:T(8,128)(2,1)} %get-tuple-element.117.refs_11_.refs_0_, bf16[640,512]{1,0:T(8,128)(2,1)} %copy-done.26, ...), custom_call_target="tpu_custom_call" | custom-call | bytes 3145 | tf_op jit(solution)/shard_map/halve_step/pallas_call | solution.py:1356
  236.0 1.5 collective-permute-start.7
  239.4 1.9 all-to-all-done.4
  241.4 6.0 %sort_back.1 = (f32[72,512]{1,0:T(8,128)S(1)}, f32[64,512]{1,0:T(8,128)S(1)}) custom-call(s32[1]{0:T(128)} %bitcast.31.me_ref, s32[64]{0:T(128)S(1)} %copy-done.23, f32[6,64,64]{2,1,0:T(8,128)S(1)} %bitcast.57, f32[6,64,64]{2,1,0:T(8,128)S(1)} %copy-done.9, bf16[384,512]{1,0:T(8,128)(2,1)S(1)} %bitcast.58, bf16[64,512]{1,0:T(8,128)(2,1)S(1)} %bitcast.63, ...), custom_call_target="tpu_custom_call" | custom-call | flops 4915 | bytes 786 | tf_op jit(solution)/shard_map/sort_back/pallas_call | solution.py:550
  248.8 2.3 halve_step.7
  251.4 1.8 collective-permute-start.8
  253.2 5.7 %base.1.refs_3_.refs_1_ = bf16[2048,512]{1,0:T(8,128)(2,1)} custom-call(bf16[2048,512]{1,0:T(8,128)(2,1)} %copy-done.1, bf16[2048,512]{1,0:T(8,128)(2,1)} %get-tuple-element.121.gmid_ref, bf16[2048,512]{1,0:T(8,128)(2,1)} %get-tuple-element.125.gn_ref, f32[64,512]{1,0:T(8,128)} %copy-done.16, f32[1,512]{1,0:T(1,128)} %bitcast.69), custom_call_target="tpu_custom_call" | custom-call | flops 20971 | bytes 8388 | tf_op jit(solution)/shard_map/base/pallas_call | solution.py:1187
  259.0 1.5 collective-permute-start.12
  263.3 2.0 collective-permute-start.10
  266.0 10.6 %collective-permute-done.14 = bf16[192,512]{1,0:T(8,128)(2,1)S(1)} collective-permute-done((bf16[192,512]{1,0:T(8,128)(2,1)S(1)}, bf16[192,512]{1,0:T(8,128)(2,1)S(1)}, u32[]{:S(2)}, u32[]{:S(2)}) %collective-permute-start.14) | collective-permute-done | bytes 196640 | tf_op jit(solution)/shard_map/ppermute | solution.py:1275
  276.7 4.1 %collective-permute-done.10.refs_0_ = bf16[192,512]{1,0:T(8,128)(2,1)S(1)} collective-permute-done((bf16[192,512]{1,0:T(8,128)(2,1)S(1)}, bf16[192,512]{1,0:T(8,128)(2,1)S(1)}, u32[]{:S(2)}, u32[]{:S(2)}) %collective-permute-start.10) | collective-permute-done | bytes 196640 | tf_op jit(solution)/shard_map/ppermute | solution.py:1275
  282.5 2.4 collective-permute-done.15.refs_3_
  284.9 4.3 %collective-permute-done.13.refs_1_ = bf16[192,512]{1,0:T(8,128)(2,1)S(1)} collective-permute-done((bf16[192,512]{1,0:T(8,128)(2,1)S(1)}, bf16[192,512]{1,0:T(8,128)(2,1)S(1)}, u32[]{:S(2)}, u32[]{:S(2)}) %collective-permute-start.13) | collective-permute-done | bytes 196640 | tf_op jit(solution)/shard_map/ppermute | solution.py:1275
  290.3 1.5 collective-permute-start.16
  292.4 8.0 %collective-permute-done.16.refs_1_ = bf16[384,512]{1,0:T(8,128)(2,1)S(1)} collective-permute-done((bf16[384,512]{1,0:T(8,128)(2,1)S(1)}, bf16[384,512]{1,0:T(8,128)(2,1)S(1)}, u32[]{:S(2)}, u32[]{:S(2)}) %collective-permute-start.16) | collective-permute-done | bytes 393248 | tf_op jit(solution)/shard_map/ppermute | solution.py:1275
  305.7 12.7 %last.1 = (bf16[1024,512]{1,0:T(8,128)(2,1)}, bf16[1024,512]{1,0:T(8,128)(2,1)}) custom-call(s32[120]{0:T(128)} %convert_element_type.69.table_ref, s32[64]{0:T(128)} %get-tuple-element.96.refs_1_.place_ref, bf16[2048,512]{1,0:T(8,128)(2,1)} %bitcast.26.refs_3_.refs_0_, bf16[1920,512]{1,0:T(8,128)(2,1)} %bitcast.55, ...), custom_call_target="tpu_custom_call" | custom-call | flops 20971 | bytes 12582 | tf_op jit(solution)/shard_map/last/pallas_call | solution.py:1247
  318.4 2.1 collective-permute-done.18.refs_1_
  322.0 2.5 double_step.5.values_ref
  325.3 3.4 %assemble.2 = (f32[512,2048]{1,0:T(8,128)}, f32[2048,512]{1,0:T(8,128)}, f32[512,512]{1,0:T(8,128)}, f32[512,1536]{1,0:T(8,128)}, f32[8,512]{1,0:T(8,128)S(1)}) custom-call(s32[1]{0:T(128)} %bitcast.4.refs_2_.core_ref, bf16[3072,512]{1,0:T(8,128)(2,1)S(1)} %double_step.5.values_ref, bf16[512,2048]{1,0:T(8,128)(2,1)S(1)} %copy-done.2, ...), custom_call_target="tpu_custom_call" | custom-call | bytes 9437 | tf_op jit(solution)/shard_map/assemble/pallas_call | solution.py:1482
  328.7 1.6 collective-permute-done.20.values_ref
  330.3 3.4 %assemble.3 = (f32[512,2048]{1,0:T(8,128)}, f32[2048,512]{1,0:T(8,128)}, f32[512,512]{1,0:T(8,128)}, f32[512,1536]{1,0:T(8,128)}, f32[8,512]{1,0:T(8,128)S(1)}) custom-call(s32[1]{0:T(128)} %bitcast.4.refs_2_.core_ref, ...), custom_call_target="tpu_custom_call", output_to_operand_aliasing={{0}: (5, {}), {1}: (6, {}), {2}: (7, {}), {3}: (8, {})} | custom-call | bytes 9437 | tf_op jit(solution)/shard_map/assemble/pallas_call | solution.py:1482
  (153 shorter events, 35.0 us)
Async XLA Ops:
  25.7 24.3 %copy-start.29 = (f32[8,56,128]{2,1,0:T(8,128)}, f32[8,56,128]{2,1,0:T(8,128)S(1)}, u32[]{:S(2)}) copy-start(f32[8,56,128]{2,1,0:T(8,128)S(1)} %all_to_all.25) | copy-start | bytes 688132
  29.9 4.7 %copy-start.3 = (bf16[2048,512]{1,0:T(8,128)(2,1)S(1)}, bf16[2048,512]{1,0:T(8,128)(2,1)}, u32[]{:S(2)}) copy-start(bf16[2048,512]{1,0:T(8,128)(2,1)} %get-tuple-element.89.x_ref.refs_2_) | copy-start | bytes 6291460
  29.9 4.7 %copy-start.11 = (bf16[2,512,512]{2,1,0:T(8,128)(2,1)S(1)}, bf16[2,512,512]{2,1,0:T(8,128)(2,1)}, u32[]{:S(2)}) copy-start(bf16[2,512,512]{2,1,0:T(8,128)(2,1)} %param.26) | copy-start | bytes 3145732
  29.9 4.7 %copy-start.22 = (s32[64]{0:T(128)S(1)}, s32[64]{0:T(128)}, u32[]{:S(2)}) copy-start(s32[64]{0:T(128)} %get-tuple-element.85.perm_ref) | copy-start | bytes 772
  29.9 51.7 %all-to-all-start.1 = ((bf16[8,256,512]{2,1,0:T(8,128)(2,1)}), bf16[8,256,512]{2,1,0:T(8,128)(2,1)}, u32[]{:S(2)}, u32[]{:S(2)}) async-start(bf16[8,256,512]{2,1,0:T(8,128)(2,1)} %bitcast.74), calls=%async_computation.1 | async-start | bytes 4194304 | tf_op jit(solution)/shard_map/all_to_all | solution.py:1502
  40.3 9.4 %copy-start.14 = (f32[48,512]{1,0:T(8,128)S(1)}, f32[48,512]{1,0:T(8,128)}, u32[]{:S(2)}) copy-start(f32[48,512]{1,0:T(8,128)} %get-tuple-element.92.means_ref) | copy-start | bytes 294916
  40.3 9.4 %copy-start.18 = (f32[512]{0:T(512)S(1)}, f32[512]{0:T(512)}, u32[]{:S(2)}) copy-start(f32[512]{0:T(512)} %convert_element_type.62) | copy-start | bytes 6148
  58.7 27.4 %copy-start.38 = (bf16[512]{0:T(512)(128)(2,1)S(1)}, bf16[512]{0:T(512)(128)(2,1)}, u32[]{:S(2)}) copy-start(bf16[512]{0:T(512)(128)(2,1)} %param.23) | copy-start | bytes 3076
  81.6 50.6 %all-to-all-start.2 = ((bf16[8,240,512]{2,1,0:T(8,128)(2,1)}), bf16[8,240,512]{2,1,0:T(8,128)(2,1)}, u32[]{:S(2)}, u32[]{:S(2)}) async-start(bf16[8,240,512]{2,1,0:T(8,128)(2,1)} %bitcast.20), calls=%async_computation.2 | async-start | bytes 3932160 | tf_op jit(solution)/shard_map/all_to_all | solution.py:1502
  132.2 57.9 %all-to-all-start.3 = ((bf16[8,256,512]{2,1,0:T(8,128)(2,1)}), bf16[8,256,512]{2,1,0:T(8,128)(2,1)}, u32[]{:S(2)}, u32[]{:S(2)}) async-start(bf16[8,256,512]{2,1,0:T(8,128)(2,1)} %bitcast.73), calls=%async_computation.3 | async-start | bytes 4194304 | tf_op jit(solution)/shard_map/all_to_all | solution.py:1502
  161.3 5.4 %collective-permute-start = (bf16[2304,512]{1,0:T(8,128)(2,1)}, bf16[2304,512]{1,0:T(8,128)(2,1)}, u32[]{:S(2)}, u32[]{:S(2)}) collective-permute-start(bf16[2304,512]{1,0:T(8,128)(2,1)} %get-tuple-element.116), channel_id=1, source_target_pairs={{0,8},{8,0},{16,24},{24,16},{1,9},{9,1},{17,25},{25,17},{2,10},{10... | collective-permute-start | bytes 7077896 | tf_op jit(solution)/shard_map/ppermute | solution.py:1275
  171.4 18.6 %collective-permute-start.1 = (bf16[640,512]{1,0:T(8,128)(2,1)}, bf16[640,512]{1,0:T(8,128)(2,1)S(1)}, u32[]{:S(2)}, u32[]{:S(2)}) collective-permute-start(bf16[640,512]{1,0:T(8,128)(2,1)} %get-tuple-element.119), channel_id=1, source_target_pairs={{0,16},{8,24},{16,0},{24,8},{1,17},{9,25},{17,1},{25,9},{2,18},{10... | collective-permute-start | bytes 1966088 | tf_op jit(solution)/shard_map/ppermute | solution.py:1275
  172.9 17.1 %collective-permute-start.2 = (bf16[512,512]{1,0:T(8,128)(2,1)}, bf16[512,512]{1,0:T(8,128)(2,1)S(1)}, u32[]{:S(2)}, u32[]{:S(2)}) collective-permute-start(bf16[512,512]{1,0:T(8,128)(2,1)} %get-tuple-element.120), channel_id=1, source_target_pairs={{0,1},{1,0},{2,3},{3,2},{4,5},{5,4},{6,7},{7,6},{8,9},{9,8},{10,11... | collective-permute-start | bytes 1572872 | tf_op jit(solution)/shard_map/ppermute | solution.py:1275
  191.1 50.3 %all-to-all-start.4 = ((bf16[8,240,512]{2,1,0:T(8,128)(2,1)}), bf16[8,240,512]{2,1,0:T(8,128)(2,1)S(1)}, u32[]{:S(2)}, u32[]{:S(2)}) async-start(bf16[8,240,512]{2,1,0:T(8,128)(2,1)} %bitcast.72), calls=%async_computation.4 | async-start | bytes 3932160 | tf_op jit(solution)/shard_map/all_to_all | solution.py:1502
  210.5 2.7 collective-permute-start.3
  216.2 14.9 %collective-permute-start.5 = (bf16[256,512]{1,0:T(8,128)(2,1)}, bf16[256,512]{1,0:T(8,128)(2,1)S(1)}, u32[]{:S(2)}, u32[]{:S(2)}) collective-permute-start(bf16[256,512]{1,0:T(8,128)(2,1)} %get-tuple-element.132), channel_id=1, source_target_pairs={{0,1},{1,0},{2,3},{3,2},{4,5},{5,4},{6,7},{7,6},{8,9},{9,8},{10,11... | collective-permute-start | bytes 786440 | tf_op jit(solution)/shard_map/ppermute | solution.py:1275
  218.3 5.5 %collective-permute-start.4 = (bf16[128,512]{1,0:T(8,128)(2,1)}, bf16[128,512]{1,0:T(8,128)(2,1)S(1)}, u32[]{:S(2)}, u32[]{:S(2)}) collective-permute-start(bf16[128,512]{1,0:T(8,128)(2,1)} %get-tuple-element.129), channel_id=1, source_target_pairs={{0,16},{8,24},{16,0},{24,8},{1,17},{9,25},{17,1},{25,9},{2,18},{10... | collective-permute-start | bytes 393224 | tf_op jit(solution)/shard_map/ppermute | solution.py:1275
  223.8 7.4 %copy-start.36 = (bf16[128,512]{1,0:T(8,128)(2,1)}, bf16[128,512]{1,0:T(8,128)(2,1)S(1)}, u32[]{:S(2)}) copy-start(bf16[128,512]{1,0:T(8,128)(2,1)S(1)} %collective-permute-done.4.refs_3_) | copy-start | bytes 393220
  231.9 9.5 %copy-start.17 = (bf16[512,64]{0,1:T(8,128)(2,1)S(1)}, bf16[512,64]{0,1:T(8,128)(2,1)}, u32[]{:S(2)}) copy-start(bf16[512,64]{0,1:T(8,128)(2,1)} %param.22) | copy-start | bytes 196612
  235.8 5.6 %copy-start.8 = (f32[6,64,128]{2,1,0:T(8,128)S(1)}, f32[6,64,128]{2,1,0:T(8,128)}, u32[]{:S(2)}) copy-start(f32[6,64,128]{2,1,0:T(8,128)} %copy-done.7) | copy-start | bytes 589828
  235.8 5.5 %copy-start.9 = (f32[6,64,64]{2,1,0:T(8,128)S(1)}, f32[6,64,64]{2,1,0:T(8,128)}, u32[]{:S(2)}) copy-start(f32[6,64,64]{2,1,0:T(8,128)} %fusion.picked_ref) | copy-start | bytes 294916
  235.8 5.5 %copy-start.10 = (bf16[384,512]{1,0:T(8,128)(2,1)S(1)}, bf16[384,512]{1,0:T(8,128)(2,1)}, u32[]{:S(2)}) copy-start(bf16[384,512]{1,0:T(8,128)(2,1)} %get-tuple-element.133.token_ref.refs_0_) | copy-start | bytes 1179652
  235.8 5.5 %copy-start.15 = (f32[48,512]{1,0:T(8,128)S(1)}, f32[48,512]{1,0:T(8,128)}, u32[]{:S(2)}) copy-start(f32[48,512]{1,0:T(8,128)} %get-tuple-element.92.means_ref) | copy-start | bytes 294916
  235.8 5.5 %copy-start.19 = (f32[512]{0:T(512)S(1)}, f32[512]{0:T(512)}, u32[]{:S(2)}) copy-start(f32[512]{0:T(512)} %convert_element_type.62) | copy-start | bytes 6148
  235.9 5.5 %copy-start.23 = (s32[64]{0:T(128)S(1)}, s32[64]{0:T(128)}, u32[]{:S(2)}) copy-start(s32[64]{0:T(128)} %get-tuple-element.85.perm_ref) | copy-start | bytes 772
  235.9 12.9 %collective-permute-start.6 = (bf16[384,512]{1,0:T(8,128)(2,1)}, bf16[384,512]{1,0:T(8,128)(2,1)}, u32[]{:S(2)}, u32[]{:S(2)}) collective-permute-start(bf16[384,512]{1,0:T(8,128)(2,1)} %get-tuple-element.137), channel_id=1, source_target_pairs={{0,1},{1,0},{2,3},{3,2},{4,5},{5,4},{6,7},{7,6},{8,9},{9,8},{10,11... | collective-permute-start | bytes 1179656 | tf_op jit(solution)/shard_map/ppermute | solution.py:1275
  236.0 12.8 %collective-permute-start.7 = (bf16[384,512]{1,0:T(8,128)(2,1)}, bf16[384,512]{1,0:T(8,128)(2,1)}, u32[]{:S(2)}, u32[]{:S(2)}) collective-permute-start(bf16[384,512]{1,0:T(8,128)(2,1)} %get-tuple-element.139), channel_id=1, source_target_pairs={{0,16},{8,24},{16,0},{24,8},{1,17},{9,25},{17,1},{25,9},{2,18},{10... | collective-permute-start | bytes 1179656 | tf_op jit(solution)/shard_map/ppermute | solution.py:1275
  241.3 9.8 %copy-start.5 = (bf16[8,240,512]{2,1,0:T(8,128)(2,1)}, bf16[8,240,512]{2,1,0:T(8,128)(2,1)S(1)}, u32[]{:S(2)}) copy-start(bf16[8,240,512]{2,1,0:T(8,128)(2,1)S(1)} %all-to-all-done.4) | copy-start | bytes 5898244
  251.1 9.4 %collective-permute-start.9 = (bf16[192,512]{1,0:T(8,128)(2,1)}, bf16[192,512]{1,0:T(8,128)(2,1)S(1)}, u32[]{:S(2)}, u32[]{:S(2)}) collective-permute-start(bf16[192,512]{1,0:T(8,128)(2,1)} %get-tuple-element.142), channel_id=1, source_target_pairs={{0,2},{1,3},{2,0},{3,1},{4,6},{5,7},{6,4},{7,5},{8,10},{9,11},{10,... | collective-permute-start | bytes 589832 | tf_op jit(solution)/shard_map/ppermute | solution.py:1275
  251.4 7.5 %collective-permute-start.11 = (f32[72,512]{1,0:T(8,128)}, f32[72,512]{1,0:T(8,128)S(1)}, u32[]{:S(2)}, u32[]{:S(2)}) collective-permute-start(f32[72,512]{1,0:T(8,128)} %copy-done.20), channel_id=1, source_target_pairs={{0,8},{8,0},{16,24},{24,16},{1,9},{9,1},{17,25},{25,17},{2,10},{10... | collective-permute-start | bytes 442376 | tf_op jit(solution)/shard_map/ppermute | solution.py:1275
  251.4 10.2 %collective-permute-start.8 = (bf16[192,512]{1,0:T(8,128)(2,1)}, bf16[192,512]{1,0:T(8,128)(2,1)S(1)}, u32[]{:S(2)}, u32[]{:S(2)}) collective-permute-start(bf16[192,512]{1,0:T(8,128)(2,1)} %get-tuple-element.141), channel_id=1, source_target_pairs={{0,2},{1,3},{2,0},{3,1},{4,6},{5,7},{6,4},{7,5},{8,10},{9,11},{10,... | collective-permute-start | bytes 589832 | tf_op jit(solution)/shard_map/ppermute | solution.py:1275
  253.2 5.8 %copy-start.21 = (f32[72,512]{1,0:T(8,128)S(1)}, f32[72,512]{1,0:T(8,128)}, u32[]{:S(2)}) copy-start(f32[72,512]{1,0:T(8,128)} %copy-done.20) | copy-start | bytes 442372
  253.2 7.3 %copy-start.35 = (bf16[192,512]{1,0:T(8,128)(2,1)S(1)}, bf16[192,512]{1,0:T(8,128)(2,1)}, u32[]{:S(2)}) copy-start(bf16[192,512]{1,0:T(8,128)(2,1)} %get-tuple-element.144) | copy-start | bytes 589828
  259.0 6.3 %collective-permute-start.12 = (f32[72,512]{1,0:T(8,128)S(1)}, f32[72,512]{1,0:T(8,128)S(1)}, u32[]{:S(2)}, u32[]{:S(2)}) collective-permute-start(f32[72,512]{1,0:T(8,128)S(1)} %add.49), channel_id=1, source_target_pairs={{0,16},{8,24},{16,0},{24,8},{1,17},{9,25},{17,1},{25,9},{2,18},{10... | collective-permute-start | bytes 442376 | tf_op jit(solution)/shard_map/ppermute | solution.py:1275
  260.6 16.0 %collective-permute-start.14 = (bf16[192,512]{1,0:T(8,128)(2,1)S(1)}, bf16[192,512]{1,0:T(8,128)(2,1)S(1)}, u32[]{:S(2)}, u32[]{:S(2)}) collective-permute-start(bf16[192,512]{1,0:T(8,128)(2,1)S(1)} %add_convert_fusion.1), channel_id=1, source_target_pairs={{0,4},{1,5},{2,6},{3,7},{4,0},{5,1},{6,2},{7,3},{8,12},{9,13},{10,... | collective-permute-start | bytes 589832 | tf_op jit(solution)/shard_map/ppermute | solution.py:1275
  262.3 39.3 %copy-start.25 = (s32[2]{0:T(128)S(1)}, s32[2]{0:T(128)}, u32[]{:S(2)}) copy-start(s32[2]{0:T(128)} %pad_add_fusion.1.bits_ref) | copy-start | bytes 28
  263.3 17.5 %collective-permute-start.10 = (bf16[192,512]{1,0:T(8,128)(2,1)S(1)}, bf16[192,512]{1,0:T(8,128)(2,1)S(1)}, u32[]{:S(2)}, u32[]{:S(2)}) collective-permute-start(bf16[192,512]{1,0:T(8,128)(2,1)S(1)} %add_convert_fusion.3), channel_id=1, source_target_pairs={{0,4},{1,5},{2,6},{3,7},{4,0},{5,1},{6,2},{7,3},{8,12},{9,13},{10,... | collective-permute-start | bytes 589832 | tf_op jit(solution)/shard_map/ppermute | solution.py:1275
  276.6 8.3 %collective-permute-start.15 = (bf16[192,512]{1,0:T(8,128)(2,1)S(1)}, bf16[192,512]{1,0:T(8,128)(2,1)S(1)}, u32[]{:S(2)}, u32[]{:S(2)}) collective-permute-start(bf16[192,512]{1,0:T(8,128)(2,1)S(1)} %add_convert_fusion.refs_2_), channel_id=1, source_target_pairs={{0,2},{1,3},{2,0},{3,1},{4,6},{5,7},{6,4},{7,5},{8,10},{9,11},{10,... | collective-permute-start | bytes 589832 | tf_op jit(solution)/shard_map/ppermute | solution.py:1275
  282.4 6.8 %collective-permute-start.13 = (bf16[192,512]{1,0:T(8,128)(2,1)S(1)}, bf16[192,512]{1,0:T(8,128)(2,1)S(1)}, u32[]{:S(2)}, u32[]{:S(2)}) collective-permute-start(bf16[192,512]{1,0:T(8,128)(2,1)S(1)} %add_convert_fusion.2.refs_0_), channel_id=1, source_target_pairs={{0,2},{1,3},{2,0},{3,1},{4,6},{5,7},{6,4},{7,5},{8,10},{9,11},{10,... | collective-permute-start | bytes 589832 | tf_op jit(solution)/shard_map/ppermute | solution.py:1275
  290.3 10.1 %collective-permute-start.16 = (bf16[384,512]{1,0:T(8,128)(2,1)S(1)}, bf16[384,512]{1,0:T(8,128)(2,1)S(1)}, u32[]{:S(2)}, u32[]{:S(2)}) collective-permute-start(bf16[384,512]{1,0:T(8,128)(2,1)S(1)} %get-tuple-element.145.refs_0_), channel_id=1, source_target_pairs={{0,1},{1,0},{2,3},{3,2},{4,5},{5,4},{6,7},{7,6},{8,9},{9,8},{10,11... | collective-permute-start | bytes 1179656 | tf_op jit(solution)/shard_map/ppermute | solution.py:1275
  291.8 9.8 %collective-permute-start.17 = (bf16[384,512]{1,0:T(8,128)(2,1)S(1)}, bf16[384,512]{1,0:T(8,128)(2,1)S(1)}, u32[]{:S(2)}, u32[]{:S(2)}) collective-permute-start(bf16[384,512]{1,0:T(8,128)(2,1)S(1)} %get-tuple-element.146.refs_2_), channel_id=1, source_target_pairs={{0,16},{8,24},{16,0},{24,8},{1,17},{9,25},{17,1},{25,9},{2,18},{10... | collective-permute-start | bytes 1179656 | tf_op jit(solution)/shard_map/ppermute | solution.py:1275
  303.0 17.5 %collective-permute-start.18 = (bf16[768,512]{1,0:T(8,128)(2,1)S(1)}, bf16[768,512]{1,0:T(8,128)(2,1)}, u32[]{:S(2)}, u32[]{:S(2)}) collective-permute-start(bf16[768,512]{1,0:T(8,128)(2,1)S(1)} %get-tuple-element.147.refs_0_), channel_id=1, source_target_pairs={{0,16},{8,24},{16,0},{24,8},{1,17},{9,25},{17,1},{25,9},{2,18},{10... | collective-permute-start | bytes 2359304 | tf_op jit(solution)/shard_map/ppermute | solution.py:1275
  303.7 17.1 %collective-permute-start.19 = (bf16[768,512]{1,0:T(8,128)(2,1)S(1)}, bf16[768,512]{1,0:T(8,128)(2,1)}, u32[]{:S(2)}, u32[]{:S(2)}) collective-permute-start(bf16[768,512]{1,0:T(8,128)(2,1)S(1)} %get-tuple-element.148.refs_2_), channel_id=1, source_target_pairs={{0,1},{1,0},{2,3},{3,2},{4,5},{5,4},{6,7},{7,6},{8,9},{9,8},{10,11... | collective-permute-start | bytes 2359304 | tf_op jit(solution)/shard_map/ppermute | solution.py:1275
  305.7 15.1 %copy-start.24 = (s32[2]{0:T(128)S(1)}, s32[2]{0:T(128)}, u32[]{:S(2)}) copy-start(s32[2]{0:T(128)} %pad_add_fusion.bits_ref) | copy-start | bytes 28
  324.6 5.7 %collective-permute-start.20 = (bf16[3072,512]{1,0:T(8,128)(2,1)S(1)}, bf16[3072,512]{1,0:T(8,128)(2,1)S(1)}, u32[]{:S(2)}, u32[]{:S(2)}) collective-permute-start(bf16[3072,512]{1,0:T(8,128)(2,1)S(1)} %double_step.5.values_ref), channel_id=1, source_target_pairs={{0,8},{8,0},{16,24},{24,16},{1,9},{9,1},{17,25},{25,17},{2,10},{10... | collective-permute-start | bytes 9437192 | tf_op jit(solution)/shard_map/ppermute | solution.py:1275
  330.3 3.5 %slice-start = ((f32[72,512]{1,0:T(8,128)}), f32[1,512]{1,0:T(1,128)S(1)}, s32[]{:S(2)}) async-start(f32[72,512]{1,0:T(8,128)} %add.50.refs_1_), calls=%async_computation.5 | async-start | bytes 4096 | tf_op jit(solution)/shard_map/slice | solution.py:1766
  330.3 3.5 %copy-start.37 = (bf16[512]{0:T(512)(128)(2,1)S(1)}, bf16[512]{0:T(512)(128)(2,1)}, u32[]{:S(2)}) copy-start(bf16[512]{0:T(512)(128)(2,1)} %param.19) | copy-start | bytes 3076
  330.3 3.5 %copy-start.39 = (bf16[512]{0:T(512)(128)(2,1)S(1)}, bf16[512]{0:T(512)(128)(2,1)}, u32[]{:S(2)}) copy-start(bf16[512]{0:T(512)(128)(2,1)} %param.23) | copy-start | bytes 3076
  (18 other events, 26.6 us)
